TPU v7x, 256 devices: a whole 4x4x8 slice. The times are simulated.
256 devices in a mesh: row: 64 (over y, x, z_hi, core), rep: 4 (over z_lo).
Axes of the slice: x: 4, y: 4, z: 8 (z_hi: 2, z_lo: 4; z = z_hi * 4 + z_lo), core: 2. Of those that a mesh axis runs over, the one named last changes fastest.
Arguments:
- features: bfloat16 [65536, 128], P(('row', 'rep')), may hold values from -6 to 6
- adjacency: bfloat16 [64, 4, 256, 128, 128], P('row', 'rep'), may hold values from -0.046875 to 0.046875
- block_list: int32 [64, 4, 64, 4, 3], P('row', 'rep'), may hold values from 0 to 255, as said below
- block_counts: int32 [64, 4, 64], P('row', 'rep'), may hold values from 2 to 4
- weight: bfloat16 [128, 256], replicated, may hold values from -0.5 to 0.5
- cotangent: bfloat16 [65536, 256], P(('row', 'rep')), may hold values from -6 to 6
Outputs:
- activations: bfloat16 [65536, 256], P(('row', 'rep'))
- feature_grad: bfloat16 [65536, 128], P(('row', 'rep'))
- weight_grad: float32 [128, 256], replicated
Inputs may be any that keep to these rules, and one draw needn't show every extreme that they name: `block_list`: entry 0 is a block row 0 to 7, entry 1 a block 0 to 1, entry 2 a storage slot; the storage slots of one device are each named once.
All inputs are finite; a program needn't handle non-finite values.
Results may differ from a plain program's by a relative error of at most 0.02.
Values may be sent and summed in bfloat16 or wider, within the bound.
No kernel may reach another device: no remote copies, remote signals or barrier semaphores. Data moves between devices by JAX's collectives and lax.ppermute only.
A program may use at most 64 MiB of HBM per device.

v0:
```python
import math

import jax
import jax.numpy as jnp
from jax import lax
from jax.sharding import PartitionSpec as P


def forward_rows(stored, slot_lists, alive_slots, source, brows_n):
    sections = slot_lists.shape[0]
    group_size = math.gcd(sections, 8)
    block_size = stored.shape[1]
    in_width = source.shape[3]

    def advance(running, group_index):
        first_section = group_index * group_size
        slot_list = lax.dynamic_slice_in_dim(slot_lists, first_section, group_size, 0)
        alive_group = lax.dynamic_slice_in_dim(alive_slots, first_section, group_size, 0)
        section_index = first_section + jnp.arange(group_size)[:, None]
        picked = source[section_index, slot_list[..., 1]]
        blocks = stored[slot_list[..., 2]]
        products = jnp.einsum("gkab,gkbc->gkac", blocks, picked, preferred_element_type=jnp.float32)
        placing = (slot_list[..., 0][..., None] == jnp.arange(brows_n)[None, None, :]).astype(
            jnp.float32
        ) * alive_group[..., None]
        return (running + jnp.einsum("gkr,gkac->rac", placing, products), None)

    start_value = jnp.zeros((brows_n, block_size, in_width), jnp.float32)
    result, _ = lax.scan(advance, start_value, jnp.arange(sections // group_size))
    return result


def backward_columns(stored, slot_lists, alive_slots, value_rows, own_blocks):
    sections = slot_lists.shape[0]
    group_size = math.gcd(sections, 8)
    block_size = stored.shape[1]
    in_width = value_rows.shape[2]

    def one_group(group_index):
        first_section = group_index * group_size
        slot_list = lax.dynamic_slice_in_dim(slot_lists, first_section, group_size, 0)
        alive_group = lax.dynamic_slice_in_dim(alive_slots, first_section, group_size, 0)
        picked = value_rows[slot_list[..., 0]]
        blocks = stored[slot_list[..., 2]]
        products = jnp.einsum("gkba,gkbc->gkac", blocks, picked, preferred_element_type=jnp.float32)
        placing = (slot_list[..., 1][..., None] == jnp.arange(own_blocks)[None, None, :]).astype(
            jnp.float32
        ) * alive_group[..., None]
        return jnp.einsum("gkx,gkac->gxac", placing, products)

    result = lax.map(one_group, jnp.arange(sections // group_size))
    return result.reshape(sections, own_blocks, block_size, in_width)


def per_device(features, adjacency, block_list, block_counts, weight, cotangent):
    reps_n = lax.axis_size("rep")
    rows_n = lax.axis_size("row")
    stored = adjacency[0, 0]
    slot_lists = block_list[0, 0]
    block_tally = block_counts[0, 0]
    sections = slot_lists.shape[0]
    slot_count = slot_lists.shape[1]
    block_size = stored.shape[1]
    in_width = features.shape[1]
    own_rows = features.shape[0]
    own_blocks = own_rows // block_size
    brows_n = reps_n * own_blocks
    alive_slots = (jnp.arange(slot_count)[None, :] < block_tally[:, None]).astype(jnp.float32)
    gathered = lax.all_gather(features, "row", axis=0, tiled=True).reshape(
        sections, own_blocks, block_size, in_width
    )
    partial_value = forward_rows(stored, slot_lists, alive_slots, gathered, brows_n).reshape(
        brows_n * block_size, in_width
    )
    scaling = float(rows_n * reps_n * own_rows) ** (-0.5)
    summed = lax.psum(partial_value.astype(jnp.bfloat16), "rep")
    cotangent_all = lax.all_gather(cotangent, "rep", axis=0, tiled=True)
    hidden = jnp.dot(summed, weight, preferred_element_type=jnp.float32)
    squash = jax.nn.sigmoid(hidden)
    output_all = (hidden * squash).astype(jnp.bfloat16)
    slope = (cotangent_all.astype(jnp.float32) * squash * (1.0 + hidden * (1.0 - squash))).astype(
        jnp.bfloat16
    )
    values_all = jnp.dot(slope, weight.T, preferred_element_type=jnp.float32).astype(jnp.bfloat16)
    offset = lax.axis_index("rep") * own_rows
    output = lax.dynamic_slice_in_dim(output_all, offset, own_rows, 0)
    own_pooled = lax.dynamic_slice_in_dim(summed, offset, own_rows, 0)
    own_slope = lax.dynamic_slice_in_dim(slope, offset, own_rows, 0)
    grad_term = jnp.einsum("na,nh->ah", own_pooled, own_slope, preferred_element_type=jnp.float32)
    weight_grad = lax.psum(grad_term, ("row", "rep")) * scaling
    value_rows = values_all.reshape(brows_n, block_size, in_width)
    number = own_rows * lax.axis_size("row") // own_rows
    result = backward_columns(stored, slot_lists, alive_slots, value_rows, own_blocks)
    gradient = lax.psum_scatter(
        result.reshape(number * own_rows, in_width), "row", scatter_dimension=0, tiled=True
    )
    return (output, gradient.astype(jnp.bfloat16), weight_grad)


def solution(mesh):
    in_specs = (
        P(("row", "rep"), None),
        P("row", "rep", None, None, None),
        P("row", "rep", None, None, None),
        P("row", "rep", None),
        P(),
        P(("row", "rep"), None),
    )
    out_specs = (P(("row", "rep"), None), P(("row", "rep"), None), P())
    return jax.shard_map(
        per_device, mesh=mesh, in_specs=in_specs, out_specs=out_specs, check_vma=False
    )
```

profile of v0, /device:TPU:1, one launch (start us, length us, event | category | flops | bytes accessed | tf_op | source)
XLA Modules:
  0.0 964.7 jit_solution(16702301350735993472)
XLA Ops:
  10.1 98.6 %all-gather.2.cloned.1.call-done = bf16[16384,128]{1,0:T(8,128)(2,1)} async-done(((bf16[256,128]{1,0:T(8,128)(2,1)}), bf16[16384,128]{1,0:T(8,128)(2,1)}) %all-gather.2.cloned.1.call-update) | async-done | bytes 4194320 | tf_op jit(solution)/shard_map/all_gather | solution.py:69
  108.7 99.5 %while.22 = (s32[]{:T(128)}, f32[8,128,128]{2,0,1:T(8,128)}, s32[8]{0:T(128)S(1)}, s32[64,4,3]{1,0,2:T(8,128)}, bf16[64,4]{0,1:T(4,128)(2,1)S(1)}, /*index=5*/bf...) while((s32[]{:T(128)}, f32[8,128,128]{2,0,1:T(8,128)}, ...), condition=%wide.region_1.2_spmd.clone, body=%wide.region_0.1_spmd.clone.sunk | while | flops 142870352 | bytes 9443949 | solution.py:29
  110.8 4.1 gather_fusion.2
  115.1 2.9 gather_fusion.3
  122.4 4.1 gather_fusion.2
  134.9 4.1 gather_fusion.2
  147.5 4.1 gather_fusion.2
  160.1 4.1 gather_fusion.2
  172.7 4.1 gather_fusion.2
  185.2 4.1 gather_fusion.2
  197.8 4.1 gather_fusion.2
  210.2 15.3 %all_gather.7 = bf16[1024,256]{1,0:T(8,128)(2,1)S(1)} all-gather(bf16[256,256]{1,0:T(8,128)(2,1)S(1)} %copy-done.1), channel_id=1, replica_groups=mesh['row'=64,'rep'=4] {'rep'}, dimensions={0}, use_global_device_ids=true | all-gather | bytes 655360 | tf_op jit(solution)/shard_map/all_gather | solution.py:77
  225.6 26.2 %all-reduce.3.cloned.1.call-done = bf16[1024,128]{1,0:T(8,128)(2,1)} async-done(((bf16[1024,128]{1,0:T(8,128)(2,1)}), bf16[1024,128]{1,0:T(8,128)(2,1)}) %all-reduce.3.cloned.1.call-update) | async-done | bytes 262160 | tf_op jit(solution)/shard_map/psum | solution.py:76
  256.6 78.5 %while.21 = (s32[]{:T(128)}, f32[8,8,2,128,128]{4,3,2,1,0:T(8,128)}, s32[8]{0:T(128)S(1)}, s32[64,4,3]{1,0,2:T(8,128)}, bf16[64,4]{0,1:T(4,128)(2,1)S(1)}, /*ind...) while((s32[]{:T(128)}, ...), condition=%wide.region_4.5_spmd, body=%wide.region_3.4_spmd.sunk | while | flops 136317248 | bytes 11545503 | solution.py:51
  258.7 4.1 gather_fusion
  268.5 4.2 gather_fusion
  278.3 4.2 gather_fusion
  288.1 4.1 gather_fusion
  297.9 4.2 gather_fusion
  307.7 4.2 gather_fusion
  317.6 4.1 gather_fusion
  327.4 4.1 gather_fusion
  336.9 163.5 %all-reduce.5.cloned.1.call-done = f32[128,256]{1,0:T(8,128)} async-done(((f32[128,256]{1,0:T(8,128)}), f32[128,256]{1,0:T(8,128)}) %all-reduce.5.cloned.1.call-update) | async-done | bytes 131088 | tf_op jit(solution)/shard_map/psum | solution.py:90
  502.0 454.7 %reduce-scatter.2.cloned.1.call-done = f32[256,128]{1,0:T(8,128)} async-done(((f32[16384,128]{1,0:T(8,128)}), f32[256,128]{1,0:T(8,128)}) %reduce-scatter.2.cloned.1.call-update) | async-done | bytes 131088 | tf_op jit(solution)/shard_map/reduce_scatter | solution.py:94
  (208 shorter events, 112.5 us)
Async XLA Ops:
  7.2 244.6 %copy-start = (bf16[128,256]{1,0:T(8,128)(2,1)S(1)}, bf16[128,256]{1,0:T(8,128)(2,1)}, u32[]{:S(2)}) copy-start(bf16[128,256]{1,0:T(8,128)(2,1)} %param.14) | copy-start | bytes 196612
  7.2 101.5 %all-gather.2.cloned.1.call-start = ((), (), s32[]{:S(2)}) async-start(), calls=%async_computation.1 | async-start | bytes 4259840 | tf_op jit(solution)/shard_map/all_gather | solution.py:69
  7.9 243.8 %all-reduce.3.cloned.1.call-start = ((), (), s32[]{:S(2)}) async-start(), calls=%async_computation.2 | async-start | bytes 524288 | tf_op jit(solution)/shard_map/psum | solution.py:76
  108.7 101.5 %copy-start.1 = (bf16[256,256]{1,0:T(8,128)(2,1)S(1)}, bf16[256,256]{1,0:T(8,128)(2,1)}, u32[]{:S(2)}) copy-start(bf16[256,256]{1,0:T(8,128)(2,1)} %param.15) | copy-start | bytes 393220
  210.2 290.2 %all-reduce.5.cloned.1.call-start = ((), (), s32[]{:S(2)}) async-start(), calls=%async_computation.4 | async-start | bytes 262144 | tf_op jit(solution)/shard_map/psum | solution.py:90
  256.5 700.1 %reduce-scatter.2.cloned.1.call-start = ((), (), s32[]{:S(2)}) async-start(), calls=%async_computation.3 | async-start | bytes 8519680 | tf_op jit(solution)/shard_map/reduce_scatter | solution.py:94
Sparse Core Ops, SparseCore 0:
  11.5 97.1 all-gather.1
  210.3 41.3 all-reduce.2
  258.7 241.6 all-reduce.4
  502.9 453.6 reduce-scatter.1
where the time goes:
time: 974 us; the launch traced here: 965 us
  waiting for transfers between devices  744 us (76%)
  local copies, waits for them, and re-layouts  123 us (13%)
  matrix products  39.9 us (4%)
  other arithmetic  18 us (2%)
  blocking collectives  15.3 us (2%)
  between operations  13.8 us (1%)
  loops' own time  10.8 us (1%)
    reduce_scatter x1, waiting for transfers between devices, per_device(): lax.psum_scatter(result.reshape(number * own_rows, in_width), 'row', scat...  455 us
    psum x1, waiting for transfers between devices, per_device(): weight_grad = lax.psum(grad_term, ('row', 'rep')) * scaling  164 us
    all_gather x1, waiting for transfers between devices, per_device(): lax.all_gather(features, 'row', axis=0, tiled=True)  98.6 us
    gather x8, local copies, waits for them, and re-layouts, one_group(): blocks = stored[slot_list[..., 2]]  33.2 us
    gather x8, local copies, waits for them, and re-layouts, advance(): blocks = stored[slot_list[..., 2]]  33 us
    psum x1, waiting for transfers between devices, per_device(): summed = lax.psum(partial_value.astype(jnp.bfloat16), 'rep')  26.2 us
    gather x8, local copies, waits for them, and re-layouts, advance(): picked = source[section_index, slot_list[..., 1]]  23.5 us
    dot_general x8, matrix products, advance(): return (running + jnp.einsum('gkr,gkac->rac', placing, products), None)  20.3 us
  transfers between devices with their start and end apart: 4, of which 4 were waited for; matrix products, arithmetic and copies ran while one was open for 8% of the time, Pallas kernels for 0%

commit v1 on v0

v1 whole, which is shorter than its diff:
```python
import functools

import jax
import jax.numpy as jnp
import numpy as np
from jax import lax
from jax.experimental import pallas as pl
from jax.experimental.pallas import tpu as pltpu
from jax.sharding import PartitionSpec as P

B = 128
SLOTS = 4
BROWS = 8
SECTIONS = 64
ROWS = 2 * B
PIECE = 64
SPLIT = 3 * PIECE
COST = B * B * 8
F32 = jnp.float32
BF16 = jnp.bfloat16
VMEM = pl.BlockSpec(memory_space=pltpu.VMEM)
SMEM = pl.BlockSpec(memory_space=pltpu.SMEM)

COUNTS = SECTIONS * SLOTS * 3
FORWARD_ORDER = COUNTS + SECTIONS
BACKWARD_ORDER = FORWARD_ORDER + SECTIONS
PLACE = BACKWARD_ORDER + SECTIONS


def group(flip, e, ds=(0, 1, 2, 3)):
    return [(flip, e, d, u) for d in ds for u in range(2)]


FORWARD_GROUPS = [
    [group(0, 0)],
    [group(0, 1), group(0, 3)],
    [group(1, 0), group(1, 1), group(1, 3)],
    [group(0, 2), group(1, 2)],
]
BACKWARD_GROUPS = [group(1, 2), group(1, 1) + group(1, 3), group(0, 2), group(1, 0), group(0, 1) + group(0, 3), group(0, 0)]


def section_order(r, entries, sign):
    flip, e, d, u = (np.array(column, np.int32) for column in zip(*entries))
    y, x, z, core = r // 16, (r // 4) % 4, (r // 2) % 2, r % 2
    role = core ^ flip
    dy, dx = jnp.where(role == 0, e, d), jnp.where(role == 0, d, e)
    return ((y + sign * dy) & 3) * 16 + ((x + sign * dx) & 3) * 4 + (z ^ role) * 2 + u


def at(y, x, z, core):
    return (y % 4) * 16 + (x % 4) * 4 + z * 2 + core


def row_permute(array, target):
    pairs = []
    for r in range(64):
        to = target(r // 16, (r // 4) % 4, (r // 2) % 2, r % 2)
        if to is not None:
            pairs.append((r, to))
    return lax.ppermute(array, "row", pairs)


def small_axis(array, d):
    return row_permute(array, lambda y, x, z, c: at(y + d * c, x + d * (1 - c), z, c))


def large_axis(array, e):
    return row_permute(array, lambda y, x, z, c: at(y + e * (1 - c), x + e * c, z, c))


def sibling(array):
    return row_permute(array, lambda y, x, z, c: at(y, x, z, 1 - c))


def cross(array, forwards):
    if forwards:
        return row_permute(array, lambda y, x, z, c: at(y, x, z, 0) if c else at(y, x, 1 - z, 1))
    return row_permute(array, lambda y, x, z, c: at(y, x, 1 - z, 0) if c else at(y, x, z, 1))


def other_z(array):
    return row_permute(array, lambda y, x, z, c: at(y, x, 1 - z, 1) if c else None)


def turn(array, d):
    return lax.ppermute(array, "rep", [(q, (q + d) % 4) for q in range(4)])


def params():
    return pltpu.CompilerParams(vmem_limit_bytes=20 * 1024 * 1024)


def cost(slots):
    return pl.CostEstimate(flops=slots * COST, bytes_accessed=slots * COST, transcendentals=0)


def small_cost(size):
    return pl.CostEstimate(flops=size // 64, bytes_accessed=size // 64, transcendentals=0)


def touch_kernel(meta, stored, out):
    out[...] = stored[0, 0:16, :].astype(F32)


def touch(meta, stored):
    return pl.pallas_call(
        touch_kernel,
        out_shape=jax.ShapeDtypeStruct((16, B), F32),
        in_specs=[SMEM, VMEM],
        out_specs=VMEM,
        compiler_params=params(),
        cost_estimate=small_cost(1 << 10),
        name="touch_blocks",
    )(meta, stored)


def pair_up_kernel(core, own, near, far, out):
    first = core[0] == 0
    out[0:ROWS] = jnp.where(first, own[...], near[...])
    out[ROWS : 2 * ROWS] = jnp.where(first, near[...], far[...])


def pair_up(core, own, near, far):
    return pl.pallas_call(
        pair_up_kernel,
        out_shape=jax.ShapeDtypeStruct((2 * ROWS, B), BF16),
        in_specs=[SMEM] + [VMEM] * 3,
        out_specs=VMEM,
        compiler_params=params(),
        cost_estimate=small_cost(1 << 16),
        name="pair_up",
    )(core, own, near, far)


def place_kernel(counts, parts, *refs):
    sources, outs = refs[: len(counts)], refs[-len(parts) :]
    for out, pieces in zip(outs, parts):
        row = 0
        for source, start, size in pieces:
            out[row : row + size * ROWS] = sources[source][start * ROWS : (start + size) * ROWS]
            row += size * ROWS


def place(name, parts, sources, after=()):
    shapes = [jax.ShapeDtypeStruct((sum(p[2] for p in pieces) * ROWS, B), BF16) for pieces in parts]
    args = [*sources, *after]
    return pl.pallas_call(
        functools.partial(place_kernel, tuple(range(len(sources))), parts),
        out_shape=shapes,
        in_specs=[VMEM] * len(args),
        out_specs=[VMEM] * len(shapes),
        compiler_params=params(),
        cost_estimate=small_cost(1 << 18),
        name=name,
    )(*args)


STEP = 4


def forward_kernel(first_section, sizes, first, last, after, *refs):
    meta, stored = refs[:2]
    chunk_refs = refs[2 : 2 + len(sizes)]
    refs = refs[2 + len(sizes) + after :]
    if first:
        out_refs, acc = refs[:-1], refs[-1]
        acc[...] = jnp.zeros_like(acc)
    else:
        out_refs, acc = refs[1:-1], refs[-1]
        acc[0:BROWS] = refs[0][...]
    begin = first_section
    for size, chunk_ref in zip(sizes, chunk_refs):

        def step(g, carry, begin=begin, chunk_ref=chunk_ref):
            products, places = [], []
            for n in range(STEP):
                sid = meta[FORWARD_ORDER + begin + g * STEP + n]
                count = meta[COUNTS + sid]
                for k in range(SLOTS):
                    base = sid * (SLOTS * 3) + 3 * k
                    start = pl.multiple_of((g * STEP + n) * ROWS + meta[base + 1] * B, B)
                    source = chunk_ref[pl.ds(start, B)]
                    products.append(jnp.dot(stored[meta[base + 2]], source, preferred_element_type=F32))
                    places.append(jnp.where(k < count, meta[base], BROWS))
            for product, place in zip(products, places):
                acc[place] += product
            return carry

        lax.fori_loop(0, size // STEP, step, 0)
        begin += size
    if not last:
        out_refs[0][...] = acc[0:BROWS]
        return
    rep = meta[PLACE]
    for d in range(4):
        for b in range(2):
            piece = acc[lax.rem(rep + d, 4) * 2 + b]
            out_refs[d][b * B : (b + 1) * B] = piece.astype(out_refs[d].dtype)


def forward(meta, stored, first_section, chunk_list, start, last, after=()):
    sizes = tuple(chunk.shape[0] // ROWS for chunk in chunk_list)
    first = start is None
    if last:
        out_shape = [jax.ShapeDtypeStruct((2 * B, B), F32)] + [jax.ShapeDtypeStruct((2 * B, B), BF16)] * 3
    else:
        out_shape = [jax.ShapeDtypeStruct((BROWS, B, B), F32)]
    args = [meta, stored, *chunk_list, *after] + ([] if first else [start])
    return pl.pallas_call(
        functools.partial(forward_kernel, first_section, sizes, first, last, len(after)),
        out_shape=out_shape,
        in_specs=[SMEM] + [VMEM] * (len(args) - 1),
        out_specs=[VMEM] * len(out_shape),
        scratch_shapes=[pltpu.VMEM((BROWS + 1, B, B), F32)],
        compiler_params=params(),
        cost_estimate=cost(sum(sizes) * SLOTS),
        name="forward_slots",
    )(*args)


def middle_kernel(meta, own, p1, p2, p3, weight, cot, act, values, m1, m2, m3, w0):
    pooled = (own[...] + p1[...].astype(F32) + p2[...].astype(F32) + p3[...].astype(F32)).astype(BF16)
    hidden = jnp.dot(pooled, weight[...], preferred_element_type=F32)
    squash = jax.nn.sigmoid(hidden)
    act[...] = (hidden * squash).astype(BF16)
    slope = (cot[...].astype(F32) * squash * (1.0 + hidden * (1.0 - squash))).astype(BF16)
    values_t = lax.dot_general(weight[...], slope, (((1,), (1,)), ((), ())), preferred_element_type=F32)
    values_t = values_t.astype(BF16)
    for out in (values, m1, m2, m3):
        out[0:B] = values_t[:, :B]
        out[B:ROWS] = values_t[:, B:]
    term = lax.dot_general(pooled, slope, (((0,), (0,)), ((), ())), preferred_element_type=F32)
    rep = meta[PLACE]
    for q in range(4):
        piece = jnp.concatenate([term[q * 32 : (q + 1) * 32, :B], term[q * 32 : (q + 1) * 32, B:]], axis=0)

        @pl.when(rep == q)
        def _(piece=piece):
            w0[...] = piece

        for d, out in enumerate((m1, m2, m3)):

            @pl.when(lax.rem(rep + d + 1, 4) == q)
            def _(out=out, piece=piece):
                out[ROWS : ROWS + PIECE] = piece.astype(BF16)


def middle(meta, own, pieces, weight, cot):
    return pl.pallas_call(
        middle_kernel,
        out_shape=[jax.ShapeDtypeStruct((2 * B, 2 * B), BF16), jax.ShapeDtypeStruct((ROWS, B), BF16)]
        + [jax.ShapeDtypeStruct((ROWS + PIECE, B), BF16)] * 3
        + [jax.ShapeDtypeStruct((PIECE, B), F32)],
        in_specs=[SMEM] + [VMEM] * 6,
        out_specs=[VMEM] * 6,
        compiler_params=params(),
        cost_estimate=small_cost(1 << 16),
        name="middle_rows",
    )(meta, own, *pieces, weight, cot)


def split(total, out_ref, row):
    rest = total
    for n in range(3):
        part = rest.astype(BF16)
        out_ref[row + n * PIECE : row + (n + 1) * PIECE] = part
        rest = rest - part.astype(F32)


def joined(ref, row):
    parts = [ref[row + n * PIECE : row + (n + 1) * PIECE].astype(F32) for n in range(3)]
    return (parts[2] + parts[1]) + parts[0]


def gather_terms(extra, outs, extra_outs):
    total = extra[0][...]
    for ref in extra[1:]:
        total = total + ref[ROWS : ROWS + PIECE].astype(F32)
    split(total, outs[0], 8 * ROWS)
    extra_outs[0][...] = total


def sibling_terms(extra, outs, extra_outs):
    total = extra[0][...] + joined(extra[1], 8 * ROWS)
    split(total, outs[0], 4 * ROWS)
    extra_outs[0][...] = total
    extra_outs[1][...] = extra[2][...]


def spread_terms(extra, outs, extra_outs):
    half_1, half_3, own, passed = extra
    extra_outs[0][...] = passed[...]
    first, second = slice(0, 4 * ROWS), slice(4 * ROWS, 8 * ROWS)
    outs[0][first] = (outs[0][first].astype(F32) + half_1[first].astype(F32)).astype(BF16)
    outs[1][second] = (outs[1][second].astype(F32) + half_3[...].astype(F32)).astype(BF16)
    for out in outs:
        split(own[...], out, 8 * ROWS)
    outs[0][8 * ROWS + SPLIT :] = half_1[4 * ROWS :]


def backward_kernel(first_section, sizes, added, extras, finish, *refs):
    meta, stored = refs[:2]
    value_refs, refs = refs[2:6], refs[6:]
    if added:
        add_ref, refs = refs[0], refs[1:]
    extra, refs = refs[:extras], refs[extras:]
    out_refs, extra_outs, values = refs[: len(sizes)], refs[len(sizes) : -1], refs[-1]
    rep = meta[PLACE]
    for d in range(4):
        for b in range(2):
            values[lax.rem(rep + 4 - d, 4) * 2 + b] = value_refs[d][b * B : (b + 1) * B]
    values[BROWS] = jnp.zeros((B, B), BF16)

    begin = 0
    for size, out_ref in zip(sizes, out_refs):

        def step(g, carry, begin=begin, out_ref=out_ref):
            for m in range(STEP):
                n = g * STEP + m
                sid = meta[BACKWARD_ORDER + first_section + begin + n]
                count = meta[COUNTS + sid]
                base = sid * (SLOTS * 3)
                rows = []
                for j in range(2):
                    columns = []
                    for k in range(SLOTS):
                        live = (k < count) & (meta[base + 3 * k + 1] == j)
                        columns.append(values[jnp.where(live, meta[base + 3 * k], BROWS)])
                    rows.append(jnp.concatenate(columns, axis=1))
                left = jnp.concatenate(rows, axis=0)
                right = jnp.concatenate([stored[meta[base + 3 * k + 2]] for k in range(SLOTS)], axis=0)
                result = jnp.dot(left, right, preferred_element_type=F32)
                if added:
                    result = result + add_ref[pl.ds(pl.multiple_of((begin + n) * ROWS, ROWS), ROWS)].astype(F32)
                out_ref[pl.ds(pl.multiple_of(n * ROWS, ROWS), ROWS)] = result.astype(BF16)
            return carry

        lax.fori_loop(0, size // STEP, step, 0)
        begin += size
    if finish is not None:
        finish(extra, out_refs, extra_outs)


def backward(meta, stored, values, first_section, sizes, add=None, extra=(), finish=None, tails=None, extra_out=()):
    added = add is not None
    args = [meta, stored, *values] + ([add] if added else []) + list(extra)
    tails = tails or (0,) * len(sizes)
    shapes = [jax.ShapeDtypeStruct((size * ROWS + tail, B), BF16) for size, tail in zip(sizes, tails)]
    shapes += [jax.ShapeDtypeStruct(a.shape, a.dtype) for a in extra_out]
    return pl.pallas_call(
        functools.partial(backward_kernel, first_section, sizes, added, len(extra), finish),
        out_shape=shapes,
        in_specs=[SMEM] + [VMEM] * (len(args) - 1),
        out_specs=[VMEM] * len(shapes),
        scratch_shapes=[pltpu.VMEM((BROWS + 1, B, B), BF16)],
        compiler_params=params(),
        cost_estimate=cost(sum(sizes) * SLOTS),
        name="backward_slots",
    )(*args)


def sum_kernel(a, b, c, own, t0, t1, t2, t3, w):
    row = 8 * ROWS
    total = (own[...] + joined(b, row + SPLIT)) + (joined(b, row) + joined(c, row))
    w[...] = total
    for d, out in enumerate((t0, t1, t2, t3)):
        part = slice(2 * ROWS * d, 2 * ROWS * (d + 1))
        group_sum = a[part].astype(F32) + b[part].astype(F32) + c[part].astype(F32)
        out[0 : 2 * ROWS] = group_sum.astype(BF16)
        if d:
            split(total, out, 2 * ROWS)


def sum_groups(*arrays):
    return pl.pallas_call(
        sum_kernel,
        out_shape=[jax.ShapeDtypeStruct((2 * ROWS, B), BF16)]
        + [jax.ShapeDtypeStruct((2 * ROWS + SPLIT, B), BF16)] * 3
        + [jax.ShapeDtypeStruct((PIECE, B), F32)],
        in_specs=[VMEM] * 4,
        out_specs=[VMEM] * 5,
        compiler_params=params(),
        cost_estimate=small_cost(1 << 18),
        name="sum_groups",
    )(*arrays)


def unit_sum(meta, refs, out, flip):
    core = meta[PLACE + 1]
    unit = 1 - core if flip else core
    part = pl.ds(pl.multiple_of(unit * ROWS, ROWS), ROWS)
    total = refs[0][part].astype(F32)
    for ref in refs[1:]:
        total = total + ref[part].astype(F32)
    out[...] = total.astype(BF16)


def mine_kernel(meta, a, b, c, d, own, mine, w):
    unit_sum(meta, (a, b, c, d), mine, False)
    w[...] = (own[...] + joined(c, 2 * ROWS)) + (joined(b, 2 * ROWS) + joined(d, 2 * ROWS))


def sum_mine(meta, *arrays):
    return pl.pallas_call(
        mine_kernel,
        out_shape=[jax.ShapeDtypeStruct((ROWS, B), BF16), jax.ShapeDtypeStruct((PIECE, B), F32)],
        in_specs=[SMEM] + [VMEM] * 5,
        out_specs=[VMEM] * 2,
        compiler_params=params(),
        cost_estimate=small_cost(1 << 17),
        name="sum_mine",
    )(meta, *arrays)


def other_kernel(meta, mine, a, b, c, d, other):
    unit_sum(meta, (a, b, c, d), other, True)


def sum_other(meta, *arrays):
    return pl.pallas_call(
        other_kernel,
        out_shape=jax.ShapeDtypeStruct((ROWS, B), BF16),
        in_specs=[SMEM] + [VMEM] * 5,
        out_specs=VMEM,
        compiler_params=params(),
        cost_estimate=small_cost(1 << 17),
        name="sum_other",
    )(meta, *arrays)


def meet_kernel(meta, mine, far, w, w_z, own, total):
    first = meta[PLACE + 1] == 0
    own[...] = jnp.where(first, mine[...], far[...])
    total[...] = w[...] + w_z[...]


def meet(meta, *arrays):
    return pl.pallas_call(
        meet_kernel,
        out_shape=[jax.ShapeDtypeStruct((ROWS, B), BF16), jax.ShapeDtypeStruct((PIECE, B), F32)],
        in_specs=[SMEM] + [VMEM] * 4,
        out_specs=[VMEM] * 2,
        compiler_params=params(),
        cost_estimate=small_cost(1 << 15),
        name="meet_other_z",
    )(meta, *arrays)


def last_kernel(scaling, meta, own, crossed, w0, w1, w2, w3, out, weight_grad):
    for s in range(2):
        part = slice(s * B, (s + 1) * B)
        out[part] = (own[part].astype(F32) + crossed[part].astype(F32)).T.astype(BF16)
    rep = meta[PLACE]
    for back, piece in enumerate((w0, w1, w2, w3)):
        rows = pl.ds(pl.multiple_of(lax.rem(rep + 4 - back, 4) * 32, 32), 32)
        weight_grad[rows, 0:B] = piece[0:32] * scaling
        weight_grad[rows, B : 2 * B] = piece[32:64] * scaling


def last_sum(meta, scaling, *arrays):
    return pl.pallas_call(
        functools.partial(last_kernel, scaling),
        out_shape=[jax.ShapeDtypeStruct((ROWS, B), BF16), jax.ShapeDtypeStruct((B, 2 * B), F32)],
        in_specs=[SMEM] + [VMEM] * 6,
        out_specs=[VMEM] * 2,
        compiler_params=params(),
        cost_estimate=small_cost(1 << 16),
        name="last_sum",
    )(meta, *arrays)


def per_device(features, adjacency, block_list, block_counts, weight, cotangent):
    stored = adjacency[0, 0]
    r = lax.axis_index("row").astype(jnp.int32)
    rep = lax.axis_index("rep").astype(jnp.int32)
    core = r % 2
    nodes = float(features.shape[0] * 256)

    order = [entry for call in FORWARD_GROUPS for part in call for entry in part]
    back_order = [entry for part in BACKWARD_GROUPS for entry in part]
    meta = jnp.concatenate(
        [
            block_list.reshape(-1),
            block_counts.reshape(-1),
            section_order(r, order, -1),
            section_order(r, back_order, 1),
            jnp.stack([rep, core]),
        ]
    )

    near_unit, far_unit = cross(features, True), other_z(features)
    pair = pair_up(core.reshape(1), features, near_unit, far_unit)
    pairs = [pair] + [small_axis(pair, d) for d in (1, 2, 3)]
    touched = touch(meta, stored)
    (quad,) = place("place_quad", [[(n, 0, 2) for n in range(4)]], pairs, [touched])
    n1, n3 = large_axis(quad, 1), large_axis(quad, 3)
    (acc,) = forward(meta, stored, 0, [quad], None, False)
    parts = [[(0, 0, 8), (1, 0, 8), (2, 0, 8)], [(1, 0, 4)], [(2, 4, 4)]]
    near, h1, h3 = place("place_near", parts, [quad, n1, n3], [acc])
    f1, f3 = large_axis(h1, 1), large_axis(h3, 3)
    near_s = sibling(near)
    (acc,) = forward(meta, stored, 8, [n1, n3], acc, False, after=[h1])
    (far,) = place("place_far", [[(0, 0, 4), (1, 0, 4)]], [f1, f3], [acc])
    far_s = sibling(far)
    (acc,) = forward(meta, stored, 24, [near_s], acc, False)
    own_part, *pieces = forward(meta, stored, 48, [far, far_s], acc, True)

    pieces = [turn(piece, d + 1) for d, piece in enumerate(pieces)]
    activations, values, m1, m2, m3, w = middle(meta, own_part, pieces, weight, cotangent)
    messages = [turn(m1, 1), turn(m2, 2), turn(m3, 3)]

    bwd = functools.partial(backward, meta, stored, [values] + messages)
    far_b, w4 = bwd(0, (8,), extra=[w] + messages, finish=gather_terms, tails=(SPLIT,), extra_out=[w])
    far_s = sibling(far_b)
    (near_b,) = bwd(8, (16,), extra=[far_b])
    h1, h3, w8, near_b = bwd(
        24, (4, 4), far_s, extra=[w4, far_s, near_b], finish=sibling_terms, tails=(SPLIT, 0), extra_out=[w, near_b]
    )
    f1, f3, near_s = large_axis(h1, 1), large_axis(h3, 3), sibling(near_b)
    (own_b,) = bwd(32, (8,), extra=[h1])
    g1, g3, own_b = bwd(
        40,
        (8, 8),
        near_s,
        extra=[f1, f3, w8, own_b],
        finish=spread_terms,
        tails=(2 * SPLIT, SPLIT),
        extra_out=[own_b],
    )
    r1, r3, own_s = large_axis(g1, 1), large_axis(g3, 3), sibling(own_b)
    (g0,) = bwd(56, (8,), own_s, extra=[g1])
    t0, t1, t2, t3, w32 = sum_groups(g0, r1, r3, w8)
    sums = [t0, small_axis(t1, 1), small_axis(t2, 2), small_axis(t3, 3)]
    mine, w = sum_mine(meta, *sums, w32)
    far = other_z(mine)
    w_z = row_permute(w, lambda y, x, z, c: at(y, x, 1 - z, c))
    crossed = cross(sum_other(meta, mine, *sums), False)
    own, w = meet(meta, mine, far, w, w_z)
    feature_grad, weight_grad = last_sum(
        meta, nodes ** (-0.5), own, crossed, w, *[turn(w, d) for d in (1, 2, 3)]
    )
    return activations, feature_grad, weight_grad


def solution(mesh):
    in_specs = (
        P(("row", "rep"), None),
        P("row", "rep", None, None, None),
        P("row", "rep", None, None, None),
        P("row", "rep", None),
        P(),
        P(("row", "rep"), None),
    )
    out_specs = (P(("row", "rep"), None), P(("row", "rep"), None), P())
    return jax.shard_map(
        per_device, mesh=mesh, in_specs=in_specs, out_specs=out_specs, check_vma=False
    )
```

time: 974 us -> 130 us (0.13)
  waiting for transfers between devices: 744 us -> 46.1 us
  local copies, waits for them, and re-layouts: 123 us -> 6 us
  starting transfers between devices: 0.16 us -> 51.3 us
  matrix products: 39.9 us -> 0 us
  Pallas kernels: 0 us -> 24.5 us
  other arithmetic: 18 us -> 0.75 us
  blocking collectives: 15.3 us -> 0 us
  between operations: 13.8 us -> 0.99 us
  loops' own time: 10.8 us -> 0 us
    reduce_scatter x1 -> x0, waiting for transfers between devices: 455 us -> none  [per_device(): lax.psum_scatter(result.reshape(number * own_rows, in_width), 'row', scat...]
    psum x2 -> x0, waiting for transfers between devices: 190 us -> none  [the longest x1 164 us: per_device(): weight_grad = lax.psum(grad_term, ('row', 'rep')) * scaling]
    all_gather x1 -> x0, waiting for transfers between devices: 98.6 us -> none  [per_device(): lax.all_gather(features, 'row', axis=0, tiled=True)]
    gather x32 -> x0, local copies, waits for them, and re-layouts: 95.8 us -> none  [the longest x8 33.2 us: one_group(): blocks = stored[slot_list[..., 2]]]
    ppermute x0 -> x33, starting transfers between devices: none -> 51.3 us  [the longest x24 40.6 us: row_permute(): return lax.ppermute(array, 'row', pairs)]
    ppermute x0 -> x33, waiting for transfers between devices: none -> 46.1 us  [the longest x24 30.8 us: row_permute(): return lax.ppermute(array, 'row', pairs)]
    dot_general x35 -> x0, matrix products: 39.9 us -> none  [the longest x8 20.3 us: advance(): return (running + jnp.einsum('gkr,gkac->rac', placing, products), None)]
    pallas_call x0 -> x21, Pallas kernels: none -> 24.5 us  [the longest x6 10.6 us: backward(): pl.pallas_call(functools.partial(backward_kernel, first_section, sizes, a...]
  transfers between devices with their start and end apart: 4 -> 33, of which waited for: 4 -> 21; matrix products, arithmetic and copies ran while one was open for 8% -> 2% of each run, Pallas kernels for 0% -> 10%
where the time goes in v1:
time: 130 us
  starting transfers between devices  51.3 us (39%)
  waiting for transfers between devices  46.1 us (35%)
  Pallas kernels  24.5 us (19%)
  local copies, waits for them, and re-layouts  6 us (5%)
    ppermute x24, starting transfers between devices, row_permute(): return lax.ppermute(array, 'row', pairs)  40.6 us
    ppermute x24, waiting for transfers between devices, row_permute(): return lax.ppermute(array, 'row', pairs)  30.8 us
    ppermute x9, waiting for transfers between devices, turn(): return lax.ppermute(array, 'rep', [(q, (q + d) % 4) for q in range(4)])  15.3 us
    ppermute x9, starting transfers between devices, turn(): return lax.ppermute(array, 'rep', [(q, (q + d) % 4) for q in range(4)])  10.8 us
    pallas_call x6, Pallas kernels, backward(): pl.pallas_call(functools.partial(backward_kernel, first_section, sizes, a...  10.6 us
    pallas_call x4, Pallas kernels, forward(): pl.pallas_call(functools.partial(forward_kernel, first_section, sizes, fi...  7.66 us
    unnamed x11, local copies, waits for them, and re-layouts  5.05 us
  transfers between devices with their start and end apart: 33, of which 21 were waited for; matrix products, arithmetic and copies ran while one was open for 2% of the time, Pallas kernels for 10%

profile of v1, /device:TPU:1, one launch (start us, length us, event | category | flops | bytes accessed | tf_op | source)
XLA Modules:
  0.0 129.8 jit_solution(467511025428729168)
XLA Ops:
  0.6 3.3 %collective-permute-start = (bf16[256,128]{1,0:T(8,128)(2,1)}, bf16[256,128]{1,0:T(8,128)(2,1)S(1)}, u32[]{:S(2)}, u32[]{:S(2)}) collective-permute-start(bf16[256,128]{1,0:T(8,128)(2,1)} %own.1), channel_id=1, source_target_pairs={{0,12},{4,0},{8,4},{12,8},{16,28},{20,16},{24,20},{28,24},{32,44},... | collective-permute-start | bytes 196616 | tf_op jit(solution)/shard_map/ppermute | solution.py:61
  3.9 7.1 %collective-permute-start.1 = (bf16[256,128]{1,0:T(8,128)(2,1)}, bf16[256,128]{1,0:T(8,128)(2,1)S(1)}, u32[]{:S(2)}, u32[]{:S(2)}) collective-permute-start(bf16[256,128]{1,0:T(8,128)(2,1)} %own.1), channel_id=1, source_target_pairs={{4,12},{12,4},{20,28},{28,20},{36,44},{44,36},{52,60},{60,52},{68,... | collective-permute-start | bytes 196616 | tf_op jit(solution)/shard_map/ppermute | solution.py:61
  13.9 2.7 %collective-permute-start.4 = (bf16[512,128]{1,0:T(8,128)(2,1)S(1)}, bf16[512,128]{1,0:T(8,128)(2,1)S(1)}, u32[]{:S(2)}, u32[]{:S(2)}) collective-permute-start(bf16[512,128]{1,0:T(8,128)(2,1)S(1)} %pair_up.1.refs_0_), channel_id=1, source_target_pairs={{0,48},{4,196},{8,56},{12,204},{16,0},{20,212},{24,8},{28,220},{32... | collective-permute-start | bytes 393224 | tf_op jit(solution)/shard_map/ppermute | solution.py:61
  19.2 3.4 %copy-done = bf16[1,1,256,128,128]{4,3,2,1,0:T(8,128)(2,1)S(1)} copy-done((bf16[1,1,256,128,128]{4,3,2,1,0:T(8,128)(2,1)S(1)}, bf16[1,1,256,128,128]{4,3,2,1,0:T(8,128)(2,1)}, u32[]{:S(2)}) %copy-start) | copy-done | bytes 8388632
  23.4 2.6 %collective-permute-start.6 = (bf16[2048,128]{1,0:T(8,128)(2,1)S(1)}, bf16[2048,128]{1,0:T(8,128)(2,1)S(1)}, u32[]{:S(2)}, u32[]{:S(2)}) collective-permute-start(bf16[2048,128]{1,0:T(8,128)(2,1)S(1)} %place_quad.1.refs_2_.refs_0_), channel_id=1, source_target_pairs={{0,192},{4,52},{8,200},{12,60},{16,208},{20,4},{24,216},{28,12},{3... | collective-permute-start | bytes 1572872 | tf_op jit(solution)/shard_map/ppermute | solution.py:61
  27.3 4.8 %collective-permute-done.6.refs_2_.refs_3_ = bf16[2048,128]{1,0:T(8,128)(2,1)S(1)} collective-permute-done((bf16[2048,128]{1,0:T(8,128)(2,1)S(1)}, bf16[2048,128]{1,0:T(8,128)(2,1)S(1)}, u32[]{:S(2)}, u32[]{:S(2)}) %collective-permute-start.6) | collective-permute-done | bytes 524320 | tf_op jit(solution)/shard_map/ppermute | solution.py:61
  32.1 3.4 %collective-permute-done.5.refs_1_.refs_2_ = bf16[2048,128]{1,0:T(8,128)(2,1)S(1)} collective-permute-done((bf16[2048,128]{1,0:T(8,128)(2,1)S(1)}, bf16[2048,128]{1,0:T(8,128)(2,1)S(1)}, u32[]{:S(2)}, u32[]{:S(2)}) %collective-permute-start.5) | collective-permute-done | bytes 524320 | tf_op jit(solution)/shard_map/ppermute | solution.py:61
  39.8 2.1 %collective-permute-done.8.refs_1_ = bf16[1024,128]{1,0:T(8,128)(2,1)S(1)} collective-permute-done((bf16[1024,128]{1,0:T(8,128)(2,1)S(1)}, bf16[1024,128]{1,0:T(8,128)(2,1)S(1)}, u32[]{:S(2)}, u32[]{:S(2)}) %collective-permute-start.8) | collective-permute-done | bytes 262176 | tf_op jit(solution)/shard_map/ppermute | solution.py:61
  41.9 2.6 %collective-permute-done.7.refs_0_ = bf16[1024,128]{1,0:T(8,128)(2,1)S(1)} collective-permute-done((bf16[1024,128]{1,0:T(8,128)(2,1)S(1)}, bf16[1024,128]{1,0:T(8,128)(2,1)S(1)}, u32[]{:S(2)}, u32[]{:S(2)}) %collective-permute-start.7) | collective-permute-done | bytes 262176 | tf_op jit(solution)/shard_map/ppermute | solution.py:61
  45.7 2.5 %forward_slots.6.refs_4_ = f32[8,128,128]{2,1,0:T(8,128)S(1)} custom-call(s32[962]{0:T(1024)S(1)} %concatenate.3.meta.refs_0_, bf16[256,128,128]{2,1,0:T(8,128)(2,1)S(1)} %bitcast.7, bf16[6144,128]{1,0:T(8,128)(2,1)S(1)} %collective-permute-done.10.refs_2_, f32[8,128,128]{2,1,0:T(8,128)S(1)} %forward_slots.5.refs_2_.refs_3_), custom_call_target="tpu_custom_call" | custom-call | flops 12582912 | bytes 12582912 | tf_op jit(solution)/shard_map/forward_slots/pallas_call | solution.py:210
  55.8 3.2 %collective-permute-done.12.p2 = bf16[256,128]{1,0:T(8,128)(2,1)S(1)} collective-permute-done((bf16[256,128]{1,0:T(8,128)(2,1)S(1)}, bf16[256,128]{1,0:T(8,128)(2,1)S(1)}, u32[]{:S(2)}, u32[]{:S(2)}) %collective-permute-start.12) | collective-permute-done | bytes 65568 | tf_op jit(solution)/shard_map/ppermute | solution.py:87
  62.6 2.1 %collective-permute-start.16 = (bf16[320,128]{1,0:T(8,128)(2,1)S(1)}, bf16[320,128]{1,0:T(8,128)(2,1)S(1)}, u32[]{:S(2)}, u32[]{:S(2)}) collective-permute-start(bf16[320,128]{1,0:T(8,128)(2,1)S(1)} %get-tuple-element.47), channel_id=1, source_target_pairs={{0,3},{1,0},{2,1},{3,2},{4,7},{5,4},{6,5},{7,6},{8,11},{9,8},{10,9... | collective-permute-start | bytes 245768 | tf_op jit(solution)/shard_map/ppermute | solution.py:87
  66.0 4.5 %collective-permute-done.15.refs_4_.refs_8_ = bf16[320,128]{1,0:T(8,128)(2,1)S(1)} collective-permute-done((bf16[320,128]{1,0:T(8,128)(2,1)S(1)}, bf16[320,128]{1,0:T(8,128)(2,1)S(1)}, u32[]{:S(2)}, u32[]{:S(2)}) %collective-permute-start.15) | collective-permute-done | bytes 81952 | tf_op jit(solution)/shard_map/ppermute | solution.py:87
  72.7 2.3 %backward_slots.7.refs_9_ = bf16[4096,128]{1,0:T(8,128)(2,1)S(1)} custom-call(s32[962]{0:T(1024)S(1)} %concatenate.3.meta.refs_0_, bf16[256,128,128]{2,1,0:T(8,128)(2,1)S(1)} %bitcast.10, bf16[256,128]{1,0:T(8,128)(2,1)S(1)} %get-tuple-element.44.refs_2_, bf16[320,128]{1,0:T(8,128)(2,1)S(1)} %collective-permute-done.14.refs_3_.refs_7_, ...), custom_call_target="tpu_custom_call" | custom-call | flops 8388608 | bytes 8388608 | tf_op jit(solution)/shard_map/backward_slots/pallas_call | solution.py:351
  76.6 2.7 %collective-permute-start.20 = (bf16[1024,128]{1,0:T(8,128)(2,1)S(1)}, bf16[1024,128]{1,0:T(8,128)(2,1)S(1)}, u32[]{:S(2)}, u32[]{:S(2)}) collective-permute-start(bf16[1024,128]{1,0:T(8,128)(2,1)S(1)} %get-tuple-element.53), channel_id=1, source_target_pairs={{0,192},{4,52},{8,200},{12,60},{16,208},{20,4},{24,216},{28,12},{3... | collective-permute-start | bytes 786440 | tf_op jit(solution)/shard_map/ppermute | solution.py:61
  83.9 2.5 %backward_slots.10 = (bf16[2432,128]{1,0:T(8,128)(2,1)S(1)}, bf16[2240,128]{1,0:T(8,128)(2,1)S(1)}, bf16[2048,128]{1,0:T(8,128)(2,1)S(1)}) custom-call(s32[962]{0:T(1024)S(1)} %concatenate.3.meta.refs_0_, bf16[256,128,128]{2,1,0:T(8,128)(2,1)S(1)} %bitcast.13, bf16[256,128]{1,0:T(8,128)(2,1)S(1)} %get-tuple-element.44.refs_2_, ...), custom_call_target="tpu_custom_call" | custom-call | flops 8388608 | bytes 8388608 | tf_op jit(solution)/shard_map/backward_slots/pallas_call | solution.py:351
  86.5 2.7 %collective-permute-start.23 = (bf16[2240,128]{1,0:T(8,128)(2,1)S(1)}, bf16[2240,128]{1,0:T(8,128)(2,1)S(1)}, u32[]{:S(2)}, u32[]{:S(2)}) collective-permute-start(bf16[2240,128]{1,0:T(8,128)(2,1)S(1)} %get-tuple-element.57), channel_id=1, source_target_pairs={{0,192},{4,52},{8,200},{12,60},{16,208},{20,4},{24,216},{28,12},{3... | collective-permute-start | bytes 1720328 | tf_op jit(solution)/shard_map/ppermute | solution.py:61
  98.0 2.1 %collective-permute-start.26 = (bf16[704,128]{1,0:T(8,128)(2,1)S(1)}, bf16[704,128]{1,0:T(8,128)(2,1)S(1)}, u32[]{:S(2)}, u32[]{:S(2)}) collective-permute-start(bf16[704,128]{1,0:T(8,128)(2,1)S(1)} %get-tuple-element.61), channel_id=1, source_target_pairs={{0,48},{4,196},{8,56},{12,204},{16,0},{20,212},{24,8},{28,220},{32... | collective-permute-start | bytes 540680 | tf_op jit(solution)/shard_map/ppermute | solution.py:61
  100.1 5.1 %collective-permute-done.24.b = bf16[704,128]{1,0:T(8,128)(2,1)S(1)} collective-permute-done((bf16[704,128]{1,0:T(8,128)(2,1)S(1)}, bf16[704,128]{1,0:T(8,128)(2,1)S(1)}, u32[]{:S(2)}, u32[]{:S(2)}) %collective-permute-start.24) | collective-permute-done | bytes 180256 | tf_op jit(solution)/shard_map/ppermute | solution.py:61
  106.4 6.9 %collective-permute-start.27 = (bf16[256,128]{1,0:T(8,128)(2,1)S(1)}, bf16[256,128]{1,0:T(8,128)(2,1)S(1)}, u32[]{:S(2)}, u32[]{:S(2)}) collective-permute-start(bf16[256,128]{1,0:T(8,128)(2,1)S(1)} %get-tuple-element.63.mine), channel_id=1, source_target_pairs={{4,12},{12,4},{20,28},{28,20},{36,44},{44,36},{52,60},{60,52},{68,... | collective-permute-start | bytes 196616 | tf_op jit(solution)/shard_map/ppermute | solution.py:61
  114.5 2.3 %collective-permute-start.29 = (bf16[256,128]{1,0:T(8,128)(2,1)S(1)}, bf16[256,128]{1,0:T(8,128)(2,1)S(1)}, u32[]{:S(2)}, u32[]{:S(2)}) collective-permute-start(bf16[256,128]{1,0:T(8,128)(2,1)S(1)} %sum_other.1), channel_id=1, source_target_pairs={{0,4},{4,8},{8,12},{12,0},{16,20},{20,24},{24,28},{28,16},{32,36},... | collective-permute-start | bytes 196616 | tf_op jit(solution)/shard_map/ppermute | solution.py:61
  116.7 3.3 %collective-permute-done.28.w_z = f32[64,128]{1,0:T(8,128)S(1)} collective-permute-done((f32[64,128]{1,0:T(8,128)S(1)}, f32[64,128]{1,0:T(8,128)S(1)}, u32[]{:S(2)}, u32[]{:S(2)}) %collective-permute-start.28) | collective-permute-done | bytes 32800 | tf_op jit(solution)/shard_map/ppermute | solution.py:61
  120.7 2.5 %collective-permute-start.32 = (f32[64,128]{1,0:T(8,128)S(1)}, f32[64,128]{1,0:T(8,128)S(1)}, u32[]{:S(2)}, u32[]{:S(2)}) collective-permute-start(f32[64,128]{1,0:T(8,128)S(1)} %get-tuple-element.66.w0), channel_id=1, source_target_pairs={{0,3},{1,0},{2,1},{3,2},{4,7},{5,4},{6,5},{7,6},{8,11},{9,8},{10,9... | collective-permute-start | bytes 98312 | tf_op jit(solution)/shard_map/ppermute | solution.py:87
  124.3 2.5 %collective-permute-done.31.w2 = f32[64,128]{1,0:T(8,128)S(1)} collective-permute-done((f32[64,128]{1,0:T(8,128)S(1)}, f32[64,128]{1,0:T(8,128)S(1)}, u32[]{:S(2)}, u32[]{:S(2)}) %collective-permute-start.31) | collective-permute-done | bytes 32800 | tf_op jit(solution)/shard_map/ppermute | solution.py:87
  (77 shorter events, 49.7 us)
Async XLA Ops:
  0.6 11.5 %collective-permute-start = (bf16[256,128]{1,0:T(8,128)(2,1)}, bf16[256,128]{1,0:T(8,128)(2,1)S(1)}, u32[]{:S(2)}, u32[]{:S(2)}) collective-permute-start(bf16[256,128]{1,0:T(8,128)(2,1)} %own.1), channel_id=1, source_target_pairs={{0,12},{4,0},{8,4},{12,8},{16,28},{20,16},{24,20},{28,24},{32,44},... | collective-permute-start | bytes 196616 | tf_op jit(solution)/shard_map/ppermute | solution.py:61
  3.9 9.1 %collective-permute-start.1 = (bf16[256,128]{1,0:T(8,128)(2,1)}, bf16[256,128]{1,0:T(8,128)(2,1)S(1)}, u32[]{:S(2)}, u32[]{:S(2)}) collective-permute-start(bf16[256,128]{1,0:T(8,128)(2,1)} %own.1), channel_id=1, source_target_pairs={{4,12},{12,4},{20,28},{28,20},{36,44},{44,36},{52,60},{60,52},{68,... | collective-permute-start | bytes 196616 | tf_op jit(solution)/shard_map/ppermute | solution.py:61
  13.9 9.2 %collective-permute-start.4 = (bf16[512,128]{1,0:T(8,128)(2,1)S(1)}, bf16[512,128]{1,0:T(8,128)(2,1)S(1)}, u32[]{:S(2)}, u32[]{:S(2)}) collective-permute-start(bf16[512,128]{1,0:T(8,128)(2,1)S(1)} %pair_up.1.refs_0_), channel_id=1, source_target_pairs={{0,48},{4,196},{8,56},{12,204},{16,0},{20,212},{24,8},{28,220},{32... | collective-permute-start | bytes 393224 | tf_op jit(solution)/shard_map/ppermute | solution.py:61
  16.6 6.5 %collective-permute-start.3 = (bf16[512,128]{1,0:T(8,128)(2,1)S(1)}, bf16[512,128]{1,0:T(8,128)(2,1)S(1)}, u32[]{:S(2)}, u32[]{:S(2)}) collective-permute-start(bf16[512,128]{1,0:T(8,128)(2,1)S(1)} %pair_up.1.refs_0_), channel_id=1, source_target_pairs={{0,32},{4,132},{8,40},{12,140},{16,48},{20,148},{24,56},{28,156},{... | collective-permute-start | bytes 393224 | tf_op jit(solution)/shard_map/ppermute | solution.py:61
  17.0 6.4 %collective-permute-start.2 = (bf16[512,128]{1,0:T(8,128)(2,1)S(1)}, bf16[512,128]{1,0:T(8,128)(2,1)S(1)}, u32[]{:S(2)}, u32[]{:S(2)}) collective-permute-start(bf16[512,128]{1,0:T(8,128)(2,1)S(1)} %pair_up.1.refs_0_), channel_id=1, source_target_pairs={{0,16},{4,68},{8,24},{12,76},{16,32},{20,84},{24,40},{28,92},{32,4... | collective-permute-start | bytes 393224 | tf_op jit(solution)/shard_map/ppermute | solution.py:61
  23.4 8.7 %collective-permute-start.6 = (bf16[2048,128]{1,0:T(8,128)(2,1)S(1)}, bf16[2048,128]{1,0:T(8,128)(2,1)S(1)}, u32[]{:S(2)}, u32[]{:S(2)}) collective-permute-start(bf16[2048,128]{1,0:T(8,128)(2,1)S(1)} %place_quad.1.refs_2_.refs_0_), channel_id=1, source_target_pairs={{0,192},{4,52},{8,200},{12,60},{16,208},{20,4},{24,216},{28,12},{3... | collective-permute-start | bytes 1572872 | tf_op jit(solution)/shard_map/ppermute | solution.py:61
  25.9 9.5 %collective-permute-start.5 = (bf16[2048,128]{1,0:T(8,128)(2,1)S(1)}, bf16[2048,128]{1,0:T(8,128)(2,1)S(1)}, u32[]{:S(2)}, u32[]{:S(2)}) collective-permute-start(bf16[2048,128]{1,0:T(8,128)(2,1)S(1)} %place_quad.1.refs_2_.refs_0_), channel_id=1, source_target_pairs={{0,64},{4,20},{8,72},{12,28},{16,80},{20,36},{24,88},{28,44},{32,9... | collective-permute-start | bytes 1572872 | tf_op jit(solution)/shard_map/ppermute | solution.py:61
  35.6 10.1 %collective-permute-start.10 = (bf16[6144,128]{1,0:T(8,128)(2,1)S(1)}, bf16[6144,128]{1,0:T(8,128)(2,1)S(1)}, u32[]{:S(2)}, u32[]{:S(2)}) collective-permute-start(bf16[6144,128]{1,0:T(8,128)(2,1)S(1)} %get-tuple-element.38), channel_id=1, source_target_pairs={{0,4},{4,0},{8,12},{12,8},{16,20},{20,16},{24,28},{28,24},{32,36},... | collective-permute-start | bytes 4718600 | tf_op jit(solution)/shard_map/ppermute | solution.py:61
  37.8 6.7 %collective-permute-start.7 = (bf16[1024,128]{1,0:T(8,128)(2,1)S(1)}, bf16[1024,128]{1,0:T(8,128)(2,1)S(1)}, u32[]{:S(2)}, u32[]{:S(2)}) collective-permute-start(bf16[1024,128]{1,0:T(8,128)(2,1)S(1)} %get-tuple-element.36.refs_4_), channel_id=1, source_target_pairs={{0,64},{4,20},{8,72},{12,28},{16,80},{20,36},{24,88},{28,44},{32,9... | collective-permute-start | bytes 786440 | tf_op jit(solution)/shard_map/ppermute | solution.py:61
  51.7 7.2 %collective-permute-start.12 = (bf16[256,128]{1,0:T(8,128)(2,1)S(1)}, bf16[256,128]{1,0:T(8,128)(2,1)S(1)}, u32[]{:S(2)}, u32[]{:S(2)}) collective-permute-start(bf16[256,128]{1,0:T(8,128)(2,1)S(1)} %get-tuple-element.41), channel_id=1, source_target_pairs={{0,2},{1,3},{2,0},{3,1},{4,6},{5,7},{6,4},{7,5},{8,10},{9,11},{10,... | collective-permute-start | bytes 196616 | tf_op jit(solution)/shard_map/ppermute | solution.py:87
  53.3 5.6 %collective-permute-start.13 = (bf16[256,128]{1,0:T(8,128)(2,1)S(1)}, bf16[256,128]{1,0:T(8,128)(2,1)S(1)}, u32[]{:S(2)}, u32[]{:S(2)}) collective-permute-start(bf16[256,128]{1,0:T(8,128)(2,1)S(1)} %get-tuple-element.42), channel_id=1, source_target_pairs={{0,3},{1,0},{2,1},{3,2},{4,7},{5,4},{6,5},{7,6},{8,11},{9,8},{10,9... | collective-permute-start | bytes 196616 | tf_op jit(solution)/shard_map/ppermute | solution.py:87
  62.6 8.0 %collective-permute-start.15 = (bf16[320,128]{1,0:T(8,128)(2,1)S(1)}, bf16[320,128]{1,0:T(8,128)(2,1)S(1)}, u32[]{:S(2)}, u32[]{:S(2)}) collective-permute-start(bf16[320,128]{1,0:T(8,128)(2,1)S(1)} %get-tuple-element.46), channel_id=1, source_target_pairs={{0,2},{1,3},{2,0},{3,1},{4,6},{5,7},{6,4},{7,5},{8,10},{9,11},{10,... | collective-permute-start | bytes 245768 | tf_op jit(solution)/shard_map/ppermute | solution.py:87
  62.6 8.0 %collective-permute-start.16 = (bf16[320,128]{1,0:T(8,128)(2,1)S(1)}, bf16[320,128]{1,0:T(8,128)(2,1)S(1)}, u32[]{:S(2)}, u32[]{:S(2)}) collective-permute-start(bf16[320,128]{1,0:T(8,128)(2,1)S(1)} %get-tuple-element.47), channel_id=1, source_target_pairs={{0,3},{1,0},{2,1},{3,2},{4,7},{5,4},{6,5},{7,6},{8,11},{9,8},{10,9... | collective-permute-start | bytes 245768 | tf_op jit(solution)/shard_map/ppermute | solution.py:87
  76.5 7.4 %collective-permute-start.18 = (bf16[4096,128]{1,0:T(8,128)(2,1)S(1)}, bf16[4096,128]{1,0:T(8,128)(2,1)S(1)}, u32[]{:S(2)}, u32[]{:S(2)}) collective-permute-start(bf16[4096,128]{1,0:T(8,128)(2,1)S(1)} %get-tuple-element.51), channel_id=1, source_target_pairs={{0,4},{4,0},{8,12},{12,8},{16,20},{20,16},{24,28},{28,24},{32,36},... | collective-permute-start | bytes 3145736 | tf_op jit(solution)/shard_map/ppermute | solution.py:61
  76.6 7.3 %collective-permute-start.19 = (bf16[1216,128]{1,0:T(8,128)(2,1)S(1)}, bf16[1216,128]{1,0:T(8,128)(2,1)S(1)}, u32[]{:S(2)}, u32[]{:S(2)}) collective-permute-start(bf16[1216,128]{1,0:T(8,128)(2,1)S(1)} %get-tuple-element.52.refs_6_), channel_id=1, source_target_pairs={{0,64},{4,20},{8,72},{12,28},{16,80},{20,36},{24,88},{28,44},{32,9... | collective-permute-start | bytes 933896 | tf_op jit(solution)/shard_map/ppermute | solution.py:61
  76.6 6.0 %collective-permute-start.20 = (bf16[1024,128]{1,0:T(8,128)(2,1)S(1)}, bf16[1024,128]{1,0:T(8,128)(2,1)S(1)}, u32[]{:S(2)}, u32[]{:S(2)}) collective-permute-start(bf16[1024,128]{1,0:T(8,128)(2,1)S(1)} %get-tuple-element.53), channel_id=1, source_target_pairs={{0,192},{4,52},{8,200},{12,60},{16,208},{20,4},{24,216},{28,12},{3... | collective-permute-start | bytes 786440 | tf_op jit(solution)/shard_map/ppermute | solution.py:61
  86.4 10.7 %collective-permute-start.22 = (bf16[2432,128]{1,0:T(8,128)(2,1)S(1)}, bf16[2432,128]{1,0:T(8,128)(2,1)S(1)}, u32[]{:S(2)}, u32[]{:S(2)}) collective-permute-start(bf16[2432,128]{1,0:T(8,128)(2,1)S(1)} %get-tuple-element.56.refs_7_), channel_id=1, source_target_pairs={{0,64},{4,20},{8,72},{12,28},{16,80},{20,36},{24,88},{28,44},{32,9... | collective-permute-start | bytes 1867784 | tf_op jit(solution)/shard_map/ppermute | solution.py:61
  86.5 9.3 %collective-permute-start.23 = (bf16[2240,128]{1,0:T(8,128)(2,1)S(1)}, bf16[2240,128]{1,0:T(8,128)(2,1)S(1)}, u32[]{:S(2)}, u32[]{:S(2)}) collective-permute-start(bf16[2240,128]{1,0:T(8,128)(2,1)S(1)} %get-tuple-element.57), channel_id=1, source_target_pairs={{0,192},{4,52},{8,200},{12,60},{16,208},{20,4},{24,216},{28,12},{3... | collective-permute-start | bytes 1720328 | tf_op jit(solution)/shard_map/ppermute | solution.py:61
  97.3 7.9 %collective-permute-start.24 = (bf16[704,128]{1,0:T(8,128)(2,1)S(1)}, bf16[704,128]{1,0:T(8,128)(2,1)S(1)}, u32[]{:S(2)}, u32[]{:S(2)}) collective-permute-start(bf16[704,128]{1,0:T(8,128)(2,1)S(1)} %get-tuple-element.59), channel_id=1, source_target_pairs={{0,16},{4,68},{8,24},{12,76},{16,32},{20,84},{24,40},{28,92},{32,4... | collective-permute-start | bytes 540680 | tf_op jit(solution)/shard_map/ppermute | solution.py:61
  97.4 7.8 %collective-permute-start.25 = (bf16[704,128]{1,0:T(8,128)(2,1)S(1)}, bf16[704,128]{1,0:T(8,128)(2,1)S(1)}, u32[]{:S(2)}, u32[]{:S(2)}) collective-permute-start(bf16[704,128]{1,0:T(8,128)(2,1)S(1)} %get-tuple-element.60), channel_id=1, source_target_pairs={{0,32},{4,132},{8,40},{12,140},{16,48},{20,148},{24,56},{28,156},{... | collective-permute-start | bytes 540680 | tf_op jit(solution)/shard_map/ppermute | solution.py:61
  98.0 7.8 %collective-permute-start.26 = (bf16[704,128]{1,0:T(8,128)(2,1)S(1)}, bf16[704,128]{1,0:T(8,128)(2,1)S(1)}, u32[]{:S(2)}, u32[]{:S(2)}) collective-permute-start(bf16[704,128]{1,0:T(8,128)(2,1)S(1)} %get-tuple-element.61), channel_id=1, source_target_pairs={{0,48},{4,196},{8,56},{12,204},{16,0},{20,212},{24,8},{28,220},{32... | collective-permute-start | bytes 540680 | tf_op jit(solution)/shard_map/ppermute | solution.py:61
  106.4 13.6 %collective-permute-start.27 = (bf16[256,128]{1,0:T(8,128)(2,1)S(1)}, bf16[256,128]{1,0:T(8,128)(2,1)S(1)}, u32[]{:S(2)}, u32[]{:S(2)}) collective-permute-start(bf16[256,128]{1,0:T(8,128)(2,1)S(1)} %get-tuple-element.63.mine), channel_id=1, source_target_pairs={{4,12},{12,4},{20,28},{28,20},{36,44},{44,36},{52,60},{60,52},{68,... | collective-permute-start | bytes 196616 | tf_op jit(solution)/shard_map/ppermute | solution.py:61
  113.3 6.8 %collective-permute-start.28 = (f32[64,128]{1,0:T(8,128)S(1)}, f32[64,128]{1,0:T(8,128)S(1)}, u32[]{:S(2)}, u32[]{:S(2)}) collective-permute-start(f32[64,128]{1,0:T(8,128)S(1)} %get-tuple-element.64.w), channel_id=1, source_target_pairs={{0,8},{4,12},{8,0},{12,4},{16,24},{20,28},{24,16},{28,20},{32,40},... | collective-permute-start | bytes 98312 | tf_op jit(solution)/shard_map/ppermute | solution.py:61
  114.5 9.4 %collective-permute-start.29 = (bf16[256,128]{1,0:T(8,128)(2,1)S(1)}, bf16[256,128]{1,0:T(8,128)(2,1)S(1)}, u32[]{:S(2)}, u32[]{:S(2)}) collective-permute-start(bf16[256,128]{1,0:T(8,128)(2,1)S(1)} %sum_other.1), channel_id=1, source_target_pairs={{0,4},{4,8},{8,12},{12,0},{16,20},{20,24},{24,28},{28,16},{32,36},... | collective-permute-start | bytes 196616 | tf_op jit(solution)/shard_map/ppermute | solution.py:61
  (14 other events, 67.2 us)

commit v2 on v1

--- a/solution.py
+++ b/solution.py
@@ -16,6 +16,7 @@
 PIECE = 64
 SPLIT = 3 * PIECE
 COST = B * B * 8
+LONG = 1 << 40
 F32 = jnp.float32
 BF16 = jnp.bfloat16
 VMEM = pl.BlockSpec(memory_space=pltpu.VMEM)
@@ -37,7 +38,16 @@
     [group(1, 0), group(1, 1), group(1, 3)],
     [group(0, 2), group(1, 2)],
 ]
-BACKWARD_GROUPS = [group(1, 2), group(1, 1) + group(1, 3), group(0, 2), group(1, 0), group(0, 1) + group(0, 3), group(0, 0)]
+LOW, HIGH = (0, 1), (2, 3)
+BACKWARD_GROUPS = [
+    group(1, 2),
+    group(1, 1, HIGH) + group(1, 3, LOW) + group(1, 1, LOW) + group(1, 3, HIGH),
+    group(0, 2),
+    group(1, 0),
+    group(0, 1, HIGH) + group(0, 3, LOW),
+    group(0, 1, LOW) + group(0, 3, HIGH),
+    group(0, 0),
+]
 
 
 def section_order(r, entries, sign):
@@ -142,7 +152,7 @@
             row += size * ROWS
 
 
-def place(name, parts, sources, after=()):
+def place(name, parts, sources, after=(), size=1 << 18):
     shapes = [jax.ShapeDtypeStruct((sum(p[2] for p in pieces) * ROWS, B), BF16) for pieces in parts]
     args = [*sources, *after]
     return pl.pallas_call(
@@ -151,7 +161,7 @@
         in_specs=[VMEM] * len(args),
         out_specs=[VMEM] * len(shapes),
         compiler_params=params(),
-        cost_estimate=small_cost(1 << 18),
+        cost_estimate=small_cost(size),
         name=name,
     )(*args)
 
@@ -289,17 +299,25 @@
 
 
 def spread_terms(extra, outs, extra_outs):
-    half_1, half_3, own, passed = extra
-    extra_outs[0][...] = passed[...]
-    first, second = slice(0, 4 * ROWS), slice(4 * ROWS, 8 * ROWS)
-    outs[0][first] = (outs[0][first].astype(F32) + half_1[first].astype(F32)).astype(BF16)
-    outs[1][second] = (outs[1][second].astype(F32) + half_3[...].astype(F32)).astype(BF16)
-    for out in outs:
-        split(own[...], out, 8 * ROWS)
-    outs[0][8 * ROWS + SPLIT :] = half_1[4 * ROWS :]
-
-
-def backward_kernel(first_section, sizes, added, extras, finish, *refs):
+    half_1, half_3, own = extra[:3]
+    part = slice(0, 4 * ROWS)
+    for out, half in zip(outs, (half_1, half_3)):
+        out[part] = (out[part].astype(F32) + half[part].astype(F32)).astype(BF16)
+        split(own[...], out, 4 * ROWS)
+    outs[0][4 * ROWS + SPLIT :] = half_1[4 * ROWS :]
+
+
+def pass_on(extra, outs, extra_outs):
+    extra_outs[0][...] = extra[0][...]
+
+
+def add_halves(extra, outs, extra_outs):
+    for half, start in zip(extra[:2], (4 * ROWS, 0)):
+        part = slice(start, start + 4 * ROWS)
+        outs[0][part] = (outs[0][part].astype(F32) + half[...].astype(F32)).astype(BF16)
+
+
+def backward_kernel(first_section, sizes, added, add_from, extras, finish, *refs):
     meta, stored = refs[:2]
     value_refs, refs = refs[2:6], refs[6:]
     if added:
@@ -332,7 +350,7 @@
                 right = jnp.concatenate([stored[meta[base + 3 * k + 2]] for k in range(SLOTS)], axis=0)
                 result = jnp.dot(left, right, preferred_element_type=F32)
                 if added:
-                    result = result + add_ref[pl.ds(pl.multiple_of((begin + n) * ROWS, ROWS), ROWS)].astype(F32)
+                    result = result + add_ref[pl.ds(pl.multiple_of((add_from + begin + n) * ROWS, ROWS), ROWS)].astype(F32)
                 out_ref[pl.ds(pl.multiple_of(n * ROWS, ROWS), ROWS)] = result.astype(BF16)
             return carry
 
@@ -342,32 +360,32 @@
         finish(extra, out_refs, extra_outs)
 
 
-def backward(meta, stored, values, first_section, sizes, add=None, extra=(), finish=None, tails=None, extra_out=()):
+def backward(meta, stored, values, first_section, sizes, add=None, add_from=0, extra=(), finish=None, tails=None, extra_out=(), size=0):
     added = add is not None
     args = [meta, stored, *values] + ([add] if added else []) + list(extra)
     tails = tails or (0,) * len(sizes)
     shapes = [jax.ShapeDtypeStruct((size * ROWS + tail, B), BF16) for size, tail in zip(sizes, tails)]
     shapes += [jax.ShapeDtypeStruct(a.shape, a.dtype) for a in extra_out]
     return pl.pallas_call(
-        functools.partial(backward_kernel, first_section, sizes, added, len(extra), finish),
+        functools.partial(backward_kernel, first_section, sizes, added, add_from, len(extra), finish),
         out_shape=shapes,
         in_specs=[SMEM] + [VMEM] * (len(args) - 1),
         out_specs=[VMEM] * len(shapes),
         scratch_shapes=[pltpu.VMEM((BROWS + 1, B, B), BF16)],
         compiler_params=params(),
-        cost_estimate=cost(sum(sizes) * SLOTS),
+        cost_estimate=small_cost(size) if size else cost(sum(sizes) * SLOTS),
         name="backward_slots",
     )(*args)
 
 
-def sum_kernel(a, b, c, own, t0, t1, t2, t3, w):
-    row = 8 * ROWS
-    total = (own[...] + joined(b, row + SPLIT)) + (joined(b, row) + joined(c, row))
+def sum_kernel(a, low, high, own, t0, t1, t2, t3, w):
+    row = 4 * ROWS
+    total = (own[...] + joined(low, row + SPLIT)) + (joined(low, row) + joined(high, row))
     w[...] = total
     for d, out in enumerate((t0, t1, t2, t3)):
-        part = slice(2 * ROWS * d, 2 * ROWS * (d + 1))
-        group_sum = a[part].astype(F32) + b[part].astype(F32) + c[part].astype(F32)
-        out[0 : 2 * ROWS] = group_sum.astype(BF16)
+        half_ref = high if d >= 2 else low
+        part, half = (slice(2 * ROWS * n, 2 * ROWS * (n + 1)) for n in (d, d % 2))
+        out[0 : 2 * ROWS] = (a[part].astype(F32) + half_ref[half].astype(F32)).astype(BF16)
         if d:
             split(total, out, 2 * ROWS)
 
@@ -491,17 +509,19 @@
 
     near_unit, far_unit = cross(features, True), other_z(features)
     pair = pair_up(core.reshape(1), features, near_unit, far_unit)
-    pairs = [pair] + [small_axis(pair, d) for d in (1, 2, 3)]
+    x1, x2, x3 = small_axis(pair, 1), small_axis(pair, 2), small_axis(pair, 3)
     touched = touch(meta, stored)
-    (quad,) = place("place_quad", [[(n, 0, 2) for n in range(4)]], pairs, [touched])
-    n1, n3 = large_axis(quad, 1), large_axis(quad, 3)
-    (acc,) = forward(meta, stored, 0, [quad], None, False)
-    parts = [[(0, 0, 8), (1, 0, 8), (2, 0, 8)], [(1, 0, 4)], [(2, 4, 4)]]
-    near, h1, h3 = place("place_near", parts, [quad, n1, n3], [acc])
-    f1, f3 = large_axis(h1, 1), large_axis(h3, 3)
+    (low,) = place("place_low", [[(0, 0, 2), (1, 0, 2)]], [pair, x1])
+    n1_low, n3_low = large_axis(low, 1), large_axis(low, 3)
+    (high,) = place("place_high", [[(0, 0, 2), (1, 0, 2)]], [x2, x3], [touched, low])
+    n1_high, n3_high = large_axis(high, 1), large_axis(high, 3)
+    (acc,) = forward(meta, stored, 0, [low, high], None, False)
+    f1, f3 = large_axis(n1_low, 1), large_axis(n3_high, 3)
+    halves = [low, high, n1_low, n1_high, n3_low, n3_high]
+    (near,) = place("place_near", [[(n, 0, 4) for n in range(6)]], halves, [acc])
     near_s = sibling(near)
-    (acc,) = forward(meta, stored, 8, [n1, n3], acc, False, after=[h1])
-    (far,) = place("place_far", [[(0, 0, 4), (1, 0, 4)]], [f1, f3], [acc])
+    (acc,) = forward(meta, stored, 8, halves[2:], acc, False)
+    (far,) = place("place_far", [[(0, 0, 4), (1, 0, 4)]], [f1, f3], [acc], size=LONG)
     far_s = sibling(far)
     (acc,) = forward(meta, stored, 24, [near_s], acc, False)
     own_part, *pieces = forward(meta, stored, 48, [far, far_s], acc, True)
@@ -519,18 +539,22 @@
     )
     f1, f3, near_s = large_axis(h1, 1), large_axis(h3, 3), sibling(near_b)
     (own_b,) = bwd(32, (8,), extra=[h1])
-    g1, g3, own_b = bwd(
-        40,
-        (8, 8),
+    g1_high, g3_low, own_b = bwd(40, (4, 4), near_s, extra=[own_b], finish=pass_on, extra_out=[own_b])
+    r1_high, r3_low = large_axis(g1_high, 1), large_axis(g3_low, 3)
+    own_s = sibling(own_b)
+    g1_low, g3_high = bwd(
+        48,
+        (4, 4),
         near_s,
-        extra=[f1, f3, w8, own_b],
+        add_from=8,
+        extra=[f1, f3, w8, g1_high],
         finish=spread_terms,
         tails=(2 * SPLIT, SPLIT),
-        extra_out=[own_b],
+        size=LONG,
     )
-    r1, r3, own_s = large_axis(g1, 1), large_axis(g3, 3), sibling(own_b)
-    (g0,) = bwd(56, (8,), own_s, extra=[g1])
-    t0, t1, t2, t3, w32 = sum_groups(g0, r1, r3, w8)
+    r1_low, r3_high = large_axis(g1_low, 1), large_axis(g3_high, 3)
+    (g0,) = bwd(56, (8,), own_s, extra=[r1_high, r3_low, g1_low], finish=add_halves, size=LONG)
+    t0, t1, t2, t3, w32 = sum_groups(g0, r1_low, r3_high, w8)
     sums = [t0, small_axis(t1, 1), small_axis(t2, 2), small_axis(t3, 3)]
     mine, w = sum_mine(meta, *sums, w32)
     far = other_z(mine)

time: 130 us -> 123 us (0.946)
  waiting for transfers between devices: 46.1 us -> 33.1 us
  starting transfers between devices: 51.3 us -> 57.5 us
    ppermute x24 -> x28, waiting for transfers between devices: 30.8 us -> 17.9 us  [row_permute(): return lax.ppermute(array, 'row', pairs)]
    ppermute x24 -> x28, starting transfers between devices: 40.6 us -> 45.9 us  [row_permute(): return lax.ppermute(array, 'row', pairs)]
    pallas_call x6 -> x7, Pallas kernels: 10.6 us -> 11 us  [backward(): pl.pallas_call(functools.partial(backward_kernel, first_section, sizes, a...]
  transfers between devices with their start and end apart: 33 -> 37, of which waited for: 21 -> 18; matrix products, arithmetic and copies ran while one was open for 2% -> 2% of each run, Pallas kernels for 10% -> 13%
where the time goes in v2:
time: 123 us; the launch traced here: 122 us
  starting transfers between devices  57.5 us (47%)
  waiting for transfers between devices  33.1 us (27%)
  Pallas kernels  24.1 us (20%)
  local copies, waits for them, and re-layouts  6 us (5%)
    ppermute x28, starting transfers between devices, row_permute(): return lax.ppermute(array, 'row', pairs)  45.9 us
    ppermute x28, waiting for transfers between devices, row_permute(): return lax.ppermute(array, 'row', pairs)  17.9 us
    ppermute x9, waiting for transfers between devices, turn(): return lax.ppermute(array, 'rep', [(q, (q + d) % 4) for q in range(4)])  15.2 us
    ppermute x9, starting transfers between devices, turn(): return lax.ppermute(array, 'rep', [(q, (q + d) % 4) for q in range(4)])  11.6 us
    pallas_call x7, Pallas kernels, backward(): pl.pallas_call(functools.partial(backward_kernel, first_section, sizes, a...  11 us
    pallas_call x4, Pallas kernels, forward(): pl.pallas_call(functools.partial(forward_kernel, first_section, sizes, fi...  7.13 us
    unnamed x11, local copies, waits for them, and re-layouts  5.05 us
  transfers between devices with their start and end apart: 37, of which 18 were waited for; matrix products, arithmetic and copies ran while one was open for 2% of the time, Pallas kernels for 13%

profile of v2, /device:TPU:1, one launch (start us, length us, event | category | flops | bytes accessed | tf_op | source)
XLA Modules:
  0.0 122.4 jit_solution(13296478946743469358)
XLA Ops:
  0.6 3.3 %collective-permute-start = (bf16[256,128]{1,0:T(8,128)(2,1)}, bf16[256,128]{1,0:T(8,128)(2,1)S(1)}, u32[]{:S(2)}, u32[]{:S(2)}) collective-permute-start(bf16[256,128]{1,0:T(8,128)(2,1)} %own.1), channel_id=1, source_target_pairs={{0,12},{4,0},{8,4},{12,8},{16,28},{20,16},{24,20},{28,24},{32,44},... | collective-permute-start | bytes 196616 | tf_op jit(solution)/shard_map/ppermute | solution.py:71
  3.9 7.1 %collective-permute-start.1 = (bf16[256,128]{1,0:T(8,128)(2,1)}, bf16[256,128]{1,0:T(8,128)(2,1)S(1)}, u32[]{:S(2)}, u32[]{:S(2)}) collective-permute-start(bf16[256,128]{1,0:T(8,128)(2,1)} %own.1), channel_id=1, source_target_pairs={{4,12},{12,4},{20,28},{28,20},{36,44},{44,36},{52,60},{60,52},{68,... | collective-permute-start | bytes 196616 | tf_op jit(solution)/shard_map/ppermute | solution.py:71
  13.9 2.7 %collective-permute-start.6 = (bf16[512,128]{1,0:T(8,128)(2,1)S(1)}, bf16[512,128]{1,0:T(8,128)(2,1)S(1)}, u32[]{:S(2)}, u32[]{:S(2)}) collective-permute-start(bf16[512,128]{1,0:T(8,128)(2,1)S(1)} %pair_up.1.refs_0_), channel_id=1, source_target_pairs={{0,48},{4,196},{8,56},{12,204},{16,0},{20,212},{24,8},{28,220},{32... | collective-permute-start | bytes 393224 | tf_op jit(solution)/shard_map/ppermute | solution.py:71
  19.2 3.4 %copy-done = bf16[1,1,256,128,128]{4,3,2,1,0:T(8,128)(2,1)S(1)} copy-done((bf16[1,1,256,128,128]{4,3,2,1,0:T(8,128)(2,1)S(1)}, bf16[1,1,256,128,128]{4,3,2,1,0:T(8,128)(2,1)}, u32[]{:S(2)}) %copy-start) | copy-done | bytes 8388632
  23.4 2.6 %collective-permute-start.7 = (bf16[1024,128]{1,0:T(8,128)(2,1)S(1)}, bf16[1024,128]{1,0:T(8,128)(2,1)S(1)}, u32[]{:S(2)}, u32[]{:S(2)}) collective-permute-start(bf16[1024,128]{1,0:T(8,128)(2,1)S(1)} %place_high.1.refs_3_.refs_1_), channel_id=1, source_target_pairs={{0,192},{4,52},{8,200},{12,60},{16,208},{20,4},{24,216},{28,12},{3... | collective-permute-start | bytes 786440 | tf_op jit(solution)/shard_map/ppermute | solution.py:71
  26.2 2.5 %collective-permute-start.10 = (bf16[1024,128]{1,0:T(8,128)(2,1)S(1)}, bf16[1024,128]{1,0:T(8,128)(2,1)S(1)}, u32[]{:S(2)}, u32[]{:S(2)}) collective-permute-start(bf16[1024,128]{1,0:T(8,128)(2,1)S(1)} %place_low.1.refs_3_.refs_2_.refs_0_), channel_id=1, source_target_pairs={{0,192},{4,52},{8,200},{12,60},{16,208},{20,4},{24,216},{28,12},{3... | collective-permute-start | bytes 786440 | tf_op jit(solution)/shard_map/ppermute | solution.py:71
  29.3 3.4 %collective-permute-start.8 = (bf16[1024,128]{1,0:T(8,128)(2,1)S(1)}, bf16[1024,128]{1,0:T(8,128)(2,1)S(1)}, u32[]{:S(2)}, u32[]{:S(2)}) collective-permute-start(bf16[1024,128]{1,0:T(8,128)(2,1)S(1)} %collective-permute-done.7.refs_5_), channel_id=1, source_target_pairs={{0,192},{4,52},{8,200},{12,60},{16,208},{20,4},{24,216},{28,12},{3... | collective-permute-start | bytes 786440 | tf_op jit(solution)/shard_map/ppermute | solution.py:71
  41.1 2.5 %forward_slots.6.refs_4_ = f32[8,128,128]{2,1,0:T(8,128)S(1)} custom-call(s32[962]{0:T(1024)S(1)} %concatenate.3.meta.refs_0_, bf16[256,128,128]{2,1,0:T(8,128)(2,1)S(1)} %bitcast.7, bf16[6144,128]{1,0:T(8,128)(2,1)S(1)} %collective-permute-done.12.refs_2_, f32[8,128,128]{2,1,0:T(8,128)S(1)} %forward_slots.5.refs_2_.refs_3_), custom_call_target="tpu_custom_call" | custom-call | flops 12582912 | bytes 12582912 | tf_op jit(solution)/shard_map/forward_slots/pallas_call | solution.py:220
  43.7 1.9 %forward_slots.7 = (f32[256,128]{1,0:T(8,128)S(1)}, bf16[256,128]{1,0:T(8,128)(2,1)S(1)}, bf16[256,128]{1,0:T(8,128)(2,1)S(1)}, bf16[256,128]{1,0:T(8,128)(2,1)S(1)}) custom-call(s32[962]{0:T(1024)S(1)} %concatenate.3.meta.refs_0_, bf16[256,128,128]{2,1,0:T(8,128)(2,1)S(1)} %bitcast.8, bf16[2048,128]{1,0:T(8,128)(2,1)S(1)} %place_far.1.refs_2_, ...), custom_call_target="tpu_custom_call" | custom-call | flops 8388608 | bytes 8388608 | tf_op jit(solution)/shard_map/forward_slots/pallas_call | solution.py:220
  49.4 2.0 %collective-permute-done.13.p1 = bf16[256,128]{1,0:T(8,128)(2,1)S(1)} collective-permute-done((bf16[256,128]{1,0:T(8,128)(2,1)S(1)}, bf16[256,128]{1,0:T(8,128)(2,1)S(1)}, u32[]{:S(2)}, u32[]{:S(2)}) %collective-permute-start.13) | collective-permute-done | bytes 65568 | tf_op jit(solution)/shard_map/ppermute | solution.py:97
  51.4 2.8 %collective-permute-done.14.p2 = bf16[256,128]{1,0:T(8,128)(2,1)S(1)} collective-permute-done((bf16[256,128]{1,0:T(8,128)(2,1)S(1)}, bf16[256,128]{1,0:T(8,128)(2,1)S(1)}, u32[]{:S(2)}, u32[]{:S(2)}) %collective-permute-start.14) | collective-permute-done | bytes 65568 | tf_op jit(solution)/shard_map/ppermute | solution.py:97
  54.2 1.7 %middle_rows.1 = (bf16[256,256]{1,0:T(8,128)(2,1)}, bf16[256,128]{1,0:T(8,128)(2,1)S(1)}, bf16[320,128]{1,0:T(8,128)(2,1)S(1)}, bf16[320,128]{1,0:T(8,128)(2,1)S...) custom-call(s32[962]{0:T(1024)S(1)} %concatenate.3.meta.refs_0_, f32[256,128]{1,0:T(8,128)S(1)} %get-tuple-element.35.own, ...), custom_call_target="tpu_custom_call" | custom-call | flops 1024 | bytes 1024 | tf_op jit(solution)/shard_map/middle_rows/pallas_call | solution.py:260
  61.0 4.6 %collective-permute-done.17.refs_4_.refs_8_ = bf16[320,128]{1,0:T(8,128)(2,1)S(1)} collective-permute-done((bf16[320,128]{1,0:T(8,128)(2,1)S(1)}, bf16[320,128]{1,0:T(8,128)(2,1)S(1)}, u32[]{:S(2)}, u32[]{:S(2)}) %collective-permute-start.17) | collective-permute-done | bytes 81952 | tf_op jit(solution)/shard_map/ppermute | solution.py:97
  67.8 2.3 %backward_slots.8.refs_9_ = bf16[4096,128]{1,0:T(8,128)(2,1)S(1)} custom-call(s32[962]{0:T(1024)S(1)} %concatenate.3.meta.refs_0_, bf16[256,128,128]{2,1,0:T(8,128)(2,1)S(1)} %bitcast.10, bf16[256,128]{1,0:T(8,128)(2,1)S(1)} %get-tuple-element.40.refs_2_, bf16[320,128]{1,0:T(8,128)(2,1)S(1)} %collective-permute-done.16.refs_3_.refs_7_, ...), custom_call_target="tpu_custom_call" | custom-call | flops 8388608 | bytes 8388608 | tf_op jit(solution)/shard_map/backward_slots/pallas_call | solution.py:369
  72.5 1.9 %collective-permute-start.25 = (bf16[1024,128]{1,0:T(8,128)(2,1)S(1)}, bf16[1024,128]{1,0:T(8,128)(2,1)S(1)}, u32[]{:S(2)}, u32[]{:S(2)}) collective-permute-start(bf16[1024,128]{1,0:T(8,128)(2,1)S(1)} %get-tuple-element.52), channel_id=1, source_target_pairs={{0,192},{4,52},{8,200},{12,60},{16,208},{20,4},{24,216},{28,12},{3... | collective-permute-start | bytes 786440 | tf_op jit(solution)/shard_map/ppermute | solution.py:71
  85.8 2.2 %collective-permute-done.27.high = bf16[1216,128]{1,0:T(8,128)(2,1)S(1)} collective-permute-done((bf16[1216,128]{1,0:T(8,128)(2,1)S(1)}, bf16[1216,128]{1,0:T(8,128)(2,1)S(1)}, u32[]{:S(2)}, u32[]{:S(2)}) %collective-permute-start.27) | collective-permute-done | bytes 311328 | tf_op jit(solution)/shard_map/ppermute | solution.py:71
  88.0 3.1 %collective-permute-done.26.low = bf16[1408,128]{1,0:T(8,128)(2,1)S(1)} collective-permute-done((bf16[1408,128]{1,0:T(8,128)(2,1)S(1)}, bf16[1408,128]{1,0:T(8,128)(2,1)S(1)}, u32[]{:S(2)}, u32[]{:S(2)}) %collective-permute-start.26) | collective-permute-done | bytes 360480 | tf_op jit(solution)/shard_map/ppermute | solution.py:71
  91.4 2.1 %collective-permute-start.29 = (bf16[704,128]{1,0:T(8,128)(2,1)S(1)}, bf16[704,128]{1,0:T(8,128)(2,1)S(1)}, u32[]{:S(2)}, u32[]{:S(2)}) collective-permute-start(bf16[704,128]{1,0:T(8,128)(2,1)S(1)} %get-tuple-element.58), channel_id=1, source_target_pairs={{0,32},{4,132},{8,40},{12,140},{16,48},{20,148},{24,56},{28,156},{... | collective-permute-start | bytes 540680 | tf_op jit(solution)/shard_map/ppermute | solution.py:71
  94.1 5.1 %collective-permute-done.28.b = bf16[704,128]{1,0:T(8,128)(2,1)S(1)} collective-permute-done((bf16[704,128]{1,0:T(8,128)(2,1)S(1)}, bf16[704,128]{1,0:T(8,128)(2,1)S(1)}, u32[]{:S(2)}, u32[]{:S(2)}) %collective-permute-start.28) | collective-permute-done | bytes 180256 | tf_op jit(solution)/shard_map/ppermute | solution.py:71
  100.4 4.6 %collective-permute-start.31 = (bf16[256,128]{1,0:T(8,128)(2,1)S(1)}, bf16[256,128]{1,0:T(8,128)(2,1)S(1)}, u32[]{:S(2)}, u32[]{:S(2)}) collective-permute-start(bf16[256,128]{1,0:T(8,128)(2,1)S(1)} %get-tuple-element.61.mine), channel_id=1, source_target_pairs={{4,12},{12,4},{20,28},{28,20},{36,44},{44,36},{52,60},{60,52},{68,... | collective-permute-start | bytes 196616 | tf_op jit(solution)/shard_map/ppermute | solution.py:71
  105.1 2.7 %collective-permute-start.32 = (f32[64,128]{1,0:T(8,128)S(1)}, f32[64,128]{1,0:T(8,128)S(1)}, u32[]{:S(2)}, u32[]{:S(2)}) collective-permute-start(f32[64,128]{1,0:T(8,128)S(1)} %get-tuple-element.62.w), channel_id=1, source_target_pairs={{0,8},{4,12},{8,0},{12,4},{16,24},{20,28},{24,16},{28,20},{32,40},... | collective-permute-start | bytes 98312 | tf_op jit(solution)/shard_map/ppermute | solution.py:71
  108.5 2.2 %collective-permute-start.33 = (bf16[256,128]{1,0:T(8,128)(2,1)S(1)}, bf16[256,128]{1,0:T(8,128)(2,1)S(1)}, u32[]{:S(2)}, u32[]{:S(2)}) collective-permute-start(bf16[256,128]{1,0:T(8,128)(2,1)S(1)} %sum_other.1), channel_id=1, source_target_pairs={{0,4},{4,8},{8,12},{12,0},{16,20},{20,24},{24,28},{28,16},{32,36},... | collective-permute-start | bytes 196616 | tf_op jit(solution)/shard_map/ppermute | solution.py:71
  112.5 2.5 %collective-permute-start.36 = (f32[64,128]{1,0:T(8,128)S(1)}, f32[64,128]{1,0:T(8,128)S(1)}, u32[]{:S(2)}, u32[]{:S(2)}) collective-permute-start(f32[64,128]{1,0:T(8,128)S(1)} %get-tuple-element.64.w0), channel_id=1, source_target_pairs={{0,3},{1,0},{2,1},{3,2},{4,7},{5,4},{6,5},{7,6},{8,11},{9,8},{10,9... | collective-permute-start | bytes 98312 | tf_op jit(solution)/shard_map/ppermute | solution.py:97
  116.6 2.7 %collective-permute-done.35.w2 = f32[64,128]{1,0:T(8,128)S(1)} collective-permute-done((f32[64,128]{1,0:T(8,128)S(1)}, f32[64,128]{1,0:T(8,128)S(1)}, u32[]{:S(2)}, u32[]{:S(2)}) %collective-permute-start.35) | collective-permute-done | bytes 32800 | tf_op jit(solution)/shard_map/ppermute | solution.py:97
  (87 shorter events, 49.4 us)
Async XLA Ops:
  0.6 11.5 %collective-permute-start = (bf16[256,128]{1,0:T(8,128)(2,1)}, bf16[256,128]{1,0:T(8,128)(2,1)S(1)}, u32[]{:S(2)}, u32[]{:S(2)}) collective-permute-start(bf16[256,128]{1,0:T(8,128)(2,1)} %own.1), channel_id=1, source_target_pairs={{0,12},{4,0},{8,4},{12,8},{16,28},{20,16},{24,20},{28,24},{32,44},... | collective-permute-start | bytes 196616 | tf_op jit(solution)/shard_map/ppermute | solution.py:71
  3.9 9.1 %collective-permute-start.1 = (bf16[256,128]{1,0:T(8,128)(2,1)}, bf16[256,128]{1,0:T(8,128)(2,1)S(1)}, u32[]{:S(2)}, u32[]{:S(2)}) collective-permute-start(bf16[256,128]{1,0:T(8,128)(2,1)} %own.1), channel_id=1, source_target_pairs={{4,12},{12,4},{20,28},{28,20},{36,44},{44,36},{52,60},{60,52},{68,... | collective-permute-start | bytes 196616 | tf_op jit(solution)/shard_map/ppermute | solution.py:71
  13.9 9.4 %collective-permute-start.6 = (bf16[512,128]{1,0:T(8,128)(2,1)S(1)}, bf16[512,128]{1,0:T(8,128)(2,1)S(1)}, u32[]{:S(2)}, u32[]{:S(2)}) collective-permute-start(bf16[512,128]{1,0:T(8,128)(2,1)S(1)} %pair_up.1.refs_0_), channel_id=1, source_target_pairs={{0,48},{4,196},{8,56},{12,204},{16,0},{20,212},{24,8},{28,220},{32... | collective-permute-start | bytes 393224 | tf_op jit(solution)/shard_map/ppermute | solution.py:71
  16.6 6.8 %collective-permute-start.5 = (bf16[512,128]{1,0:T(8,128)(2,1)S(1)}, bf16[512,128]{1,0:T(8,128)(2,1)S(1)}, u32[]{:S(2)}, u32[]{:S(2)}) collective-permute-start(bf16[512,128]{1,0:T(8,128)(2,1)S(1)} %pair_up.1.refs_0_), channel_id=1, source_target_pairs={{0,32},{4,132},{8,40},{12,140},{16,48},{20,148},{24,56},{28,156},{... | collective-permute-start | bytes 393224 | tf_op jit(solution)/shard_map/ppermute | solution.py:71
  17.0 6.4 %collective-permute-start.2 = (bf16[512,128]{1,0:T(8,128)(2,1)S(1)}, bf16[512,128]{1,0:T(8,128)(2,1)S(1)}, u32[]{:S(2)}, u32[]{:S(2)}) collective-permute-start(bf16[512,128]{1,0:T(8,128)(2,1)S(1)} %pair_up.1.refs_0_), channel_id=1, source_target_pairs={{0,16},{4,68},{8,24},{12,76},{16,32},{20,84},{24,40},{28,92},{32,4... | collective-permute-start | bytes 393224 | tf_op jit(solution)/shard_map/ppermute | solution.py:71
  26.0 6.7 %collective-permute-start.3 = (bf16[1024,128]{1,0:T(8,128)(2,1)S(1)}, bf16[1024,128]{1,0:T(8,128)(2,1)S(1)}, u32[]{:S(2)}, u32[]{:S(2)}) collective-permute-start(bf16[1024,128]{1,0:T(8,128)(2,1)S(1)} %place_low.1.refs_3_.refs_2_.refs_0_), channel_id=1, source_target_pairs={{0,64},{4,20},{8,72},{12,28},{16,80},{20,36},{24,88},{28,44},{32,9... | collective-permute-start | bytes 786440 | tf_op jit(solution)/shard_map/ppermute | solution.py:71
  26.0 9.5 %collective-permute-start.9 = (bf16[1024,128]{1,0:T(8,128)(2,1)S(1)}, bf16[1024,128]{1,0:T(8,128)(2,1)S(1)}, u32[]{:S(2)}, u32[]{:S(2)}) collective-permute-start(bf16[1024,128]{1,0:T(8,128)(2,1)S(1)} %place_high.1.refs_3_.refs_1_), channel_id=1, source_target_pairs={{0,64},{4,20},{8,72},{12,28},{16,80},{20,36},{24,88},{28,44},{32,9... | collective-permute-start | bytes 786440 | tf_op jit(solution)/shard_map/ppermute | solution.py:71
  26.2 9.3 %collective-permute-start.10 = (bf16[1024,128]{1,0:T(8,128)(2,1)S(1)}, bf16[1024,128]{1,0:T(8,128)(2,1)S(1)}, u32[]{:S(2)}, u32[]{:S(2)}) collective-permute-start(bf16[1024,128]{1,0:T(8,128)(2,1)S(1)} %place_low.1.refs_3_.refs_2_.refs_0_), channel_id=1, source_target_pairs={{0,192},{4,52},{8,200},{12,60},{16,208},{20,4},{24,216},{28,12},{3... | collective-permute-start | bytes 786440 | tf_op jit(solution)/shard_map/ppermute | solution.py:71
  29.3 8.7 %collective-permute-start.8 = (bf16[1024,128]{1,0:T(8,128)(2,1)S(1)}, bf16[1024,128]{1,0:T(8,128)(2,1)S(1)}, u32[]{:S(2)}, u32[]{:S(2)}) collective-permute-start(bf16[1024,128]{1,0:T(8,128)(2,1)S(1)} %collective-permute-done.7.refs_5_), channel_id=1, source_target_pairs={{0,192},{4,52},{8,200},{12,60},{16,208},{20,4},{24,216},{28,12},{3... | collective-permute-start | bytes 786440 | tf_op jit(solution)/shard_map/ppermute | solution.py:71
  32.7 6.7 %collective-permute-start.4 = (bf16[1024,128]{1,0:T(8,128)(2,1)S(1)}, bf16[1024,128]{1,0:T(8,128)(2,1)S(1)}, u32[]{:S(2)}, u32[]{:S(2)}) collective-permute-start(bf16[1024,128]{1,0:T(8,128)(2,1)S(1)} %collective-permute-done.3.refs_2_), channel_id=1, source_target_pairs={{0,64},{4,20},{8,72},{12,28},{16,80},{20,36},{24,88},{28,44},{32,9... | collective-permute-start | bytes 786440 | tf_op jit(solution)/shard_map/ppermute | solution.py:71
  46.6 7.6 %collective-permute-start.14 = (bf16[256,128]{1,0:T(8,128)(2,1)S(1)}, bf16[256,128]{1,0:T(8,128)(2,1)S(1)}, u32[]{:S(2)}, u32[]{:S(2)}) collective-permute-start(bf16[256,128]{1,0:T(8,128)(2,1)S(1)} %get-tuple-element.37), channel_id=1, source_target_pairs={{0,2},{1,3},{2,0},{3,1},{4,6},{5,7},{6,4},{7,5},{8,10},{9,11},{10,... | collective-permute-start | bytes 196616 | tf_op jit(solution)/shard_map/ppermute | solution.py:97
  47.8 6.4 %collective-permute-start.15 = (bf16[256,128]{1,0:T(8,128)(2,1)S(1)}, bf16[256,128]{1,0:T(8,128)(2,1)S(1)}, u32[]{:S(2)}, u32[]{:S(2)}) collective-permute-start(bf16[256,128]{1,0:T(8,128)(2,1)S(1)} %get-tuple-element.38), channel_id=1, source_target_pairs={{0,3},{1,0},{2,1},{3,2},{4,7},{5,4},{6,5},{7,6},{8,11},{9,8},{10,9... | collective-permute-start | bytes 196616 | tf_op jit(solution)/shard_map/ppermute | solution.py:97
  57.6 8.0 %collective-permute-start.17 = (bf16[320,128]{1,0:T(8,128)(2,1)S(1)}, bf16[320,128]{1,0:T(8,128)(2,1)S(1)}, u32[]{:S(2)}, u32[]{:S(2)}) collective-permute-start(bf16[320,128]{1,0:T(8,128)(2,1)S(1)} %get-tuple-element.42), channel_id=1, source_target_pairs={{0,2},{1,3},{2,0},{3,1},{4,6},{5,7},{6,4},{7,5},{8,10},{9,11},{10,... | collective-permute-start | bytes 245768 | tf_op jit(solution)/shard_map/ppermute | solution.py:97
  58.6 7.0 %collective-permute-start.18 = (bf16[320,128]{1,0:T(8,128)(2,1)S(1)}, bf16[320,128]{1,0:T(8,128)(2,1)S(1)}, u32[]{:S(2)}, u32[]{:S(2)}) collective-permute-start(bf16[320,128]{1,0:T(8,128)(2,1)S(1)} %get-tuple-element.43), channel_id=1, source_target_pairs={{0,3},{1,0},{2,1},{3,2},{4,7},{5,4},{6,5},{7,6},{8,11},{9,8},{10,9... | collective-permute-start | bytes 245768 | tf_op jit(solution)/shard_map/ppermute | solution.py:97
  71.6 8.7 %collective-permute-start.24 = (bf16[1216,128]{1,0:T(8,128)(2,1)S(1)}, bf16[1216,128]{1,0:T(8,128)(2,1)S(1)}, u32[]{:S(2)}, u32[]{:S(2)}) collective-permute-start(bf16[1216,128]{1,0:T(8,128)(2,1)S(1)} %get-tuple-element.48.refs_6_), channel_id=1, source_target_pairs={{0,64},{4,20},{8,72},{12,28},{16,80},{20,36},{24,88},{28,44},{32,9... | collective-permute-start | bytes 933896 | tf_op jit(solution)/shard_map/ppermute | solution.py:71
  72.5 7.8 %collective-permute-start.25 = (bf16[1024,128]{1,0:T(8,128)(2,1)S(1)}, bf16[1024,128]{1,0:T(8,128)(2,1)S(1)}, u32[]{:S(2)}, u32[]{:S(2)}) collective-permute-start(bf16[1024,128]{1,0:T(8,128)(2,1)S(1)} %get-tuple-element.52), channel_id=1, source_target_pairs={{0,192},{4,52},{8,200},{12,60},{16,208},{20,4},{24,216},{28,12},{3... | collective-permute-start | bytes 786440 | tf_op jit(solution)/shard_map/ppermute | solution.py:71
  77.5 6.7 %collective-permute-start.22 = (bf16[1024,128]{1,0:T(8,128)(2,1)S(1)}, bf16[1024,128]{1,0:T(8,128)(2,1)S(1)}, u32[]{:S(2)}, u32[]{:S(2)}) collective-permute-start(bf16[1024,128]{1,0:T(8,128)(2,1)S(1)} %get-tuple-element.50.refs_10_), channel_id=1, source_target_pairs={{0,64},{4,20},{8,72},{12,28},{16,80},{20,36},{24,88},{28,44},{32,9... | collective-permute-start | bytes 786440 | tf_op jit(solution)/shard_map/ppermute | solution.py:71
  81.7 6.3 %collective-permute-start.27 = (bf16[1216,128]{1,0:T(8,128)(2,1)S(1)}, bf16[1216,128]{1,0:T(8,128)(2,1)S(1)}, u32[]{:S(2)}, u32[]{:S(2)}) collective-permute-start(bf16[1216,128]{1,0:T(8,128)(2,1)S(1)} %get-tuple-element.55), channel_id=1, source_target_pairs={{0,192},{4,52},{8,200},{12,60},{16,208},{20,4},{24,216},{28,12},{3... | collective-permute-start | bytes 933896 | tf_op jit(solution)/shard_map/ppermute | solution.py:71
  83.3 7.8 %collective-permute-start.26 = (bf16[1408,128]{1,0:T(8,128)(2,1)S(1)}, bf16[1408,128]{1,0:T(8,128)(2,1)S(1)}, u32[]{:S(2)}, u32[]{:S(2)}) collective-permute-start(bf16[1408,128]{1,0:T(8,128)(2,1)S(1)} %get-tuple-element.54.refs_9_), channel_id=1, source_target_pairs={{0,64},{4,20},{8,72},{12,28},{16,80},{20,36},{24,88},{28,44},{32,9... | collective-permute-start | bytes 1081352 | tf_op jit(solution)/shard_map/ppermute | solution.py:71
  91.3 7.9 %collective-permute-start.28 = (bf16[704,128]{1,0:T(8,128)(2,1)S(1)}, bf16[704,128]{1,0:T(8,128)(2,1)S(1)}, u32[]{:S(2)}, u32[]{:S(2)}) collective-permute-start(bf16[704,128]{1,0:T(8,128)(2,1)S(1)} %get-tuple-element.57), channel_id=1, source_target_pairs={{0,16},{4,68},{8,24},{12,76},{16,32},{20,84},{24,40},{28,92},{32,4... | collective-permute-start | bytes 540680 | tf_op jit(solution)/shard_map/ppermute | solution.py:71
  91.4 7.8 %collective-permute-start.29 = (bf16[704,128]{1,0:T(8,128)(2,1)S(1)}, bf16[704,128]{1,0:T(8,128)(2,1)S(1)}, u32[]{:S(2)}, u32[]{:S(2)}) collective-permute-start(bf16[704,128]{1,0:T(8,128)(2,1)S(1)} %get-tuple-element.58), channel_id=1, source_target_pairs={{0,32},{4,132},{8,40},{12,140},{16,48},{20,148},{24,56},{28,156},{... | collective-permute-start | bytes 540680 | tf_op jit(solution)/shard_map/ppermute | solution.py:71
  100.4 11.5 %collective-permute-start.31 = (bf16[256,128]{1,0:T(8,128)(2,1)S(1)}, bf16[256,128]{1,0:T(8,128)(2,1)S(1)}, u32[]{:S(2)}, u32[]{:S(2)}) collective-permute-start(bf16[256,128]{1,0:T(8,128)(2,1)S(1)} %get-tuple-element.61.mine), channel_id=1, source_target_pairs={{4,12},{12,4},{20,28},{28,20},{36,44},{44,36},{52,60},{60,52},{68,... | collective-permute-start | bytes 196616 | tf_op jit(solution)/shard_map/ppermute | solution.py:71
  105.1 6.8 %collective-permute-start.32 = (f32[64,128]{1,0:T(8,128)S(1)}, f32[64,128]{1,0:T(8,128)S(1)}, u32[]{:S(2)}, u32[]{:S(2)}) collective-permute-start(f32[64,128]{1,0:T(8,128)S(1)} %get-tuple-element.62.w), channel_id=1, source_target_pairs={{0,8},{4,12},{8,0},{12,4},{16,24},{20,28},{24,16},{28,20},{32,40},... | collective-permute-start | bytes 98312 | tf_op jit(solution)/shard_map/ppermute | solution.py:71
  108.5 8.1 %collective-permute-start.33 = (bf16[256,128]{1,0:T(8,128)(2,1)S(1)}, bf16[256,128]{1,0:T(8,128)(2,1)S(1)}, u32[]{:S(2)}, u32[]{:S(2)}) collective-permute-start(bf16[256,128]{1,0:T(8,128)(2,1)S(1)} %sum_other.1), channel_id=1, source_target_pairs={{0,4},{4,8},{8,12},{12,0},{16,20},{20,24},{24,28},{28,16},{32,36},... | collective-permute-start | bytes 196616 | tf_op jit(solution)/shard_map/ppermute | solution.py:71
  (18 other events, 100.3 us)

commit v3 on v2

--- a/solution.py
+++ b/solution.py
@@ -109,22 +109,6 @@
     return pl.CostEstimate(flops=size // 64, bytes_accessed=size // 64, transcendentals=0)
 
 
-def touch_kernel(meta, stored, out):
-    out[...] = stored[0, 0:16, :].astype(F32)
-
-
-def touch(meta, stored):
-    return pl.pallas_call(
-        touch_kernel,
-        out_shape=jax.ShapeDtypeStruct((16, B), F32),
-        in_specs=[SMEM, VMEM],
-        out_specs=VMEM,
-        compiler_params=params(),
-        cost_estimate=small_cost(1 << 10),
-        name="touch_blocks",
-    )(meta, stored)
-
-
 def pair_up_kernel(core, own, near, far, out):
     first = core[0] == 0
     out[0:ROWS] = jnp.where(first, own[...], near[...])
@@ -138,7 +122,7 @@
         in_specs=[SMEM] + [VMEM] * 3,
         out_specs=VMEM,
         compiler_params=params(),
-        cost_estimate=small_cost(1 << 16),
+        cost_estimate=small_cost(LONG),
         name="pair_up",
     )(core, own, near, far)
 
@@ -293,18 +277,18 @@
 
 def sibling_terms(extra, outs, extra_outs):
     total = extra[0][...] + joined(extra[1], 8 * ROWS)
-    split(total, outs[0], 4 * ROWS)
     extra_outs[0][...] = total
     extra_outs[1][...] = extra[2][...]
 
 
 def spread_terms(extra, outs, extra_outs):
-    half_1, half_3, own = extra[:3]
-    part = slice(0, 4 * ROWS)
+    half_1, half_3, own, other = extra[:4]
+    total = own[...] + other[...]
     for out, half in zip(outs, (half_1, half_3)):
-        out[part] = (out[part].astype(F32) + half[part].astype(F32)).astype(BF16)
-        split(own[...], out, 4 * ROWS)
-    outs[0][4 * ROWS + SPLIT :] = half_1[4 * ROWS :]
+        part = slice(0, 4 * ROWS)
+        out[part] = (out[part].astype(F32) + half[...].astype(F32)).astype(BF16)
+        split(total, out, 4 * ROWS)
+    extra_outs[0][...] = total
 
 
 def pass_on(extra, outs, extra_outs):
@@ -378,9 +362,9 @@
     )(*args)
 
 
-def sum_kernel(a, low, high, own, t0, t1, t2, t3, w):
+def sum_kernel(a, low, high, own, two, t0, t1, t2, t3, w):
     row = 4 * ROWS
-    total = (own[...] + joined(low, row + SPLIT)) + (joined(low, row) + joined(high, row))
+    total = (own[...] + two[...]) + (joined(low, row) + joined(high, row))
     w[...] = total
     for d, out in enumerate((t0, t1, t2, t3)):
         half_ref = high if d >= 2 else low
@@ -396,7 +380,7 @@
         out_shape=[jax.ShapeDtypeStruct((2 * ROWS, B), BF16)]
         + [jax.ShapeDtypeStruct((2 * ROWS + SPLIT, B), BF16)] * 3
         + [jax.ShapeDtypeStruct((PIECE, B), F32)],
-        in_specs=[VMEM] * 4,
+        in_specs=[VMEM] * 5,
         out_specs=[VMEM] * 5,
         compiler_params=params(),
         cost_estimate=small_cost(1 << 18),
@@ -447,28 +431,9 @@
     )(meta, *arrays)
 
 
-def meet_kernel(meta, mine, far, w, w_z, own, total):
+def meet_kernel(scaling, meta, mine, far, w0, w1, w2, w3, own, weight_grad):
     first = meta[PLACE + 1] == 0
     own[...] = jnp.where(first, mine[...], far[...])
-    total[...] = w[...] + w_z[...]
-
-
-def meet(meta, *arrays):
-    return pl.pallas_call(
-        meet_kernel,
-        out_shape=[jax.ShapeDtypeStruct((ROWS, B), BF16), jax.ShapeDtypeStruct((PIECE, B), F32)],
-        in_specs=[SMEM] + [VMEM] * 4,
-        out_specs=[VMEM] * 2,
-        compiler_params=params(),
-        cost_estimate=small_cost(1 << 15),
-        name="meet_other_z",
-    )(meta, *arrays)
-
-
-def last_kernel(scaling, meta, own, crossed, w0, w1, w2, w3, out, weight_grad):
-    for s in range(2):
-        part = slice(s * B, (s + 1) * B)
-        out[part] = (own[part].astype(F32) + crossed[part].astype(F32)).T.astype(BF16)
     rep = meta[PLACE]
     for back, piece in enumerate((w0, w1, w2, w3)):
         rows = pl.ds(pl.multiple_of(lax.rem(rep + 4 - back, 4) * 32, 32), 32)
@@ -476,16 +441,34 @@
         weight_grad[rows, B : 2 * B] = piece[32:64] * scaling
 
 
-def last_sum(meta, scaling, *arrays):
-    return pl.pallas_call(
-        functools.partial(last_kernel, scaling),
+def meet(meta, scaling, *arrays):
+    return pl.pallas_call(
+        functools.partial(meet_kernel, scaling),
         out_shape=[jax.ShapeDtypeStruct((ROWS, B), BF16), jax.ShapeDtypeStruct((B, 2 * B), F32)],
         in_specs=[SMEM] + [VMEM] * 6,
         out_specs=[VMEM] * 2,
         compiler_params=params(),
+        cost_estimate=small_cost(LONG),
+        name="meet_other_z",
+    )(meta, *arrays)
+
+
+def last_kernel(own, crossed, out):
+    for s in range(2):
+        part = slice(s * B, (s + 1) * B)
+        out[part] = (own[part].astype(F32) + crossed[part].astype(F32)).T.astype(BF16)
+
+
+def last_sum(*arrays):
+    return pl.pallas_call(
+        last_kernel,
+        out_shape=jax.ShapeDtypeStruct((ROWS, B), BF16),
+        in_specs=[VMEM] * 2,
+        out_specs=VMEM,
+        compiler_params=params(),
         cost_estimate=small_cost(1 << 16),
         name="last_sum",
-    )(meta, *arrays)
+    )(*arrays)
 
 
 def per_device(features, adjacency, block_list, block_counts, weight, cotangent):
@@ -510,10 +493,9 @@
     near_unit, far_unit = cross(features, True), other_z(features)
     pair = pair_up(core.reshape(1), features, near_unit, far_unit)
     x1, x2, x3 = small_axis(pair, 1), small_axis(pair, 2), small_axis(pair, 3)
-    touched = touch(meta, stored)
-    (low,) = place("place_low", [[(0, 0, 2), (1, 0, 2)]], [pair, x1])
+    (low,) = place("place_low", [[(0, 0, 2), (1, 0, 2)]], [pair, x1], [meta])
     n1_low, n3_low = large_axis(low, 1), large_axis(low, 3)
-    (high,) = place("place_high", [[(0, 0, 2), (1, 0, 2)]], [x2, x3], [touched, low])
+    (high,) = place("place_high", [[(0, 0, 2), (1, 0, 2)]], [x2, x3], [low])
     n1_high, n3_high = large_axis(high, 1), large_axis(high, 3)
     (acc,) = forward(meta, stored, 0, [low, high], None, False)
     f1, f3 = large_axis(n1_low, 1), large_axis(n3_high, 3)
@@ -535,35 +517,34 @@
     far_s = sibling(far_b)
     (near_b,) = bwd(8, (16,), extra=[far_b])
     h1, h3, w8, near_b = bwd(
-        24, (4, 4), far_s, extra=[w4, far_s, near_b], finish=sibling_terms, tails=(SPLIT, 0), extra_out=[w, near_b]
+        24, (4, 4), far_s, extra=[w4, far_s, near_b], finish=sibling_terms, extra_out=[w, near_b]
     )
     f1, f3, near_s = large_axis(h1, 1), large_axis(h3, 3), sibling(near_b)
+    w8_z = row_permute(w8, lambda y, x, z, c: at(y, x, 1 - z, c))
     (own_b,) = bwd(32, (8,), extra=[h1])
     g1_high, g3_low, own_b = bwd(40, (4, 4), near_s, extra=[own_b], finish=pass_on, extra_out=[own_b])
     r1_high, r3_low = large_axis(g1_high, 1), large_axis(g3_low, 3)
     own_s = sibling(own_b)
-    g1_low, g3_high = bwd(
+    g1_low, g3_high, w16 = bwd(
         48,
         (4, 4),
         near_s,
         add_from=8,
-        extra=[f1, f3, w8, g1_high],
+        extra=[f1, f3, w8, w8_z, g1_high],
         finish=spread_terms,
-        tails=(2 * SPLIT, SPLIT),
+        tails=(SPLIT, SPLIT),
+        extra_out=[w8],
         size=LONG,
     )
-    r1_low, r3_high = large_axis(g1_low, 1), large_axis(g3_high, 3)
+    r1_low, r3_high, w16_two = large_axis(g1_low, 1), large_axis(g3_high, 3), large_axis(w16, 2)
     (g0,) = bwd(56, (8,), own_s, extra=[r1_high, r3_low, g1_low], finish=add_halves, size=LONG)
-    t0, t1, t2, t3, w32 = sum_groups(g0, r1_low, r3_high, w8)
+    t0, t1, t2, t3, w64 = sum_groups(g0, r1_low, r3_high, w16, w16_two)
     sums = [t0, small_axis(t1, 1), small_axis(t2, 2), small_axis(t3, 3)]
-    mine, w = sum_mine(meta, *sums, w32)
-    far = other_z(mine)
-    w_z = row_permute(w, lambda y, x, z, c: at(y, x, 1 - z, c))
+    mine, w = sum_mine(meta, *sums, w64)
+    far, pieces = other_z(mine), [w] + [turn(w, d) for d in (1, 2, 3)]
     crossed = cross(sum_other(meta, mine, *sums), False)
-    own, w = meet(meta, mine, far, w, w_z)
-    feature_grad, weight_grad = last_sum(
-        meta, nodes ** (-0.5), own, crossed, w, *[turn(w, d) for d in (1, 2, 3)]
-    )
+    own, weight_grad = meet(meta, nodes ** (-0.5), mine, far, *pieces)
+    feature_grad = last_sum(own, crossed)
     return activations, feature_grad, weight_grad
 
 

time: 123 us -> 123 us (level)
  starting transfers between devices: 57.5 us -> 59.4 us
  waiting for transfers between devices: 33.1 us -> 31.4 us
    ppermute x28 -> x29, starting transfers between devices: 45.9 us -> 48.1 us  [row_permute(): return lax.ppermute(array, 'row', pairs)]
    unnamed x11 -> x27, local copies, waits for them, and re-layouts: 5.05 us -> 6.42 us
    ppermute x28 -> x29, waiting for transfers between devices: 17.9 us -> 17.3 us  [row_permute(): return lax.ppermute(array, 'row', pairs)]
    pallas_call x3 -> x2, Pallas kernels: 2.56 us -> 2.02 us  [the longest x1 1.28 us: meet(): pl.pallas_call(functools.partial(meet_kernel, scaling), out_shape=[jax.Sh...]
  transfers between devices with their start and end apart: 37 -> 38, of which waited for: 18 -> 14; matrix products, arithmetic and copies ran while one was open for 2% -> 1% of each run, Pallas kernels for 13% -> 13%
where the time goes in v3:
time: 123 us; the launch traced here: 122 us
  starting transfers between devices  59.4 us (48%)
  waiting for transfers between devices  31.4 us (26%)
  Pallas kernels  23.5 us (19%)
  local copies, waits for them, and re-layouts  6.72 us (5%)
    ppermute x29, starting transfers between devices, row_permute(): return lax.ppermute(array, 'row', pairs)  48.1 us
    ppermute x29, waiting for transfers between devices, row_permute(): return lax.ppermute(array, 'row', pairs)  17.3 us
    ppermute x9, waiting for transfers between devices, turn(): return lax.ppermute(array, 'rep', [(q, (q + d) % 4) for q in range(4)])  14.1 us
    ppermute x9, starting transfers between devices, turn(): return lax.ppermute(array, 'rep', [(q, (q + d) % 4) for q in range(4)])  11.3 us
    pallas_call x7, Pallas kernels, backward(): pl.pallas_call(functools.partial(backward_kernel, first_section, sizes, a...  11 us
    pallas_call x4, Pallas kernels, forward(): pl.pallas_call(functools.partial(forward_kernel, first_section, sizes, fi...  7.12 us
    unnamed x27, local copies, waits for them, and re-layouts  6.42 us
  transfers between devices with their start and end apart: 38, of which 14 were waited for; matrix products, arithmetic and copies ran while one was open for 1% of the time, Pallas kernels for 13%

profile of v3, /device:TPU:1, one launch (start us, length us, event | category | flops | bytes accessed | tf_op | source)
XLA Modules:
  0.0 122.2 jit_solution(9779868752445678173)
XLA Ops:
  0.6 3.3 %collective-permute-start = (bf16[256,128]{1,0:T(8,128)(2,1)}, bf16[256,128]{1,0:T(8,128)(2,1)S(1)}, u32[]{:S(2)}, u32[]{:S(2)}) collective-permute-start(bf16[256,128]{1,0:T(8,128)(2,1)} %own.1), channel_id=1, source_target_pairs={{0,12},{4,0},{8,4},{12,8},{16,28},{20,16},{24,20},{28,24},{32,44},... | collective-permute-start | bytes 196616 | tf_op jit(solution)/shard_map/ppermute | solution.py:71
  3.9 7.1 %collective-permute-start.1 = (bf16[256,128]{1,0:T(8,128)(2,1)}, bf16[256,128]{1,0:T(8,128)(2,1)S(1)}, u32[]{:S(2)}, u32[]{:S(2)}) collective-permute-start(bf16[256,128]{1,0:T(8,128)(2,1)} %own.1), channel_id=1, source_target_pairs={{4,12},{12,4},{20,28},{28,20},{36,44},{44,36},{52,60},{60,52},{68,... | collective-permute-start | bytes 196616 | tf_op jit(solution)/shard_map/ppermute | solution.py:71
  14.0 2.7 %collective-permute-start.6 = (bf16[512,128]{1,0:T(8,128)(2,1)S(1)}, bf16[512,128]{1,0:T(8,128)(2,1)S(1)}, u32[]{:S(2)}, u32[]{:S(2)}) collective-permute-start(bf16[512,128]{1,0:T(8,128)(2,1)S(1)} %pair_up.1.refs_0_), channel_id=1, source_target_pairs={{0,48},{4,196},{8,56},{12,204},{16,0},{20,212},{24,8},{28,220},{32... | collective-permute-start | bytes 393224 | tf_op jit(solution)/shard_map/ppermute | solution.py:71
  17.9 5.5 %collective-permute-done.2.refs_1_ = bf16[512,128]{1,0:T(8,128)(2,1)S(1)} collective-permute-done((bf16[512,128]{1,0:T(8,128)(2,1)S(1)}, bf16[512,128]{1,0:T(8,128)(2,1)S(1)}, u32[]{:S(2)}, u32[]{:S(2)}) %collective-permute-start.2) | collective-permute-done | bytes 131104 | tf_op jit(solution)/shard_map/ppermute | solution.py:71
  23.5 2.6 %collective-permute-start.7 = (bf16[1024,128]{1,0:T(8,128)(2,1)S(1)}, bf16[1024,128]{1,0:T(8,128)(2,1)S(1)}, u32[]{:S(2)}, u32[]{:S(2)}) collective-permute-start(bf16[1024,128]{1,0:T(8,128)(2,1)S(1)} %place_high.1.refs_3_.refs_1_), channel_id=1, source_target_pairs={{0,192},{4,52},{8,200},{12,60},{16,208},{20,4},{24,216},{28,12},{3... | collective-permute-start | bytes 786440 | tf_op jit(solution)/shard_map/ppermute | solution.py:71
  26.2 2.5 %collective-permute-start.10 = (bf16[1024,128]{1,0:T(8,128)(2,1)S(1)}, bf16[1024,128]{1,0:T(8,128)(2,1)S(1)}, u32[]{:S(2)}, u32[]{:S(2)}) collective-permute-start(bf16[1024,128]{1,0:T(8,128)(2,1)S(1)} %place_low.1.refs_2_.refs_0_), channel_id=1, source_target_pairs={{0,192},{4,52},{8,200},{12,60},{16,208},{20,4},{24,216},{28,12},{3... | collective-permute-start | bytes 786440 | tf_op jit(solution)/shard_map/ppermute | solution.py:71
  29.4 3.4 %collective-permute-start.8 = (bf16[1024,128]{1,0:T(8,128)(2,1)S(1)}, bf16[1024,128]{1,0:T(8,128)(2,1)S(1)}, u32[]{:S(2)}, u32[]{:S(2)}) collective-permute-start(bf16[1024,128]{1,0:T(8,128)(2,1)S(1)} %collective-permute-done.7.refs_5_), channel_id=1, source_target_pairs={{0,192},{4,52},{8,200},{12,60},{16,208},{20,4},{24,216},{28,12},{3... | collective-permute-start | bytes 786440 | tf_op jit(solution)/shard_map/ppermute | solution.py:71
  32.8 3.4 %copy-done = bf16[1,1,256,128,128]{4,3,2,1,0:T(8,128)(2,1)S(1)} copy-done((bf16[1,1,256,128,128]{4,3,2,1,0:T(8,128)(2,1)S(1)}, bf16[1,1,256,128,128]{4,3,2,1,0:T(8,128)(2,1)}, u32[]{:S(2)}) %copy-start) | copy-done | bytes 8388632
  41.9 2.5 %forward_slots.6.refs_4_ = f32[8,128,128]{2,1,0:T(8,128)S(1)} custom-call(s32[962]{0:T(1024)S(1)} %concatenate.3.refs_2_.refs_0_.meta, bf16[256,128,128]{2,1,0:T(8,128)(2,1)S(1)} %bitcast.6, bf16[6144,128]{1,0:T(8,128)(2,1)S(1)} %collective-permute-done.12.refs_2_, f32[8,128,128]{2,1,0:T(8,128)S(1)} %forward_slots.5.refs_2_.refs_3_), custom_call_target="tpu_custom_call" | custom-call | flops 12582912 | bytes 12582912 | tf_op jit(solution)/shard_map/forward_slots/pallas_call | solution.py:204
  44.5 1.9 %forward_slots.7 = (f32[256,128]{1,0:T(8,128)S(1)}, bf16[256,128]{1,0:T(8,128)(2,1)S(1)}, bf16[256,128]{1,0:T(8,128)(2,1)S(1)}, bf16[256,128]{1,0:T(8,128)(2,1)S(1)}) custom-call(s32[962]{0:T(1024)S(1)} %concatenate.3.refs_2_.refs_0_.meta, bf16[256,128,128]{2,1,0:T(8,128)(2,1)S(1)} %bitcast.7, bf16[2048,128]{1,0:T(8,128)(2,1)S(1)} %place_far.1.refs_2_, ...), custom_call_target="tpu_custom_call" | custom-call | flops 8388608 | bytes 8388608 | tf_op jit(solution)/shard_map/forward_slots/pallas_call | solution.py:204
  50.3 2.0 %collective-permute-done.13.p1 = bf16[256,128]{1,0:T(8,128)(2,1)S(1)} collective-permute-done((bf16[256,128]{1,0:T(8,128)(2,1)S(1)}, bf16[256,128]{1,0:T(8,128)(2,1)S(1)}, u32[]{:S(2)}, u32[]{:S(2)}) %collective-permute-start.13) | collective-permute-done | bytes 65568 | tf_op jit(solution)/shard_map/ppermute | solution.py:97
  52.3 2.7 %collective-permute-done.14.p2 = bf16[256,128]{1,0:T(8,128)(2,1)S(1)} collective-permute-done((bf16[256,128]{1,0:T(8,128)(2,1)S(1)}, bf16[256,128]{1,0:T(8,128)(2,1)S(1)}, u32[]{:S(2)}, u32[]{:S(2)}) %collective-permute-start.14) | collective-permute-done | bytes 65568 | tf_op jit(solution)/shard_map/ppermute | solution.py:97
  61.8 4.6 %collective-permute-done.17.refs_4_.refs_8_ = bf16[320,128]{1,0:T(8,128)(2,1)S(1)} collective-permute-done((bf16[320,128]{1,0:T(8,128)(2,1)S(1)}, bf16[320,128]{1,0:T(8,128)(2,1)S(1)}, u32[]{:S(2)}, u32[]{:S(2)}) %collective-permute-start.17) | collective-permute-done | bytes 81952 | tf_op jit(solution)/shard_map/ppermute | solution.py:97
  68.8 2.3 %backward_slots.8.refs_9_ = bf16[4096,128]{1,0:T(8,128)(2,1)S(1)} custom-call(s32[962]{0:T(1024)S(1)} %concatenate.3.refs_2_.refs_0_.meta, bf16[256,128,128]{2,1,0:T(8,128)(2,1)S(1)} %bitcast.9, bf16[256,128]{1,0:T(8,128)(2,1)S(1)} %get-tuple-element.39.refs_2_, bf16[320,128]{1,0:T(8,128)(2,1)S(1)} %collective-permute-done.16.refs_3_.refs_7_, ...), custom_call_target="tpu_custom_call" | custom-call | flops 8388608 | bytes 8388608 | tf_op jit(solution)/shard_map/backward_slots/pallas_call | solution.py:353
  72.6 2.2 %collective-permute-start.25 = (bf16[1024,128]{1,0:T(8,128)(2,1)S(1)}, bf16[1024,128]{1,0:T(8,128)(2,1)S(1)}, u32[]{:S(2)}, u32[]{:S(2)}) collective-permute-start(bf16[1024,128]{1,0:T(8,128)(2,1)S(1)} %get-tuple-element.51), channel_id=1, source_target_pairs={{0,192},{4,52},{8,200},{12,60},{16,208},{20,4},{24,216},{28,12},{3... | collective-permute-start | bytes 786440 | tf_op jit(solution)/shard_map/ppermute | solution.py:71
  74.8 5.9 %collective-permute-start.26 = (f32[64,128]{1,0:T(8,128)S(1)}, f32[64,128]{1,0:T(8,128)S(1)}, u32[]{:S(2)}, u32[]{:S(2)}) collective-permute-start(f32[64,128]{1,0:T(8,128)S(1)} %get-tuple-element.52.refs_9_), channel_id=1, source_target_pairs={{0,8},{4,12},{8,0},{12,4},{16,24},{20,28},{24,16},{28,20},{32,40},... | collective-permute-start | bytes 98312 | tf_op jit(solution)/shard_map/ppermute | solution.py:71
  83.5 2.8 %collective-permute-start.23 = (bf16[1024,128]{1,0:T(8,128)(2,1)S(1)}, bf16[1024,128]{1,0:T(8,128)(2,1)S(1)}, u32[]{:S(2)}, u32[]{:S(2)}) collective-permute-start(bf16[1024,128]{1,0:T(8,128)(2,1)S(1)} %get-tuple-element.50), channel_id=1, source_target_pairs={{0,192},{4,52},{8,200},{12,60},{16,208},{20,4},{24,216},{28,12},{3... | collective-permute-start | bytes 786440 | tf_op jit(solution)/shard_map/ppermute | solution.py:71
  91.2 2.1 %collective-permute-done.22.refs_7_ = bf16[1024,128]{1,0:T(8,128)(2,1)S(1)} collective-permute-done((bf16[1024,128]{1,0:T(8,128)(2,1)S(1)}, bf16[1024,128]{1,0:T(8,128)(2,1)S(1)}, u32[]{:S(2)}, u32[]{:S(2)}) %collective-permute-start.22) | collective-permute-done | bytes 262176 | tf_op jit(solution)/shard_map/ppermute | solution.py:71
  96.1 1.8 %collective-permute-done.27.low = bf16[1216,128]{1,0:T(8,128)(2,1)S(1)} collective-permute-done((bf16[1216,128]{1,0:T(8,128)(2,1)S(1)}, bf16[1216,128]{1,0:T(8,128)(2,1)S(1)}, u32[]{:S(2)}, u32[]{:S(2)}) %collective-permute-start.27) | collective-permute-done | bytes 311328 | tf_op jit(solution)/shard_map/ppermute | solution.py:71
  98.2 3.8 %collective-permute-start.31 = (bf16[704,128]{1,0:T(8,128)(2,1)S(1)}, bf16[704,128]{1,0:T(8,128)(2,1)S(1)}, u32[]{:S(2)}, u32[]{:S(2)}) collective-permute-start(bf16[704,128]{1,0:T(8,128)(2,1)S(1)} %get-tuple-element.58), channel_id=1, source_target_pairs={{0,32},{4,132},{8,40},{12,140},{16,48},{20,148},{24,56},{28,156},{... | collective-permute-start | bytes 540680 | tf_op jit(solution)/shard_map/ppermute | solution.py:71
  102.1 2.0 %collective-permute-done.30.b = bf16[704,128]{1,0:T(8,128)(2,1)S(1)} collective-permute-done((bf16[704,128]{1,0:T(8,128)(2,1)S(1)}, bf16[704,128]{1,0:T(8,128)(2,1)S(1)}, u32[]{:S(2)}, u32[]{:S(2)}) %collective-permute-start.30) | collective-permute-done | bytes 180256 | tf_op jit(solution)/shard_map/ppermute | solution.py:71
  104.1 3.1 %collective-permute-done.31.c = bf16[704,128]{1,0:T(8,128)(2,1)S(1)} collective-permute-done((bf16[704,128]{1,0:T(8,128)(2,1)S(1)}, bf16[704,128]{1,0:T(8,128)(2,1)S(1)}, u32[]{:S(2)}, u32[]{:S(2)}) %collective-permute-start.31) | collective-permute-done | bytes 180256 | tf_op jit(solution)/shard_map/ppermute | solution.py:71
  107.8 3.3 %collective-permute-start.33 = (bf16[256,128]{1,0:T(8,128)(2,1)S(1)}, bf16[256,128]{1,0:T(8,128)(2,1)S(1)}, u32[]{:S(2)}, u32[]{:S(2)}) collective-permute-start(bf16[256,128]{1,0:T(8,128)(2,1)S(1)} %get-tuple-element.61.mine), channel_id=1, source_target_pairs={{4,12},{12,4},{20,28},{28,20},{36,44},{44,36},{52,60},{60,52},{68,... | collective-permute-start | bytes 196616 | tf_op jit(solution)/shard_map/ppermute | solution.py:71
  111.1 2.6 %collective-permute-start.36 = (f32[64,128]{1,0:T(8,128)S(1)}, f32[64,128]{1,0:T(8,128)S(1)}, u32[]{:S(2)}, u32[]{:S(2)}) collective-permute-start(f32[64,128]{1,0:T(8,128)S(1)} %get-tuple-element.62.w0), channel_id=1, source_target_pairs={{0,3},{1,0},{2,1},{3,2},{4,7},{5,4},{6,5},{7,6},{8,11},{9,8},{10,9... | collective-permute-start | bytes 98312 | tf_op jit(solution)/shard_map/ppermute | solution.py:97
  (104 shorter events, 44.9 us)
Async XLA Ops:
  0.6 11.5 %collective-permute-start = (bf16[256,128]{1,0:T(8,128)(2,1)}, bf16[256,128]{1,0:T(8,128)(2,1)S(1)}, u32[]{:S(2)}, u32[]{:S(2)}) collective-permute-start(bf16[256,128]{1,0:T(8,128)(2,1)} %own.1), channel_id=1, source_target_pairs={{0,12},{4,0},{8,4},{12,8},{16,28},{20,16},{24,20},{28,24},{32,44},... | collective-permute-start | bytes 196616 | tf_op jit(solution)/shard_map/ppermute | solution.py:71
  3.9 9.1 %collective-permute-start.1 = (bf16[256,128]{1,0:T(8,128)(2,1)}, bf16[256,128]{1,0:T(8,128)(2,1)S(1)}, u32[]{:S(2)}, u32[]{:S(2)}) collective-permute-start(bf16[256,128]{1,0:T(8,128)(2,1)} %own.1), channel_id=1, source_target_pairs={{4,12},{12,4},{20,28},{28,20},{36,44},{44,36},{52,60},{60,52},{68,... | collective-permute-start | bytes 196616 | tf_op jit(solution)/shard_map/ppermute | solution.py:71
  14.0 9.4 %collective-permute-start.6 = (bf16[512,128]{1,0:T(8,128)(2,1)S(1)}, bf16[512,128]{1,0:T(8,128)(2,1)S(1)}, u32[]{:S(2)}, u32[]{:S(2)}) collective-permute-start(bf16[512,128]{1,0:T(8,128)(2,1)S(1)} %pair_up.1.refs_0_), channel_id=1, source_target_pairs={{0,48},{4,196},{8,56},{12,204},{16,0},{20,212},{24,8},{28,220},{32... | collective-permute-start | bytes 393224 | tf_op jit(solution)/shard_map/ppermute | solution.py:71
  16.7 6.8 %collective-permute-start.5 = (bf16[512,128]{1,0:T(8,128)(2,1)S(1)}, bf16[512,128]{1,0:T(8,128)(2,1)S(1)}, u32[]{:S(2)}, u32[]{:S(2)}) collective-permute-start(bf16[512,128]{1,0:T(8,128)(2,1)S(1)} %pair_up.1.refs_0_), channel_id=1, source_target_pairs={{0,32},{4,132},{8,40},{12,140},{16,48},{20,148},{24,56},{28,156},{... | collective-permute-start | bytes 393224 | tf_op jit(solution)/shard_map/ppermute | solution.py:71
  26.1 6.7 %collective-permute-start.3 = (bf16[1024,128]{1,0:T(8,128)(2,1)S(1)}, bf16[1024,128]{1,0:T(8,128)(2,1)S(1)}, u32[]{:S(2)}, u32[]{:S(2)}) collective-permute-start(bf16[1024,128]{1,0:T(8,128)(2,1)S(1)} %place_low.1.refs_2_.refs_0_), channel_id=1, source_target_pairs={{0,64},{4,20},{8,72},{12,28},{16,80},{20,36},{24,88},{28,44},{32,9... | collective-permute-start | bytes 786440 | tf_op jit(solution)/shard_map/ppermute | solution.py:71
  26.1 11.3 %collective-permute-start.9 = (bf16[1024,128]{1,0:T(8,128)(2,1)S(1)}, bf16[1024,128]{1,0:T(8,128)(2,1)S(1)}, u32[]{:S(2)}, u32[]{:S(2)}) collective-permute-start(bf16[1024,128]{1,0:T(8,128)(2,1)S(1)} %place_high.1.refs_3_.refs_1_), channel_id=1, source_target_pairs={{0,64},{4,20},{8,72},{12,28},{16,80},{20,36},{24,88},{28,44},{32,9... | collective-permute-start | bytes 786440 | tf_op jit(solution)/shard_map/ppermute | solution.py:71
  26.2 11.1 %collective-permute-start.10 = (bf16[1024,128]{1,0:T(8,128)(2,1)S(1)}, bf16[1024,128]{1,0:T(8,128)(2,1)S(1)}, u32[]{:S(2)}, u32[]{:S(2)}) collective-permute-start(bf16[1024,128]{1,0:T(8,128)(2,1)S(1)} %place_low.1.refs_2_.refs_0_), channel_id=1, source_target_pairs={{0,192},{4,52},{8,200},{12,60},{16,208},{20,4},{24,216},{28,12},{3... | collective-permute-start | bytes 786440 | tf_op jit(solution)/shard_map/ppermute | solution.py:71
  29.4 11.7 %collective-permute-start.8 = (bf16[1024,128]{1,0:T(8,128)(2,1)S(1)}, bf16[1024,128]{1,0:T(8,128)(2,1)S(1)}, u32[]{:S(2)}, u32[]{:S(2)}) collective-permute-start(bf16[1024,128]{1,0:T(8,128)(2,1)S(1)} %collective-permute-done.7.refs_5_), channel_id=1, source_target_pairs={{0,192},{4,52},{8,200},{12,60},{16,208},{20,4},{24,216},{28,12},{3... | collective-permute-start | bytes 786440 | tf_op jit(solution)/shard_map/ppermute | solution.py:71
  32.8 8.3 %collective-permute-start.4 = (bf16[1024,128]{1,0:T(8,128)(2,1)S(1)}, bf16[1024,128]{1,0:T(8,128)(2,1)S(1)}, u32[]{:S(2)}, u32[]{:S(2)}) collective-permute-start(bf16[1024,128]{1,0:T(8,128)(2,1)S(1)} %collective-permute-done.3.refs_2_), channel_id=1, source_target_pairs={{0,64},{4,20},{8,72},{12,28},{16,80},{20,36},{24,88},{28,44},{32,9... | collective-permute-start | bytes 786440 | tf_op jit(solution)/shard_map/ppermute | solution.py:71
  47.4 7.6 %collective-permute-start.14 = (bf16[256,128]{1,0:T(8,128)(2,1)S(1)}, bf16[256,128]{1,0:T(8,128)(2,1)S(1)}, u32[]{:S(2)}, u32[]{:S(2)}) collective-permute-start(bf16[256,128]{1,0:T(8,128)(2,1)S(1)} %get-tuple-element.36), channel_id=1, source_target_pairs={{0,2},{1,3},{2,0},{3,1},{4,6},{5,7},{6,4},{7,5},{8,10},{9,11},{10,... | collective-permute-start | bytes 196616 | tf_op jit(solution)/shard_map/ppermute | solution.py:97
  58.4 8.0 %collective-permute-start.17 = (bf16[320,128]{1,0:T(8,128)(2,1)S(1)}, bf16[320,128]{1,0:T(8,128)(2,1)S(1)}, u32[]{:S(2)}, u32[]{:S(2)}) collective-permute-start(bf16[320,128]{1,0:T(8,128)(2,1)S(1)} %get-tuple-element.41), channel_id=1, source_target_pairs={{0,2},{1,3},{2,0},{3,1},{4,6},{5,7},{6,4},{7,5},{8,10},{9,11},{10,... | collective-permute-start | bytes 245768 | tf_op jit(solution)/shard_map/ppermute | solution.py:97
  59.7 6.7 %collective-permute-start.18 = (bf16[320,128]{1,0:T(8,128)(2,1)S(1)}, bf16[320,128]{1,0:T(8,128)(2,1)S(1)}, u32[]{:S(2)}, u32[]{:S(2)}) collective-permute-start(bf16[320,128]{1,0:T(8,128)(2,1)S(1)} %get-tuple-element.42), channel_id=1, source_target_pairs={{0,3},{1,0},{2,1},{3,2},{4,7},{5,4},{6,5},{7,6},{8,11},{9,8},{10,9... | collective-permute-start | bytes 245768 | tf_op jit(solution)/shard_map/ppermute | solution.py:97
  72.5 9.7 %collective-permute-start.20 = (bf16[4096,128]{1,0:T(8,128)(2,1)S(1)}, bf16[4096,128]{1,0:T(8,128)(2,1)S(1)}, u32[]{:S(2)}, u32[]{:S(2)}) collective-permute-start(bf16[4096,128]{1,0:T(8,128)(2,1)S(1)} %get-tuple-element.46), channel_id=1, source_target_pairs={{0,4},{4,0},{8,12},{12,8},{16,20},{20,16},{24,28},{28,24},{32,36},... | collective-permute-start | bytes 3145736 | tf_op jit(solution)/shard_map/ppermute | solution.py:71
  72.6 14.0 %collective-permute-start.25 = (bf16[1024,128]{1,0:T(8,128)(2,1)S(1)}, bf16[1024,128]{1,0:T(8,128)(2,1)S(1)}, u32[]{:S(2)}, u32[]{:S(2)}) collective-permute-start(bf16[1024,128]{1,0:T(8,128)(2,1)S(1)} %get-tuple-element.51), channel_id=1, source_target_pairs={{0,192},{4,52},{8,200},{12,60},{16,208},{20,4},{24,216},{28,12},{3... | collective-permute-start | bytes 786440 | tf_op jit(solution)/shard_map/ppermute | solution.py:71
  74.8 11.7 %collective-permute-start.24 = (bf16[1024,128]{1,0:T(8,128)(2,1)S(1)}, bf16[1024,128]{1,0:T(8,128)(2,1)S(1)}, u32[]{:S(2)}, u32[]{:S(2)}) collective-permute-start(bf16[1024,128]{1,0:T(8,128)(2,1)S(1)} %get-tuple-element.47.refs_6_), channel_id=1, source_target_pairs={{0,64},{4,20},{8,72},{12,28},{16,80},{20,36},{24,88},{28,44},{32,9... | collective-permute-start | bytes 786440 | tf_op jit(solution)/shard_map/ppermute | solution.py:71
  74.8 11.5 %collective-permute-start.26 = (f32[64,128]{1,0:T(8,128)S(1)}, f32[64,128]{1,0:T(8,128)S(1)}, u32[]{:S(2)}, u32[]{:S(2)}) collective-permute-start(f32[64,128]{1,0:T(8,128)S(1)} %get-tuple-element.52.refs_9_), channel_id=1, source_target_pairs={{0,8},{4,12},{8,0},{12,4},{16,24},{20,28},{24,16},{28,20},{32,40},... | collective-permute-start | bytes 98312 | tf_op jit(solution)/shard_map/ppermute | solution.py:71
  83.5 7.2 %collective-permute-start.23 = (bf16[1024,128]{1,0:T(8,128)(2,1)S(1)}, bf16[1024,128]{1,0:T(8,128)(2,1)S(1)}, u32[]{:S(2)}, u32[]{:S(2)}) collective-permute-start(bf16[1024,128]{1,0:T(8,128)(2,1)S(1)} %get-tuple-element.50), channel_id=1, source_target_pairs={{0,192},{4,52},{8,200},{12,60},{16,208},{20,4},{24,216},{28,12},{3... | collective-permute-start | bytes 786440 | tf_op jit(solution)/shard_map/ppermute | solution.py:71
  86.3 7.1 %collective-permute-start.22 = (bf16[1024,128]{1,0:T(8,128)(2,1)S(1)}, bf16[1024,128]{1,0:T(8,128)(2,1)S(1)}, u32[]{:S(2)}, u32[]{:S(2)}) collective-permute-start(bf16[1024,128]{1,0:T(8,128)(2,1)S(1)} %get-tuple-element.49.refs_11_), channel_id=1, source_target_pairs={{0,64},{4,20},{8,72},{12,28},{16,80},{20,36},{24,88},{28,44},{32,9... | collective-permute-start | bytes 786440 | tf_op jit(solution)/shard_map/ppermute | solution.py:71
  86.3 7.1 %collective-permute-start.21 = (bf16[2048,128]{1,0:T(8,128)(2,1)S(1)}, bf16[2048,128]{1,0:T(8,128)(2,1)S(1)}, u32[]{:S(2)}, u32[]{:S(2)}) collective-permute-start(bf16[2048,128]{1,0:T(8,128)(2,1)S(1)} %get-tuple-element.48), channel_id=1, source_target_pairs={{0,4},{4,0},{8,12},{12,8},{16,20},{20,16},{24,28},{28,24},{32,36},... | collective-permute-start | bytes 1572872 | tf_op jit(solution)/shard_map/ppermute | solution.py:71
  87.9 7.1 %collective-permute-start.29 = (f32[64,128]{1,0:T(8,128)S(1)}, f32[64,128]{1,0:T(8,128)S(1)}, u32[]{:S(2)}, u32[]{:S(2)}) collective-permute-start(f32[64,128]{1,0:T(8,128)S(1)} %get-tuple-element.55.own), channel_id=1, source_target_pairs={{0,128},{4,36},{8,136},{12,44},{16,144},{20,52},{24,152},{28,60},{... | collective-permute-start | bytes 98312 | tf_op jit(solution)/shard_map/ppermute | solution.py:71
  89.1 7.0 %collective-permute-start.28 = (bf16[1216,128]{1,0:T(8,128)(2,1)S(1)}, bf16[1216,128]{1,0:T(8,128)(2,1)S(1)}, u32[]{:S(2)}, u32[]{:S(2)}) collective-permute-start(bf16[1216,128]{1,0:T(8,128)(2,1)S(1)} %get-tuple-element.54), channel_id=1, source_target_pairs={{0,192},{4,52},{8,200},{12,60},{16,208},{20,4},{24,216},{28,12},{3... | collective-permute-start | bytes 933896 | tf_op jit(solution)/shard_map/ppermute | solution.py:71
  90.7 7.3 %collective-permute-start.27 = (bf16[1216,128]{1,0:T(8,128)(2,1)S(1)}, bf16[1216,128]{1,0:T(8,128)(2,1)S(1)}, u32[]{:S(2)}, u32[]{:S(2)}) collective-permute-start(bf16[1216,128]{1,0:T(8,128)(2,1)S(1)} %get-tuple-element.53.refs_9_), channel_id=1, source_target_pairs={{0,64},{4,20},{8,72},{12,28},{16,80},{20,36},{24,88},{28,44},{32,9... | collective-permute-start | bytes 933896 | tf_op jit(solution)/shard_map/ppermute | solution.py:71
  98.2 8.9 %collective-permute-start.31 = (bf16[704,128]{1,0:T(8,128)(2,1)S(1)}, bf16[704,128]{1,0:T(8,128)(2,1)S(1)}, u32[]{:S(2)}, u32[]{:S(2)}) collective-permute-start(bf16[704,128]{1,0:T(8,128)(2,1)S(1)} %get-tuple-element.58), channel_id=1, source_target_pairs={{0,32},{4,132},{8,40},{12,140},{16,48},{20,148},{24,56},{28,156},{... | collective-permute-start | bytes 540680 | tf_op jit(solution)/shard_map/ppermute | solution.py:71
  107.8 12.3 %collective-permute-start.33 = (bf16[256,128]{1,0:T(8,128)(2,1)S(1)}, bf16[256,128]{1,0:T(8,128)(2,1)S(1)}, u32[]{:S(2)}, u32[]{:S(2)}) collective-permute-start(bf16[256,128]{1,0:T(8,128)(2,1)S(1)} %get-tuple-element.61.mine), channel_id=1, source_target_pairs={{4,12},{12,4},{20,28},{28,20},{36,44},{44,36},{52,60},{60,52},{68,... | collective-permute-start | bytes 196616 | tf_op jit(solution)/shard_map/ppermute | solution.py:71
  (27 other events, 132.2 us)

commit v4 on v3

--- a/solution.py
+++ b/solution.py
@@ -109,20 +109,45 @@
     return pl.CostEstimate(flops=size // 64, bytes_accessed=size // 64, transcendentals=0)
 
 
-def pair_up_kernel(core, own, near, far, out):
-    first = core[0] == 0
-    out[0:ROWS] = jnp.where(first, own[...], near[...])
-    out[ROWS : 2 * ROWS] = jnp.where(first, near[...], far[...])
+def touch_kernel(meta, stored, out):
+    out[...] = stored[0, 0:16, :].astype(F32)
+
+
+def touch(meta, stored):
+    return pl.pallas_call(
+        touch_kernel,
+        out_shape=jax.ShapeDtypeStruct((16, B), F32),
+        in_specs=[SMEM, VMEM],
+        out_specs=VMEM,
+        compiler_params=params(),
+        cost_estimate=small_cost(1 << 10),
+        name="touch_blocks",
+    )(meta, stored)
+
+
+def pair_up_kernel(core, own, near, far, out, sem):
+    @pl.when(core[0] == 0)
+    def _():
+        copy = pltpu.make_async_copy(own, out.at[pl.ds(0, ROWS)], sem)
+        copy.start()
+        out[ROWS : 2 * ROWS] = near[...]
+        copy.wait()
+
+    @pl.when(core[0] == 1)
+    def _():
+        out[0:ROWS] = near[...]
+        out[ROWS : 2 * ROWS] = far[...]
 
 
 def pair_up(core, own, near, far):
     return pl.pallas_call(
         pair_up_kernel,
         out_shape=jax.ShapeDtypeStruct((2 * ROWS, B), BF16),
-        in_specs=[SMEM] + [VMEM] * 3,
+        in_specs=[SMEM, pl.BlockSpec(memory_space=pl.ANY)] + [VMEM] * 2,
         out_specs=VMEM,
-        compiler_params=params(),
-        cost_estimate=small_cost(LONG),
+        scratch_shapes=[pltpu.SemaphoreType.DMA],
+        compiler_params=params(),
+        cost_estimate=small_cost(1 << 16),
         name="pair_up",
     )(core, own, near, far)
 
@@ -388,52 +413,33 @@
     )(*arrays)
 
 
-def unit_sum(meta, refs, out, flip):
+def pair_kernel(meta, a, b, c, d, own, mine, other, w):
     core = meta[PLACE + 1]
-    unit = 1 - core if flip else core
-    part = pl.ds(pl.multiple_of(unit * ROWS, ROWS), ROWS)
-    total = refs[0][part].astype(F32)
-    for ref in refs[1:]:
-        total = total + ref[part].astype(F32)
-    out[...] = total.astype(BF16)
-
-
-def mine_kernel(meta, a, b, c, d, own, mine, w):
-    unit_sum(meta, (a, b, c, d), mine, False)
+    for out, unit in ((mine, core), (other, 1 - core)):
+        part = pl.ds(pl.multiple_of(unit * ROWS, ROWS), ROWS)
+        total = a[part].astype(F32) + b[part].astype(F32) + c[part].astype(F32) + d[part].astype(F32)
+        out[...] = total.astype(BF16)
     w[...] = (own[...] + joined(c, 2 * ROWS)) + (joined(b, 2 * ROWS) + joined(d, 2 * ROWS))
 
 
-def sum_mine(meta, *arrays):
-    return pl.pallas_call(
-        mine_kernel,
-        out_shape=[jax.ShapeDtypeStruct((ROWS, B), BF16), jax.ShapeDtypeStruct((PIECE, B), F32)],
+def sum_pairs(meta, *arrays):
+    return pl.pallas_call(
+        pair_kernel,
+        out_shape=[jax.ShapeDtypeStruct((ROWS, B), BF16)] * 2 + [jax.ShapeDtypeStruct((PIECE, B), F32)],
         in_specs=[SMEM] + [VMEM] * 5,
-        out_specs=[VMEM] * 2,
+        out_specs=[VMEM] * 3,
         compiler_params=params(),
         cost_estimate=small_cost(1 << 17),
-        name="sum_mine",
+        name="sum_pairs",
     )(meta, *arrays)
 
 
-def other_kernel(meta, mine, a, b, c, d, other):
-    unit_sum(meta, (a, b, c, d), other, True)
-
-
-def sum_other(meta, *arrays):
-    return pl.pallas_call(
-        other_kernel,
-        out_shape=jax.ShapeDtypeStruct((ROWS, B), BF16),
-        in_specs=[SMEM] + [VMEM] * 5,
-        out_specs=VMEM,
-        compiler_params=params(),
-        cost_estimate=small_cost(1 << 17),
-        name="sum_other",
-    )(meta, *arrays)
-
-
-def meet_kernel(scaling, meta, mine, far, w0, w1, w2, w3, own, weight_grad):
+def last_kernel(scaling, meta, mine, crossed, far, w0, w1, w2, w3, out, weight_grad):
     first = meta[PLACE + 1] == 0
-    own[...] = jnp.where(first, mine[...], far[...])
+    for s in range(2):
+        part = slice(s * B, (s + 1) * B)
+        own = jnp.where(first, mine[part].astype(F32), far[part].astype(F32))
+        out[part] = (own + crossed[part].astype(F32)).T.astype(BF16)
     rep = meta[PLACE]
     for back, piece in enumerate((w0, w1, w2, w3)):
         rows = pl.ds(pl.multiple_of(lax.rem(rep + 4 - back, 4) * 32, 32), 32)
@@ -441,34 +447,16 @@
         weight_grad[rows, B : 2 * B] = piece[32:64] * scaling
 
 
-def meet(meta, scaling, *arrays):
-    return pl.pallas_call(
-        functools.partial(meet_kernel, scaling),
+def last_sum(meta, scaling, *arrays):
+    return pl.pallas_call(
+        functools.partial(last_kernel, scaling),
         out_shape=[jax.ShapeDtypeStruct((ROWS, B), BF16), jax.ShapeDtypeStruct((B, 2 * B), F32)],
-        in_specs=[SMEM] + [VMEM] * 6,
+        in_specs=[SMEM] + [VMEM] * 7,
         out_specs=[VMEM] * 2,
-        compiler_params=params(),
-        cost_estimate=small_cost(LONG),
-        name="meet_other_z",
-    )(meta, *arrays)
-
-
-def last_kernel(own, crossed, out):
-    for s in range(2):
-        part = slice(s * B, (s + 1) * B)
-        out[part] = (own[part].astype(F32) + crossed[part].astype(F32)).T.astype(BF16)
-
-
-def last_sum(*arrays):
-    return pl.pallas_call(
-        last_kernel,
-        out_shape=jax.ShapeDtypeStruct((ROWS, B), BF16),
-        in_specs=[VMEM] * 2,
-        out_specs=VMEM,
         compiler_params=params(),
         cost_estimate=small_cost(1 << 16),
         name="last_sum",
-    )(*arrays)
+    )(meta, *arrays)
 
 
 def per_device(features, adjacency, block_list, block_counts, weight, cotangent):
@@ -493,9 +481,10 @@
     near_unit, far_unit = cross(features, True), other_z(features)
     pair = pair_up(core.reshape(1), features, near_unit, far_unit)
     x1, x2, x3 = small_axis(pair, 1), small_axis(pair, 2), small_axis(pair, 3)
-    (low,) = place("place_low", [[(0, 0, 2), (1, 0, 2)]], [pair, x1], [meta])
+    touched = touch(meta, stored)
+    (low,) = place("place_low", [[(0, 0, 2), (1, 0, 2)]], [pair, x1])
     n1_low, n3_low = large_axis(low, 1), large_axis(low, 3)
-    (high,) = place("place_high", [[(0, 0, 2), (1, 0, 2)]], [x2, x3], [low])
+    (high,) = place("place_high", [[(0, 0, 2), (1, 0, 2)]], [x2, x3], [touched, low])
     n1_high, n3_high = large_axis(high, 1), large_axis(high, 3)
     (acc,) = forward(meta, stored, 0, [low, high], None, False)
     f1, f3 = large_axis(n1_low, 1), large_axis(n3_high, 3)
@@ -540,11 +529,11 @@
     (g0,) = bwd(56, (8,), own_s, extra=[r1_high, r3_low, g1_low], finish=add_halves, size=LONG)
     t0, t1, t2, t3, w64 = sum_groups(g0, r1_low, r3_high, w16, w16_two)
     sums = [t0, small_axis(t1, 1), small_axis(t2, 2), small_axis(t3, 3)]
-    mine, w = sum_mine(meta, *sums, w64)
-    far, pieces = other_z(mine), [w] + [turn(w, d) for d in (1, 2, 3)]
-    crossed = cross(sum_other(meta, mine, *sums), False)
-    own, weight_grad = meet(meta, nodes ** (-0.5), mine, far, *pieces)
-    feature_grad = last_sum(own, crossed)
+    mine, other, w = sum_pairs(meta, *sums, w64)
+    far, crossed = other_z(mine), cross(other, False)
+    feature_grad, weight_grad = last_sum(
+        meta, nodes ** (-0.5), mine, crossed, far, w, *[turn(w, d) for d in (1, 2, 3)]
+    )
     return activations, feature_grad, weight_grad
 
 

time: 123 us -> 124 us (level)
  starting transfers between devices: 59.4 us -> 63 us
    ppermute x29, starting transfers between devices: 48.1 us -> 52.2 us  [row_permute(): return lax.ppermute(array, 'row', pairs)]
    ppermute x29, waiting for transfers between devices: 17.3 us -> 15.1 us  [row_permute(): return lax.ppermute(array, 'row', pairs)]
    unnamed x27 -> x11, local copies, waits for them, and re-layouts: 6.42 us -> 5.05 us
    pallas_call x4 -> x3, Pallas kernels: 3.32 us -> 2.63 us  [the longest x1 1.34 us: last_sum(): pl.pallas_call(functools.partial(last_kernel, scaling), out_shape=[jax.Sh...]
  transfers between devices with their start and end apart: 38 -> 38, of which waited for: 14 -> 18; matrix products, arithmetic and copies ran while one was open for 1% -> 2% of each run, Pallas kernels for 13% -> 11%
where the time goes in v4:
time: 124 us
  starting transfers between devices  63 us (51%)
  waiting for transfers between devices  30.3 us (24%)
  Pallas kernels  22.8 us (18%)
  local copies, waits for them, and re-layouts  6 us (5%)
    ppermute x29, starting transfers between devices, row_permute(): return lax.ppermute(array, 'row', pairs)  52.2 us
    ppermute x9, waiting for transfers between devices, turn(): return lax.ppermute(array, 'rep', [(q, (q + d) % 4) for q in range(4)])  15.2 us
    ppermute x29, waiting for transfers between devices, row_permute(): return lax.ppermute(array, 'row', pairs)  15.1 us
    pallas_call x7, Pallas kernels, backward(): pl.pallas_call(functools.partial(backward_kernel, first_section, sizes, a...  11 us
    ppermute x9, starting transfers between devices, turn(): return lax.ppermute(array, 'rep', [(q, (q + d) % 4) for q in range(4)])  10.8 us
    pallas_call x4, Pallas kernels, forward(): pl.pallas_call(functools.partial(forward_kernel, first_section, sizes, fi...  7.12 us
    unnamed x11, local copies, waits for them, and re-layouts  5.05 us
  transfers between devices with their start and end apart: 38, of which 18 were waited for; matrix products, arithmetic and copies ran while one was open for 2% of the time, Pallas kernels for 11%

profile of v4, /device:TPU:1, one launch (start us, length us, event | category | flops | bytes accessed | tf_op | source)
XLA Modules:
  0.0 123.9 jit_solution(10520406106443902424)
XLA Ops:
  0.6 3.3 %collective-permute-start = (bf16[256,128]{1,0:T(8,128)(2,1)}, bf16[256,128]{1,0:T(8,128)(2,1)S(1)}, u32[]{:S(2)}, u32[]{:S(2)}) collective-permute-start(bf16[256,128]{1,0:T(8,128)(2,1)} %own.1), channel_id=1, source_target_pairs={{0,12},{4,0},{8,4},{12,8},{16,28},{20,16},{24,20},{28,24},{32,44},... | collective-permute-start | bytes 196616 | tf_op jit(solution)/shard_map/ppermute | solution.py:71
  3.9 7.1 %collective-permute-start.1 = (bf16[256,128]{1,0:T(8,128)(2,1)}, bf16[256,128]{1,0:T(8,128)(2,1)S(1)}, u32[]{:S(2)}, u32[]{:S(2)}) collective-permute-start(bf16[256,128]{1,0:T(8,128)(2,1)} %own.1), channel_id=1, source_target_pairs={{4,12},{12,4},{20,28},{28,20},{36,44},{44,36},{52,60},{60,52},{68,... | collective-permute-start | bytes 196616 | tf_op jit(solution)/shard_map/ppermute | solution.py:71
  13.9 2.7 %collective-permute-start.6 = (bf16[512,128]{1,0:T(8,128)(2,1)S(1)}, bf16[512,128]{1,0:T(8,128)(2,1)S(1)}, u32[]{:S(2)}, u32[]{:S(2)}) collective-permute-start(bf16[512,128]{1,0:T(8,128)(2,1)S(1)} %pair_up.1.refs_0_), channel_id=1, source_target_pairs={{0,48},{4,196},{8,56},{12,204},{16,0},{20,212},{24,8},{28,220},{32... | collective-permute-start | bytes 393224 | tf_op jit(solution)/shard_map/ppermute | solution.py:71
  19.2 3.4 %copy-done = bf16[1,1,256,128,128]{4,3,2,1,0:T(8,128)(2,1)S(1)} copy-done((bf16[1,1,256,128,128]{4,3,2,1,0:T(8,128)(2,1)S(1)}, bf16[1,1,256,128,128]{4,3,2,1,0:T(8,128)(2,1)}, u32[]{:S(2)}) %copy-start) | copy-done | bytes 8388632
  23.4 2.6 %collective-permute-start.7 = (bf16[1024,128]{1,0:T(8,128)(2,1)S(1)}, bf16[1024,128]{1,0:T(8,128)(2,1)S(1)}, u32[]{:S(2)}, u32[]{:S(2)}) collective-permute-start(bf16[1024,128]{1,0:T(8,128)(2,1)S(1)} %place_high.1.refs_3_.refs_1_), channel_id=1, source_target_pairs={{0,192},{4,52},{8,200},{12,60},{16,208},{20,4},{24,216},{28,12},{3... | collective-permute-start | bytes 786440 | tf_op jit(solution)/shard_map/ppermute | solution.py:71
  26.2 2.5 %collective-permute-start.10 = (bf16[1024,128]{1,0:T(8,128)(2,1)S(1)}, bf16[1024,128]{1,0:T(8,128)(2,1)S(1)}, u32[]{:S(2)}, u32[]{:S(2)}) collective-permute-start(bf16[1024,128]{1,0:T(8,128)(2,1)S(1)} %place_low.1.refs_3_.refs_2_.refs_0_), channel_id=1, source_target_pairs={{0,192},{4,52},{8,200},{12,60},{16,208},{20,4},{24,216},{28,12},{3... | collective-permute-start | bytes 786440 | tf_op jit(solution)/shard_map/ppermute | solution.py:71
  29.3 3.4 %collective-permute-start.8 = (bf16[1024,128]{1,0:T(8,128)(2,1)S(1)}, bf16[1024,128]{1,0:T(8,128)(2,1)S(1)}, u32[]{:S(2)}, u32[]{:S(2)}) collective-permute-start(bf16[1024,128]{1,0:T(8,128)(2,1)S(1)} %collective-permute-done.7.refs_5_), channel_id=1, source_target_pairs={{0,192},{4,52},{8,200},{12,60},{16,208},{20,4},{24,216},{28,12},{3... | collective-permute-start | bytes 786440 | tf_op jit(solution)/shard_map/ppermute | solution.py:71
  41.2 2.5 %forward_slots.6.refs_4_ = f32[8,128,128]{2,1,0:T(8,128)S(1)} custom-call(s32[962]{0:T(1024)S(1)} %concatenate.3.meta.refs_0_, bf16[256,128,128]{2,1,0:T(8,128)(2,1)S(1)} %bitcast.7, bf16[6144,128]{1,0:T(8,128)(2,1)S(1)} %collective-permute-done.12.refs_2_, f32[8,128,128]{2,1,0:T(8,128)S(1)} %forward_slots.5.refs_2_.refs_3_), custom_call_target="tpu_custom_call" | custom-call | flops 12582912 | bytes 12582912 | tf_op jit(solution)/shard_map/forward_slots/pallas_call | solution.py:229
  43.7 1.9 %forward_slots.7 = (f32[256,128]{1,0:T(8,128)S(1)}, bf16[256,128]{1,0:T(8,128)(2,1)S(1)}, bf16[256,128]{1,0:T(8,128)(2,1)S(1)}, bf16[256,128]{1,0:T(8,128)(2,1)S(1)}) custom-call(s32[962]{0:T(1024)S(1)} %concatenate.3.meta.refs_0_, bf16[256,128,128]{2,1,0:T(8,128)(2,1)S(1)} %bitcast.8, bf16[2048,128]{1,0:T(8,128)(2,1)S(1)} %place_far.1.refs_2_, ...), custom_call_target="tpu_custom_call" | custom-call | flops 8388608 | bytes 8388608 | tf_op jit(solution)/shard_map/forward_slots/pallas_call | solution.py:229
  49.5 2.0 %collective-permute-done.13.p1 = bf16[256,128]{1,0:T(8,128)(2,1)S(1)} collective-permute-done((bf16[256,128]{1,0:T(8,128)(2,1)S(1)}, bf16[256,128]{1,0:T(8,128)(2,1)S(1)}, u32[]{:S(2)}, u32[]{:S(2)}) %collective-permute-start.13) | collective-permute-done | bytes 65568 | tf_op jit(solution)/shard_map/ppermute | solution.py:97
  51.5 2.7 %collective-permute-done.14.p2 = bf16[256,128]{1,0:T(8,128)(2,1)S(1)} collective-permute-done((bf16[256,128]{1,0:T(8,128)(2,1)S(1)}, bf16[256,128]{1,0:T(8,128)(2,1)S(1)}, u32[]{:S(2)}, u32[]{:S(2)}) %collective-permute-start.14) | collective-permute-done | bytes 65568 | tf_op jit(solution)/shard_map/ppermute | solution.py:97
  61.0 4.6 %collective-permute-done.17.refs_4_.refs_8_ = bf16[320,128]{1,0:T(8,128)(2,1)S(1)} collective-permute-done((bf16[320,128]{1,0:T(8,128)(2,1)S(1)}, bf16[320,128]{1,0:T(8,128)(2,1)S(1)}, u32[]{:S(2)}, u32[]{:S(2)}) %collective-permute-start.17) | collective-permute-done | bytes 81952 | tf_op jit(solution)/shard_map/ppermute | solution.py:97
  67.8 2.3 %backward_slots.8.refs_9_ = bf16[4096,128]{1,0:T(8,128)(2,1)S(1)} custom-call(s32[962]{0:T(1024)S(1)} %concatenate.3.meta.refs_0_, bf16[256,128,128]{2,1,0:T(8,128)(2,1)S(1)} %bitcast.10, bf16[256,128]{1,0:T(8,128)(2,1)S(1)} %get-tuple-element.40.refs_2_, bf16[320,128]{1,0:T(8,128)(2,1)S(1)} %collective-permute-done.16.refs_3_.refs_7_, ...), custom_call_target="tpu_custom_call" | custom-call | flops 8388608 | bytes 8388608 | tf_op jit(solution)/shard_map/backward_slots/pallas_call | solution.py:378
  73.2 3.3 %collective-permute-start.26 = (f32[64,128]{1,0:T(8,128)S(1)}, f32[64,128]{1,0:T(8,128)S(1)}, u32[]{:S(2)}, u32[]{:S(2)}) collective-permute-start(f32[64,128]{1,0:T(8,128)S(1)} %get-tuple-element.53.refs_9_), channel_id=1, source_target_pairs={{0,8},{4,12},{8,0},{12,4},{16,24},{20,28},{24,16},{28,20},{32,40},... | collective-permute-start | bytes 98312 | tf_op jit(solution)/shard_map/ppermute | solution.py:71
  79.3 2.1 %collective-permute-start.23 = (bf16[1024,128]{1,0:T(8,128)(2,1)S(1)}, bf16[1024,128]{1,0:T(8,128)(2,1)S(1)}, u32[]{:S(2)}, u32[]{:S(2)}) collective-permute-start(bf16[1024,128]{1,0:T(8,128)(2,1)S(1)} %get-tuple-element.51), channel_id=1, source_target_pairs={{0,192},{4,52},{8,200},{12,60},{16,208},{20,4},{24,216},{28,12},{3... | collective-permute-start | bytes 786440 | tf_op jit(solution)/shard_map/ppermute | solution.py:71
  81.4 2.7 %collective-permute-start.21 = (bf16[2048,128]{1,0:T(8,128)(2,1)S(1)}, bf16[2048,128]{1,0:T(8,128)(2,1)S(1)}, u32[]{:S(2)}, u32[]{:S(2)}) collective-permute-start(bf16[2048,128]{1,0:T(8,128)(2,1)S(1)} %get-tuple-element.49), channel_id=1, source_target_pairs={{0,4},{4,0},{8,12},{12,8},{16,20},{20,16},{24,28},{28,24},{32,36},... | collective-permute-start | bytes 1572872 | tf_op jit(solution)/shard_map/ppermute | solution.py:71
  89.9 2.1 %collective-permute-done.28.high = bf16[1216,128]{1,0:T(8,128)(2,1)S(1)} collective-permute-done((bf16[1216,128]{1,0:T(8,128)(2,1)S(1)}, bf16[1216,128]{1,0:T(8,128)(2,1)S(1)}, u32[]{:S(2)}, u32[]{:S(2)}) %collective-permute-start.28) | collective-permute-done | bytes 311328 | tf_op jit(solution)/shard_map/ppermute | solution.py:71
  91.9 2.3 %collective-permute-done.27.low = bf16[1216,128]{1,0:T(8,128)(2,1)S(1)} collective-permute-done((bf16[1216,128]{1,0:T(8,128)(2,1)S(1)}, bf16[1216,128]{1,0:T(8,128)(2,1)S(1)}, u32[]{:S(2)}, u32[]{:S(2)}) %collective-permute-start.27) | collective-permute-done | bytes 311328 | tf_op jit(solution)/shard_map/ppermute | solution.py:71
  94.5 3.6 %collective-permute-start.31 = (bf16[704,128]{1,0:T(8,128)(2,1)S(1)}, bf16[704,128]{1,0:T(8,128)(2,1)S(1)}, u32[]{:S(2)}, u32[]{:S(2)}) collective-permute-start(bf16[704,128]{1,0:T(8,128)(2,1)S(1)} %get-tuple-element.59), channel_id=1, source_target_pairs={{0,32},{4,132},{8,40},{12,140},{16,48},{20,148},{24,56},{28,156},{... | collective-permute-start | bytes 540680 | tf_op jit(solution)/shard_map/ppermute | solution.py:71
  98.1 1.9 %collective-permute-done.30.b = bf16[704,128]{1,0:T(8,128)(2,1)S(1)} collective-permute-done((bf16[704,128]{1,0:T(8,128)(2,1)S(1)}, bf16[704,128]{1,0:T(8,128)(2,1)S(1)}, u32[]{:S(2)}, u32[]{:S(2)}) %collective-permute-start.30) | collective-permute-done | bytes 180256 | tf_op jit(solution)/shard_map/ppermute | solution.py:71
  100.1 2.9 %collective-permute-done.31.c = bf16[704,128]{1,0:T(8,128)(2,1)S(1)} collective-permute-done((bf16[704,128]{1,0:T(8,128)(2,1)S(1)}, bf16[704,128]{1,0:T(8,128)(2,1)S(1)}, u32[]{:S(2)}, u32[]{:S(2)}) %collective-permute-start.31) | collective-permute-done | bytes 180256 | tf_op jit(solution)/shard_map/ppermute | solution.py:71
  103.6 5.9 %collective-permute-start.33 = (bf16[256,128]{1,0:T(8,128)(2,1)S(1)}, bf16[256,128]{1,0:T(8,128)(2,1)S(1)}, u32[]{:S(2)}, u32[]{:S(2)}) collective-permute-start(bf16[256,128]{1,0:T(8,128)(2,1)S(1)} %get-tuple-element.63), channel_id=1, source_target_pairs={{0,4},{4,8},{8,12},{12,0},{16,20},{20,24},{24,28},{28,16},{32,36},... | collective-permute-start | bytes 196616 | tf_op jit(solution)/shard_map/ppermute | solution.py:71
  109.5 5.2 %collective-permute-start.34 = (bf16[256,128]{1,0:T(8,128)(2,1)S(1)}, bf16[256,128]{1,0:T(8,128)(2,1)S(1)}, u32[]{:S(2)}, u32[]{:S(2)}) collective-permute-start(bf16[256,128]{1,0:T(8,128)(2,1)S(1)} %get-tuple-element.62.mine), channel_id=1, source_target_pairs={{4,12},{12,4},{20,28},{28,20},{36,44},{44,36},{52,60},{60,52},{68,... | collective-permute-start | bytes 196616 | tf_op jit(solution)/shard_map/ppermute | solution.py:71
  114.8 2.3 %collective-permute-start.37 = (f32[64,128]{1,0:T(8,128)S(1)}, f32[64,128]{1,0:T(8,128)S(1)}, u32[]{:S(2)}, u32[]{:S(2)}) collective-permute-start(f32[64,128]{1,0:T(8,128)S(1)} %get-tuple-element.64.w0), channel_id=1, source_target_pairs={{0,3},{1,0},{2,1},{3,2},{4,7},{5,4},{6,5},{7,6},{8,11},{9,8},{10,9... | collective-permute-start | bytes 98312 | tf_op jit(solution)/shard_map/ppermute | solution.py:97
  (87 shorter events, 47.4 us)
Async XLA Ops:
  0.6 11.5 %collective-permute-start = (bf16[256,128]{1,0:T(8,128)(2,1)}, bf16[256,128]{1,0:T(8,128)(2,1)S(1)}, u32[]{:S(2)}, u32[]{:S(2)}) collective-permute-start(bf16[256,128]{1,0:T(8,128)(2,1)} %own.1), channel_id=1, source_target_pairs={{0,12},{4,0},{8,4},{12,8},{16,28},{20,16},{24,20},{28,24},{32,44},... | collective-permute-start | bytes 196616 | tf_op jit(solution)/shard_map/ppermute | solution.py:71
  3.9 9.1 %collective-permute-start.1 = (bf16[256,128]{1,0:T(8,128)(2,1)}, bf16[256,128]{1,0:T(8,128)(2,1)S(1)}, u32[]{:S(2)}, u32[]{:S(2)}) collective-permute-start(bf16[256,128]{1,0:T(8,128)(2,1)} %own.1), channel_id=1, source_target_pairs={{4,12},{12,4},{20,28},{28,20},{36,44},{44,36},{52,60},{60,52},{68,... | collective-permute-start | bytes 196616 | tf_op jit(solution)/shard_map/ppermute | solution.py:71
  13.9 9.4 %collective-permute-start.6 = (bf16[512,128]{1,0:T(8,128)(2,1)S(1)}, bf16[512,128]{1,0:T(8,128)(2,1)S(1)}, u32[]{:S(2)}, u32[]{:S(2)}) collective-permute-start(bf16[512,128]{1,0:T(8,128)(2,1)S(1)} %pair_up.1.refs_0_), channel_id=1, source_target_pairs={{0,48},{4,196},{8,56},{12,204},{16,0},{20,212},{24,8},{28,220},{32... | collective-permute-start | bytes 393224 | tf_op jit(solution)/shard_map/ppermute | solution.py:71
  16.6 6.8 %collective-permute-start.5 = (bf16[512,128]{1,0:T(8,128)(2,1)S(1)}, bf16[512,128]{1,0:T(8,128)(2,1)S(1)}, u32[]{:S(2)}, u32[]{:S(2)}) collective-permute-start(bf16[512,128]{1,0:T(8,128)(2,1)S(1)} %pair_up.1.refs_0_), channel_id=1, source_target_pairs={{0,32},{4,132},{8,40},{12,140},{16,48},{20,148},{24,56},{28,156},{... | collective-permute-start | bytes 393224 | tf_op jit(solution)/shard_map/ppermute | solution.py:71
  17.0 6.4 %collective-permute-start.2 = (bf16[512,128]{1,0:T(8,128)(2,1)S(1)}, bf16[512,128]{1,0:T(8,128)(2,1)S(1)}, u32[]{:S(2)}, u32[]{:S(2)}) collective-permute-start(bf16[512,128]{1,0:T(8,128)(2,1)S(1)} %pair_up.1.refs_0_), channel_id=1, source_target_pairs={{0,16},{4,68},{8,24},{12,76},{16,32},{20,84},{24,40},{28,92},{32,4... | collective-permute-start | bytes 393224 | tf_op jit(solution)/shard_map/ppermute | solution.py:71
  26.0 6.7 %collective-permute-start.3 = (bf16[1024,128]{1,0:T(8,128)(2,1)S(1)}, bf16[1024,128]{1,0:T(8,128)(2,1)S(1)}, u32[]{:S(2)}, u32[]{:S(2)}) collective-permute-start(bf16[1024,128]{1,0:T(8,128)(2,1)S(1)} %place_low.1.refs_3_.refs_2_.refs_0_), channel_id=1, source_target_pairs={{0,64},{4,20},{8,72},{12,28},{16,80},{20,36},{24,88},{28,44},{32,9... | collective-permute-start | bytes 786440 | tf_op jit(solution)/shard_map/ppermute | solution.py:71
  26.0 9.5 %collective-permute-start.9 = (bf16[1024,128]{1,0:T(8,128)(2,1)S(1)}, bf16[1024,128]{1,0:T(8,128)(2,1)S(1)}, u32[]{:S(2)}, u32[]{:S(2)}) collective-permute-start(bf16[1024,128]{1,0:T(8,128)(2,1)S(1)} %place_high.1.refs_3_.refs_1_), channel_id=1, source_target_pairs={{0,64},{4,20},{8,72},{12,28},{16,80},{20,36},{24,88},{28,44},{32,9... | collective-permute-start | bytes 786440 | tf_op jit(solution)/shard_map/ppermute | solution.py:71
  26.2 9.3 %collective-permute-start.10 = (bf16[1024,128]{1,0:T(8,128)(2,1)S(1)}, bf16[1024,128]{1,0:T(8,128)(2,1)S(1)}, u32[]{:S(2)}, u32[]{:S(2)}) collective-permute-start(bf16[1024,128]{1,0:T(8,128)(2,1)S(1)} %place_low.1.refs_3_.refs_2_.refs_0_), channel_id=1, source_target_pairs={{0,192},{4,52},{8,200},{12,60},{16,208},{20,4},{24,216},{28,12},{3... | collective-permute-start | bytes 786440 | tf_op jit(solution)/shard_map/ppermute | solution.py:71
  29.3 8.7 %collective-permute-start.8 = (bf16[1024,128]{1,0:T(8,128)(2,1)S(1)}, bf16[1024,128]{1,0:T(8,128)(2,1)S(1)}, u32[]{:S(2)}, u32[]{:S(2)}) collective-permute-start(bf16[1024,128]{1,0:T(8,128)(2,1)S(1)} %collective-permute-done.7.refs_5_), channel_id=1, source_target_pairs={{0,192},{4,52},{8,200},{12,60},{16,208},{20,4},{24,216},{28,12},{3... | collective-permute-start | bytes 786440 | tf_op jit(solution)/shard_map/ppermute | solution.py:71
  32.7 6.7 %collective-permute-start.4 = (bf16[1024,128]{1,0:T(8,128)(2,1)S(1)}, bf16[1024,128]{1,0:T(8,128)(2,1)S(1)}, u32[]{:S(2)}, u32[]{:S(2)}) collective-permute-start(bf16[1024,128]{1,0:T(8,128)(2,1)S(1)} %collective-permute-done.3.refs_2_), channel_id=1, source_target_pairs={{0,64},{4,20},{8,72},{12,28},{16,80},{20,36},{24,88},{28,44},{32,9... | collective-permute-start | bytes 786440 | tf_op jit(solution)/shard_map/ppermute | solution.py:71
  46.7 7.6 %collective-permute-start.14 = (bf16[256,128]{1,0:T(8,128)(2,1)S(1)}, bf16[256,128]{1,0:T(8,128)(2,1)S(1)}, u32[]{:S(2)}, u32[]{:S(2)}) collective-permute-start(bf16[256,128]{1,0:T(8,128)(2,1)S(1)} %get-tuple-element.37), channel_id=1, source_target_pairs={{0,2},{1,3},{2,0},{3,1},{4,6},{5,7},{6,4},{7,5},{8,10},{9,11},{10,... | collective-permute-start | bytes 196616 | tf_op jit(solution)/shard_map/ppermute | solution.py:97
  57.6 8.0 %collective-permute-start.17 = (bf16[320,128]{1,0:T(8,128)(2,1)S(1)}, bf16[320,128]{1,0:T(8,128)(2,1)S(1)}, u32[]{:S(2)}, u32[]{:S(2)}) collective-permute-start(bf16[320,128]{1,0:T(8,128)(2,1)S(1)} %get-tuple-element.42), channel_id=1, source_target_pairs={{0,2},{1,3},{2,0},{3,1},{4,6},{5,7},{6,4},{7,5},{8,10},{9,11},{10,... | collective-permute-start | bytes 245768 | tf_op jit(solution)/shard_map/ppermute | solution.py:97
  58.7 7.0 %collective-permute-start.18 = (bf16[320,128]{1,0:T(8,128)(2,1)S(1)}, bf16[320,128]{1,0:T(8,128)(2,1)S(1)}, u32[]{:S(2)}, u32[]{:S(2)}) collective-permute-start(bf16[320,128]{1,0:T(8,128)(2,1)S(1)} %get-tuple-element.43), channel_id=1, source_target_pairs={{0,3},{1,0},{2,1},{3,2},{4,7},{5,4},{6,5},{7,6},{8,11},{9,8},{10,9... | collective-permute-start | bytes 245768 | tf_op jit(solution)/shard_map/ppermute | solution.py:97
  71.5 6.4 %collective-permute-start.20 = (bf16[4096,128]{1,0:T(8,128)(2,1)S(1)}, bf16[4096,128]{1,0:T(8,128)(2,1)S(1)}, u32[]{:S(2)}, u32[]{:S(2)}) collective-permute-start(bf16[4096,128]{1,0:T(8,128)(2,1)S(1)} %get-tuple-element.47), channel_id=1, source_target_pairs={{0,4},{4,0},{8,12},{12,8},{16,20},{20,16},{24,28},{28,24},{32,36},... | collective-permute-start | bytes 3145736 | tf_op jit(solution)/shard_map/ppermute | solution.py:71
  71.6 12.5 %collective-permute-start.25 = (bf16[1024,128]{1,0:T(8,128)(2,1)S(1)}, bf16[1024,128]{1,0:T(8,128)(2,1)S(1)}, u32[]{:S(2)}, u32[]{:S(2)}) collective-permute-start(bf16[1024,128]{1,0:T(8,128)(2,1)S(1)} %get-tuple-element.52), channel_id=1, source_target_pairs={{0,192},{4,52},{8,200},{12,60},{16,208},{20,4},{24,216},{28,12},{3... | collective-permute-start | bytes 786440 | tf_op jit(solution)/shard_map/ppermute | solution.py:71
  73.1 11.1 %collective-permute-start.24 = (bf16[1024,128]{1,0:T(8,128)(2,1)S(1)}, bf16[1024,128]{1,0:T(8,128)(2,1)S(1)}, u32[]{:S(2)}, u32[]{:S(2)}) collective-permute-start(bf16[1024,128]{1,0:T(8,128)(2,1)S(1)} %get-tuple-element.48.refs_6_), channel_id=1, source_target_pairs={{0,64},{4,20},{8,72},{12,28},{16,80},{20,36},{24,88},{28,44},{32,9... | collective-permute-start | bytes 786440 | tf_op jit(solution)/shard_map/ppermute | solution.py:71
  73.2 8.2 %collective-permute-start.26 = (f32[64,128]{1,0:T(8,128)S(1)}, f32[64,128]{1,0:T(8,128)S(1)}, u32[]{:S(2)}, u32[]{:S(2)}) collective-permute-start(f32[64,128]{1,0:T(8,128)S(1)} %get-tuple-element.53.refs_9_), channel_id=1, source_target_pairs={{0,8},{4,12},{8,0},{12,4},{16,24},{20,28},{24,16},{28,20},{32,40},... | collective-permute-start | bytes 98312 | tf_op jit(solution)/shard_map/ppermute | solution.py:71
  79.3 7.7 %collective-permute-start.23 = (bf16[1024,128]{1,0:T(8,128)(2,1)S(1)}, bf16[1024,128]{1,0:T(8,128)(2,1)S(1)}, u32[]{:S(2)}, u32[]{:S(2)}) collective-permute-start(bf16[1024,128]{1,0:T(8,128)(2,1)S(1)} %get-tuple-element.51), channel_id=1, source_target_pairs={{0,192},{4,52},{8,200},{12,60},{16,208},{20,4},{24,216},{28,12},{3... | collective-permute-start | bytes 786440 | tf_op jit(solution)/shard_map/ppermute | solution.py:71
  81.4 6.4 %collective-permute-start.22 = (bf16[1024,128]{1,0:T(8,128)(2,1)S(1)}, bf16[1024,128]{1,0:T(8,128)(2,1)S(1)}, u32[]{:S(2)}, u32[]{:S(2)}) collective-permute-start(bf16[1024,128]{1,0:T(8,128)(2,1)S(1)} %get-tuple-element.50.refs_11_), channel_id=1, source_target_pairs={{0,64},{4,20},{8,72},{12,28},{16,80},{20,36},{24,88},{28,44},{32,9... | collective-permute-start | bytes 786440 | tf_op jit(solution)/shard_map/ppermute | solution.py:71
  81.4 6.4 %collective-permute-start.21 = (bf16[2048,128]{1,0:T(8,128)(2,1)S(1)}, bf16[2048,128]{1,0:T(8,128)(2,1)S(1)}, u32[]{:S(2)}, u32[]{:S(2)}) collective-permute-start(bf16[2048,128]{1,0:T(8,128)(2,1)S(1)} %get-tuple-element.49), channel_id=1, source_target_pairs={{0,4},{4,0},{8,12},{12,8},{16,20},{20,16},{24,28},{28,24},{32,36},... | collective-permute-start | bytes 1572872 | tf_op jit(solution)/shard_map/ppermute | solution.py:71
  87.0 7.3 %collective-permute-start.27 = (bf16[1216,128]{1,0:T(8,128)(2,1)S(1)}, bf16[1216,128]{1,0:T(8,128)(2,1)S(1)}, u32[]{:S(2)}, u32[]{:S(2)}) collective-permute-start(bf16[1216,128]{1,0:T(8,128)(2,1)S(1)} %get-tuple-element.54.refs_9_), channel_id=1, source_target_pairs={{0,64},{4,20},{8,72},{12,28},{16,80},{20,36},{24,88},{28,44},{32,9... | collective-permute-start | bytes 933896 | tf_op jit(solution)/shard_map/ppermute | solution.py:71
  94.5 8.4 %collective-permute-start.31 = (bf16[704,128]{1,0:T(8,128)(2,1)S(1)}, bf16[704,128]{1,0:T(8,128)(2,1)S(1)}, u32[]{:S(2)}, u32[]{:S(2)}) collective-permute-start(bf16[704,128]{1,0:T(8,128)(2,1)S(1)} %get-tuple-element.59), channel_id=1, source_target_pairs={{0,32},{4,132},{8,40},{12,140},{16,48},{20,148},{24,56},{28,156},{... | collective-permute-start | bytes 540680 | tf_op jit(solution)/shard_map/ppermute | solution.py:71
  103.6 18.9 %collective-permute-start.33 = (bf16[256,128]{1,0:T(8,128)(2,1)S(1)}, bf16[256,128]{1,0:T(8,128)(2,1)S(1)}, u32[]{:S(2)}, u32[]{:S(2)}) collective-permute-start(bf16[256,128]{1,0:T(8,128)(2,1)S(1)} %get-tuple-element.63), channel_id=1, source_target_pairs={{0,4},{4,8},{8,12},{12,0},{16,20},{20,24},{24,28},{28,16},{32,36},... | collective-permute-start | bytes 196616 | tf_op jit(solution)/shard_map/ppermute | solution.py:71
  109.5 13.0 %collective-permute-start.34 = (bf16[256,128]{1,0:T(8,128)(2,1)S(1)}, bf16[256,128]{1,0:T(8,128)(2,1)S(1)}, u32[]{:S(2)}, u32[]{:S(2)}) collective-permute-start(bf16[256,128]{1,0:T(8,128)(2,1)S(1)} %get-tuple-element.62.mine), channel_id=1, source_target_pairs={{4,12},{12,4},{20,28},{28,20},{36,44},{44,36},{52,60},{60,52},{68,... | collective-permute-start | bytes 196616 | tf_op jit(solution)/shard_map/ppermute | solution.py:71
  (19 other events, 105.3 us)

commit v5 on v4

--- a/solution.py
+++ b/solution.py
@@ -40,13 +40,10 @@
 ]
 LOW, HIGH = (0, 1), (2, 3)
 BACKWARD_GROUPS = [
-    group(1, 2),
-    group(1, 1, HIGH) + group(1, 3, LOW) + group(1, 1, LOW) + group(1, 3, HIGH),
-    group(0, 2),
-    group(1, 0),
-    group(0, 1, HIGH) + group(0, 3, LOW),
-    group(0, 1, LOW) + group(0, 3, HIGH),
-    group(0, 0),
+    group(1, 2) + group(1, 1, HIGH) + group(1, 3, LOW),
+    group(1, 1, LOW) + group(1, 3, HIGH) + group(1, 0),
+    group(0, 2) + group(0, 1, HIGH) + group(0, 3, LOW),
+    group(0, 1, LOW) + group(0, 3, HIGH) + group(0, 0),
 ]
 
 
@@ -296,37 +293,15 @@
     total = extra[0][...]
     for ref in extra[1:]:
         total = total + ref[ROWS : ROWS + PIECE].astype(F32)
-    split(total, outs[0], 8 * ROWS)
+    split(total, outs[0], 16 * ROWS)
     extra_outs[0][...] = total
 
 
 def sibling_terms(extra, outs, extra_outs):
-    total = extra[0][...] + joined(extra[1], 8 * ROWS)
-    extra_outs[0][...] = total
-    extra_outs[1][...] = extra[2][...]
-
-
-def spread_terms(extra, outs, extra_outs):
-    half_1, half_3, own, other = extra[:4]
-    total = own[...] + other[...]
-    for out, half in zip(outs, (half_1, half_3)):
-        part = slice(0, 4 * ROWS)
-        out[part] = (out[part].astype(F32) + half[...].astype(F32)).astype(BF16)
-        split(total, out, 4 * ROWS)
-    extra_outs[0][...] = total
-
-
-def pass_on(extra, outs, extra_outs):
-    extra_outs[0][...] = extra[0][...]
-
-
-def add_halves(extra, outs, extra_outs):
-    for half, start in zip(extra[:2], (4 * ROWS, 0)):
-        part = slice(start, start + 4 * ROWS)
-        outs[0][part] = (outs[0][part].astype(F32) + half[...].astype(F32)).astype(BF16)
-
-
-def backward_kernel(first_section, sizes, added, add_from, extras, finish, *refs):
+    extra_outs[0][...] = extra[0][...] + joined(extra[1], 16 * ROWS)
+
+
+def backward_kernel(first_section, sizes, added, extras, finish, *refs):
     meta, stored = refs[:2]
     value_refs, refs = refs[2:6], refs[6:]
     if added:
@@ -359,7 +334,7 @@
                 right = jnp.concatenate([stored[meta[base + 3 * k + 2]] for k in range(SLOTS)], axis=0)
                 result = jnp.dot(left, right, preferred_element_type=F32)
                 if added:
-                    result = result + add_ref[pl.ds(pl.multiple_of((add_from + begin + n) * ROWS, ROWS), ROWS)].astype(F32)
+                    result = result + add_ref[pl.ds(pl.multiple_of((begin + n) * ROWS, ROWS), ROWS)].astype(F32)
                 out_ref[pl.ds(pl.multiple_of(n * ROWS, ROWS), ROWS)] = result.astype(BF16)
             return carry
 
@@ -369,14 +344,14 @@
         finish(extra, out_refs, extra_outs)
 
 
-def backward(meta, stored, values, first_section, sizes, add=None, add_from=0, extra=(), finish=None, tails=None, extra_out=(), size=0):
+def backward(meta, stored, values, first_section, sizes, add=None, extra=(), finish=None, tails=None, extra_out=(), size=0):
     added = add is not None
     args = [meta, stored, *values] + ([add] if added else []) + list(extra)
     tails = tails or (0,) * len(sizes)
     shapes = [jax.ShapeDtypeStruct((size * ROWS + tail, B), BF16) for size, tail in zip(sizes, tails)]
     shapes += [jax.ShapeDtypeStruct(a.shape, a.dtype) for a in extra_out]
     return pl.pallas_call(
-        functools.partial(backward_kernel, first_section, sizes, added, add_from, len(extra), finish),
+        functools.partial(backward_kernel, first_section, sizes, added, len(extra), finish),
         out_shape=shapes,
         in_specs=[SMEM] + [VMEM] * (len(args) - 1),
         out_specs=[VMEM] * len(shapes),
@@ -385,6 +360,44 @@
         cost_estimate=small_cost(size) if size else cost(sum(sizes) * SLOTS),
         name="backward_slots",
     )(*args)
+
+
+def late_kernel(a, b, half_1, half_3, own, other, out_1, out_3, w):
+    total = own[...] + other[...]
+    w[...] = total
+    for near, half, out in ((a, half_1, out_1), (b, half_3, out_3)):
+        out[0 : 4 * ROWS] = (near[...].astype(F32) + half[...].astype(F32)).astype(BF16)
+        split(total, out, 4 * ROWS)
+
+
+def add_late(*arrays):
+    return pl.pallas_call(
+        late_kernel,
+        out_shape=[jax.ShapeDtypeStruct((4 * ROWS + SPLIT, B), BF16)] * 2 + [jax.ShapeDtypeStruct((PIECE, B), F32)],
+        in_specs=[VMEM] * 6,
+        out_specs=[VMEM] * 3,
+        compiler_params=params(),
+        cost_estimate=small_cost(1 << 18),
+        name="add_late",
+    )(*arrays)
+
+
+def early_kernel(a, high, low, after, out):
+    for half, start in ((low, 0), (high, 4 * ROWS)):
+        part = slice(start, start + 4 * ROWS)
+        out[part] = (a[part].astype(F32) + half[...].astype(F32)).astype(BF16)
+
+
+def add_early(*arrays):
+    return pl.pallas_call(
+        early_kernel,
+        out_shape=jax.ShapeDtypeStruct((8 * ROWS, B), BF16),
+        in_specs=[VMEM] * 4,
+        out_specs=VMEM,
+        compiler_params=params(),
+        cost_estimate=small_cost(LONG),
+        name="add_early",
+    )(*arrays)
 
 
 def sum_kernel(a, low, high, own, two, t0, t1, t2, t3, w):
@@ -434,7 +447,7 @@
     )(meta, *arrays)
 
 
-def last_kernel(scaling, meta, mine, crossed, far, w0, w1, w2, w3, out, weight_grad):
+def last_kernel(scaling, meta, mine, far, crossed, w0, w1, w2, w3, out, weight_grad):
     first = meta[PLACE + 1] == 0
     for s in range(2):
         part = slice(s * B, (s + 1) * B)
@@ -502,37 +515,26 @@
     messages = [turn(m1, 1), turn(m2, 2), turn(m3, 3)]
 
     bwd = functools.partial(backward, meta, stored, [values] + messages)
-    far_b, w4 = bwd(0, (8,), extra=[w] + messages, finish=gather_terms, tails=(SPLIT,), extra_out=[w])
-    far_s = sibling(far_b)
-    (near_b,) = bwd(8, (16,), extra=[far_b])
-    h1, h3, w8, near_b = bwd(
-        24, (4, 4), far_s, extra=[w4, far_s, near_b], finish=sibling_terms, extra_out=[w, near_b]
+    first_b, w4 = bwd(0, (16,), extra=[w] + messages, finish=gather_terms, tails=(SPLIT,), extra_out=[w])
+    first_s = sibling(first_b)
+    (second_b,) = bwd(16, (16,), extra=[first_b])
+    second_s = sibling(second_b)
+    h1, h3, g1_high, g3_low, w8 = bwd(
+        32, (4, 4, 4, 4), first_s, extra=[w4, first_s, second_b], finish=sibling_terms, extra_out=[w], size=LONG
     )
-    f1, f3, near_s = large_axis(h1, 1), large_axis(h3, 3), sibling(near_b)
+    f1, f3 = large_axis(h1, 1), large_axis(h3, 3)
+    r1_high, r3_low = large_axis(g1_high, 1), large_axis(g3_low, 3)
     w8_z = row_permute(w8, lambda y, x, z, c: at(y, x, 1 - z, c))
-    (own_b,) = bwd(32, (8,), extra=[h1])
-    g1_high, g3_low, own_b = bwd(40, (4, 4), near_s, extra=[own_b], finish=pass_on, extra_out=[own_b])
-    r1_high, r3_low = large_axis(g1_high, 1), large_axis(g3_low, 3)
-    own_s = sibling(own_b)
-    g1_low, g3_high, w16 = bwd(
-        48,
-        (4, 4),
-        near_s,
-        add_from=8,
-        extra=[f1, f3, w8, w8_z, g1_high],
-        finish=spread_terms,
-        tails=(SPLIT, SPLIT),
-        extra_out=[w8],
-        size=LONG,
-    )
+    l1_low, l3_high, g0 = bwd(48, (4, 4, 8), second_s, extra=[h1])
+    g1_low, g3_high, w16 = add_late(l1_low, l3_high, f1, f3, w8, w8_z)
     r1_low, r3_high, w16_two = large_axis(g1_low, 1), large_axis(g3_high, 3), large_axis(w16, 2)
-    (g0,) = bwd(56, (8,), own_s, extra=[r1_high, r3_low, g1_low], finish=add_halves, size=LONG)
+    g0 = add_early(g0, r1_high, r3_low, g1_low)
     t0, t1, t2, t3, w64 = sum_groups(g0, r1_low, r3_high, w16, w16_two)
     sums = [t0, small_axis(t1, 1), small_axis(t2, 2), small_axis(t3, 3)]
     mine, other, w = sum_pairs(meta, *sums, w64)
     far, crossed = other_z(mine), cross(other, False)
     feature_grad, weight_grad = last_sum(
-        meta, nodes ** (-0.5), mine, crossed, far, w, *[turn(w, d) for d in (1, 2, 3)]
+        meta, nodes ** (-0.5), mine, far, crossed, w, *[turn(w, d) for d in (1, 2, 3)]
     )
     return activations, feature_grad, weight_grad
 

time: 124 us -> 120 us (0.968)
  waiting for transfers between devices: 30.3 us -> 28.1 us
  Pallas kernels: 22.8 us -> 20.9 us
    ppermute x9, waiting for transfers between devices: 15.2 us -> 12.4 us  [turn(): return lax.ppermute(array, 'rep', [(q, (q + d) % 4) for q in range(4)])]
    pallas_call x7 -> x4, Pallas kernels: 11 us -> 8.79 us  [backward(): pl.pallas_call(functools.partial(backward_kernel, first_section, sizes, a...]
    ppermute x29 -> x28, waiting for transfers between devices: 15.1 us -> 15.7 us  [row_permute(): return lax.ppermute(array, 'row', pairs)]
    ppermute x29 -> x28, starting transfers between devices: 52.2 us -> 52 us  [row_permute(): return lax.ppermute(array, 'row', pairs)]
  transfers between devices with their start and end apart: 38 -> 37, of which waited for: 18 -> 15; matrix products, arithmetic and copies ran while one was open for 2% -> 2% of each run, Pallas kernels for 11% -> 11%
where the time goes in v5:
time: 120 us
  starting transfers between devices  63.1 us (53%)
  waiting for transfers between devices  28.1 us (23%)
  Pallas kernels  20.9 us (17%)
  local copies, waits for them, and re-layouts  6 us (5%)
    ppermute x28, starting transfers between devices, row_permute(): return lax.ppermute(array, 'row', pairs)  52 us
    ppermute x28, waiting for transfers between devices, row_permute(): return lax.ppermute(array, 'row', pairs)  15.7 us
    ppermute x9, waiting for transfers between devices, turn(): return lax.ppermute(array, 'rep', [(q, (q + d) % 4) for q in range(4)])  12.4 us
    ppermute x9, starting transfers between devices, turn(): return lax.ppermute(array, 'rep', [(q, (q + d) % 4) for q in range(4)])  11.2 us
    pallas_call x4, Pallas kernels, backward(): pl.pallas_call(functools.partial(backward_kernel, first_section, sizes, a...  8.79 us
    pallas_call x4, Pallas kernels, forward(): pl.pallas_call(functools.partial(forward_kernel, first_section, sizes, fi...  7.13 us
    unnamed x11, local copies, waits for them, and re-layouts  5.05 us
  transfers between devices with their start and end apart: 37, of which 15 were waited for; matrix products, arithmetic and copies ran while one was open for 2% of the time, Pallas kernels for 11%

profile of v5, /device:TPU:1, one launch (start us, length us, event | category | flops | bytes accessed | tf_op | source)
XLA Modules:
  0.0 119.9 jit_solution(18357979026412211063)
XLA Ops:
  0.6 3.3 %collective-permute-start = (bf16[256,128]{1,0:T(8,128)(2,1)}, bf16[256,128]{1,0:T(8,128)(2,1)S(1)}, u32[]{:S(2)}, u32[]{:S(2)}) collective-permute-start(bf16[256,128]{1,0:T(8,128)(2,1)} %own.1), channel_id=1, source_target_pairs={{0,12},{4,0},{8,4},{12,8},{16,28},{20,16},{24,20},{28,24},{32,44},... | collective-permute-start | bytes 196616 | tf_op jit(solution)/shard_map/ppermute | solution.py:68
  3.9 7.1 %collective-permute-start.1 = (bf16[256,128]{1,0:T(8,128)(2,1)}, bf16[256,128]{1,0:T(8,128)(2,1)S(1)}, u32[]{:S(2)}, u32[]{:S(2)}) collective-permute-start(bf16[256,128]{1,0:T(8,128)(2,1)} %own.1), channel_id=1, source_target_pairs={{4,12},{12,4},{20,28},{28,20},{36,44},{44,36},{52,60},{60,52},{68,... | collective-permute-start | bytes 196616 | tf_op jit(solution)/shard_map/ppermute | solution.py:68
  15.2 2.6 %collective-permute-start.5 = (bf16[512,128]{1,0:T(8,128)(2,1)S(1)}, bf16[512,128]{1,0:T(8,128)(2,1)S(1)}, u32[]{:S(2)}, u32[]{:S(2)}) collective-permute-start(bf16[512,128]{1,0:T(8,128)(2,1)S(1)} %pair_up.1.refs_0_), channel_id=1, source_target_pairs={{0,32},{4,132},{8,40},{12,140},{16,48},{20,148},{24,56},{28,156},{... | collective-permute-start | bytes 393224 | tf_op jit(solution)/shard_map/ppermute | solution.py:68
  20.4 3.4 %copy-done = bf16[1,1,256,128,128]{4,3,2,1,0:T(8,128)(2,1)S(1)} copy-done((bf16[1,1,256,128,128]{4,3,2,1,0:T(8,128)(2,1)S(1)}, bf16[1,1,256,128,128]{4,3,2,1,0:T(8,128)(2,1)}, u32[]{:S(2)}) %copy-start) | copy-done | bytes 8388632
  24.5 2.6 %collective-permute-start.7 = (bf16[1024,128]{1,0:T(8,128)(2,1)S(1)}, bf16[1024,128]{1,0:T(8,128)(2,1)S(1)}, u32[]{:S(2)}, u32[]{:S(2)}) collective-permute-start(bf16[1024,128]{1,0:T(8,128)(2,1)S(1)} %place_high.1.refs_3_.refs_1_), channel_id=1, source_target_pairs={{0,192},{4,52},{8,200},{12,60},{16,208},{20,4},{24,216},{28,12},{3... | collective-permute-start | bytes 786440 | tf_op jit(solution)/shard_map/ppermute | solution.py:68
  27.2 2.5 %collective-permute-start.10 = (bf16[1024,128]{1,0:T(8,128)(2,1)S(1)}, bf16[1024,128]{1,0:T(8,128)(2,1)S(1)}, u32[]{:S(2)}, u32[]{:S(2)}) collective-permute-start(bf16[1024,128]{1,0:T(8,128)(2,1)S(1)} %place_low.1.refs_3_.refs_2_.refs_0_), channel_id=1, source_target_pairs={{0,192},{4,52},{8,200},{12,60},{16,208},{20,4},{24,216},{28,12},{3... | collective-permute-start | bytes 786440 | tf_op jit(solution)/shard_map/ppermute | solution.py:68
  30.3 3.4 %collective-permute-start.8 = (bf16[1024,128]{1,0:T(8,128)(2,1)S(1)}, bf16[1024,128]{1,0:T(8,128)(2,1)S(1)}, u32[]{:S(2)}, u32[]{:S(2)}) collective-permute-start(bf16[1024,128]{1,0:T(8,128)(2,1)S(1)} %collective-permute-done.7.refs_5_), channel_id=1, source_target_pairs={{0,192},{4,52},{8,200},{12,60},{16,208},{20,4},{24,216},{28,12},{3... | collective-permute-start | bytes 786440 | tf_op jit(solution)/shard_map/ppermute | solution.py:68
  38.5 1.9 %collective-permute-done.4.refs_0_ = bf16[1024,128]{1,0:T(8,128)(2,1)S(1)} collective-permute-done((bf16[1024,128]{1,0:T(8,128)(2,1)S(1)}, bf16[1024,128]{1,0:T(8,128)(2,1)S(1)}, u32[]{:S(2)}, u32[]{:S(2)}) %collective-permute-start.4) | collective-permute-done | bytes 262176 | tf_op jit(solution)/shard_map/ppermute | solution.py:68
  41.7 2.5 %forward_slots.6.refs_4_ = f32[8,128,128]{2,1,0:T(8,128)S(1)} custom-call(s32[962]{0:T(1024)S(1)} %concatenate.3.meta.refs_0_, bf16[256,128,128]{2,1,0:T(8,128)(2,1)S(1)} %bitcast.7, bf16[6144,128]{1,0:T(8,128)(2,1)S(1)} %collective-permute-done.12.refs_2_, f32[8,128,128]{2,1,0:T(8,128)S(1)} %forward_slots.5.refs_2_.refs_3_), custom_call_target="tpu_custom_call" | custom-call | flops 12582912 | bytes 12582912 | tf_op jit(solution)/shard_map/forward_slots/pallas_call | solution.py:226
  44.3 1.9 %forward_slots.7 = (f32[256,128]{1,0:T(8,128)S(1)}, bf16[256,128]{1,0:T(8,128)(2,1)S(1)}, bf16[256,128]{1,0:T(8,128)(2,1)S(1)}, bf16[256,128]{1,0:T(8,128)(2,1)S(1)}) custom-call(s32[962]{0:T(1024)S(1)} %concatenate.3.meta.refs_0_, bf16[256,128,128]{2,1,0:T(8,128)(2,1)S(1)} %bitcast.8, bf16[2048,128]{1,0:T(8,128)(2,1)S(1)} %place_far.1.refs_2_, ...), custom_call_target="tpu_custom_call" | custom-call | flops 8388608 | bytes 8388608 | tf_op jit(solution)/shard_map/forward_slots/pallas_call | solution.py:226
  50.0 1.9 %collective-permute-done.13.p1 = bf16[256,128]{1,0:T(8,128)(2,1)S(1)} collective-permute-done((bf16[256,128]{1,0:T(8,128)(2,1)S(1)}, bf16[256,128]{1,0:T(8,128)(2,1)S(1)}, u32[]{:S(2)}, u32[]{:S(2)}) %collective-permute-start.13) | collective-permute-done | bytes 65568 | tf_op jit(solution)/shard_map/ppermute | solution.py:94
  51.9 2.8 %collective-permute-done.14.p2 = bf16[256,128]{1,0:T(8,128)(2,1)S(1)} collective-permute-done((bf16[256,128]{1,0:T(8,128)(2,1)S(1)}, bf16[256,128]{1,0:T(8,128)(2,1)S(1)}, u32[]{:S(2)}, u32[]{:S(2)}) %collective-permute-start.14) | collective-permute-done | bytes 65568 | tf_op jit(solution)/shard_map/ppermute | solution.py:94
  61.6 4.6 %collective-permute-done.17.refs_4_.refs_8_ = bf16[320,128]{1,0:T(8,128)(2,1)S(1)} collective-permute-done((bf16[320,128]{1,0:T(8,128)(2,1)S(1)}, bf16[320,128]{1,0:T(8,128)(2,1)S(1)}, u32[]{:S(2)}, u32[]{:S(2)}) %collective-permute-start.17) | collective-permute-done | bytes 81952 | tf_op jit(solution)/shard_map/ppermute | solution.py:94
  66.2 2.3 %backward_slots.4 = (bf16[4288,128]{1,0:T(8,128)(2,1)S(1)}, f32[64,128]{1,0:T(8,128)S(1)}) custom-call(s32[962]{0:T(1024)S(1)} %concatenate.3.meta.refs_0_, bf16[256,128,128]{2,1,0:T(8,128)(2,1)S(1)} %bitcast.9, bf16[256,128]{1,0:T(8,128)(2,1)S(1)} %get-tuple-element.41.refs_2_, bf16[320,128]{1,0:T(8,128)(2,1)S(1)} %collective-permute-done.16.refs_3_.refs_7_, ...), custom_call_target="tpu_custom_call" | custom-call | flops 8388608 | bytes 8388608 | tf_op jit(solution)/shard_map/backward_slots/pallas_call | solution.py:353
  69.2 2.3 %backward_slots.5.refs_9_ = bf16[4096,128]{1,0:T(8,128)(2,1)S(1)} custom-call(s32[962]{0:T(1024)S(1)} %concatenate.3.meta.refs_0_, bf16[256,128,128]{2,1,0:T(8,128)(2,1)S(1)} %bitcast.10, bf16[256,128]{1,0:T(8,128)(2,1)S(1)} %get-tuple-element.41.refs_2_, bf16[320,128]{1,0:T(8,128)(2,1)S(1)} %collective-permute-done.16.refs_3_.refs_7_, ...), custom_call_target="tpu_custom_call" | custom-call | flops 8388608 | bytes 8388608 | tf_op jit(solution)/shard_map/backward_slots/pallas_call | solution.py:353
  73.9 2.4 %collective-permute-start.24 = (bf16[1024,128]{1,0:T(8,128)(2,1)S(1)}, bf16[1024,128]{1,0:T(8,128)(2,1)S(1)}, u32[]{:S(2)}, u32[]{:S(2)}) collective-permute-start(bf16[1024,128]{1,0:T(8,128)(2,1)S(1)} %get-tuple-element.54), channel_id=1, source_target_pairs={{0,192},{4,52},{8,200},{12,60},{16,208},{20,4},{24,216},{28,12},{3... | collective-permute-start | bytes 786440 | tf_op jit(solution)/shard_map/ppermute | solution.py:68
  76.4 2.7 %collective-permute-start.22 = (bf16[1024,128]{1,0:T(8,128)(2,1)S(1)}, bf16[1024,128]{1,0:T(8,128)(2,1)S(1)}, u32[]{:S(2)}, u32[]{:S(2)}) collective-permute-start(bf16[1024,128]{1,0:T(8,128)(2,1)S(1)} %get-tuple-element.51), channel_id=1, source_target_pairs={{0,192},{4,52},{8,200},{12,60},{16,208},{20,4},{24,216},{28,12},{3... | collective-permute-start | bytes 786440 | tf_op jit(solution)/shard_map/ppermute | solution.py:68
  79.0 3.9 %collective-permute-start.25 = (f32[64,128]{1,0:T(8,128)S(1)}, f32[64,128]{1,0:T(8,128)S(1)}, u32[]{:S(2)}, u32[]{:S(2)}) collective-permute-start(f32[64,128]{1,0:T(8,128)S(1)} %get-tuple-element.55.own), channel_id=1, source_target_pairs={{0,8},{4,12},{8,0},{12,4},{16,24},{20,28},{24,16},{28,20},{32,40},... | collective-permute-start | bytes 98312 | tf_op jit(solution)/shard_map/ppermute | solution.py:68
  82.9 2.2 %backward_slots.7 = (bf16[1024,128]{1,0:T(8,128)(2,1)S(1)}, bf16[1024,128]{1,0:T(8,128)(2,1)S(1)}, bf16[2048,128]{1,0:T(8,128)(2,1)S(1)}) custom-call(s32[962]{0:T(1024)S(1)} %concatenate.3.meta.refs_0_, bf16[256,128,128]{2,1,0:T(8,128)(2,1)S(1)} %bitcast.12, bf16[256,128]{1,0:T(8,128)(2,1)S(1)} %get-tuple-element.41.refs_2_, ...), custom_call_target="tpu_custom_call" | custom-call | flops 8388608 | bytes 8388608 | tf_op jit(solution)/shard_map/backward_slots/pallas_call | solution.py:353
  86.2 2.7 %collective-permute-start.27 = (bf16[1216,128]{1,0:T(8,128)(2,1)S(1)}, bf16[1216,128]{1,0:T(8,128)(2,1)S(1)}, u32[]{:S(2)}, u32[]{:S(2)}) collective-permute-start(bf16[1216,128]{1,0:T(8,128)(2,1)S(1)} %get-tuple-element.57), channel_id=1, source_target_pairs={{0,192},{4,52},{8,200},{12,60},{16,208},{20,4},{24,216},{28,12},{3... | collective-permute-start | bytes 933896 | tf_op jit(solution)/shard_map/ppermute | solution.py:68
  89.0 4.2 %collective-permute-done.28.two = f32[64,128]{1,0:T(8,128)S(1)} collective-permute-done((f32[64,128]{1,0:T(8,128)S(1)}, f32[64,128]{1,0:T(8,128)S(1)}, u32[]{:S(2)}, u32[]{:S(2)}) %collective-permute-start.28) | collective-permute-done | bytes 32800 | tf_op jit(solution)/shard_map/ppermute | solution.py:68
  96.7 4.8 %collective-permute-done.29.b = bf16[704,128]{1,0:T(8,128)(2,1)S(1)} collective-permute-done((bf16[704,128]{1,0:T(8,128)(2,1)S(1)}, bf16[704,128]{1,0:T(8,128)(2,1)S(1)}, u32[]{:S(2)}, u32[]{:S(2)}) %collective-permute-start.29) | collective-permute-done | bytes 180256 | tf_op jit(solution)/shard_map/ppermute | solution.py:68
  102.8 6.2 %collective-permute-start.32 = (bf16[256,128]{1,0:T(8,128)(2,1)S(1)}, bf16[256,128]{1,0:T(8,128)(2,1)S(1)}, u32[]{:S(2)}, u32[]{:S(2)}) collective-permute-start(bf16[256,128]{1,0:T(8,128)(2,1)S(1)} %get-tuple-element.64.mine), channel_id=1, source_target_pairs={{4,12},{12,4},{20,28},{28,20},{36,44},{44,36},{52,60},{60,52},{68,... | collective-permute-start | bytes 196616 | tf_op jit(solution)/shard_map/ppermute | solution.py:68
  109.0 4.3 %collective-permute-start.33 = (bf16[256,128]{1,0:T(8,128)(2,1)S(1)}, bf16[256,128]{1,0:T(8,128)(2,1)S(1)}, u32[]{:S(2)}, u32[]{:S(2)}) collective-permute-start(bf16[256,128]{1,0:T(8,128)(2,1)S(1)} %get-tuple-element.65), channel_id=1, source_target_pairs={{0,4},{4,8},{8,12},{12,0},{16,20},{20,24},{24,28},{28,16},{32,36},... | collective-permute-start | bytes 196616 | tf_op jit(solution)/shard_map/ppermute | solution.py:68
  (84 shorter events, 40.3 us)
Async XLA Ops:
  0.6 11.5 %collective-permute-start = (bf16[256,128]{1,0:T(8,128)(2,1)}, bf16[256,128]{1,0:T(8,128)(2,1)S(1)}, u32[]{:S(2)}, u32[]{:S(2)}) collective-permute-start(bf16[256,128]{1,0:T(8,128)(2,1)} %own.1), channel_id=1, source_target_pairs={{0,12},{4,0},{8,4},{12,8},{16,28},{20,16},{24,20},{28,24},{32,44},... | collective-permute-start | bytes 196616 | tf_op jit(solution)/shard_map/ppermute | solution.py:68
  3.9 9.1 %collective-permute-start.1 = (bf16[256,128]{1,0:T(8,128)(2,1)}, bf16[256,128]{1,0:T(8,128)(2,1)S(1)}, u32[]{:S(2)}, u32[]{:S(2)}) collective-permute-start(bf16[256,128]{1,0:T(8,128)(2,1)} %own.1), channel_id=1, source_target_pairs={{4,12},{12,4},{20,28},{28,20},{36,44},{44,36},{52,60},{60,52},{68,... | collective-permute-start | bytes 196616 | tf_op jit(solution)/shard_map/ppermute | solution.py:68
  13.9 10.4 %collective-permute-start.2 = (bf16[512,128]{1,0:T(8,128)(2,1)S(1)}, bf16[512,128]{1,0:T(8,128)(2,1)S(1)}, u32[]{:S(2)}, u32[]{:S(2)}) collective-permute-start(bf16[512,128]{1,0:T(8,128)(2,1)S(1)} %pair_up.1.refs_0_), channel_id=1, source_target_pairs={{0,16},{4,68},{8,24},{12,76},{16,32},{20,84},{24,40},{28,92},{32,4... | collective-permute-start | bytes 393224 | tf_op jit(solution)/shard_map/ppermute | solution.py:68
  15.2 9.2 %collective-permute-start.5 = (bf16[512,128]{1,0:T(8,128)(2,1)S(1)}, bf16[512,128]{1,0:T(8,128)(2,1)S(1)}, u32[]{:S(2)}, u32[]{:S(2)}) collective-permute-start(bf16[512,128]{1,0:T(8,128)(2,1)S(1)} %pair_up.1.refs_0_), channel_id=1, source_target_pairs={{0,32},{4,132},{8,40},{12,140},{16,48},{20,148},{24,56},{28,156},{... | collective-permute-start | bytes 393224 | tf_op jit(solution)/shard_map/ppermute | solution.py:68
  27.0 6.7 %collective-permute-start.3 = (bf16[1024,128]{1,0:T(8,128)(2,1)S(1)}, bf16[1024,128]{1,0:T(8,128)(2,1)S(1)}, u32[]{:S(2)}, u32[]{:S(2)}) collective-permute-start(bf16[1024,128]{1,0:T(8,128)(2,1)S(1)} %place_low.1.refs_3_.refs_2_.refs_0_), channel_id=1, source_target_pairs={{0,64},{4,20},{8,72},{12,28},{16,80},{20,36},{24,88},{28,44},{32,9... | collective-permute-start | bytes 786440 | tf_op jit(solution)/shard_map/ppermute | solution.py:68
  27.0 9.4 %collective-permute-start.9 = (bf16[1024,128]{1,0:T(8,128)(2,1)S(1)}, bf16[1024,128]{1,0:T(8,128)(2,1)S(1)}, u32[]{:S(2)}, u32[]{:S(2)}) collective-permute-start(bf16[1024,128]{1,0:T(8,128)(2,1)S(1)} %place_high.1.refs_3_.refs_1_), channel_id=1, source_target_pairs={{0,64},{4,20},{8,72},{12,28},{16,80},{20,36},{24,88},{28,44},{32,9... | collective-permute-start | bytes 786440 | tf_op jit(solution)/shard_map/ppermute | solution.py:68
  27.2 9.2 %collective-permute-start.10 = (bf16[1024,128]{1,0:T(8,128)(2,1)S(1)}, bf16[1024,128]{1,0:T(8,128)(2,1)S(1)}, u32[]{:S(2)}, u32[]{:S(2)}) collective-permute-start(bf16[1024,128]{1,0:T(8,128)(2,1)S(1)} %place_low.1.refs_3_.refs_2_.refs_0_), channel_id=1, source_target_pairs={{0,192},{4,52},{8,200},{12,60},{16,208},{20,4},{24,216},{28,12},{3... | collective-permute-start | bytes 786440 | tf_op jit(solution)/shard_map/ppermute | solution.py:68
  30.3 8.2 %collective-permute-start.8 = (bf16[1024,128]{1,0:T(8,128)(2,1)S(1)}, bf16[1024,128]{1,0:T(8,128)(2,1)S(1)}, u32[]{:S(2)}, u32[]{:S(2)}) collective-permute-start(bf16[1024,128]{1,0:T(8,128)(2,1)S(1)} %collective-permute-done.7.refs_5_), channel_id=1, source_target_pairs={{0,192},{4,52},{8,200},{12,60},{16,208},{20,4},{24,216},{28,12},{3... | collective-permute-start | bytes 786440 | tf_op jit(solution)/shard_map/ppermute | solution.py:68
  33.7 6.7 %collective-permute-start.4 = (bf16[1024,128]{1,0:T(8,128)(2,1)S(1)}, bf16[1024,128]{1,0:T(8,128)(2,1)S(1)}, u32[]{:S(2)}, u32[]{:S(2)}) collective-permute-start(bf16[1024,128]{1,0:T(8,128)(2,1)S(1)} %collective-permute-done.3.refs_2_), channel_id=1, source_target_pairs={{0,64},{4,20},{8,72},{12,28},{16,80},{20,36},{24,88},{28,44},{32,9... | collective-permute-start | bytes 786440 | tf_op jit(solution)/shard_map/ppermute | solution.py:68
  47.2 7.6 %collective-permute-start.14 = (bf16[256,128]{1,0:T(8,128)(2,1)S(1)}, bf16[256,128]{1,0:T(8,128)(2,1)S(1)}, u32[]{:S(2)}, u32[]{:S(2)}) collective-permute-start(bf16[256,128]{1,0:T(8,128)(2,1)S(1)} %get-tuple-element.38), channel_id=1, source_target_pairs={{0,2},{1,3},{2,0},{3,1},{4,6},{5,7},{6,4},{7,5},{8,10},{9,11},{10,... | collective-permute-start | bytes 196616 | tf_op jit(solution)/shard_map/ppermute | solution.py:94
  58.2 8.0 %collective-permute-start.17 = (bf16[320,128]{1,0:T(8,128)(2,1)S(1)}, bf16[320,128]{1,0:T(8,128)(2,1)S(1)}, u32[]{:S(2)}, u32[]{:S(2)}) collective-permute-start(bf16[320,128]{1,0:T(8,128)(2,1)S(1)} %get-tuple-element.43), channel_id=1, source_target_pairs={{0,2},{1,3},{2,0},{3,1},{4,6},{5,7},{6,4},{7,5},{8,10},{9,11},{10,... | collective-permute-start | bytes 245768 | tf_op jit(solution)/shard_map/ppermute | solution.py:94
  59.2 7.0 %collective-permute-start.18 = (bf16[320,128]{1,0:T(8,128)(2,1)S(1)}, bf16[320,128]{1,0:T(8,128)(2,1)S(1)}, u32[]{:S(2)}, u32[]{:S(2)}) collective-permute-start(bf16[320,128]{1,0:T(8,128)(2,1)S(1)} %get-tuple-element.44), channel_id=1, source_target_pairs={{0,3},{1,0},{2,1},{3,2},{4,7},{5,4},{6,5},{7,6},{8,11},{9,8},{10,9... | collective-permute-start | bytes 245768 | tf_op jit(solution)/shard_map/ppermute | solution.py:94
  71.6 7.5 %collective-permute-start.19 = (bf16[4096,128]{1,0:T(8,128)(2,1)S(1)}, bf16[4096,128]{1,0:T(8,128)(2,1)S(1)}, u32[]{:S(2)}, u32[]{:S(2)}) collective-permute-start(bf16[4096,128]{1,0:T(8,128)(2,1)S(1)} %backward_slots.5.refs_9_), channel_id=1, source_target_pairs={{0,4},{4,0},{8,12},{12,8},{16,20},{20,16},{24,28},{28,24},{32,36},... | collective-permute-start | bytes 3145736 | tf_op jit(solution)/shard_map/ppermute | solution.py:68
  73.6 12.1 %collective-permute-start.23 = (bf16[1024,128]{1,0:T(8,128)(2,1)S(1)}, bf16[1024,128]{1,0:T(8,128)(2,1)S(1)}, u32[]{:S(2)}, u32[]{:S(2)}) collective-permute-start(bf16[1024,128]{1,0:T(8,128)(2,1)S(1)} %get-tuple-element.48.refs_7_), channel_id=1, source_target_pairs={{0,64},{4,20},{8,72},{12,28},{16,80},{20,36},{24,88},{28,44},{32,9... | collective-permute-start | bytes 786440 | tf_op jit(solution)/shard_map/ppermute | solution.py:68
  73.9 11.8 %collective-permute-start.24 = (bf16[1024,128]{1,0:T(8,128)(2,1)S(1)}, bf16[1024,128]{1,0:T(8,128)(2,1)S(1)}, u32[]{:S(2)}, u32[]{:S(2)}) collective-permute-start(bf16[1024,128]{1,0:T(8,128)(2,1)S(1)} %get-tuple-element.54), channel_id=1, source_target_pairs={{0,192},{4,52},{8,200},{12,60},{16,208},{20,4},{24,216},{28,12},{3... | collective-permute-start | bytes 786440 | tf_op jit(solution)/shard_map/ppermute | solution.py:68
  76.3 12.5 %collective-permute-start.21 = (bf16[1024,128]{1,0:T(8,128)(2,1)S(1)}, bf16[1024,128]{1,0:T(8,128)(2,1)S(1)}, u32[]{:S(2)}, u32[]{:S(2)}) collective-permute-start(bf16[1024,128]{1,0:T(8,128)(2,1)S(1)} %get-tuple-element.50), channel_id=1, source_target_pairs={{0,64},{4,20},{8,72},{12,28},{16,80},{20,36},{24,88},{28,44},{32,9... | collective-permute-start | bytes 786440 | tf_op jit(solution)/shard_map/ppermute | solution.py:68
  76.4 12.5 %collective-permute-start.22 = (bf16[1024,128]{1,0:T(8,128)(2,1)S(1)}, bf16[1024,128]{1,0:T(8,128)(2,1)S(1)}, u32[]{:S(2)}, u32[]{:S(2)}) collective-permute-start(bf16[1024,128]{1,0:T(8,128)(2,1)S(1)} %get-tuple-element.51), channel_id=1, source_target_pairs={{0,192},{4,52},{8,200},{12,60},{16,208},{20,4},{24,216},{28,12},{3... | collective-permute-start | bytes 786440 | tf_op jit(solution)/shard_map/ppermute | solution.py:68
  85.8 7.9 %collective-permute-start.26 = (bf16[1216,128]{1,0:T(8,128)(2,1)S(1)}, bf16[1216,128]{1,0:T(8,128)(2,1)S(1)}, u32[]{:S(2)}, u32[]{:S(2)}) collective-permute-start(bf16[1216,128]{1,0:T(8,128)(2,1)S(1)} %get-tuple-element.56.after), channel_id=1, source_target_pairs={{0,64},{4,20},{8,72},{12,28},{16,80},{20,36},{24,88},{28,44},{32,9... | collective-permute-start | bytes 933896 | tf_op jit(solution)/shard_map/ppermute | solution.py:68
  86.2 7.6 %collective-permute-start.27 = (bf16[1216,128]{1,0:T(8,128)(2,1)S(1)}, bf16[1216,128]{1,0:T(8,128)(2,1)S(1)}, u32[]{:S(2)}, u32[]{:S(2)}) collective-permute-start(bf16[1216,128]{1,0:T(8,128)(2,1)S(1)} %get-tuple-element.57), channel_id=1, source_target_pairs={{0,192},{4,52},{8,200},{12,60},{16,208},{20,4},{24,216},{28,12},{3... | collective-permute-start | bytes 933896 | tf_op jit(solution)/shard_map/ppermute | solution.py:68
  93.9 7.6 %collective-permute-start.29 = (bf16[704,128]{1,0:T(8,128)(2,1)S(1)}, bf16[704,128]{1,0:T(8,128)(2,1)S(1)}, u32[]{:S(2)}, u32[]{:S(2)}) collective-permute-start(bf16[704,128]{1,0:T(8,128)(2,1)S(1)} %get-tuple-element.60), channel_id=1, source_target_pairs={{0,16},{4,68},{8,24},{12,76},{16,32},{20,84},{24,40},{28,92},{32,4... | collective-permute-start | bytes 540680 | tf_op jit(solution)/shard_map/ppermute | solution.py:68
  94.0 7.5 %collective-permute-start.30 = (bf16[704,128]{1,0:T(8,128)(2,1)S(1)}, bf16[704,128]{1,0:T(8,128)(2,1)S(1)}, u32[]{:S(2)}, u32[]{:S(2)}) collective-permute-start(bf16[704,128]{1,0:T(8,128)(2,1)S(1)} %get-tuple-element.61), channel_id=1, source_target_pairs={{0,32},{4,132},{8,40},{12,140},{16,48},{20,148},{24,56},{28,156},{... | collective-permute-start | bytes 540680 | tf_op jit(solution)/shard_map/ppermute | solution.py:68
  95.1 7.0 %collective-permute-start.31 = (bf16[704,128]{1,0:T(8,128)(2,1)S(1)}, bf16[704,128]{1,0:T(8,128)(2,1)S(1)}, u32[]{:S(2)}, u32[]{:S(2)}) collective-permute-start(bf16[704,128]{1,0:T(8,128)(2,1)S(1)} %get-tuple-element.62), channel_id=1, source_target_pairs={{0,48},{4,196},{8,56},{12,204},{16,0},{20,212},{24,8},{28,220},{32... | collective-permute-start | bytes 540680 | tf_op jit(solution)/shard_map/ppermute | solution.py:68
  102.8 15.8 %collective-permute-start.32 = (bf16[256,128]{1,0:T(8,128)(2,1)S(1)}, bf16[256,128]{1,0:T(8,128)(2,1)S(1)}, u32[]{:S(2)}, u32[]{:S(2)}) collective-permute-start(bf16[256,128]{1,0:T(8,128)(2,1)S(1)} %get-tuple-element.64.mine), channel_id=1, source_target_pairs={{4,12},{12,4},{20,28},{28,20},{36,44},{44,36},{52,60},{60,52},{68,... | collective-permute-start | bytes 196616 | tf_op jit(solution)/shard_map/ppermute | solution.py:68
  109.0 9.6 %collective-permute-start.33 = (bf16[256,128]{1,0:T(8,128)(2,1)S(1)}, bf16[256,128]{1,0:T(8,128)(2,1)S(1)}, u32[]{:S(2)}, u32[]{:S(2)}) collective-permute-start(bf16[256,128]{1,0:T(8,128)(2,1)S(1)} %get-tuple-element.65), channel_id=1, source_target_pairs={{0,4},{4,8},{8,12},{12,0},{16,20},{20,24},{24,28},{28,16},{32,36},... | collective-permute-start | bytes 196616 | tf_op jit(solution)/shard_map/ppermute | solution.py:68
  (18 other events, 99.7 us)

commit v6 on v5

--- a/solution.py
+++ b/solution.py
@@ -87,7 +87,7 @@
 
 
 def other_z(array):
-    return row_permute(array, lambda y, x, z, c: at(y, x, 1 - z, 1) if c else None)
+    return row_permute(array, lambda y, x, z, c: at(y, x, 1 - z, 1) if c else at(y, x, z, 0))
 
 
 def turn(array, d):
@@ -122,31 +122,22 @@
     )(meta, stored)
 
 
-def pair_up_kernel(core, own, near, far, out, sem):
-    @pl.when(core[0] == 0)
-    def _():
-        copy = pltpu.make_async_copy(own, out.at[pl.ds(0, ROWS)], sem)
-        copy.start()
-        out[ROWS : 2 * ROWS] = near[...]
-        copy.wait()
-
-    @pl.when(core[0] == 1)
-    def _():
-        out[0:ROWS] = near[...]
-        out[ROWS : 2 * ROWS] = far[...]
-
-
-def pair_up(core, own, near, far):
+def pair_up_kernel(core, near, far, out):
+    first = core[0] == 0
+    out[0:ROWS] = jnp.where(first, far[...], near[...])
+    out[ROWS : 2 * ROWS] = jnp.where(first, near[...], far[...])
+
+
+def pair_up(core, near, far):
     return pl.pallas_call(
         pair_up_kernel,
         out_shape=jax.ShapeDtypeStruct((2 * ROWS, B), BF16),
-        in_specs=[SMEM, pl.BlockSpec(memory_space=pl.ANY)] + [VMEM] * 2,
+        in_specs=[SMEM] + [VMEM] * 2,
         out_specs=VMEM,
-        scratch_shapes=[pltpu.SemaphoreType.DMA],
         compiler_params=params(),
         cost_estimate=small_cost(1 << 16),
         name="pair_up",
-    )(core, own, near, far)
+    )(core, near, far)
 
 
 def place_kernel(counts, parts, *refs):
@@ -298,7 +289,7 @@
 
 
 def sibling_terms(extra, outs, extra_outs):
-    extra_outs[0][...] = extra[0][...] + joined(extra[1], 16 * ROWS)
+    extra_outs[0][...] = (extra[0][...] + joined(extra[1], 16 * ROWS)).astype(BF16)
 
 
 def backward_kernel(first_section, sizes, added, extras, finish, *refs):
@@ -363,17 +354,17 @@
 
 
 def late_kernel(a, b, half_1, half_3, own, other, out_1, out_3, w):
-    total = own[...] + other[...]
+    total = (own[...].astype(F32) + other[...].astype(F32)).astype(BF16)
     w[...] = total
     for near, half, out in ((a, half_1, out_1), (b, half_3, out_3)):
         out[0 : 4 * ROWS] = (near[...].astype(F32) + half[...].astype(F32)).astype(BF16)
-        split(total, out, 4 * ROWS)
+        out[4 * ROWS :] = total
 
 
 def add_late(*arrays):
     return pl.pallas_call(
         late_kernel,
-        out_shape=[jax.ShapeDtypeStruct((4 * ROWS + SPLIT, B), BF16)] * 2 + [jax.ShapeDtypeStruct((PIECE, B), F32)],
+        out_shape=[jax.ShapeDtypeStruct((4 * ROWS + PIECE, B), BF16)] * 2 + [jax.ShapeDtypeStruct((PIECE, B), BF16)],
         in_specs=[VMEM] * 6,
         out_specs=[VMEM] * 3,
         compiler_params=params(),
@@ -401,8 +392,9 @@
 
 
 def sum_kernel(a, low, high, own, two, t0, t1, t2, t3, w):
-    row = 4 * ROWS
-    total = (own[...] + two[...]) + (joined(low, row) + joined(high, row))
+    tail = slice(4 * ROWS, 4 * ROWS + PIECE)
+    total = own[...].astype(F32) + two[...].astype(F32)
+    total = total + (low[tail].astype(F32) + high[tail].astype(F32))
     w[...] = total
     for d, out in enumerate((t0, t1, t2, t3)):
         half_ref = high if d >= 2 else low
@@ -447,12 +439,10 @@
     )(meta, *arrays)
 
 
-def last_kernel(scaling, meta, mine, far, crossed, w0, w1, w2, w3, out, weight_grad):
-    first = meta[PLACE + 1] == 0
+def last_kernel(scaling, meta, far, crossed, w0, w1, w2, w3, out, weight_grad):
     for s in range(2):
         part = slice(s * B, (s + 1) * B)
-        own = jnp.where(first, mine[part].astype(F32), far[part].astype(F32))
-        out[part] = (own + crossed[part].astype(F32)).T.astype(BF16)
+        out[part] = (far[part].astype(F32) + crossed[part].astype(F32)).T.astype(BF16)
     rep = meta[PLACE]
     for back, piece in enumerate((w0, w1, w2, w3)):
         rows = pl.ds(pl.multiple_of(lax.rem(rep + 4 - back, 4) * 32, 32), 32)
@@ -464,7 +454,7 @@
     return pl.pallas_call(
         functools.partial(last_kernel, scaling),
         out_shape=[jax.ShapeDtypeStruct((ROWS, B), BF16), jax.ShapeDtypeStruct((B, 2 * B), F32)],
-        in_specs=[SMEM] + [VMEM] * 7,
+        in_specs=[SMEM] + [VMEM] * 6,
         out_specs=[VMEM] * 2,
         compiler_params=params(),
         cost_estimate=small_cost(1 << 16),
@@ -492,7 +482,7 @@
     )
 
     near_unit, far_unit = cross(features, True), other_z(features)
-    pair = pair_up(core.reshape(1), features, near_unit, far_unit)
+    pair = pair_up(core.reshape(1), near_unit, far_unit)
     x1, x2, x3 = small_axis(pair, 1), small_axis(pair, 2), small_axis(pair, 3)
     touched = touch(meta, stored)
     (low,) = place("place_low", [[(0, 0, 2), (1, 0, 2)]], [pair, x1])
@@ -520,7 +510,7 @@
     (second_b,) = bwd(16, (16,), extra=[first_b])
     second_s = sibling(second_b)
     h1, h3, g1_high, g3_low, w8 = bwd(
-        32, (4, 4, 4, 4), first_s, extra=[w4, first_s, second_b], finish=sibling_terms, extra_out=[w], size=LONG
+        32, (4, 4, 4, 4), first_s, extra=[w4, first_s, second_b], finish=sibling_terms, extra_out=[messages[0][:PIECE]], size=LONG
     )
     f1, f3 = large_axis(h1, 1), large_axis(h3, 3)
     r1_high, r3_low = large_axis(g1_high, 1), large_axis(g3_low, 3)
@@ -534,7 +524,7 @@
     mine, other, w = sum_pairs(meta, *sums, w64)
     far, crossed = other_z(mine), cross(other, False)
     feature_grad, weight_grad = last_sum(
-        meta, nodes ** (-0.5), mine, far, crossed, w, *[turn(w, d) for d in (1, 2, 3)]
+        meta, nodes ** (-0.5), far, crossed, w, *[turn(w, d) for d in (1, 2, 3)]
     )
     return activations, feature_grad, weight_grad
 

time: 120 us -> 119 us (level)
    unnamed x11 -> x9, local copies, waits for them, and re-layouts: 5.05 us -> 4.21 us
  transfers between devices with their start and end apart: 37 -> 37, of which waited for: 15 -> 14; matrix products, arithmetic and copies ran while one was open for 2% -> 2% of each run, Pallas kernels for 11% -> 11%
where the time goes in v6:
time: 119 us
  starting transfers between devices  63.5 us (53%)
  waiting for transfers between devices  27.5 us (23%)
  Pallas kernels  20.8 us (17%)
  local copies, waits for them, and re-layouts  5.16 us (4%)
    ppermute x28, starting transfers between devices, row_permute(): return lax.ppermute(array, 'row', pairs)  51.9 us
    ppermute x28, waiting for transfers between devices, row_permute(): return lax.ppermute(array, 'row', pairs)  14.9 us
    ppermute x9, waiting for transfers between devices, turn(): return lax.ppermute(array, 'rep', [(q, (q + d) % 4) for q in range(4)])  12.6 us
    ppermute x9, starting transfers between devices, turn(): return lax.ppermute(array, 'rep', [(q, (q + d) % 4) for q in range(4)])  11.6 us
    pallas_call x4, Pallas kernels, backward(): pl.pallas_call(functools.partial(backward_kernel, first_section, sizes, a...  8.77 us
    pallas_call x4, Pallas kernels, forward(): pl.pallas_call(functools.partial(forward_kernel, first_section, sizes, fi...  7.12 us
    unnamed x9, local copies, waits for them, and re-layouts  4.21 us
  transfers between devices with their start and end apart: 37, of which 14 were waited for; matrix products, arithmetic and copies ran while one was open for 2% of the time, Pallas kernels for 11%

profile of v6, /device:TPU:1, one launch (start us, length us, event | category | flops | bytes accessed | tf_op | source)
XLA Modules:
  0.0 118.8 jit_solution(7889003190635373323)
XLA Ops:
  0.6 3.3 %collective-permute-start = (bf16[256,128]{1,0:T(8,128)(2,1)}, bf16[256,128]{1,0:T(8,128)(2,1)S(1)}, u32[]{:S(2)}, u32[]{:S(2)}) collective-permute-start(bf16[256,128]{1,0:T(8,128)(2,1)} %param.14), channel_id=1, source_target_pairs={{0,12},{4,0},{8,4},{12,8},{16,28},{20,16},{24,20},{28,24},{32,44},... | collective-permute-start | bytes 196616 | tf_op jit(solution)/shard_map/ppermute | solution.py:68
  3.9 7.1 %collective-permute-start.1 = (bf16[256,128]{1,0:T(8,128)(2,1)}, bf16[256,128]{1,0:T(8,128)(2,1)S(1)}, u32[]{:S(2)}, u32[]{:S(2)}) collective-permute-start(bf16[256,128]{1,0:T(8,128)(2,1)} %param.14), channel_id=1, source_target_pairs={{0,0},{4,12},{8,8},{12,4},{16,16},{20,28},{24,24},{28,20},{32,32},... | collective-permute-start | bytes 196616 | tf_op jit(solution)/shard_map/ppermute | solution.py:68
  14.3 2.6 %collective-permute-start.5 = (bf16[512,128]{1,0:T(8,128)(2,1)S(1)}, bf16[512,128]{1,0:T(8,128)(2,1)S(1)}, u32[]{:S(2)}, u32[]{:S(2)}) collective-permute-start(bf16[512,128]{1,0:T(8,128)(2,1)S(1)} %pair_up.1.refs_0_), channel_id=1, source_target_pairs={{0,32},{4,132},{8,40},{12,140},{16,48},{20,148},{24,56},{28,156},{... | collective-permute-start | bytes 393224 | tf_op jit(solution)/shard_map/ppermute | solution.py:68
  19.5 3.4 %copy-done = bf16[1,1,256,128,128]{4,3,2,1,0:T(8,128)(2,1)S(1)} copy-done((bf16[1,1,256,128,128]{4,3,2,1,0:T(8,128)(2,1)S(1)}, bf16[1,1,256,128,128]{4,3,2,1,0:T(8,128)(2,1)}, u32[]{:S(2)}) %copy-start) | copy-done | bytes 8388632
  23.6 2.6 %collective-permute-start.7 = (bf16[1024,128]{1,0:T(8,128)(2,1)S(1)}, bf16[1024,128]{1,0:T(8,128)(2,1)S(1)}, u32[]{:S(2)}, u32[]{:S(2)}) collective-permute-start(bf16[1024,128]{1,0:T(8,128)(2,1)S(1)} %place_high.1.refs_3_.refs_1_), channel_id=1, source_target_pairs={{0,192},{4,52},{8,200},{12,60},{16,208},{20,4},{24,216},{28,12},{3... | collective-permute-start | bytes 786440 | tf_op jit(solution)/shard_map/ppermute | solution.py:68
  26.4 2.5 %collective-permute-start.10 = (bf16[1024,128]{1,0:T(8,128)(2,1)S(1)}, bf16[1024,128]{1,0:T(8,128)(2,1)S(1)}, u32[]{:S(2)}, u32[]{:S(2)}) collective-permute-start(bf16[1024,128]{1,0:T(8,128)(2,1)S(1)} %place_low.1.refs_3_.refs_2_.refs_0_), channel_id=1, source_target_pairs={{0,192},{4,52},{8,200},{12,60},{16,208},{20,4},{24,216},{28,12},{3... | collective-permute-start | bytes 786440 | tf_op jit(solution)/shard_map/ppermute | solution.py:68
  29.5 3.4 %collective-permute-start.8 = (bf16[1024,128]{1,0:T(8,128)(2,1)S(1)}, bf16[1024,128]{1,0:T(8,128)(2,1)S(1)}, u32[]{:S(2)}, u32[]{:S(2)}) collective-permute-start(bf16[1024,128]{1,0:T(8,128)(2,1)S(1)} %collective-permute-done.7.refs_5_), channel_id=1, source_target_pairs={{0,192},{4,52},{8,200},{12,60},{16,208},{20,4},{24,216},{28,12},{3... | collective-permute-start | bytes 786440 | tf_op jit(solution)/shard_map/ppermute | solution.py:68
  41.2 2.5 %forward_slots.6.refs_4_ = f32[8,128,128]{2,1,0:T(8,128)S(1)} custom-call(s32[962]{0:T(1024)S(1)} %concatenate.3.meta.refs_0_, bf16[256,128,128]{2,1,0:T(8,128)(2,1)S(1)} %bitcast.7, bf16[6144,128]{1,0:T(8,128)(2,1)S(1)} %collective-permute-done.12.refs_2_, f32[8,128,128]{2,1,0:T(8,128)S(1)} %forward_slots.5.refs_2_.refs_3_), custom_call_target="tpu_custom_call" | custom-call | flops 12582912 | bytes 12582912 | tf_op jit(solution)/shard_map/forward_slots/pallas_call | solution.py:217
  43.7 1.9 %forward_slots.7 = (f32[256,128]{1,0:T(8,128)S(1)}, bf16[256,128]{1,0:T(8,128)(2,1)S(1)}, bf16[256,128]{1,0:T(8,128)(2,1)S(1)}, bf16[256,128]{1,0:T(8,128)(2,1)S(1)}) custom-call(s32[962]{0:T(1024)S(1)} %concatenate.3.meta.refs_0_, bf16[256,128,128]{2,1,0:T(8,128)(2,1)S(1)} %bitcast.8, bf16[2048,128]{1,0:T(8,128)(2,1)S(1)} %place_far.1.refs_2_, ...), custom_call_target="tpu_custom_call" | custom-call | flops 8388608 | bytes 8388608 | tf_op jit(solution)/shard_map/forward_slots/pallas_call | solution.py:217
  49.5 2.0 %collective-permute-done.13.p1 = bf16[256,128]{1,0:T(8,128)(2,1)S(1)} collective-permute-done((bf16[256,128]{1,0:T(8,128)(2,1)S(1)}, bf16[256,128]{1,0:T(8,128)(2,1)S(1)}, u32[]{:S(2)}, u32[]{:S(2)}) %collective-permute-start.13) | collective-permute-done | bytes 65568 | tf_op jit(solution)/shard_map/ppermute | solution.py:94
  51.5 2.8 %collective-permute-done.14.p2 = bf16[256,128]{1,0:T(8,128)(2,1)S(1)} collective-permute-done((bf16[256,128]{1,0:T(8,128)(2,1)S(1)}, bf16[256,128]{1,0:T(8,128)(2,1)S(1)}, u32[]{:S(2)}, u32[]{:S(2)}) %collective-permute-start.14) | collective-permute-done | bytes 65568 | tf_op jit(solution)/shard_map/ppermute | solution.py:94
  61.1 4.6 %collective-permute-done.17.refs_4_.refs_8_ = bf16[320,128]{1,0:T(8,128)(2,1)S(1)} collective-permute-done((bf16[320,128]{1,0:T(8,128)(2,1)S(1)}, bf16[320,128]{1,0:T(8,128)(2,1)S(1)}, u32[]{:S(2)}, u32[]{:S(2)}) %collective-permute-start.17) | collective-permute-done | bytes 81952 | tf_op jit(solution)/shard_map/ppermute | solution.py:94
  65.7 2.3 %backward_slots.4 = (bf16[4288,128]{1,0:T(8,128)(2,1)S(1)}, f32[64,128]{1,0:T(8,128)S(1)}) custom-call(s32[962]{0:T(1024)S(1)} %concatenate.3.meta.refs_0_, bf16[256,128,128]{2,1,0:T(8,128)(2,1)S(1)} %bitcast.9, bf16[256,128]{1,0:T(8,128)(2,1)S(1)} %get-tuple-element.41.refs_2_, bf16[320,128]{1,0:T(8,128)(2,1)S(1)} %collective-permute-done.16.refs_3_.refs_7_, ...), custom_call_target="tpu_custom_call" | custom-call | flops 8388608 | bytes 8388608 | tf_op jit(solution)/shard_map/backward_slots/pallas_call | solution.py:344
  68.7 2.3 %backward_slots.5.refs_9_ = bf16[4096,128]{1,0:T(8,128)(2,1)S(1)} custom-call(s32[962]{0:T(1024)S(1)} %concatenate.3.meta.refs_0_, bf16[256,128,128]{2,1,0:T(8,128)(2,1)S(1)} %bitcast.10, bf16[256,128]{1,0:T(8,128)(2,1)S(1)} %get-tuple-element.41.refs_2_, bf16[320,128]{1,0:T(8,128)(2,1)S(1)} %collective-permute-done.16.refs_3_.refs_7_, ...), custom_call_target="tpu_custom_call" | custom-call | flops 8388608 | bytes 8388608 | tf_op jit(solution)/shard_map/backward_slots/pallas_call | solution.py:344
  73.4 2.4 %collective-permute-start.24 = (bf16[1024,128]{1,0:T(8,128)(2,1)S(1)}, bf16[1024,128]{1,0:T(8,128)(2,1)S(1)}, u32[]{:S(2)}, u32[]{:S(2)}) collective-permute-start(bf16[1024,128]{1,0:T(8,128)(2,1)S(1)} %get-tuple-element.54), channel_id=1, source_target_pairs={{0,192},{4,52},{8,200},{12,60},{16,208},{20,4},{24,216},{28,12},{3... | collective-permute-start | bytes 786440 | tf_op jit(solution)/shard_map/ppermute | solution.py:68
  75.8 2.7 %collective-permute-start.22 = (bf16[1024,128]{1,0:T(8,128)(2,1)S(1)}, bf16[1024,128]{1,0:T(8,128)(2,1)S(1)}, u32[]{:S(2)}, u32[]{:S(2)}) collective-permute-start(bf16[1024,128]{1,0:T(8,128)(2,1)S(1)} %get-tuple-element.51), channel_id=1, source_target_pairs={{0,192},{4,52},{8,200},{12,60},{16,208},{20,4},{24,216},{28,12},{3... | collective-permute-start | bytes 786440 | tf_op jit(solution)/shard_map/ppermute | solution.py:68
  78.5 3.6 %collective-permute-start.25 = (bf16[64,128]{1,0:T(8,128)(2,1)S(1)}, bf16[64,128]{1,0:T(8,128)(2,1)S(1)}, u32[]{:S(2)}, u32[]{:S(2)}) collective-permute-start(bf16[64,128]{1,0:T(8,128)(2,1)S(1)} %get-tuple-element.55.own), channel_id=1, source_target_pairs={{0,8},{4,12},{8,0},{12,4},{16,24},{20,28},{24,16},{28,20},{32,40},... | collective-permute-start | bytes 49160 | tf_op jit(solution)/shard_map/ppermute | solution.py:68
  82.1 2.2 %backward_slots.7 = (bf16[1024,128]{1,0:T(8,128)(2,1)S(1)}, bf16[1024,128]{1,0:T(8,128)(2,1)S(1)}, bf16[2048,128]{1,0:T(8,128)(2,1)S(1)}) custom-call(s32[962]{0:T(1024)S(1)} %concatenate.3.meta.refs_0_, bf16[256,128,128]{2,1,0:T(8,128)(2,1)S(1)} %bitcast.12, bf16[256,128]{1,0:T(8,128)(2,1)S(1)} %get-tuple-element.41.refs_2_, ...), custom_call_target="tpu_custom_call" | custom-call | flops 8388608 | bytes 8388608 | tf_op jit(solution)/shard_map/backward_slots/pallas_call | solution.py:344
  85.4 2.7 %collective-permute-start.27 = (bf16[1088,128]{1,0:T(8,128)(2,1)S(1)}, bf16[1088,128]{1,0:T(8,128)(2,1)S(1)}, u32[]{:S(2)}, u32[]{:S(2)}) collective-permute-start(bf16[1088,128]{1,0:T(8,128)(2,1)S(1)} %get-tuple-element.57), channel_id=1, source_target_pairs={{0,192},{4,52},{8,200},{12,60},{16,208},{20,4},{24,216},{28,12},{3... | collective-permute-start | bytes 835592 | tf_op jit(solution)/shard_map/ppermute | solution.py:68
  88.2 4.0 %collective-permute-done.28.two = bf16[64,128]{1,0:T(8,128)(2,1)S(1)} collective-permute-done((bf16[64,128]{1,0:T(8,128)(2,1)S(1)}, bf16[64,128]{1,0:T(8,128)(2,1)S(1)}, u32[]{:S(2)}, u32[]{:S(2)}) %collective-permute-start.28) | collective-permute-done | bytes 16416 | tf_op jit(solution)/shard_map/ppermute | solution.py:68
  95.1 4.9 %collective-permute-done.29.b = bf16[704,128]{1,0:T(8,128)(2,1)S(1)} collective-permute-done((bf16[704,128]{1,0:T(8,128)(2,1)S(1)}, bf16[704,128]{1,0:T(8,128)(2,1)S(1)}, u32[]{:S(2)}, u32[]{:S(2)}) %collective-permute-start.29) | collective-permute-done | bytes 180256 | tf_op jit(solution)/shard_map/ppermute | solution.py:68
  101.2 5.5 %collective-permute-start.32 = (bf16[256,128]{1,0:T(8,128)(2,1)S(1)}, bf16[256,128]{1,0:T(8,128)(2,1)S(1)}, u32[]{:S(2)}, u32[]{:S(2)}) collective-permute-start(bf16[256,128]{1,0:T(8,128)(2,1)S(1)} %get-tuple-element.64), channel_id=1, source_target_pairs={{0,0},{4,12},{8,8},{12,4},{16,16},{20,28},{24,24},{28,20},{32,32},... | collective-permute-start | bytes 196616 | tf_op jit(solution)/shard_map/ppermute | solution.py:68
  106.7 4.8 %collective-permute-start.33 = (bf16[256,128]{1,0:T(8,128)(2,1)S(1)}, bf16[256,128]{1,0:T(8,128)(2,1)S(1)}, u32[]{:S(2)}, u32[]{:S(2)}) collective-permute-start(bf16[256,128]{1,0:T(8,128)(2,1)S(1)} %get-tuple-element.65), channel_id=1, source_target_pairs={{0,4},{4,8},{8,12},{12,0},{16,20},{20,24},{24,28},{28,16},{32,36},... | collective-permute-start | bytes 196616 | tf_op jit(solution)/shard_map/ppermute | solution.py:68
  111.5 1.9 %collective-permute-start.34 = (f32[64,128]{1,0:T(8,128)S(1)}, f32[64,128]{1,0:T(8,128)S(1)}, u32[]{:S(2)}, u32[]{:S(2)}) collective-permute-start(f32[64,128]{1,0:T(8,128)S(1)} %get-tuple-element.66.w0), channel_id=1, source_target_pairs={{0,1},{1,2},{2,3},{3,0},{4,5},{5,6},{6,7},{7,4},{8,9},{9,10},{10,1... | collective-permute-start | bytes 98312 | tf_op jit(solution)/shard_map/ppermute | solution.py:94
  (82 shorter events, 40.0 us)
Async XLA Ops:
  0.6 11.5 %collective-permute-start = (bf16[256,128]{1,0:T(8,128)(2,1)}, bf16[256,128]{1,0:T(8,128)(2,1)S(1)}, u32[]{:S(2)}, u32[]{:S(2)}) collective-permute-start(bf16[256,128]{1,0:T(8,128)(2,1)} %param.14), channel_id=1, source_target_pairs={{0,12},{4,0},{8,4},{12,8},{16,28},{20,16},{24,20},{28,24},{32,44},... | collective-permute-start | bytes 196616 | tf_op jit(solution)/shard_map/ppermute | solution.py:68
  3.9 9.1 %collective-permute-start.1 = (bf16[256,128]{1,0:T(8,128)(2,1)}, bf16[256,128]{1,0:T(8,128)(2,1)S(1)}, u32[]{:S(2)}, u32[]{:S(2)}) collective-permute-start(bf16[256,128]{1,0:T(8,128)(2,1)} %param.14), channel_id=1, source_target_pairs={{0,0},{4,12},{8,8},{12,4},{16,16},{20,28},{24,24},{28,20},{32,32},... | collective-permute-start | bytes 196616 | tf_op jit(solution)/shard_map/ppermute | solution.py:68
  13.1 10.4 %collective-permute-start.2 = (bf16[512,128]{1,0:T(8,128)(2,1)S(1)}, bf16[512,128]{1,0:T(8,128)(2,1)S(1)}, u32[]{:S(2)}, u32[]{:S(2)}) collective-permute-start(bf16[512,128]{1,0:T(8,128)(2,1)S(1)} %pair_up.1.refs_0_), channel_id=1, source_target_pairs={{0,16},{4,68},{8,24},{12,76},{16,32},{20,84},{24,40},{28,92},{32,4... | collective-permute-start | bytes 393224 | tf_op jit(solution)/shard_map/ppermute | solution.py:68
  14.3 9.2 %collective-permute-start.5 = (bf16[512,128]{1,0:T(8,128)(2,1)S(1)}, bf16[512,128]{1,0:T(8,128)(2,1)S(1)}, u32[]{:S(2)}, u32[]{:S(2)}) collective-permute-start(bf16[512,128]{1,0:T(8,128)(2,1)S(1)} %pair_up.1.refs_0_), channel_id=1, source_target_pairs={{0,32},{4,132},{8,40},{12,140},{16,48},{20,148},{24,56},{28,156},{... | collective-permute-start | bytes 393224 | tf_op jit(solution)/shard_map/ppermute | solution.py:68
  26.2 6.7 %collective-permute-start.3 = (bf16[1024,128]{1,0:T(8,128)(2,1)S(1)}, bf16[1024,128]{1,0:T(8,128)(2,1)S(1)}, u32[]{:S(2)}, u32[]{:S(2)}) collective-permute-start(bf16[1024,128]{1,0:T(8,128)(2,1)S(1)} %place_low.1.refs_3_.refs_2_.refs_0_), channel_id=1, source_target_pairs={{0,64},{4,20},{8,72},{12,28},{16,80},{20,36},{24,88},{28,44},{32,9... | collective-permute-start | bytes 786440 | tf_op jit(solution)/shard_map/ppermute | solution.py:68
  26.2 9.5 %collective-permute-start.9 = (bf16[1024,128]{1,0:T(8,128)(2,1)S(1)}, bf16[1024,128]{1,0:T(8,128)(2,1)S(1)}, u32[]{:S(2)}, u32[]{:S(2)}) collective-permute-start(bf16[1024,128]{1,0:T(8,128)(2,1)S(1)} %place_high.1.refs_3_.refs_1_), channel_id=1, source_target_pairs={{0,64},{4,20},{8,72},{12,28},{16,80},{20,36},{24,88},{28,44},{32,9... | collective-permute-start | bytes 786440 | tf_op jit(solution)/shard_map/ppermute | solution.py:68
  26.4 9.3 %collective-permute-start.10 = (bf16[1024,128]{1,0:T(8,128)(2,1)S(1)}, bf16[1024,128]{1,0:T(8,128)(2,1)S(1)}, u32[]{:S(2)}, u32[]{:S(2)}) collective-permute-start(bf16[1024,128]{1,0:T(8,128)(2,1)S(1)} %place_low.1.refs_3_.refs_2_.refs_0_), channel_id=1, source_target_pairs={{0,192},{4,52},{8,200},{12,60},{16,208},{20,4},{24,216},{28,12},{3... | collective-permute-start | bytes 786440 | tf_op jit(solution)/shard_map/ppermute | solution.py:68
  29.5 8.5 %collective-permute-start.8 = (bf16[1024,128]{1,0:T(8,128)(2,1)S(1)}, bf16[1024,128]{1,0:T(8,128)(2,1)S(1)}, u32[]{:S(2)}, u32[]{:S(2)}) collective-permute-start(bf16[1024,128]{1,0:T(8,128)(2,1)S(1)} %collective-permute-done.7.refs_5_), channel_id=1, source_target_pairs={{0,192},{4,52},{8,200},{12,60},{16,208},{20,4},{24,216},{28,12},{3... | collective-permute-start | bytes 786440 | tf_op jit(solution)/shard_map/ppermute | solution.py:68
  32.9 6.7 %collective-permute-start.4 = (bf16[1024,128]{1,0:T(8,128)(2,1)S(1)}, bf16[1024,128]{1,0:T(8,128)(2,1)S(1)}, u32[]{:S(2)}, u32[]{:S(2)}) collective-permute-start(bf16[1024,128]{1,0:T(8,128)(2,1)S(1)} %collective-permute-done.3.refs_2_), channel_id=1, source_target_pairs={{0,64},{4,20},{8,72},{12,28},{16,80},{20,36},{24,88},{28,44},{32,9... | collective-permute-start | bytes 786440 | tf_op jit(solution)/shard_map/ppermute | solution.py:68
  46.7 7.6 %collective-permute-start.14 = (bf16[256,128]{1,0:T(8,128)(2,1)S(1)}, bf16[256,128]{1,0:T(8,128)(2,1)S(1)}, u32[]{:S(2)}, u32[]{:S(2)}) collective-permute-start(bf16[256,128]{1,0:T(8,128)(2,1)S(1)} %get-tuple-element.38), channel_id=1, source_target_pairs={{0,2},{1,3},{2,0},{3,1},{4,6},{5,7},{6,4},{7,5},{8,10},{9,11},{10,... | collective-permute-start | bytes 196616 | tf_op jit(solution)/shard_map/ppermute | solution.py:94
  57.6 8.0 %collective-permute-start.17 = (bf16[320,128]{1,0:T(8,128)(2,1)S(1)}, bf16[320,128]{1,0:T(8,128)(2,1)S(1)}, u32[]{:S(2)}, u32[]{:S(2)}) collective-permute-start(bf16[320,128]{1,0:T(8,128)(2,1)S(1)} %get-tuple-element.43), channel_id=1, source_target_pairs={{0,2},{1,3},{2,0},{3,1},{4,6},{5,7},{6,4},{7,5},{8,10},{9,11},{10,... | collective-permute-start | bytes 245768 | tf_op jit(solution)/shard_map/ppermute | solution.py:94
  58.7 6.9 %collective-permute-start.18 = (bf16[320,128]{1,0:T(8,128)(2,1)S(1)}, bf16[320,128]{1,0:T(8,128)(2,1)S(1)}, u32[]{:S(2)}, u32[]{:S(2)}) collective-permute-start(bf16[320,128]{1,0:T(8,128)(2,1)S(1)} %get-tuple-element.44), channel_id=1, source_target_pairs={{0,3},{1,0},{2,1},{3,2},{4,7},{5,4},{6,5},{7,6},{8,11},{9,8},{10,9... | collective-permute-start | bytes 245768 | tf_op jit(solution)/shard_map/ppermute | solution.py:94
  71.0 7.5 %collective-permute-start.19 = (bf16[4096,128]{1,0:T(8,128)(2,1)S(1)}, bf16[4096,128]{1,0:T(8,128)(2,1)S(1)}, u32[]{:S(2)}, u32[]{:S(2)}) collective-permute-start(bf16[4096,128]{1,0:T(8,128)(2,1)S(1)} %backward_slots.5.refs_9_), channel_id=1, source_target_pairs={{0,4},{4,0},{8,12},{12,8},{16,20},{20,16},{24,28},{28,24},{32,36},... | collective-permute-start | bytes 3145736 | tf_op jit(solution)/shard_map/ppermute | solution.py:68
  73.0 11.9 %collective-permute-start.23 = (bf16[1024,128]{1,0:T(8,128)(2,1)S(1)}, bf16[1024,128]{1,0:T(8,128)(2,1)S(1)}, u32[]{:S(2)}, u32[]{:S(2)}) collective-permute-start(bf16[1024,128]{1,0:T(8,128)(2,1)S(1)} %get-tuple-element.48.refs_7_), channel_id=1, source_target_pairs={{0,64},{4,20},{8,72},{12,28},{16,80},{20,36},{24,88},{28,44},{32,9... | collective-permute-start | bytes 786440 | tf_op jit(solution)/shard_map/ppermute | solution.py:68
  73.4 11.5 %collective-permute-start.24 = (bf16[1024,128]{1,0:T(8,128)(2,1)S(1)}, bf16[1024,128]{1,0:T(8,128)(2,1)S(1)}, u32[]{:S(2)}, u32[]{:S(2)}) collective-permute-start(bf16[1024,128]{1,0:T(8,128)(2,1)S(1)} %get-tuple-element.54), channel_id=1, source_target_pairs={{0,192},{4,52},{8,200},{12,60},{16,208},{20,4},{24,216},{28,12},{3... | collective-permute-start | bytes 786440 | tf_op jit(solution)/shard_map/ppermute | solution.py:68
  75.8 12.3 %collective-permute-start.21 = (bf16[1024,128]{1,0:T(8,128)(2,1)S(1)}, bf16[1024,128]{1,0:T(8,128)(2,1)S(1)}, u32[]{:S(2)}, u32[]{:S(2)}) collective-permute-start(bf16[1024,128]{1,0:T(8,128)(2,1)S(1)} %get-tuple-element.50), channel_id=1, source_target_pairs={{0,64},{4,20},{8,72},{12,28},{16,80},{20,36},{24,88},{28,44},{32,9... | collective-permute-start | bytes 786440 | tf_op jit(solution)/shard_map/ppermute | solution.py:68
  75.8 12.3 %collective-permute-start.22 = (bf16[1024,128]{1,0:T(8,128)(2,1)S(1)}, bf16[1024,128]{1,0:T(8,128)(2,1)S(1)}, u32[]{:S(2)}, u32[]{:S(2)}) collective-permute-start(bf16[1024,128]{1,0:T(8,128)(2,1)S(1)} %get-tuple-element.51), channel_id=1, source_target_pairs={{0,192},{4,52},{8,200},{12,60},{16,208},{20,4},{24,216},{28,12},{3... | collective-permute-start | bytes 786440 | tf_op jit(solution)/shard_map/ppermute | solution.py:68
  85.1 7.1 %collective-permute-start.26 = (bf16[1088,128]{1,0:T(8,128)(2,1)S(1)}, bf16[1088,128]{1,0:T(8,128)(2,1)S(1)}, u32[]{:S(2)}, u32[]{:S(2)}) collective-permute-start(bf16[1088,128]{1,0:T(8,128)(2,1)S(1)} %get-tuple-element.56.after), channel_id=1, source_target_pairs={{0,64},{4,20},{8,72},{12,28},{16,80},{20,36},{24,88},{28,44},{32,9... | collective-permute-start | bytes 835592 | tf_op jit(solution)/shard_map/ppermute | solution.py:68
  85.4 6.8 %collective-permute-start.27 = (bf16[1088,128]{1,0:T(8,128)(2,1)S(1)}, bf16[1088,128]{1,0:T(8,128)(2,1)S(1)}, u32[]{:S(2)}, u32[]{:S(2)}) collective-permute-start(bf16[1088,128]{1,0:T(8,128)(2,1)S(1)} %get-tuple-element.57), channel_id=1, source_target_pairs={{0,192},{4,52},{8,200},{12,60},{16,208},{20,4},{24,216},{28,12},{3... | collective-permute-start | bytes 835592 | tf_op jit(solution)/shard_map/ppermute | solution.py:68
  92.3 7.6 %collective-permute-start.29 = (bf16[704,128]{1,0:T(8,128)(2,1)S(1)}, bf16[704,128]{1,0:T(8,128)(2,1)S(1)}, u32[]{:S(2)}, u32[]{:S(2)}) collective-permute-start(bf16[704,128]{1,0:T(8,128)(2,1)S(1)} %get-tuple-element.60), channel_id=1, source_target_pairs={{0,16},{4,68},{8,24},{12,76},{16,32},{20,84},{24,40},{28,92},{32,4... | collective-permute-start | bytes 540680 | tf_op jit(solution)/shard_map/ppermute | solution.py:68
  92.4 7.6 %collective-permute-start.30 = (bf16[704,128]{1,0:T(8,128)(2,1)S(1)}, bf16[704,128]{1,0:T(8,128)(2,1)S(1)}, u32[]{:S(2)}, u32[]{:S(2)}) collective-permute-start(bf16[704,128]{1,0:T(8,128)(2,1)S(1)} %get-tuple-element.61), channel_id=1, source_target_pairs={{0,32},{4,132},{8,40},{12,140},{16,48},{20,148},{24,56},{28,156},{... | collective-permute-start | bytes 540680 | tf_op jit(solution)/shard_map/ppermute | solution.py:68
  93.3 7.2 %collective-permute-start.31 = (bf16[704,128]{1,0:T(8,128)(2,1)S(1)}, bf16[704,128]{1,0:T(8,128)(2,1)S(1)}, u32[]{:S(2)}, u32[]{:S(2)}) collective-permute-start(bf16[704,128]{1,0:T(8,128)(2,1)S(1)} %get-tuple-element.62), channel_id=1, source_target_pairs={{0,48},{4,196},{8,56},{12,204},{16,0},{20,212},{24,8},{28,220},{32... | collective-permute-start | bytes 540680 | tf_op jit(solution)/shard_map/ppermute | solution.py:68
  101.2 16.3 %collective-permute-start.32 = (bf16[256,128]{1,0:T(8,128)(2,1)S(1)}, bf16[256,128]{1,0:T(8,128)(2,1)S(1)}, u32[]{:S(2)}, u32[]{:S(2)}) collective-permute-start(bf16[256,128]{1,0:T(8,128)(2,1)S(1)} %get-tuple-element.64), channel_id=1, source_target_pairs={{0,0},{4,12},{8,8},{12,4},{16,16},{20,28},{24,24},{28,20},{32,32},... | collective-permute-start | bytes 196616 | tf_op jit(solution)/shard_map/ppermute | solution.py:68
  106.7 10.8 %collective-permute-start.33 = (bf16[256,128]{1,0:T(8,128)(2,1)S(1)}, bf16[256,128]{1,0:T(8,128)(2,1)S(1)}, u32[]{:S(2)}, u32[]{:S(2)}) collective-permute-start(bf16[256,128]{1,0:T(8,128)(2,1)S(1)} %get-tuple-element.65), channel_id=1, source_target_pairs={{0,4},{4,8},{8,12},{12,0},{16,20},{20,24},{24,28},{28,16},{32,36},... | collective-permute-start | bytes 196616 | tf_op jit(solution)/shard_map/ppermute | solution.py:68
  (17 other events, 99.8 us)

commit v7 on v6

--- a/solution.py
+++ b/solution.py
@@ -17,6 +17,7 @@
 SPLIT = 3 * PIECE
 COST = B * B * 8
 LONG = 1 << 40
+SECOND = 0
 F32 = jnp.float32
 BF16 = jnp.bfloat16
 VMEM = pl.BlockSpec(memory_space=pltpu.VMEM)
@@ -284,12 +285,16 @@
     total = extra[0][...]
     for ref in extra[1:]:
         total = total + ref[ROWS : ROWS + PIECE].astype(F32)
-    split(total, outs[0], 16 * ROWS)
+    total = total.astype(BF16)
+    outs[0][16 * ROWS :] = total
     extra_outs[0][...] = total
 
 
-def sibling_terms(extra, outs, extra_outs):
-    extra_outs[0][...] = (extra[0][...] + joined(extra[1], 16 * ROWS)).astype(BF16)
+def meet_terms(extra, outs, extra_outs):
+    own, first, other, cross_other = extra[:4]
+    here = own[...].astype(F32) + first[16 * ROWS :].astype(F32)
+    there = other[...].astype(F32) + cross_other[...].astype(F32)
+    extra_outs[0][...] = (here + there).astype(BF16)
 
 
 def backward_kernel(first_section, sizes, added, extras, finish, *refs):
@@ -353,20 +358,18 @@
     )(*args)
 
 
-def late_kernel(a, b, half_1, half_3, own, other, out_1, out_3, w):
-    total = (own[...].astype(F32) + other[...].astype(F32)).astype(BF16)
-    w[...] = total
+def late_kernel(a, b, half_1, half_3, w, out_1, out_3):
     for near, half, out in ((a, half_1, out_1), (b, half_3, out_3)):
         out[0 : 4 * ROWS] = (near[...].astype(F32) + half[...].astype(F32)).astype(BF16)
-        out[4 * ROWS :] = total
+        out[4 * ROWS :] = w[...]
 
 
 def add_late(*arrays):
     return pl.pallas_call(
         late_kernel,
-        out_shape=[jax.ShapeDtypeStruct((4 * ROWS + PIECE, B), BF16)] * 2 + [jax.ShapeDtypeStruct((PIECE, B), BF16)],
-        in_specs=[VMEM] * 6,
-        out_specs=[VMEM] * 3,
+        out_shape=[jax.ShapeDtypeStruct((4 * ROWS + PIECE, B), BF16)] * 2,
+        in_specs=[VMEM] * 5,
+        out_specs=[VMEM] * 2,
         compiler_params=params(),
         cost_estimate=small_cost(1 << 18),
         name="add_late",
@@ -505,19 +508,22 @@
     messages = [turn(m1, 1), turn(m2, 2), turn(m3, 3)]
 
     bwd = functools.partial(backward, meta, stored, [values] + messages)
-    first_b, w4 = bwd(0, (16,), extra=[w] + messages, finish=gather_terms, tails=(SPLIT,), extra_out=[w])
+    piece = jnp.zeros((PIECE, B), BF16)
+    first_b, w4 = bwd(0, (16,), extra=[w] + messages, finish=gather_terms, tails=(PIECE,), extra_out=[piece])
     first_s = sibling(first_b)
+    w4_z = row_permute(w4, lambda y, x, z, c: at(y, x, 1 - z, c))
+    w4_cross = row_permute(w4, lambda y, x, z, c: at(y, x, 1 - z, 1 - c))
     (second_b,) = bwd(16, (16,), extra=[first_b])
     second_s = sibling(second_b)
-    h1, h3, g1_high, g3_low, w8 = bwd(
-        32, (4, 4, 4, 4), first_s, extra=[w4, first_s, second_b], finish=sibling_terms, extra_out=[messages[0][:PIECE]], size=LONG
-    )
+    h1, h3, g1_high, g3_low = bwd(32, (4, 4, 4, 4), first_s, extra=[second_b], size=LONG)
     f1, f3 = large_axis(h1, 1), large_axis(h3, 3)
     r1_high, r3_low = large_axis(g1_high, 1), large_axis(g3_low, 3)
-    w8_z = row_permute(w8, lambda y, x, z, c: at(y, x, 1 - z, c))
-    l1_low, l3_high, g0 = bwd(48, (4, 4, 8), second_s, extra=[h1])
-    g1_low, g3_high, w16 = add_late(l1_low, l3_high, f1, f3, w8, w8_z)
-    r1_low, r3_high, w16_two = large_axis(g1_low, 1), large_axis(g3_high, 3), large_axis(w16, 2)
+    l1_low, l3_high, g0, w16 = bwd(
+        48, (4, 4, 8), second_s, extra=[w4, first_s, w4_z, w4_cross, h1], finish=meet_terms, extra_out=[piece], size=SECOND
+    )
+    w16_two = large_axis(w16, 2)
+    g1_low, g3_high = add_late(l1_low, l3_high, f1, f3, w16)
+    r1_low, r3_high = large_axis(g1_low, 1), large_axis(g3_high, 3)
     g0 = add_early(g0, r1_high, r3_low, g1_low)
     t0, t1, t2, t3, w64 = sum_groups(g0, r1_low, r3_high, w16, w16_two)
     sums = [t0, small_axis(t1, 1), small_axis(t2, 2), small_axis(t3, 3)]

time: 119 us -> 124 us (1.042)
  waiting for transfers between devices: 27.5 us -> 35.8 us
  starting transfers between devices: 63.5 us -> 59.7 us
    ppermute x28 -> x29, waiting for transfers between devices: 14.9 us -> 21.9 us  [row_permute(): return lax.ppermute(array, 'row', pairs)]
    ppermute x28 -> x29, starting transfers between devices: 51.9 us -> 48.9 us  [row_permute(): return lax.ppermute(array, 'row', pairs)]
    ppermute x9, waiting for transfers between devices: 12.6 us -> 13.9 us  [turn(): return lax.ppermute(array, 'rep', [(q, (q + d) % 4) for q in range(4)])]
  transfers between devices with their start and end apart: 37 -> 38, of which waited for: 14 -> 22; matrix products, arithmetic and copies ran while one was open for 2% -> 2% of each run, Pallas kernels for 11% -> 10%
where the time goes in v7:
time: 124 us; the launch traced here: 123 us
  starting transfers between devices  59.7 us (48%)
  waiting for transfers between devices  35.8 us (29%)
  Pallas kernels  20.8 us (17%)
  local copies, waits for them, and re-layouts  5.16 us (4%)
    ppermute x29, starting transfers between devices, row_permute(): return lax.ppermute(array, 'row', pairs)  48.9 us
    ppermute x29, waiting for transfers between devices, row_permute(): return lax.ppermute(array, 'row', pairs)  21.9 us
    ppermute x9, waiting for transfers between devices, turn(): return lax.ppermute(array, 'rep', [(q, (q + d) % 4) for q in range(4)])  13.9 us
    ppermute x9, starting transfers between devices, turn(): return lax.ppermute(array, 'rep', [(q, (q + d) % 4) for q in range(4)])  10.8 us
    pallas_call x4, Pallas kernels, backward(): pl.pallas_call(functools.partial(backward_kernel, first_section, sizes, a...  8.76 us
    pallas_call x4, Pallas kernels, forward(): pl.pallas_call(functools.partial(forward_kernel, first_section, sizes, fi...  7.14 us
    unnamed x9, local copies, waits for them, and re-layouts  4.21 us
  transfers between devices with their start and end apart: 38, of which 22 were waited for; matrix products, arithmetic and copies ran while one was open for 2% of the time, Pallas kernels for 10%

profile of v7, /device:TPU:1, one launch (start us, length us, event | category | flops | bytes accessed | tf_op | source)
XLA Modules:
  0.0 123.3 jit_solution(7093577446736212334)
XLA Ops:
  0.6 9.6 %collective-permute-start.1 = (bf16[256,128]{1,0:T(8,128)(2,1)}, bf16[256,128]{1,0:T(8,128)(2,1)S(1)}, u32[]{:S(2)}, u32[]{:S(2)}) collective-permute-start(bf16[256,128]{1,0:T(8,128)(2,1)} %param.14), channel_id=1, source_target_pairs={{0,0},{4,12},{8,8},{12,4},{16,16},{20,28},{24,24},{28,20},{32,32},... | collective-permute-start | bytes 196616 | tf_op jit(solution)/shard_map/ppermute | solution.py:69
  12.2 6.6 %collective-permute-done.near = bf16[256,128]{1,0:T(8,128)(2,1)S(1)} collective-permute-done((bf16[256,128]{1,0:T(8,128)(2,1)}, bf16[256,128]{1,0:T(8,128)(2,1)S(1)}, u32[]{:S(2)}, u32[]{:S(2)}) %collective-permute-start) | collective-permute-done | bytes 65568 | tf_op jit(solution)/shard_map/ppermute | solution.py:69
  18.8 2.8 %collective-permute-start.6 = (bf16[512,128]{1,0:T(8,128)(2,1)S(1)}, bf16[512,128]{1,0:T(8,128)(2,1)S(1)}, u32[]{:S(2)}, u32[]{:S(2)}) collective-permute-start(bf16[512,128]{1,0:T(8,128)(2,1)S(1)} %pair_up.1.refs_0_), channel_id=1, source_target_pairs={{0,48},{4,196},{8,56},{12,204},{16,0},{20,212},{24,8},{28,220},{32... | collective-permute-start | bytes 393224 | tf_op jit(solution)/shard_map/ppermute | solution.py:69
  24.2 3.4 %copy-done = bf16[1,1,256,128,128]{4,3,2,1,0:T(8,128)(2,1)S(1)} copy-done((bf16[1,1,256,128,128]{4,3,2,1,0:T(8,128)(2,1)S(1)}, bf16[1,1,256,128,128]{4,3,2,1,0:T(8,128)(2,1)}, u32[]{:S(2)}) %copy-start) | copy-done | bytes 8388632
  28.4 2.6 %collective-permute-start.7 = (bf16[1024,128]{1,0:T(8,128)(2,1)S(1)}, bf16[1024,128]{1,0:T(8,128)(2,1)S(1)}, u32[]{:S(2)}, u32[]{:S(2)}) collective-permute-start(bf16[1024,128]{1,0:T(8,128)(2,1)S(1)} %place_high.1.refs_3_.refs_1_), channel_id=1, source_target_pairs={{0,192},{4,52},{8,200},{12,60},{16,208},{20,4},{24,216},{28,12},{3... | collective-permute-start | bytes 786440 | tf_op jit(solution)/shard_map/ppermute | solution.py:69
  31.2 2.5 %collective-permute-start.10 = (bf16[1024,128]{1,0:T(8,128)(2,1)S(1)}, bf16[1024,128]{1,0:T(8,128)(2,1)S(1)}, u32[]{:S(2)}, u32[]{:S(2)}) collective-permute-start(bf16[1024,128]{1,0:T(8,128)(2,1)S(1)} %place_low.1.refs_3_.refs_2_.refs_0_), channel_id=1, source_target_pairs={{0,192},{4,52},{8,200},{12,60},{16,208},{20,4},{24,216},{28,12},{3... | collective-permute-start | bytes 786440 | tf_op jit(solution)/shard_map/ppermute | solution.py:69
  34.3 3.4 %collective-permute-start.8 = (bf16[1024,128]{1,0:T(8,128)(2,1)S(1)}, bf16[1024,128]{1,0:T(8,128)(2,1)S(1)}, u32[]{:S(2)}, u32[]{:S(2)}) collective-permute-start(bf16[1024,128]{1,0:T(8,128)(2,1)S(1)} %collective-permute-done.7.refs_5_), channel_id=1, source_target_pairs={{0,192},{4,52},{8,200},{12,60},{16,208},{20,4},{24,216},{28,12},{3... | collective-permute-start | bytes 786440 | tf_op jit(solution)/shard_map/ppermute | solution.py:69
  44.3 2.6 %forward_slots.6.refs_4_ = f32[8,128,128]{2,1,0:T(8,128)S(1)} custom-call(s32[962]{0:T(1024)S(1)} %concatenate.3.meta.refs_0_, bf16[256,128,128]{2,1,0:T(8,128)(2,1)S(1)} %bitcast.7, bf16[6144,128]{1,0:T(8,128)(2,1)S(1)} %collective-permute-done.12.refs_2_, f32[8,128,128]{2,1,0:T(8,128)S(1)} %forward_slots.5.refs_2_.refs_3_), custom_call_target="tpu_custom_call" | custom-call | flops 12582912 | bytes 12582912 | tf_op jit(solution)/shard_map/forward_slots/pallas_call | solution.py:218
  54.0 2.0 %collective-permute-done.15.p3 = bf16[256,128]{1,0:T(8,128)(2,1)S(1)} collective-permute-done((bf16[256,128]{1,0:T(8,128)(2,1)S(1)}, bf16[256,128]{1,0:T(8,128)(2,1)S(1)}, u32[]{:S(2)}, u32[]{:S(2)}) %collective-permute-start.15) | collective-permute-done | bytes 65568 | tf_op jit(solution)/shard_map/ppermute | solution.py:95
  57.8 2.1 %collective-permute-start.16 = (bf16[320,128]{1,0:T(8,128)(2,1)S(1)}, bf16[320,128]{1,0:T(8,128)(2,1)S(1)}, u32[]{:S(2)}, u32[]{:S(2)}) collective-permute-start(bf16[320,128]{1,0:T(8,128)(2,1)S(1)} %get-tuple-element.41), channel_id=1, source_target_pairs={{0,1},{1,2},{2,3},{3,0},{4,5},{5,6},{6,7},{7,4},{8,9},{9,10},{10,1... | collective-permute-start | bytes 245768 | tf_op jit(solution)/shard_map/ppermute | solution.py:95
  62.9 2.3 %collective-permute-done.17.refs_4_.refs_8_ = bf16[320,128]{1,0:T(8,128)(2,1)S(1)} collective-permute-done((bf16[320,128]{1,0:T(8,128)(2,1)S(1)}, bf16[320,128]{1,0:T(8,128)(2,1)S(1)}, u32[]{:S(2)}, u32[]{:S(2)}) %collective-permute-start.17) | collective-permute-done | bytes 81952 | tf_op jit(solution)/shard_map/ppermute | solution.py:95
  65.2 2.0 %collective-permute-done.18.refs_5_.refs_9_ = bf16[320,128]{1,0:T(8,128)(2,1)S(1)} collective-permute-done((bf16[320,128]{1,0:T(8,128)(2,1)S(1)}, bf16[320,128]{1,0:T(8,128)(2,1)S(1)}, u32[]{:S(2)}, u32[]{:S(2)}) %collective-permute-start.18) | collective-permute-done | bytes 81952 | tf_op jit(solution)/shard_map/ppermute | solution.py:95
  67.2 2.3 %backward_slots.4 = (bf16[4160,128]{1,0:T(8,128)(2,1)S(1)}, bf16[64,128]{1,0:T(8,128)(2,1)S(1)}) custom-call(s32[962]{0:T(1024)S(1)} %concatenate.3.meta.refs_0_, bf16[256,128,128]{2,1,0:T(8,128)(2,1)S(1)} %bitcast.9, bf16[256,128]{1,0:T(8,128)(2,1)S(1)} %get-tuple-element.40.refs_2_, bf16[320,128]{1,0:T(8,128)(2,1)S(1)} %collective-permute-done.16.refs_3_.refs_7_, ...), custom_call_target="tpu_custom_call" | custom-call | flops 8388608 | bytes 8388608 | tf_op jit(solution)/shard_map/backward_slots/pallas_call | solution.py:349
  71.4 3.7 %collective-permute-start.22 = (bf16[64,128]{1,0:T(8,128)(2,1)S(1)}, bf16[64,128]{1,0:T(8,128)(2,1)S(1)}, u32[]{:S(2)}, u32[]{:S(2)}) collective-permute-start(bf16[64,128]{1,0:T(8,128)(2,1)S(1)} %get-tuple-element.46.refs_7_), channel_id=1, source_target_pairs={{0,12},{4,8},{8,4},{12,0},{16,28},{20,24},{24,20},{28,16},{32,44},... | collective-permute-start | bytes 49160 | tf_op jit(solution)/shard_map/ppermute | solution.py:69
  76.7 2.3 %backward_slots.5.refs_7_ = bf16[4096,128]{1,0:T(8,128)(2,1)S(1)} custom-call(s32[962]{0:T(1024)S(1)} %concatenate.3.meta.refs_0_, bf16[256,128,128]{2,1,0:T(8,128)(2,1)S(1)} %bitcast.10, bf16[256,128]{1,0:T(8,128)(2,1)S(1)} %get-tuple-element.40.refs_2_, bf16[320,128]{1,0:T(8,128)(2,1)S(1)} %collective-permute-done.16.refs_3_.refs_7_, ...), custom_call_target="tpu_custom_call" | custom-call | flops 8388608 | bytes 8388608 | tf_op jit(solution)/shard_map/backward_slots/pallas_call | solution.py:349
  83.4 2.6 %collective-permute-start.24 = (bf16[1024,128]{1,0:T(8,128)(2,1)S(1)}, bf16[1024,128]{1,0:T(8,128)(2,1)S(1)}, u32[]{:S(2)}, u32[]{:S(2)}) collective-permute-start(bf16[1024,128]{1,0:T(8,128)(2,1)S(1)} %get-tuple-element.50), channel_id=1, source_target_pairs={{0,192},{4,52},{8,200},{12,60},{16,208},{20,4},{24,216},{28,12},{3... | collective-permute-start | bytes 786440 | tf_op jit(solution)/shard_map/ppermute | solution.py:69
  86.0 2.2 %backward_slots.7 = (bf16[1024,128]{1,0:T(8,128)(2,1)S(1)}, bf16[1024,128]{1,0:T(8,128)(2,1)S(1)}, bf16[2048,128]{1,0:T(8,128)(2,1)S(1)}, bf16[64,128]{1,0:T(8,128)(2,1)S(1)}) custom-call(s32[962]{0:T(1024)S(1)} %concatenate.3.meta.refs_0_, bf16[256,128,128]{2,1,0:T(8,128)(2,1)S(1)} %bitcast.12, bf16[256,128]{1,0:T(8,128)(2,1)S(1)} %get-tuple-element.40.refs_2_, ...), custom_call_target="tpu_custom_call" | custom-call | flops 8388608 | bytes 8388608 | tf_op jit(solution)/shard_map/backward_slots/pallas_call | solution.py:349
  92.6 2.8 %collective-permute-done.28.high = bf16[1088,128]{1,0:T(8,128)(2,1)S(1)} collective-permute-done((bf16[1088,128]{1,0:T(8,128)(2,1)S(1)}, bf16[1088,128]{1,0:T(8,128)(2,1)S(1)}, u32[]{:S(2)}, u32[]{:S(2)}) %collective-permute-start.28) | collective-permute-done | bytes 278560 | tf_op jit(solution)/shard_map/ppermute | solution.py:69
  97.9 2.2 %collective-permute-start.31 = (bf16[704,128]{1,0:T(8,128)(2,1)S(1)}, bf16[704,128]{1,0:T(8,128)(2,1)S(1)}, u32[]{:S(2)}, u32[]{:S(2)}) collective-permute-start(bf16[704,128]{1,0:T(8,128)(2,1)S(1)} %get-tuple-element.59), channel_id=1, source_target_pairs={{0,32},{4,132},{8,40},{12,140},{16,48},{20,148},{24,56},{28,156},{... | collective-permute-start | bytes 540680 | tf_op jit(solution)/shard_map/ppermute | solution.py:69
  100.4 1.9 %collective-permute-done.30.b = bf16[704,128]{1,0:T(8,128)(2,1)S(1)} collective-permute-done((bf16[704,128]{1,0:T(8,128)(2,1)S(1)}, bf16[704,128]{1,0:T(8,128)(2,1)S(1)}, u32[]{:S(2)}, u32[]{:S(2)}) %collective-permute-start.30) | collective-permute-done | bytes 180256 | tf_op jit(solution)/shard_map/ppermute | solution.py:69
  102.4 2.5 %collective-permute-done.31.c = bf16[704,128]{1,0:T(8,128)(2,1)S(1)} collective-permute-done((bf16[704,128]{1,0:T(8,128)(2,1)S(1)}, bf16[704,128]{1,0:T(8,128)(2,1)S(1)}, u32[]{:S(2)}, u32[]{:S(2)}) %collective-permute-start.31) | collective-permute-done | bytes 180256 | tf_op jit(solution)/shard_map/ppermute | solution.py:69
  105.9 6.7 %collective-permute-start.33 = (bf16[256,128]{1,0:T(8,128)(2,1)S(1)}, bf16[256,128]{1,0:T(8,128)(2,1)S(1)}, u32[]{:S(2)}, u32[]{:S(2)}) collective-permute-start(bf16[256,128]{1,0:T(8,128)(2,1)S(1)} %get-tuple-element.62), channel_id=1, source_target_pairs={{0,0},{4,12},{8,8},{12,4},{16,16},{20,28},{24,24},{28,20},{32,32},... | collective-permute-start | bytes 196616 | tf_op jit(solution)/shard_map/ppermute | solution.py:69
  113.9 2.4 %collective-permute-start.37 = (f32[64,128]{1,0:T(8,128)S(1)}, f32[64,128]{1,0:T(8,128)S(1)}, u32[]{:S(2)}, u32[]{:S(2)}) collective-permute-start(f32[64,128]{1,0:T(8,128)S(1)} %get-tuple-element.64.w0), channel_id=1, source_target_pairs={{0,3},{1,0},{2,1},{3,2},{4,7},{5,4},{6,5},{7,6},{8,11},{9,8},{10,9... | collective-permute-start | bytes 98312 | tf_op jit(solution)/shard_map/ppermute | solution.py:95
  117.0 2.2 %collective-permute-done.37.w3 = f32[64,128]{1,0:T(8,128)S(1)} collective-permute-done((f32[64,128]{1,0:T(8,128)S(1)}, f32[64,128]{1,0:T(8,128)S(1)}, u32[]{:S(2)}, u32[]{:S(2)}) %collective-permute-start.37) | collective-permute-done | bytes 32800 | tf_op jit(solution)/shard_map/ppermute | solution.py:95
  (84 shorter events, 46.4 us)
Async XLA Ops:
  0.6 11.6 %collective-permute-start.1 = (bf16[256,128]{1,0:T(8,128)(2,1)}, bf16[256,128]{1,0:T(8,128)(2,1)S(1)}, u32[]{:S(2)}, u32[]{:S(2)}) collective-permute-start(bf16[256,128]{1,0:T(8,128)(2,1)} %param.14), channel_id=1, source_target_pairs={{0,0},{4,12},{8,8},{12,4},{16,16},{20,28},{24,24},{28,20},{32,32},... | collective-permute-start | bytes 196616 | tf_op jit(solution)/shard_map/ppermute | solution.py:69
  10.3 8.5 %collective-permute-start = (bf16[256,128]{1,0:T(8,128)(2,1)}, bf16[256,128]{1,0:T(8,128)(2,1)S(1)}, u32[]{:S(2)}, u32[]{:S(2)}) collective-permute-start(bf16[256,128]{1,0:T(8,128)(2,1)} %param.14), channel_id=1, source_target_pairs={{0,12},{4,0},{8,4},{12,8},{16,28},{20,16},{24,20},{28,24},{32,44},... | collective-permute-start | bytes 196616 | tf_op jit(solution)/shard_map/ppermute | solution.py:69
  18.8 9.6 %collective-permute-start.6 = (bf16[512,128]{1,0:T(8,128)(2,1)S(1)}, bf16[512,128]{1,0:T(8,128)(2,1)S(1)}, u32[]{:S(2)}, u32[]{:S(2)}) collective-permute-start(bf16[512,128]{1,0:T(8,128)(2,1)S(1)} %pair_up.1.refs_0_), channel_id=1, source_target_pairs={{0,48},{4,196},{8,56},{12,204},{16,0},{20,212},{24,8},{28,220},{32... | collective-permute-start | bytes 393224 | tf_op jit(solution)/shard_map/ppermute | solution.py:69
  21.6 6.8 %collective-permute-start.5 = (bf16[512,128]{1,0:T(8,128)(2,1)S(1)}, bf16[512,128]{1,0:T(8,128)(2,1)S(1)}, u32[]{:S(2)}, u32[]{:S(2)}) collective-permute-start(bf16[512,128]{1,0:T(8,128)(2,1)S(1)} %pair_up.1.refs_0_), channel_id=1, source_target_pairs={{0,32},{4,132},{8,40},{12,140},{16,48},{20,148},{24,56},{28,156},{... | collective-permute-start | bytes 393224 | tf_op jit(solution)/shard_map/ppermute | solution.py:69
  22.0 6.4 %collective-permute-start.2 = (bf16[512,128]{1,0:T(8,128)(2,1)S(1)}, bf16[512,128]{1,0:T(8,128)(2,1)S(1)}, u32[]{:S(2)}, u32[]{:S(2)}) collective-permute-start(bf16[512,128]{1,0:T(8,128)(2,1)S(1)} %pair_up.1.refs_0_), channel_id=1, source_target_pairs={{0,16},{4,68},{8,24},{12,76},{16,32},{20,84},{24,40},{28,92},{32,4... | collective-permute-start | bytes 393224 | tf_op jit(solution)/shard_map/ppermute | solution.py:69
  28.4 5.9 %collective-permute-start.7 = (bf16[1024,128]{1,0:T(8,128)(2,1)S(1)}, bf16[1024,128]{1,0:T(8,128)(2,1)S(1)}, u32[]{:S(2)}, u32[]{:S(2)}) collective-permute-start(bf16[1024,128]{1,0:T(8,128)(2,1)S(1)} %place_high.1.refs_3_.refs_1_), channel_id=1, source_target_pairs={{0,192},{4,52},{8,200},{12,60},{16,208},{20,4},{24,216},{28,12},{3... | collective-permute-start | bytes 786440 | tf_op jit(solution)/shard_map/ppermute | solution.py:69
  31.0 6.7 %collective-permute-start.3 = (bf16[1024,128]{1,0:T(8,128)(2,1)S(1)}, bf16[1024,128]{1,0:T(8,128)(2,1)S(1)}, u32[]{:S(2)}, u32[]{:S(2)}) collective-permute-start(bf16[1024,128]{1,0:T(8,128)(2,1)S(1)} %place_low.1.refs_3_.refs_2_.refs_0_), channel_id=1, source_target_pairs={{0,64},{4,20},{8,72},{12,28},{16,80},{20,36},{24,88},{28,44},{32,9... | collective-permute-start | bytes 786440 | tf_op jit(solution)/shard_map/ppermute | solution.py:69
  31.0 9.5 %collective-permute-start.9 = (bf16[1024,128]{1,0:T(8,128)(2,1)S(1)}, bf16[1024,128]{1,0:T(8,128)(2,1)S(1)}, u32[]{:S(2)}, u32[]{:S(2)}) collective-permute-start(bf16[1024,128]{1,0:T(8,128)(2,1)S(1)} %place_high.1.refs_3_.refs_1_), channel_id=1, source_target_pairs={{0,64},{4,20},{8,72},{12,28},{16,80},{20,36},{24,88},{28,44},{32,9... | collective-permute-start | bytes 786440 | tf_op jit(solution)/shard_map/ppermute | solution.py:69
  31.2 9.3 %collective-permute-start.10 = (bf16[1024,128]{1,0:T(8,128)(2,1)S(1)}, bf16[1024,128]{1,0:T(8,128)(2,1)S(1)}, u32[]{:S(2)}, u32[]{:S(2)}) collective-permute-start(bf16[1024,128]{1,0:T(8,128)(2,1)S(1)} %place_low.1.refs_3_.refs_2_.refs_0_), channel_id=1, source_target_pairs={{0,192},{4,52},{8,200},{12,60},{16,208},{20,4},{24,216},{28,12},{3... | collective-permute-start | bytes 786440 | tf_op jit(solution)/shard_map/ppermute | solution.py:69
  34.3 8.0 %collective-permute-start.8 = (bf16[1024,128]{1,0:T(8,128)(2,1)S(1)}, bf16[1024,128]{1,0:T(8,128)(2,1)S(1)}, u32[]{:S(2)}, u32[]{:S(2)}) collective-permute-start(bf16[1024,128]{1,0:T(8,128)(2,1)S(1)} %collective-permute-done.7.refs_5_), channel_id=1, source_target_pairs={{0,192},{4,52},{8,200},{12,60},{16,208},{20,4},{24,216},{28,12},{3... | collective-permute-start | bytes 786440 | tf_op jit(solution)/shard_map/ppermute | solution.py:69
  37.7 6.4 %collective-permute-start.4 = (bf16[1024,128]{1,0:T(8,128)(2,1)S(1)}, bf16[1024,128]{1,0:T(8,128)(2,1)S(1)}, u32[]{:S(2)}, u32[]{:S(2)}) collective-permute-start(bf16[1024,128]{1,0:T(8,128)(2,1)S(1)} %collective-permute-done.3.refs_2_), channel_id=1, source_target_pairs={{0,64},{4,20},{8,72},{12,28},{16,80},{20,36},{24,88},{28,44},{32,9... | collective-permute-start | bytes 786440 | tf_op jit(solution)/shard_map/ppermute | solution.py:69
  61.3 5.9 %collective-permute-start.18 = (bf16[320,128]{1,0:T(8,128)(2,1)S(1)}, bf16[320,128]{1,0:T(8,128)(2,1)S(1)}, u32[]{:S(2)}, u32[]{:S(2)}) collective-permute-start(bf16[320,128]{1,0:T(8,128)(2,1)S(1)} %get-tuple-element.43), channel_id=1, source_target_pairs={{0,3},{1,0},{2,1},{3,2},{4,7},{5,4},{6,5},{7,6},{8,11},{9,8},{10,9... | collective-permute-start | bytes 245768 | tf_op jit(solution)/shard_map/ppermute | solution.py:95
  69.6 10.3 %collective-permute-start.20 = (bf16[4160,128]{1,0:T(8,128)(2,1)S(1)}, bf16[4160,128]{1,0:T(8,128)(2,1)S(1)}, u32[]{:S(2)}, u32[]{:S(2)}) collective-permute-start(bf16[4160,128]{1,0:T(8,128)(2,1)S(1)} %get-tuple-element.45.refs_6_), channel_id=1, source_target_pairs={{0,4},{4,0},{8,12},{12,8},{16,20},{20,16},{24,28},{28,24},{32,36},... | collective-permute-start | bytes 3194888 | tf_op jit(solution)/shard_map/ppermute | solution.py:69
  71.4 11.9 %collective-permute-start.22 = (bf16[64,128]{1,0:T(8,128)(2,1)S(1)}, bf16[64,128]{1,0:T(8,128)(2,1)S(1)}, u32[]{:S(2)}, u32[]{:S(2)}) collective-permute-start(bf16[64,128]{1,0:T(8,128)(2,1)S(1)} %get-tuple-element.46.refs_7_), channel_id=1, source_target_pairs={{0,12},{4,8},{8,4},{12,0},{16,28},{20,24},{24,20},{28,16},{32,44},... | collective-permute-start | bytes 49160 | tf_op jit(solution)/shard_map/ppermute | solution.py:69
  75.0 8.3 %collective-permute-start.21 = (bf16[64,128]{1,0:T(8,128)(2,1)S(1)}, bf16[64,128]{1,0:T(8,128)(2,1)S(1)}, u32[]{:S(2)}, u32[]{:S(2)}) collective-permute-start(bf16[64,128]{1,0:T(8,128)(2,1)S(1)} %get-tuple-element.46.refs_7_), channel_id=1, source_target_pairs={{0,8},{4,12},{8,0},{12,4},{16,24},{20,28},{24,16},{28,20},{32,40},... | collective-permute-start | bytes 49160 | tf_op jit(solution)/shard_map/ppermute | solution.py:69
  79.1 6.9 %collective-permute-start.19 = (bf16[4096,128]{1,0:T(8,128)(2,1)S(1)}, bf16[4096,128]{1,0:T(8,128)(2,1)S(1)}, u32[]{:S(2)}, u32[]{:S(2)}) collective-permute-start(bf16[4096,128]{1,0:T(8,128)(2,1)S(1)} %backward_slots.5.refs_7_), channel_id=1, source_target_pairs={{0,4},{4,0},{8,12},{12,8},{16,20},{20,16},{24,28},{28,24},{32,36},... | collective-permute-start | bytes 3145736 | tf_op jit(solution)/shard_map/ppermute | solution.py:69
  81.8 7.5 %collective-permute-start.26 = (bf16[1024,128]{1,0:T(8,128)(2,1)S(1)}, bf16[1024,128]{1,0:T(8,128)(2,1)S(1)}, u32[]{:S(2)}, u32[]{:S(2)}) collective-permute-start(bf16[1024,128]{1,0:T(8,128)(2,1)S(1)} %get-tuple-element.53), channel_id=1, source_target_pairs={{0,192},{4,52},{8,200},{12,60},{16,208},{20,4},{24,216},{28,12},{3... | collective-permute-start | bytes 786440 | tf_op jit(solution)/shard_map/ppermute | solution.py:69
  82.8 6.7 %collective-permute-start.25 = (bf16[1024,128]{1,0:T(8,128)(2,1)S(1)}, bf16[1024,128]{1,0:T(8,128)(2,1)S(1)}, u32[]{:S(2)}, u32[]{:S(2)}) collective-permute-start(bf16[1024,128]{1,0:T(8,128)(2,1)S(1)} %get-tuple-element.47.refs_11_), channel_id=1, source_target_pairs={{0,64},{4,20},{8,72},{12,28},{16,80},{20,36},{24,88},{28,44},{32,9... | collective-permute-start | bytes 786440 | tf_op jit(solution)/shard_map/ppermute | solution.py:69
  83.3 9.0 %collective-permute-start.23 = (bf16[1024,128]{1,0:T(8,128)(2,1)S(1)}, bf16[1024,128]{1,0:T(8,128)(2,1)S(1)}, u32[]{:S(2)}, u32[]{:S(2)}) collective-permute-start(bf16[1024,128]{1,0:T(8,128)(2,1)S(1)} %get-tuple-element.49), channel_id=1, source_target_pairs={{0,64},{4,20},{8,72},{12,28},{16,80},{20,36},{24,88},{28,44},{32,9... | collective-permute-start | bytes 786440 | tf_op jit(solution)/shard_map/ppermute | solution.py:69
  83.4 9.0 %collective-permute-start.24 = (bf16[1024,128]{1,0:T(8,128)(2,1)S(1)}, bf16[1024,128]{1,0:T(8,128)(2,1)S(1)}, u32[]{:S(2)}, u32[]{:S(2)}) collective-permute-start(bf16[1024,128]{1,0:T(8,128)(2,1)S(1)} %get-tuple-element.50), channel_id=1, source_target_pairs={{0,192},{4,52},{8,200},{12,60},{16,208},{20,4},{24,216},{28,12},{3... | collective-permute-start | bytes 786440 | tf_op jit(solution)/shard_map/ppermute | solution.py:69
  90.0 6.6 %collective-permute-start.27 = (bf16[1088,128]{1,0:T(8,128)(2,1)S(1)}, bf16[1088,128]{1,0:T(8,128)(2,1)S(1)}, u32[]{:S(2)}, u32[]{:S(2)}) collective-permute-start(bf16[1088,128]{1,0:T(8,128)(2,1)S(1)} %get-tuple-element.55.after), channel_id=1, source_target_pairs={{0,64},{4,20},{8,72},{12,28},{16,80},{20,36},{24,88},{28,44},{32,9... | collective-permute-start | bytes 835592 | tf_op jit(solution)/shard_map/ppermute | solution.py:69
  97.9 7.0 %collective-permute-start.31 = (bf16[704,128]{1,0:T(8,128)(2,1)S(1)}, bf16[704,128]{1,0:T(8,128)(2,1)S(1)}, u32[]{:S(2)}, u32[]{:S(2)}) collective-permute-start(bf16[704,128]{1,0:T(8,128)(2,1)S(1)} %get-tuple-element.59), channel_id=1, source_target_pairs={{0,32},{4,132},{8,40},{12,140},{16,48},{20,148},{24,56},{28,156},{... | collective-permute-start | bytes 540680 | tf_op jit(solution)/shard_map/ppermute | solution.py:69
  105.9 16.1 %collective-permute-start.33 = (bf16[256,128]{1,0:T(8,128)(2,1)S(1)}, bf16[256,128]{1,0:T(8,128)(2,1)S(1)}, u32[]{:S(2)}, u32[]{:S(2)}) collective-permute-start(bf16[256,128]{1,0:T(8,128)(2,1)S(1)} %get-tuple-element.62), channel_id=1, source_target_pairs={{0,0},{4,12},{8,8},{12,4},{16,16},{20,28},{24,24},{28,20},{32,32},... | collective-permute-start | bytes 196616 | tf_op jit(solution)/shard_map/ppermute | solution.py:69
  112.6 9.3 %collective-permute-start.34 = (bf16[256,128]{1,0:T(8,128)(2,1)S(1)}, bf16[256,128]{1,0:T(8,128)(2,1)S(1)}, u32[]{:S(2)}, u32[]{:S(2)}) collective-permute-start(bf16[256,128]{1,0:T(8,128)(2,1)S(1)} %get-tuple-element.63), channel_id=1, source_target_pairs={{0,4},{4,8},{8,12},{12,0},{16,20},{20,24},{24,28},{28,16},{32,36},... | collective-permute-start | bytes 196616 | tf_op jit(solution)/shard_map/ppermute | solution.py:69
  (18 other events, 100.2 us)

commit v8 on v6

--- a/solution.py
+++ b/solution.py
@@ -40,9 +40,9 @@
 ]
 LOW, HIGH = (0, 1), (2, 3)
 BACKWARD_GROUPS = [
-    group(1, 2) + group(1, 1, HIGH) + group(1, 3, LOW),
+    group(1, 2, LOW) + group(1, 1, HIGH) + group(1, 2, HIGH) + group(1, 3, LOW),
     group(1, 1, LOW) + group(1, 3, HIGH) + group(1, 0),
-    group(0, 2) + group(0, 1, HIGH) + group(0, 3, LOW),
+    group(0, 2, LOW) + group(0, 1, HIGH) + group(0, 2, HIGH) + group(0, 3, LOW),
     group(0, 1, LOW) + group(0, 3, HIGH) + group(0, 0),
 ]
 
@@ -357,7 +357,7 @@
     total = (own[...].astype(F32) + other[...].astype(F32)).astype(BF16)
     w[...] = total
     for near, half, out in ((a, half_1, out_1), (b, half_3, out_3)):
-        out[0 : 4 * ROWS] = (near[...].astype(F32) + half[...].astype(F32)).astype(BF16)
+        out[0 : 4 * ROWS] = (near[...].astype(F32) + half[0 : 4 * ROWS].astype(F32)).astype(BF16)
         out[4 * ROWS :] = total
 
 
@@ -373,33 +373,18 @@
     )(*arrays)
 
 
-def early_kernel(a, high, low, after, out):
-    for half, start in ((low, 0), (high, 4 * ROWS)):
-        part = slice(start, start + 4 * ROWS)
-        out[part] = (a[part].astype(F32) + half[...].astype(F32)).astype(BF16)
-
-
-def add_early(*arrays):
-    return pl.pallas_call(
-        early_kernel,
-        out_shape=jax.ShapeDtypeStruct((8 * ROWS, B), BF16),
-        in_specs=[VMEM] * 4,
-        out_specs=VMEM,
-        compiler_params=params(),
-        cost_estimate=small_cost(LONG),
-        name="add_early",
-    )(*arrays)
-
-
-def sum_kernel(a, low, high, own, two, t0, t1, t2, t3, w):
+def sum_kernel(a, early_1, early_3, late_1, late_3, own, two, t0, t1, t2, t3, w):
     tail = slice(4 * ROWS, 4 * ROWS + PIECE)
     total = own[...].astype(F32) + two[...].astype(F32)
-    total = total + (low[tail].astype(F32) + high[tail].astype(F32))
+    total = total + (late_1[tail].astype(F32) + late_3[tail].astype(F32))
     w[...] = total
     for d, out in enumerate((t0, t1, t2, t3)):
-        half_ref = high if d >= 2 else low
-        part, half = (slice(2 * ROWS * n, 2 * ROWS * (n + 1)) for n in (d, d % 2))
-        out[0 : 2 * ROWS] = (a[part].astype(F32) + half_ref[half].astype(F32)).astype(BF16)
+        early, late = (early_1, late_3) if d >= 2 else (early_3, late_1)
+        start = 2 * ROWS * (d % 2)
+        group_sum = a[2 * ROWS * d : 2 * ROWS * (d + 1)].astype(F32)
+        group_sum = group_sum + early[4 * ROWS + start : 6 * ROWS + start].astype(F32)
+        group_sum = group_sum + late[start : start + 2 * ROWS].astype(F32)
+        out[0 : 2 * ROWS] = group_sum.astype(BF16)
         if d:
             split(total, out, 2 * ROWS)
 
@@ -410,7 +395,7 @@
         out_shape=[jax.ShapeDtypeStruct((2 * ROWS, B), BF16)]
         + [jax.ShapeDtypeStruct((2 * ROWS + SPLIT, B), BF16)] * 3
         + [jax.ShapeDtypeStruct((PIECE, B), F32)],
-        in_specs=[VMEM] * 5,
+        in_specs=[VMEM] * 7,
         out_specs=[VMEM] * 5,
         compiler_params=params(),
         cost_estimate=small_cost(1 << 18),
@@ -509,17 +494,21 @@
     first_s = sibling(first_b)
     (second_b,) = bwd(16, (16,), extra=[first_b])
     second_s = sibling(second_b)
-    h1, h3, g1_high, g3_low, w8 = bwd(
-        32, (4, 4, 4, 4), first_s, extra=[w4, first_s, second_b], finish=sibling_terms, extra_out=[messages[0][:PIECE]], size=LONG
+    e1, e3, w8 = bwd(
+        32,
+        (8, 8),
+        first_s,
+        extra=[w4, first_s, second_b],
+        finish=sibling_terms,
+        extra_out=[messages[0][:PIECE]],
+        size=LONG,
     )
-    f1, f3 = large_axis(h1, 1), large_axis(h3, 3)
-    r1_high, r3_low = large_axis(g1_high, 1), large_axis(g3_low, 3)
+    r1, r3 = large_axis(e1, 1), large_axis(e3, 3)
     w8_z = row_permute(w8, lambda y, x, z, c: at(y, x, 1 - z, c))
-    l1_low, l3_high, g0 = bwd(48, (4, 4, 8), second_s, extra=[h1])
-    g1_low, g3_high, w16 = add_late(l1_low, l3_high, f1, f3, w8, w8_z)
-    r1_low, r3_high, w16_two = large_axis(g1_low, 1), large_axis(g3_high, 3), large_axis(w16, 2)
-    g0 = add_early(g0, r1_high, r3_low, g1_low)
-    t0, t1, t2, t3, w64 = sum_groups(g0, r1_low, r3_high, w16, w16_two)
+    l1, l3, g0 = bwd(48, (4, 4, 8), second_s, extra=[e1])
+    l1, l3, w16 = add_late(l1, l3, r1, r3, w8, w8_z)
+    l1, l3, w16_two = large_axis(l1, 1), large_axis(l3, 3), large_axis(w16, 2)
+    t0, t1, t2, t3, w64 = sum_groups(g0, r1, r3, l1, l3, w16, w16_two)
     sums = [t0, small_axis(t1, 1), small_axis(t2, 2), small_axis(t3, 3)]
     mine, other, w = sum_pairs(meta, *sums, w64)
     far, crossed = other_z(mine), cross(other, False)

time: 119 us -> 117 us (0.983)
  starting transfers between devices: 63.5 us -> 60 us
  waiting for transfers between devices: 27.5 us -> 28.7 us
    ppermute x28 -> x26, starting transfers between devices: 51.9 us -> 48.4 us  [row_permute(): return lax.ppermute(array, 'row', pairs)]
    ppermute x28 -> x26, waiting for transfers between devices: 14.9 us -> 15.6 us  [row_permute(): return lax.ppermute(array, 'row', pairs)]
  transfers between devices with their start and end apart: 37 -> 35, of which waited for: 14 -> 15; matrix products, arithmetic and copies ran while one was open for 2% -> 2% of each run, Pallas kernels for 11% -> 11%
where the time goes in v8:
time: 117 us
  starting transfers between devices  60 us (51%)
  waiting for transfers between devices  28.7 us (25%)
  Pallas kernels  21.3 us (18%)
  local copies, waits for them, and re-layouts  5.16 us (4%)
    ppermute x26, starting transfers between devices, row_permute(): return lax.ppermute(array, 'row', pairs)  48.4 us
    ppermute x26, waiting for transfers between devices, row_permute(): return lax.ppermute(array, 'row', pairs)  15.6 us
    ppermute x9, waiting for transfers between devices, turn(): return lax.ppermute(array, 'rep', [(q, (q + d) % 4) for q in range(4)])  13.1 us
    ppermute x9, starting transfers between devices, turn(): return lax.ppermute(array, 'rep', [(q, (q + d) % 4) for q in range(4)])  11.6 us
    pallas_call x4, Pallas kernels, backward(): pl.pallas_call(functools.partial(backward_kernel, first_section, sizes, a...  9.23 us
    pallas_call x4, Pallas kernels, forward(): pl.pallas_call(functools.partial(forward_kernel, first_section, sizes, fi...  7.13 us
    unnamed x9, local copies, waits for them, and re-layouts  4.21 us
  transfers between devices with their start and end apart: 35, of which 15 were waited for; matrix products, arithmetic and copies ran while one was open for 2% of the time, Pallas kernels for 11%

profile of v8, /device:TPU:1, one launch (start us, length us, event | category | flops | bytes accessed | tf_op | source)
XLA Modules:
  0.0 116.9 jit_solution(5515090094994931077)
XLA Ops:
  0.6 3.3 %collective-permute-start = (bf16[256,128]{1,0:T(8,128)(2,1)}, bf16[256,128]{1,0:T(8,128)(2,1)S(1)}, u32[]{:S(2)}, u32[]{:S(2)}) collective-permute-start(bf16[256,128]{1,0:T(8,128)(2,1)} %param.14), channel_id=1, source_target_pairs={{0,12},{4,0},{8,4},{12,8},{16,28},{20,16},{24,20},{28,24},{32,44},... | collective-permute-start | bytes 196616 | tf_op jit(solution)/shard_map/ppermute | solution.py:68
  3.9 7.1 %collective-permute-start.1 = (bf16[256,128]{1,0:T(8,128)(2,1)}, bf16[256,128]{1,0:T(8,128)(2,1)S(1)}, u32[]{:S(2)}, u32[]{:S(2)}) collective-permute-start(bf16[256,128]{1,0:T(8,128)(2,1)} %param.14), channel_id=1, source_target_pairs={{0,0},{4,12},{8,8},{12,4},{16,16},{20,28},{24,24},{28,20},{32,32},... | collective-permute-start | bytes 196616 | tf_op jit(solution)/shard_map/ppermute | solution.py:68
  14.3 2.6 %collective-permute-start.5 = (bf16[512,128]{1,0:T(8,128)(2,1)S(1)}, bf16[512,128]{1,0:T(8,128)(2,1)S(1)}, u32[]{:S(2)}, u32[]{:S(2)}) collective-permute-start(bf16[512,128]{1,0:T(8,128)(2,1)S(1)} %pair_up.1.refs_0_), channel_id=1, source_target_pairs={{0,32},{4,132},{8,40},{12,140},{16,48},{20,148},{24,56},{28,156},{... | collective-permute-start | bytes 393224 | tf_op jit(solution)/shard_map/ppermute | solution.py:68
  19.5 3.4 %copy-done = bf16[1,1,256,128,128]{4,3,2,1,0:T(8,128)(2,1)S(1)} copy-done((bf16[1,1,256,128,128]{4,3,2,1,0:T(8,128)(2,1)S(1)}, bf16[1,1,256,128,128]{4,3,2,1,0:T(8,128)(2,1)}, u32[]{:S(2)}) %copy-start) | copy-done | bytes 8388632
  23.6 2.6 %collective-permute-start.7 = (bf16[1024,128]{1,0:T(8,128)(2,1)S(1)}, bf16[1024,128]{1,0:T(8,128)(2,1)S(1)}, u32[]{:S(2)}, u32[]{:S(2)}) collective-permute-start(bf16[1024,128]{1,0:T(8,128)(2,1)S(1)} %place_high.1.refs_3_.refs_1_), channel_id=1, source_target_pairs={{0,192},{4,52},{8,200},{12,60},{16,208},{20,4},{24,216},{28,12},{3... | collective-permute-start | bytes 786440 | tf_op jit(solution)/shard_map/ppermute | solution.py:68
  26.4 2.5 %collective-permute-start.10 = (bf16[1024,128]{1,0:T(8,128)(2,1)S(1)}, bf16[1024,128]{1,0:T(8,128)(2,1)S(1)}, u32[]{:S(2)}, u32[]{:S(2)}) collective-permute-start(bf16[1024,128]{1,0:T(8,128)(2,1)S(1)} %place_low.1.refs_3_.refs_2_.refs_0_), channel_id=1, source_target_pairs={{0,192},{4,52},{8,200},{12,60},{16,208},{20,4},{24,216},{28,12},{3... | collective-permute-start | bytes 786440 | tf_op jit(solution)/shard_map/ppermute | solution.py:68
  29.5 3.4 %collective-permute-start.8 = (bf16[1024,128]{1,0:T(8,128)(2,1)S(1)}, bf16[1024,128]{1,0:T(8,128)(2,1)S(1)}, u32[]{:S(2)}, u32[]{:S(2)}) collective-permute-start(bf16[1024,128]{1,0:T(8,128)(2,1)S(1)} %collective-permute-done.7.refs_5_), channel_id=1, source_target_pairs={{0,192},{4,52},{8,200},{12,60},{16,208},{20,4},{24,216},{28,12},{3... | collective-permute-start | bytes 786440 | tf_op jit(solution)/shard_map/ppermute | solution.py:68
  41.2 2.6 %forward_slots.6.refs_4_ = f32[8,128,128]{2,1,0:T(8,128)S(1)} custom-call(s32[962]{0:T(1024)S(1)} %concatenate.3.meta.refs_0_, bf16[256,128,128]{2,1,0:T(8,128)(2,1)S(1)} %bitcast.7, bf16[6144,128]{1,0:T(8,128)(2,1)S(1)} %collective-permute-done.12.refs_2_, f32[8,128,128]{2,1,0:T(8,128)S(1)} %forward_slots.5.refs_2_.refs_3_), custom_call_target="tpu_custom_call" | custom-call | flops 12582912 | bytes 12582912 | tf_op jit(solution)/shard_map/forward_slots/pallas_call | solution.py:217
  43.8 1.9 %forward_slots.7 = (f32[256,128]{1,0:T(8,128)S(1)}, bf16[256,128]{1,0:T(8,128)(2,1)S(1)}, bf16[256,128]{1,0:T(8,128)(2,1)S(1)}, bf16[256,128]{1,0:T(8,128)(2,1)S(1)}) custom-call(s32[962]{0:T(1024)S(1)} %concatenate.3.meta.refs_0_, bf16[256,128,128]{2,1,0:T(8,128)(2,1)S(1)} %bitcast.8, bf16[2048,128]{1,0:T(8,128)(2,1)S(1)} %place_far.1.refs_2_, ...), custom_call_target="tpu_custom_call" | custom-call | flops 8388608 | bytes 8388608 | tf_op jit(solution)/shard_map/forward_slots/pallas_call | solution.py:217
  49.5 2.0 %collective-permute-done.13.p1 = bf16[256,128]{1,0:T(8,128)(2,1)S(1)} collective-permute-done((bf16[256,128]{1,0:T(8,128)(2,1)S(1)}, bf16[256,128]{1,0:T(8,128)(2,1)S(1)}, u32[]{:S(2)}, u32[]{:S(2)}) %collective-permute-start.13) | collective-permute-done | bytes 65568 | tf_op jit(solution)/shard_map/ppermute | solution.py:94
  51.5 2.7 %collective-permute-done.14.p2 = bf16[256,128]{1,0:T(8,128)(2,1)S(1)} collective-permute-done((bf16[256,128]{1,0:T(8,128)(2,1)S(1)}, bf16[256,128]{1,0:T(8,128)(2,1)S(1)}, u32[]{:S(2)}, u32[]{:S(2)}) %collective-permute-start.14) | collective-permute-done | bytes 65568 | tf_op jit(solution)/shard_map/ppermute | solution.py:94
  61.1 4.6 %collective-permute-done.17.refs_4_.refs_8_ = bf16[320,128]{1,0:T(8,128)(2,1)S(1)} collective-permute-done((bf16[320,128]{1,0:T(8,128)(2,1)S(1)}, bf16[320,128]{1,0:T(8,128)(2,1)S(1)}, u32[]{:S(2)}, u32[]{:S(2)}) %collective-permute-start.17) | collective-permute-done | bytes 81952 | tf_op jit(solution)/shard_map/ppermute | solution.py:94
  65.6 2.3 %backward_slots.4 = (bf16[4288,128]{1,0:T(8,128)(2,1)S(1)}, f32[64,128]{1,0:T(8,128)S(1)}) custom-call(s32[962]{0:T(1024)S(1)} %concatenate.3.meta.refs_0_, bf16[256,128,128]{2,1,0:T(8,128)(2,1)S(1)} %bitcast.9, bf16[256,128]{1,0:T(8,128)(2,1)S(1)} %get-tuple-element.39.refs_2_, bf16[320,128]{1,0:T(8,128)(2,1)S(1)} %collective-permute-done.16.refs_3_.refs_7_, ...), custom_call_target="tpu_custom_call" | custom-call | flops 8388608 | bytes 8388608 | tf_op jit(solution)/shard_map/backward_slots/pallas_call | solution.py:344
  68.7 2.3 %backward_slots.5.refs_9_ = bf16[4096,128]{1,0:T(8,128)(2,1)S(1)} custom-call(s32[962]{0:T(1024)S(1)} %concatenate.3.meta.refs_0_, bf16[256,128,128]{2,1,0:T(8,128)(2,1)S(1)} %bitcast.10, bf16[256,128]{1,0:T(8,128)(2,1)S(1)} %get-tuple-element.39.refs_2_, bf16[320,128]{1,0:T(8,128)(2,1)S(1)} %collective-permute-done.16.refs_3_.refs_7_, ...), custom_call_target="tpu_custom_call" | custom-call | flops 8388608 | bytes 8388608 | tf_op jit(solution)/shard_map/backward_slots/pallas_call | solution.py:344
  71.1 2.3 %backward_slots.6 = (bf16[2048,128]{1,0:T(8,128)(2,1)S(1)}, bf16[2048,128]{1,0:T(8,128)(2,1)S(1)}, bf16[64,128]{1,0:T(8,128)(2,1)S(1)}) custom-call(s32[962]{0:T(1024)S(1)} %concatenate.3.meta.refs_0_, bf16[256,128,128]{2,1,0:T(8,128)(2,1)S(1)} %bitcast.11, bf16[256,128]{1,0:T(8,128)(2,1)S(1)} %get-tuple-element.39.refs_2_, ...), custom_call_target="tpu_custom_call" | custom-call | flops 17179869184 | bytes 17179869184 | tf_op jit(solution)/shard_map/backward_slots/pallas_call | solution.py:344
  73.9 2.3 %collective-permute-start.22 = (bf16[2048,128]{1,0:T(8,128)(2,1)S(1)}, bf16[2048,128]{1,0:T(8,128)(2,1)S(1)}, u32[]{:S(2)}, u32[]{:S(2)}) collective-permute-start(bf16[2048,128]{1,0:T(8,128)(2,1)S(1)} %get-tuple-element.48), channel_id=1, source_target_pairs={{0,192},{4,52},{8,200},{12,60},{16,208},{20,4},{24,216},{28,12},{3... | collective-permute-start | bytes 1572872 | tf_op jit(solution)/shard_map/ppermute | solution.py:68
  76.2 3.6 %collective-permute-start.23 = (bf16[64,128]{1,0:T(8,128)(2,1)S(1)}, bf16[64,128]{1,0:T(8,128)(2,1)S(1)}, u32[]{:S(2)}, u32[]{:S(2)}) collective-permute-start(bf16[64,128]{1,0:T(8,128)(2,1)S(1)} %get-tuple-element.51.own), channel_id=1, source_target_pairs={{0,8},{4,12},{8,0},{12,4},{16,24},{20,28},{24,16},{28,20},{32,40},... | collective-permute-start | bytes 49160 | tf_op jit(solution)/shard_map/ppermute | solution.py:68
  79.9 2.2 %backward_slots.7 = (bf16[1024,128]{1,0:T(8,128)(2,1)S(1)}, bf16[1024,128]{1,0:T(8,128)(2,1)S(1)}, bf16[2048,128]{1,0:T(8,128)(2,1)S(1)}) custom-call(s32[962]{0:T(1024)S(1)} %concatenate.3.meta.refs_0_, bf16[256,128,128]{2,1,0:T(8,128)(2,1)S(1)} %bitcast.12, bf16[256,128]{1,0:T(8,128)(2,1)S(1)} %get-tuple-element.39.refs_2_, ...), custom_call_target="tpu_custom_call" | custom-call | flops 8388608 | bytes 8388608 | tf_op jit(solution)/shard_map/backward_slots/pallas_call | solution.py:344
  83.3 2.7 %collective-permute-start.25 = (bf16[1088,128]{1,0:T(8,128)(2,1)S(1)}, bf16[1088,128]{1,0:T(8,128)(2,1)S(1)}, u32[]{:S(2)}, u32[]{:S(2)}) collective-permute-start(bf16[1088,128]{1,0:T(8,128)(2,1)S(1)} %get-tuple-element.53), channel_id=1, source_target_pairs={{0,192},{4,52},{8,200},{12,60},{16,208},{20,4},{24,216},{28,12},{3... | collective-permute-start | bytes 835592 | tf_op jit(solution)/shard_map/ppermute | solution.py:68
  86.9 4.1 %collective-permute-done.26.two = bf16[64,128]{1,0:T(8,128)(2,1)S(1)} collective-permute-done((bf16[64,128]{1,0:T(8,128)(2,1)S(1)}, bf16[64,128]{1,0:T(8,128)(2,1)S(1)}, u32[]{:S(2)}, u32[]{:S(2)}) %collective-permute-start.26) | collective-permute-done | bytes 16416 | tf_op jit(solution)/shard_map/ppermute | solution.py:68
  94.2 5.1 %collective-permute-done.27.b = bf16[704,128]{1,0:T(8,128)(2,1)S(1)} collective-permute-done((bf16[704,128]{1,0:T(8,128)(2,1)S(1)}, bf16[704,128]{1,0:T(8,128)(2,1)S(1)}, u32[]{:S(2)}, u32[]{:S(2)}) %collective-permute-start.27) | collective-permute-done | bytes 180256 | tf_op jit(solution)/shard_map/ppermute | solution.py:68
  100.6 5.6 %collective-permute-start.30 = (bf16[256,128]{1,0:T(8,128)(2,1)S(1)}, bf16[256,128]{1,0:T(8,128)(2,1)S(1)}, u32[]{:S(2)}, u32[]{:S(2)}) collective-permute-start(bf16[256,128]{1,0:T(8,128)(2,1)S(1)} %get-tuple-element.60), channel_id=1, source_target_pairs={{0,0},{4,12},{8,8},{12,4},{16,16},{20,28},{24,24},{28,20},{32,32},... | collective-permute-start | bytes 196616 | tf_op jit(solution)/shard_map/ppermute | solution.py:68
  106.1 2.9 %collective-permute-start.31 = (bf16[256,128]{1,0:T(8,128)(2,1)S(1)}, bf16[256,128]{1,0:T(8,128)(2,1)S(1)}, u32[]{:S(2)}, u32[]{:S(2)}) collective-permute-start(bf16[256,128]{1,0:T(8,128)(2,1)S(1)} %get-tuple-element.61), channel_id=1, source_target_pairs={{0,4},{4,8},{8,12},{12,0},{16,20},{20,24},{24,28},{28,16},{32,36},... | collective-permute-start | bytes 196616 | tf_op jit(solution)/shard_map/ppermute | solution.py:68
  109.1 1.9 %collective-permute-start.32 = (f32[64,128]{1,0:T(8,128)S(1)}, f32[64,128]{1,0:T(8,128)S(1)}, u32[]{:S(2)}, u32[]{:S(2)}) collective-permute-start(f32[64,128]{1,0:T(8,128)S(1)} %get-tuple-element.62.w0), channel_id=1, source_target_pairs={{0,1},{1,2},{2,3},{3,0},{4,5},{5,6},{6,7},{7,4},{8,9},{9,10},{10,1... | collective-permute-start | bytes 98312 | tf_op jit(solution)/shard_map/ppermute | solution.py:94
  (77 shorter events, 39.8 us)
Async XLA Ops:
  0.6 11.5 %collective-permute-start = (bf16[256,128]{1,0:T(8,128)(2,1)}, bf16[256,128]{1,0:T(8,128)(2,1)S(1)}, u32[]{:S(2)}, u32[]{:S(2)}) collective-permute-start(bf16[256,128]{1,0:T(8,128)(2,1)} %param.14), channel_id=1, source_target_pairs={{0,12},{4,0},{8,4},{12,8},{16,28},{20,16},{24,20},{28,24},{32,44},... | collective-permute-start | bytes 196616 | tf_op jit(solution)/shard_map/ppermute | solution.py:68
  3.9 9.1 %collective-permute-start.1 = (bf16[256,128]{1,0:T(8,128)(2,1)}, bf16[256,128]{1,0:T(8,128)(2,1)S(1)}, u32[]{:S(2)}, u32[]{:S(2)}) collective-permute-start(bf16[256,128]{1,0:T(8,128)(2,1)} %param.14), channel_id=1, source_target_pairs={{0,0},{4,12},{8,8},{12,4},{16,16},{20,28},{24,24},{28,20},{32,32},... | collective-permute-start | bytes 196616 | tf_op jit(solution)/shard_map/ppermute | solution.py:68
  13.1 10.4 %collective-permute-start.2 = (bf16[512,128]{1,0:T(8,128)(2,1)S(1)}, bf16[512,128]{1,0:T(8,128)(2,1)S(1)}, u32[]{:S(2)}, u32[]{:S(2)}) collective-permute-start(bf16[512,128]{1,0:T(8,128)(2,1)S(1)} %pair_up.1.refs_0_), channel_id=1, source_target_pairs={{0,16},{4,68},{8,24},{12,76},{16,32},{20,84},{24,40},{28,92},{32,4... | collective-permute-start | bytes 393224 | tf_op jit(solution)/shard_map/ppermute | solution.py:68
  14.3 9.2 %collective-permute-start.5 = (bf16[512,128]{1,0:T(8,128)(2,1)S(1)}, bf16[512,128]{1,0:T(8,128)(2,1)S(1)}, u32[]{:S(2)}, u32[]{:S(2)}) collective-permute-start(bf16[512,128]{1,0:T(8,128)(2,1)S(1)} %pair_up.1.refs_0_), channel_id=1, source_target_pairs={{0,32},{4,132},{8,40},{12,140},{16,48},{20,148},{24,56},{28,156},{... | collective-permute-start | bytes 393224 | tf_op jit(solution)/shard_map/ppermute | solution.py:68
  17.0 6.6 %collective-permute-start.6 = (bf16[512,128]{1,0:T(8,128)(2,1)S(1)}, bf16[512,128]{1,0:T(8,128)(2,1)S(1)}, u32[]{:S(2)}, u32[]{:S(2)}) collective-permute-start(bf16[512,128]{1,0:T(8,128)(2,1)S(1)} %pair_up.1.refs_0_), channel_id=1, source_target_pairs={{0,48},{4,196},{8,56},{12,204},{16,0},{20,212},{24,8},{28,220},{32... | collective-permute-start | bytes 393224 | tf_op jit(solution)/shard_map/ppermute | solution.py:68
  26.2 6.7 %collective-permute-start.3 = (bf16[1024,128]{1,0:T(8,128)(2,1)S(1)}, bf16[1024,128]{1,0:T(8,128)(2,1)S(1)}, u32[]{:S(2)}, u32[]{:S(2)}) collective-permute-start(bf16[1024,128]{1,0:T(8,128)(2,1)S(1)} %place_low.1.refs_3_.refs_2_.refs_0_), channel_id=1, source_target_pairs={{0,64},{4,20},{8,72},{12,28},{16,80},{20,36},{24,88},{28,44},{32,9... | collective-permute-start | bytes 786440 | tf_op jit(solution)/shard_map/ppermute | solution.py:68
  26.2 9.5 %collective-permute-start.9 = (bf16[1024,128]{1,0:T(8,128)(2,1)S(1)}, bf16[1024,128]{1,0:T(8,128)(2,1)S(1)}, u32[]{:S(2)}, u32[]{:S(2)}) collective-permute-start(bf16[1024,128]{1,0:T(8,128)(2,1)S(1)} %place_high.1.refs_3_.refs_1_), channel_id=1, source_target_pairs={{0,64},{4,20},{8,72},{12,28},{16,80},{20,36},{24,88},{28,44},{32,9... | collective-permute-start | bytes 786440 | tf_op jit(solution)/shard_map/ppermute | solution.py:68
  26.4 9.3 %collective-permute-start.10 = (bf16[1024,128]{1,0:T(8,128)(2,1)S(1)}, bf16[1024,128]{1,0:T(8,128)(2,1)S(1)}, u32[]{:S(2)}, u32[]{:S(2)}) collective-permute-start(bf16[1024,128]{1,0:T(8,128)(2,1)S(1)} %place_low.1.refs_3_.refs_2_.refs_0_), channel_id=1, source_target_pairs={{0,192},{4,52},{8,200},{12,60},{16,208},{20,4},{24,216},{28,12},{3... | collective-permute-start | bytes 786440 | tf_op jit(solution)/shard_map/ppermute | solution.py:68
  29.5 8.5 %collective-permute-start.8 = (bf16[1024,128]{1,0:T(8,128)(2,1)S(1)}, bf16[1024,128]{1,0:T(8,128)(2,1)S(1)}, u32[]{:S(2)}, u32[]{:S(2)}) collective-permute-start(bf16[1024,128]{1,0:T(8,128)(2,1)S(1)} %collective-permute-done.7.refs_5_), channel_id=1, source_target_pairs={{0,192},{4,52},{8,200},{12,60},{16,208},{20,4},{24,216},{28,12},{3... | collective-permute-start | bytes 786440 | tf_op jit(solution)/shard_map/ppermute | solution.py:68
  32.9 6.7 %collective-permute-start.4 = (bf16[1024,128]{1,0:T(8,128)(2,1)S(1)}, bf16[1024,128]{1,0:T(8,128)(2,1)S(1)}, u32[]{:S(2)}, u32[]{:S(2)}) collective-permute-start(bf16[1024,128]{1,0:T(8,128)(2,1)S(1)} %collective-permute-done.3.refs_2_), channel_id=1, source_target_pairs={{0,64},{4,20},{8,72},{12,28},{16,80},{20,36},{24,88},{28,44},{32,9... | collective-permute-start | bytes 786440 | tf_op jit(solution)/shard_map/ppermute | solution.py:68
  46.7 7.6 %collective-permute-start.14 = (bf16[256,128]{1,0:T(8,128)(2,1)S(1)}, bf16[256,128]{1,0:T(8,128)(2,1)S(1)}, u32[]{:S(2)}, u32[]{:S(2)}) collective-permute-start(bf16[256,128]{1,0:T(8,128)(2,1)S(1)} %get-tuple-element.36), channel_id=1, source_target_pairs={{0,2},{1,3},{2,0},{3,1},{4,6},{5,7},{6,4},{7,5},{8,10},{9,11},{10,... | collective-permute-start | bytes 196616 | tf_op jit(solution)/shard_map/ppermute | solution.py:94
  57.6 8.0 %collective-permute-start.17 = (bf16[320,128]{1,0:T(8,128)(2,1)S(1)}, bf16[320,128]{1,0:T(8,128)(2,1)S(1)}, u32[]{:S(2)}, u32[]{:S(2)}) collective-permute-start(bf16[320,128]{1,0:T(8,128)(2,1)S(1)} %get-tuple-element.41), channel_id=1, source_target_pairs={{0,2},{1,3},{2,0},{3,1},{4,6},{5,7},{6,4},{7,5},{8,10},{9,11},{10,... | collective-permute-start | bytes 245768 | tf_op jit(solution)/shard_map/ppermute | solution.py:94
  58.7 6.9 %collective-permute-start.18 = (bf16[320,128]{1,0:T(8,128)(2,1)S(1)}, bf16[320,128]{1,0:T(8,128)(2,1)S(1)}, u32[]{:S(2)}, u32[]{:S(2)}) collective-permute-start(bf16[320,128]{1,0:T(8,128)(2,1)S(1)} %get-tuple-element.42), channel_id=1, source_target_pairs={{0,3},{1,0},{2,1},{3,2},{4,7},{5,4},{6,5},{7,6},{8,11},{9,8},{10,9... | collective-permute-start | bytes 245768 | tf_op jit(solution)/shard_map/ppermute | solution.py:94
  71.0 8.9 %collective-permute-start.19 = (bf16[4096,128]{1,0:T(8,128)(2,1)S(1)}, bf16[4096,128]{1,0:T(8,128)(2,1)S(1)}, u32[]{:S(2)}, u32[]{:S(2)}) collective-permute-start(bf16[4096,128]{1,0:T(8,128)(2,1)S(1)} %backward_slots.5.refs_9_), channel_id=1, source_target_pairs={{0,4},{4,0},{8,12},{12,8},{16,20},{20,16},{24,28},{28,24},{32,36},... | collective-permute-start | bytes 3145736 | tf_op jit(solution)/shard_map/ppermute | solution.py:68
  73.5 9.6 %collective-permute-start.21 = (bf16[2048,128]{1,0:T(8,128)(2,1)S(1)}, bf16[2048,128]{1,0:T(8,128)(2,1)S(1)}, u32[]{:S(2)}, u32[]{:S(2)}) collective-permute-start(bf16[2048,128]{1,0:T(8,128)(2,1)S(1)} %get-tuple-element.46.refs_7_), channel_id=1, source_target_pairs={{0,64},{4,20},{8,72},{12,28},{16,80},{20,36},{24,88},{28,44},{32,9... | collective-permute-start | bytes 1572872 | tf_op jit(solution)/shard_map/ppermute | solution.py:68
  73.9 9.2 %collective-permute-start.22 = (bf16[2048,128]{1,0:T(8,128)(2,1)S(1)}, bf16[2048,128]{1,0:T(8,128)(2,1)S(1)}, u32[]{:S(2)}, u32[]{:S(2)}) collective-permute-start(bf16[2048,128]{1,0:T(8,128)(2,1)S(1)} %get-tuple-element.48), channel_id=1, source_target_pairs={{0,192},{4,52},{8,200},{12,60},{16,208},{20,4},{24,216},{28,12},{3... | collective-permute-start | bytes 1572872 | tf_op jit(solution)/shard_map/ppermute | solution.py:68
  76.2 6.5 %collective-permute-start.23 = (bf16[64,128]{1,0:T(8,128)(2,1)S(1)}, bf16[64,128]{1,0:T(8,128)(2,1)S(1)}, u32[]{:S(2)}, u32[]{:S(2)}) collective-permute-start(bf16[64,128]{1,0:T(8,128)(2,1)S(1)} %get-tuple-element.51.own), channel_id=1, source_target_pairs={{0,8},{4,12},{8,0},{12,4},{16,24},{20,28},{24,16},{28,20},{32,40},... | collective-permute-start | bytes 49160 | tf_op jit(solution)/shard_map/ppermute | solution.py:68
  83.2 7.7 %collective-permute-start.24 = (bf16[1088,128]{1,0:T(8,128)(2,1)S(1)}, bf16[1088,128]{1,0:T(8,128)(2,1)S(1)}, u32[]{:S(2)}, u32[]{:S(2)}) collective-permute-start(bf16[1088,128]{1,0:T(8,128)(2,1)S(1)} %get-tuple-element.52), channel_id=1, source_target_pairs={{0,64},{4,20},{8,72},{12,28},{16,80},{20,36},{24,88},{28,44},{32,9... | collective-permute-start | bytes 835592 | tf_op jit(solution)/shard_map/ppermute | solution.py:68
  83.3 7.7 %collective-permute-start.25 = (bf16[1088,128]{1,0:T(8,128)(2,1)S(1)}, bf16[1088,128]{1,0:T(8,128)(2,1)S(1)}, u32[]{:S(2)}, u32[]{:S(2)}) collective-permute-start(bf16[1088,128]{1,0:T(8,128)(2,1)S(1)} %get-tuple-element.53), channel_id=1, source_target_pairs={{0,192},{4,52},{8,200},{12,60},{16,208},{20,4},{24,216},{28,12},{3... | collective-permute-start | bytes 835592 | tf_op jit(solution)/shard_map/ppermute | solution.py:68
  91.2 8.1 %collective-permute-start.27 = (bf16[704,128]{1,0:T(8,128)(2,1)S(1)}, bf16[704,128]{1,0:T(8,128)(2,1)S(1)}, u32[]{:S(2)}, u32[]{:S(2)}) collective-permute-start(bf16[704,128]{1,0:T(8,128)(2,1)S(1)} %get-tuple-element.56), channel_id=1, source_target_pairs={{0,16},{4,68},{8,24},{12,76},{16,32},{20,84},{24,40},{28,92},{32,4... | collective-permute-start | bytes 540680 | tf_op jit(solution)/shard_map/ppermute | solution.py:68
  91.5 7.8 %collective-permute-start.28 = (bf16[704,128]{1,0:T(8,128)(2,1)S(1)}, bf16[704,128]{1,0:T(8,128)(2,1)S(1)}, u32[]{:S(2)}, u32[]{:S(2)}) collective-permute-start(bf16[704,128]{1,0:T(8,128)(2,1)S(1)} %get-tuple-element.57), channel_id=1, source_target_pairs={{0,32},{4,132},{8,40},{12,140},{16,48},{20,148},{24,56},{28,156},{... | collective-permute-start | bytes 540680 | tf_op jit(solution)/shard_map/ppermute | solution.py:68
  92.7 7.2 %collective-permute-start.29 = (bf16[704,128]{1,0:T(8,128)(2,1)S(1)}, bf16[704,128]{1,0:T(8,128)(2,1)S(1)}, u32[]{:S(2)}, u32[]{:S(2)}) collective-permute-start(bf16[704,128]{1,0:T(8,128)(2,1)S(1)} %get-tuple-element.58), channel_id=1, source_target_pairs={{0,48},{4,196},{8,56},{12,204},{16,0},{20,212},{24,8},{28,220},{32... | collective-permute-start | bytes 540680 | tf_op jit(solution)/shard_map/ppermute | solution.py:68
  100.6 14.9 %collective-permute-start.30 = (bf16[256,128]{1,0:T(8,128)(2,1)S(1)}, bf16[256,128]{1,0:T(8,128)(2,1)S(1)}, u32[]{:S(2)}, u32[]{:S(2)}) collective-permute-start(bf16[256,128]{1,0:T(8,128)(2,1)S(1)} %get-tuple-element.60), channel_id=1, source_target_pairs={{0,0},{4,12},{8,8},{12,4},{16,16},{20,28},{24,24},{28,20},{32,32},... | collective-permute-start | bytes 196616 | tf_op jit(solution)/shard_map/ppermute | solution.py:68
  106.1 9.4 %collective-permute-start.31 = (bf16[256,128]{1,0:T(8,128)(2,1)S(1)}, bf16[256,128]{1,0:T(8,128)(2,1)S(1)}, u32[]{:S(2)}, u32[]{:S(2)}) collective-permute-start(bf16[256,128]{1,0:T(8,128)(2,1)S(1)} %get-tuple-element.61), channel_id=1, source_target_pairs={{0,4},{4,8},{8,12},{12,0},{16,20},{20,24},{24,28},{28,16},{32,36},... | collective-permute-start | bytes 196616 | tf_op jit(solution)/shard_map/ppermute | solution.py:68
  (15 other events, 88.4 us)

commit v9 on v8

--- a/solution.py
+++ b/solution.py
@@ -122,22 +122,26 @@
     )(meta, stored)
 
 
-def pair_up_kernel(core, near, far, out):
-    first = core[0] == 0
+def own_core():
+    return lax.rem(lax.axis_index("row"), 2)
+
+
+def pair_up_kernel(near, far, out):
+    first = own_core() == 0
     out[0:ROWS] = jnp.where(first, far[...], near[...])
     out[ROWS : 2 * ROWS] = jnp.where(first, near[...], far[...])
 
 
-def pair_up(core, near, far):
+def pair_up(near, far):
     return pl.pallas_call(
         pair_up_kernel,
         out_shape=jax.ShapeDtypeStruct((2 * ROWS, B), BF16),
-        in_specs=[SMEM] + [VMEM] * 2,
+        in_specs=[VMEM] * 2,
         out_specs=VMEM,
         compiler_params=params(),
         cost_estimate=small_cost(1 << 16),
         name="pair_up",
-    )(core, near, far)
+    )(near, far)
 
 
 def place_kernel(counts, parts, *refs):
@@ -226,7 +230,7 @@
     )(*args)
 
 
-def middle_kernel(meta, own, p1, p2, p3, weight, cot, act, values, m1, m2, m3, w0):
+def middle_kernel(own, p1, p2, p3, weight, cot, act, values, m1, m2, m3, w0):
     pooled = (own[...] + p1[...].astype(F32) + p2[...].astype(F32) + p3[...].astype(F32)).astype(BF16)
     hidden = jnp.dot(pooled, weight[...], preferred_element_type=F32)
     squash = jax.nn.sigmoid(hidden)
@@ -238,7 +242,7 @@
         out[0:B] = values_t[:, :B]
         out[B:ROWS] = values_t[:, B:]
     term = lax.dot_general(pooled, slope, (((0,), (0,)), ((), ())), preferred_element_type=F32)
-    rep = meta[PLACE]
+    rep = lax.axis_index("rep")
     for q in range(4):
         piece = jnp.concatenate([term[q * 32 : (q + 1) * 32, :B], term[q * 32 : (q + 1) * 32, B:]], axis=0)
 
@@ -253,18 +257,18 @@
                 out[ROWS : ROWS + PIECE] = piece.astype(BF16)
 
 
-def middle(meta, own, pieces, weight, cot):
+def middle(own, pieces, weight, cot):
     return pl.pallas_call(
         middle_kernel,
         out_shape=[jax.ShapeDtypeStruct((2 * B, 2 * B), BF16), jax.ShapeDtypeStruct((ROWS, B), BF16)]
         + [jax.ShapeDtypeStruct((ROWS + PIECE, B), BF16)] * 3
         + [jax.ShapeDtypeStruct((PIECE, B), F32)],
-        in_specs=[SMEM] + [VMEM] * 6,
+        in_specs=[VMEM] * 6,
         out_specs=[VMEM] * 6,
         compiler_params=params(),
         cost_estimate=small_cost(1 << 16),
         name="middle_rows",
-    )(meta, own, *pieces, weight, cot)
+    )(own, *pieces, weight, cot)
 
 
 def split(total, out_ref, row):
@@ -403,8 +407,8 @@
     )(*arrays)
 
 
-def pair_kernel(meta, a, b, c, d, own, mine, other, w):
-    core = meta[PLACE + 1]
+def pair_kernel(a, b, c, d, own, mine, other, w):
+    core = own_core()
     for out, unit in ((mine, core), (other, 1 - core)):
         part = pl.ds(pl.multiple_of(unit * ROWS, ROWS), ROWS)
         total = a[part].astype(F32) + b[part].astype(F32) + c[part].astype(F32) + d[part].astype(F32)
@@ -412,46 +416,45 @@
     w[...] = (own[...] + joined(c, 2 * ROWS)) + (joined(b, 2 * ROWS) + joined(d, 2 * ROWS))
 
 
-def sum_pairs(meta, *arrays):
+def sum_pairs(*arrays):
     return pl.pallas_call(
         pair_kernel,
         out_shape=[jax.ShapeDtypeStruct((ROWS, B), BF16)] * 2 + [jax.ShapeDtypeStruct((PIECE, B), F32)],
-        in_specs=[SMEM] + [VMEM] * 5,
+        in_specs=[VMEM] * 5,
         out_specs=[VMEM] * 3,
         compiler_params=params(),
         cost_estimate=small_cost(1 << 17),
         name="sum_pairs",
-    )(meta, *arrays)
-
-
-def last_kernel(scaling, meta, far, crossed, w0, w1, w2, w3, out, weight_grad):
+    )(*arrays)
+
+
+def last_kernel(scaling, far, crossed, w0, w1, w2, w3, out, weight_grad):
     for s in range(2):
         part = slice(s * B, (s + 1) * B)
         out[part] = (far[part].astype(F32) + crossed[part].astype(F32)).T.astype(BF16)
-    rep = meta[PLACE]
+    rep = lax.axis_index("rep")
     for back, piece in enumerate((w0, w1, w2, w3)):
         rows = pl.ds(pl.multiple_of(lax.rem(rep + 4 - back, 4) * 32, 32), 32)
         weight_grad[rows, 0:B] = piece[0:32] * scaling
         weight_grad[rows, B : 2 * B] = piece[32:64] * scaling
 
 
-def last_sum(meta, scaling, *arrays):
+def last_sum(scaling, *arrays):
     return pl.pallas_call(
         functools.partial(last_kernel, scaling),
         out_shape=[jax.ShapeDtypeStruct((ROWS, B), BF16), jax.ShapeDtypeStruct((B, 2 * B), F32)],
-        in_specs=[SMEM] + [VMEM] * 6,
+        in_specs=[VMEM] * 6,
         out_specs=[VMEM] * 2,
         compiler_params=params(),
         cost_estimate=small_cost(1 << 16),
         name="last_sum",
-    )(meta, *arrays)
+    )(*arrays)
 
 
 def per_device(features, adjacency, block_list, block_counts, weight, cotangent):
     stored = adjacency[0, 0]
     r = lax.axis_index("row").astype(jnp.int32)
     rep = lax.axis_index("rep").astype(jnp.int32)
-    core = r % 2
     nodes = float(features.shape[0] * 256)
 
     order = [entry for call in FORWARD_GROUPS for part in call for entry in part]
@@ -462,12 +465,12 @@
             block_counts.reshape(-1),
             section_order(r, order, -1),
             section_order(r, back_order, 1),
-            jnp.stack([rep, core]),
+            rep.reshape(1),
         ]
     )
 
     near_unit, far_unit = cross(features, True), other_z(features)
-    pair = pair_up(core.reshape(1), near_unit, far_unit)
+    pair = pair_up(near_unit, far_unit)
     x1, x2, x3 = small_axis(pair, 1), small_axis(pair, 2), small_axis(pair, 3)
     touched = touch(meta, stored)
     (low,) = place("place_low", [[(0, 0, 2), (1, 0, 2)]], [pair, x1])
@@ -486,7 +489,7 @@
     own_part, *pieces = forward(meta, stored, 48, [far, far_s], acc, True)
 
     pieces = [turn(piece, d + 1) for d, piece in enumerate(pieces)]
-    activations, values, m1, m2, m3, w = middle(meta, own_part, pieces, weight, cotangent)
+    activations, values, m1, m2, m3, w = middle(own_part, pieces, weight, cotangent)
     messages = [turn(m1, 1), turn(m2, 2), turn(m3, 3)]
 
     bwd = functools.partial(backward, meta, stored, [values] + messages)
@@ -510,10 +513,10 @@
     l1, l3, w16_two = large_axis(l1, 1), large_axis(l3, 3), large_axis(w16, 2)
     t0, t1, t2, t3, w64 = sum_groups(g0, r1, r3, l1, l3, w16, w16_two)
     sums = [t0, small_axis(t1, 1), small_axis(t2, 2), small_axis(t3, 3)]
-    mine, other, w = sum_pairs(meta, *sums, w64)
+    mine, other, w = sum_pairs(*sums, w64)
     far, crossed = other_z(mine), cross(other, False)
     feature_grad, weight_grad = last_sum(
-        meta, nodes ** (-0.5), far, crossed, w, *[turn(w, d) for d in (1, 2, 3)]
+        nodes ** (-0.5), far, crossed, w, *[turn(w, d) for d in (1, 2, 3)]
     )
     return activations, feature_grad, weight_grad
 

time: 117 us -> 115 us (0.983)
  Pallas kernels: 21.3 us -> 19.5 us
where the time goes in v9:
time: 115 us
  starting transfers between devices  59.9 us (52%)
  waiting for transfers between devices  28.8 us (25%)
  Pallas kernels  19.5 us (17%)
  local copies, waits for them, and re-layouts  5.16 us (4%)
    ppermute x26, starting transfers between devices, row_permute(): return lax.ppermute(array, 'row', pairs)  48.3 us
    ppermute x26, waiting for transfers between devices, row_permute(): return lax.ppermute(array, 'row', pairs)  15.7 us
    ppermute x9, waiting for transfers between devices, turn(): return lax.ppermute(array, 'rep', [(q, (q + d) % 4) for q in range(4)])  13.1 us
    ppermute x9, starting transfers between devices, turn(): return lax.ppermute(array, 'rep', [(q, (q + d) % 4) for q in range(4)])  11.6 us
    pallas_call x4, Pallas kernels, backward(): pl.pallas_call(functools.partial(backward_kernel, first_section, sizes, a...  9.22 us
    pallas_call x4, Pallas kernels, forward(): pl.pallas_call(functools.partial(forward_kernel, first_section, sizes, fi...  7.12 us
    unnamed x9, local copies, waits for them, and re-layouts  4.21 us
  transfers between devices with their start and end apart: 35, of which 15 were waited for; matrix products, arithmetic and copies ran while one was open for 2% of the time, Pallas kernels for 11%

profile of v9, /device:TPU:1, one launch (start us, length us, event | category | flops | bytes accessed | tf_op | source)
XLA Modules:
  0.0 115.0 jit_solution(17453270148766663890)
XLA Ops:
  0.6 3.3 %collective-permute-start = (bf16[256,128]{1,0:T(8,128)(2,1)}, bf16[256,128]{1,0:T(8,128)(2,1)S(1)}, u32[]{:S(2)}, u32[]{:S(2)}) collective-permute-start(bf16[256,128]{1,0:T(8,128)(2,1)} %param.14), channel_id=1, source_target_pairs={{0,12},{4,0},{8,4},{12,8},{16,28},{20,16},{24,20},{28,24},{32,44},... | collective-permute-start | bytes 196616 | tf_op jit(solution)/shard_map/ppermute | solution.py:68
  3.9 7.1 %collective-permute-start.1 = (bf16[256,128]{1,0:T(8,128)(2,1)}, bf16[256,128]{1,0:T(8,128)(2,1)S(1)}, u32[]{:S(2)}, u32[]{:S(2)}) collective-permute-start(bf16[256,128]{1,0:T(8,128)(2,1)} %param.14), channel_id=1, source_target_pairs={{0,0},{4,12},{8,8},{12,4},{16,16},{20,28},{24,24},{28,20},{32,32},... | collective-permute-start | bytes 196616 | tf_op jit(solution)/shard_map/ppermute | solution.py:68
  14.3 2.6 %collective-permute-start.5 = (bf16[512,128]{1,0:T(8,128)(2,1)S(1)}, bf16[512,128]{1,0:T(8,128)(2,1)S(1)}, u32[]{:S(2)}, u32[]{:S(2)}) collective-permute-start(bf16[512,128]{1,0:T(8,128)(2,1)S(1)} %pair_up.1.refs_0_), channel_id=1, source_target_pairs={{0,32},{4,132},{8,40},{12,140},{16,48},{20,148},{24,56},{28,156},{... | collective-permute-start | bytes 393224 | tf_op jit(solution)/shard_map/ppermute | solution.py:68
  19.5 3.4 %copy-done = bf16[1,1,256,128,128]{4,3,2,1,0:T(8,128)(2,1)S(1)} copy-done((bf16[1,1,256,128,128]{4,3,2,1,0:T(8,128)(2,1)S(1)}, bf16[1,1,256,128,128]{4,3,2,1,0:T(8,128)(2,1)}, u32[]{:S(2)}) %copy-start) | copy-done | bytes 8388632
  23.6 2.6 %collective-permute-start.7 = (bf16[1024,128]{1,0:T(8,128)(2,1)S(1)}, bf16[1024,128]{1,0:T(8,128)(2,1)S(1)}, u32[]{:S(2)}, u32[]{:S(2)}) collective-permute-start(bf16[1024,128]{1,0:T(8,128)(2,1)S(1)} %place_high.1.refs_3_.refs_1_), channel_id=1, source_target_pairs={{0,192},{4,52},{8,200},{12,60},{16,208},{20,4},{24,216},{28,12},{3... | collective-permute-start | bytes 786440 | tf_op jit(solution)/shard_map/ppermute | solution.py:68
  26.4 2.5 %collective-permute-start.10 = (bf16[1024,128]{1,0:T(8,128)(2,1)S(1)}, bf16[1024,128]{1,0:T(8,128)(2,1)S(1)}, u32[]{:S(2)}, u32[]{:S(2)}) collective-permute-start(bf16[1024,128]{1,0:T(8,128)(2,1)S(1)} %place_low.1.refs_3_.refs_2_.refs_0_), channel_id=1, source_target_pairs={{0,192},{4,52},{8,200},{12,60},{16,208},{20,4},{24,216},{28,12},{3... | collective-permute-start | bytes 786440 | tf_op jit(solution)/shard_map/ppermute | solution.py:68
  29.5 3.4 %collective-permute-start.8 = (bf16[1024,128]{1,0:T(8,128)(2,1)S(1)}, bf16[1024,128]{1,0:T(8,128)(2,1)S(1)}, u32[]{:S(2)}, u32[]{:S(2)}) collective-permute-start(bf16[1024,128]{1,0:T(8,128)(2,1)S(1)} %collective-permute-done.7.refs_5_), channel_id=1, source_target_pairs={{0,192},{4,52},{8,200},{12,60},{16,208},{20,4},{24,216},{28,12},{3... | collective-permute-start | bytes 786440 | tf_op jit(solution)/shard_map/ppermute | solution.py:68
  41.2 2.5 %forward_slots.6.refs_4_ = f32[8,128,128]{2,1,0:T(8,128)S(1)} custom-call(s32[961]{0:T(1024)S(1)} %concatenate.3.meta.refs_0_, bf16[256,128,128]{2,1,0:T(8,128)(2,1)S(1)} %bitcast.6, bf16[6144,128]{1,0:T(8,128)(2,1)S(1)} %collective-permute-done.12.refs_2_, f32[8,128,128]{2,1,0:T(8,128)S(1)} %forward_slots.5.refs_2_.refs_3_), custom_call_target="tpu_custom_call" | custom-call | flops 12582912 | bytes 12582912 | tf_op jit(solution)/shard_map/forward_slots/pallas_call | solution.py:221
  43.7 1.9 %forward_slots.7 = (f32[256,128]{1,0:T(8,128)S(1)}, bf16[256,128]{1,0:T(8,128)(2,1)S(1)}, bf16[256,128]{1,0:T(8,128)(2,1)S(1)}, bf16[256,128]{1,0:T(8,128)(2,1)S(1)}) custom-call(s32[961]{0:T(1024)S(1)} %concatenate.3.meta.refs_0_, bf16[256,128,128]{2,1,0:T(8,128)(2,1)S(1)} %bitcast.7, bf16[2048,128]{1,0:T(8,128)(2,1)S(1)} %place_far.1.refs_2_, ...), custom_call_target="tpu_custom_call" | custom-call | flops 8388608 | bytes 8388608 | tf_op jit(solution)/shard_map/forward_slots/pallas_call | solution.py:221
  49.5 2.0 %collective-permute-done.13.p1 = bf16[256,128]{1,0:T(8,128)(2,1)S(1)} collective-permute-done((bf16[256,128]{1,0:T(8,128)(2,1)S(1)}, bf16[256,128]{1,0:T(8,128)(2,1)S(1)}, u32[]{:S(2)}, u32[]{:S(2)}) %collective-permute-start.13) | collective-permute-done | bytes 65568 | tf_op jit(solution)/shard_map/ppermute | solution.py:94
  51.5 2.8 %collective-permute-done.14.p2 = bf16[256,128]{1,0:T(8,128)(2,1)S(1)} collective-permute-done((bf16[256,128]{1,0:T(8,128)(2,1)S(1)}, bf16[256,128]{1,0:T(8,128)(2,1)S(1)}, u32[]{:S(2)}, u32[]{:S(2)}) %collective-permute-start.14) | collective-permute-done | bytes 65568 | tf_op jit(solution)/shard_map/ppermute | solution.py:94
  60.5 4.6 %collective-permute-done.17.refs_4_.refs_8_ = bf16[320,128]{1,0:T(8,128)(2,1)S(1)} collective-permute-done((bf16[320,128]{1,0:T(8,128)(2,1)S(1)}, bf16[320,128]{1,0:T(8,128)(2,1)S(1)}, u32[]{:S(2)}, u32[]{:S(2)}) %collective-permute-start.17) | collective-permute-done | bytes 81952 | tf_op jit(solution)/shard_map/ppermute | solution.py:94
  65.1 2.3 %backward_slots.4 = (bf16[4288,128]{1,0:T(8,128)(2,1)S(1)}, f32[64,128]{1,0:T(8,128)S(1)}) custom-call(s32[961]{0:T(1024)S(1)} %concatenate.3.meta.refs_0_, bf16[256,128,128]{2,1,0:T(8,128)(2,1)S(1)} %bitcast.8, bf16[256,128]{1,0:T(8,128)(2,1)S(1)} %get-tuple-element.39.refs_2_, bf16[320,128]{1,0:T(8,128)(2,1)S(1)} %collective-permute-done.16.refs_3_.refs_7_, ...), custom_call_target="tpu_custom_call" | custom-call | flops 8388608 | bytes 8388608 | tf_op jit(solution)/shard_map/backward_slots/pallas_call | solution.py:348
  68.1 2.3 %backward_slots.5.refs_9_ = bf16[4096,128]{1,0:T(8,128)(2,1)S(1)} custom-call(s32[961]{0:T(1024)S(1)} %concatenate.3.meta.refs_0_, bf16[256,128,128]{2,1,0:T(8,128)(2,1)S(1)} %bitcast.9, bf16[256,128]{1,0:T(8,128)(2,1)S(1)} %get-tuple-element.39.refs_2_, bf16[320,128]{1,0:T(8,128)(2,1)S(1)} %collective-permute-done.16.refs_3_.refs_7_, ...), custom_call_target="tpu_custom_call" | custom-call | flops 8388608 | bytes 8388608 | tf_op jit(solution)/shard_map/backward_slots/pallas_call | solution.py:348
  70.5 2.3 %backward_slots.6 = (bf16[2048,128]{1,0:T(8,128)(2,1)S(1)}, bf16[2048,128]{1,0:T(8,128)(2,1)S(1)}, bf16[64,128]{1,0:T(8,128)(2,1)S(1)}) custom-call(s32[961]{0:T(1024)S(1)} %concatenate.3.meta.refs_0_, bf16[256,128,128]{2,1,0:T(8,128)(2,1)S(1)} %bitcast.10, bf16[256,128]{1,0:T(8,128)(2,1)S(1)} %get-tuple-element.39.refs_2_, ...), custom_call_target="tpu_custom_call" | custom-call | flops 17179869184 | bytes 17179869184 | tf_op jit(solution)/shard_map/backward_slots/pallas_call | solution.py:348
  73.3 2.4 %collective-permute-start.22 = (bf16[2048,128]{1,0:T(8,128)(2,1)S(1)}, bf16[2048,128]{1,0:T(8,128)(2,1)S(1)}, u32[]{:S(2)}, u32[]{:S(2)}) collective-permute-start(bf16[2048,128]{1,0:T(8,128)(2,1)S(1)} %get-tuple-element.48), channel_id=1, source_target_pairs={{0,192},{4,52},{8,200},{12,60},{16,208},{20,4},{24,216},{28,12},{3... | collective-permute-start | bytes 1572872 | tf_op jit(solution)/shard_map/ppermute | solution.py:68
  75.6 3.6 %collective-permute-start.23 = (bf16[64,128]{1,0:T(8,128)(2,1)S(1)}, bf16[64,128]{1,0:T(8,128)(2,1)S(1)}, u32[]{:S(2)}, u32[]{:S(2)}) collective-permute-start(bf16[64,128]{1,0:T(8,128)(2,1)S(1)} %get-tuple-element.51.own), channel_id=1, source_target_pairs={{0,8},{4,12},{8,0},{12,4},{16,24},{20,28},{24,16},{28,20},{32,40},... | collective-permute-start | bytes 49160 | tf_op jit(solution)/shard_map/ppermute | solution.py:68
  79.3 2.2 %backward_slots.7 = (bf16[1024,128]{1,0:T(8,128)(2,1)S(1)}, bf16[1024,128]{1,0:T(8,128)(2,1)S(1)}, bf16[2048,128]{1,0:T(8,128)(2,1)S(1)}) custom-call(s32[961]{0:T(1024)S(1)} %concatenate.3.meta.refs_0_, bf16[256,128,128]{2,1,0:T(8,128)(2,1)S(1)} %bitcast.11, bf16[256,128]{1,0:T(8,128)(2,1)S(1)} %get-tuple-element.39.refs_2_, ...), custom_call_target="tpu_custom_call" | custom-call | flops 8388608 | bytes 8388608 | tf_op jit(solution)/shard_map/backward_slots/pallas_call | solution.py:348
  82.7 2.7 %collective-permute-start.25 = (bf16[1088,128]{1,0:T(8,128)(2,1)S(1)}, bf16[1088,128]{1,0:T(8,128)(2,1)S(1)}, u32[]{:S(2)}, u32[]{:S(2)}) collective-permute-start(bf16[1088,128]{1,0:T(8,128)(2,1)S(1)} %get-tuple-element.53), channel_id=1, source_target_pairs={{0,192},{4,52},{8,200},{12,60},{16,208},{20,4},{24,216},{28,12},{3... | collective-permute-start | bytes 835592 | tf_op jit(solution)/shard_map/ppermute | solution.py:68
  86.3 4.1 %collective-permute-done.26.two = bf16[64,128]{1,0:T(8,128)(2,1)S(1)} collective-permute-done((bf16[64,128]{1,0:T(8,128)(2,1)S(1)}, bf16[64,128]{1,0:T(8,128)(2,1)S(1)}, u32[]{:S(2)}, u32[]{:S(2)}) %collective-permute-start.26) | collective-permute-done | bytes 16416 | tf_op jit(solution)/shard_map/ppermute | solution.py:68
  93.6 5.1 %collective-permute-done.27.b = bf16[704,128]{1,0:T(8,128)(2,1)S(1)} collective-permute-done((bf16[704,128]{1,0:T(8,128)(2,1)S(1)}, bf16[704,128]{1,0:T(8,128)(2,1)S(1)}, u32[]{:S(2)}, u32[]{:S(2)}) %collective-permute-start.27) | collective-permute-done | bytes 180256 | tf_op jit(solution)/shard_map/ppermute | solution.py:68
  99.4 5.5 %collective-permute-start.30 = (bf16[256,128]{1,0:T(8,128)(2,1)S(1)}, bf16[256,128]{1,0:T(8,128)(2,1)S(1)}, u32[]{:S(2)}, u32[]{:S(2)}) collective-permute-start(bf16[256,128]{1,0:T(8,128)(2,1)S(1)} %get-tuple-element.60), channel_id=1, source_target_pairs={{0,0},{4,12},{8,8},{12,4},{16,16},{20,28},{24,24},{28,20},{32,32},... | collective-permute-start | bytes 196616 | tf_op jit(solution)/shard_map/ppermute | solution.py:68
  104.9 2.9 %collective-permute-start.31 = (bf16[256,128]{1,0:T(8,128)(2,1)S(1)}, bf16[256,128]{1,0:T(8,128)(2,1)S(1)}, u32[]{:S(2)}, u32[]{:S(2)}) collective-permute-start(bf16[256,128]{1,0:T(8,128)(2,1)S(1)} %get-tuple-element.61), channel_id=1, source_target_pairs={{0,4},{4,8},{8,12},{12,0},{16,20},{20,24},{24,28},{28,16},{32,36},... | collective-permute-start | bytes 196616 | tf_op jit(solution)/shard_map/ppermute | solution.py:68
  107.8 1.9 %collective-permute-start.32 = (f32[64,128]{1,0:T(8,128)S(1)}, f32[64,128]{1,0:T(8,128)S(1)}, u32[]{:S(2)}, u32[]{:S(2)}) collective-permute-start(f32[64,128]{1,0:T(8,128)S(1)} %get-tuple-element.62.w0), channel_id=1, source_target_pairs={{0,1},{1,2},{2,3},{3,0},{4,5},{5,6},{6,7},{7,4},{8,9},{9,10},{10,1... | collective-permute-start | bytes 98312 | tf_op jit(solution)/shard_map/ppermute | solution.py:94
  (77 shorter events, 37.9 us)
Async XLA Ops:
  0.6 11.5 %collective-permute-start = (bf16[256,128]{1,0:T(8,128)(2,1)}, bf16[256,128]{1,0:T(8,128)(2,1)S(1)}, u32[]{:S(2)}, u32[]{:S(2)}) collective-permute-start(bf16[256,128]{1,0:T(8,128)(2,1)} %param.14), channel_id=1, source_target_pairs={{0,12},{4,0},{8,4},{12,8},{16,28},{20,16},{24,20},{28,24},{32,44},... | collective-permute-start | bytes 196616 | tf_op jit(solution)/shard_map/ppermute | solution.py:68
  3.9 9.1 %collective-permute-start.1 = (bf16[256,128]{1,0:T(8,128)(2,1)}, bf16[256,128]{1,0:T(8,128)(2,1)S(1)}, u32[]{:S(2)}, u32[]{:S(2)}) collective-permute-start(bf16[256,128]{1,0:T(8,128)(2,1)} %param.14), channel_id=1, source_target_pairs={{0,0},{4,12},{8,8},{12,4},{16,16},{20,28},{24,24},{28,20},{32,32},... | collective-permute-start | bytes 196616 | tf_op jit(solution)/shard_map/ppermute | solution.py:68
  13.1 10.4 %collective-permute-start.2 = (bf16[512,128]{1,0:T(8,128)(2,1)S(1)}, bf16[512,128]{1,0:T(8,128)(2,1)S(1)}, u32[]{:S(2)}, u32[]{:S(2)}) collective-permute-start(bf16[512,128]{1,0:T(8,128)(2,1)S(1)} %pair_up.1.refs_0_), channel_id=1, source_target_pairs={{0,16},{4,68},{8,24},{12,76},{16,32},{20,84},{24,40},{28,92},{32,4... | collective-permute-start | bytes 393224 | tf_op jit(solution)/shard_map/ppermute | solution.py:68
  14.3 9.2 %collective-permute-start.5 = (bf16[512,128]{1,0:T(8,128)(2,1)S(1)}, bf16[512,128]{1,0:T(8,128)(2,1)S(1)}, u32[]{:S(2)}, u32[]{:S(2)}) collective-permute-start(bf16[512,128]{1,0:T(8,128)(2,1)S(1)} %pair_up.1.refs_0_), channel_id=1, source_target_pairs={{0,32},{4,132},{8,40},{12,140},{16,48},{20,148},{24,56},{28,156},{... | collective-permute-start | bytes 393224 | tf_op jit(solution)/shard_map/ppermute | solution.py:68
  17.0 6.6 %collective-permute-start.6 = (bf16[512,128]{1,0:T(8,128)(2,1)S(1)}, bf16[512,128]{1,0:T(8,128)(2,1)S(1)}, u32[]{:S(2)}, u32[]{:S(2)}) collective-permute-start(bf16[512,128]{1,0:T(8,128)(2,1)S(1)} %pair_up.1.refs_0_), channel_id=1, source_target_pairs={{0,48},{4,196},{8,56},{12,204},{16,0},{20,212},{24,8},{28,220},{32... | collective-permute-start | bytes 393224 | tf_op jit(solution)/shard_map/ppermute | solution.py:68
  26.2 6.7 %collective-permute-start.3 = (bf16[1024,128]{1,0:T(8,128)(2,1)S(1)}, bf16[1024,128]{1,0:T(8,128)(2,1)S(1)}, u32[]{:S(2)}, u32[]{:S(2)}) collective-permute-start(bf16[1024,128]{1,0:T(8,128)(2,1)S(1)} %place_low.1.refs_3_.refs_2_.refs_0_), channel_id=1, source_target_pairs={{0,64},{4,20},{8,72},{12,28},{16,80},{20,36},{24,88},{28,44},{32,9... | collective-permute-start | bytes 786440 | tf_op jit(solution)/shard_map/ppermute | solution.py:68
  26.2 9.5 %collective-permute-start.9 = (bf16[1024,128]{1,0:T(8,128)(2,1)S(1)}, bf16[1024,128]{1,0:T(8,128)(2,1)S(1)}, u32[]{:S(2)}, u32[]{:S(2)}) collective-permute-start(bf16[1024,128]{1,0:T(8,128)(2,1)S(1)} %place_high.1.refs_3_.refs_1_), channel_id=1, source_target_pairs={{0,64},{4,20},{8,72},{12,28},{16,80},{20,36},{24,88},{28,44},{32,9... | collective-permute-start | bytes 786440 | tf_op jit(solution)/shard_map/ppermute | solution.py:68
  26.4 9.3 %collective-permute-start.10 = (bf16[1024,128]{1,0:T(8,128)(2,1)S(1)}, bf16[1024,128]{1,0:T(8,128)(2,1)S(1)}, u32[]{:S(2)}, u32[]{:S(2)}) collective-permute-start(bf16[1024,128]{1,0:T(8,128)(2,1)S(1)} %place_low.1.refs_3_.refs_2_.refs_0_), channel_id=1, source_target_pairs={{0,192},{4,52},{8,200},{12,60},{16,208},{20,4},{24,216},{28,12},{3... | collective-permute-start | bytes 786440 | tf_op jit(solution)/shard_map/ppermute | solution.py:68
  29.5 8.5 %collective-permute-start.8 = (bf16[1024,128]{1,0:T(8,128)(2,1)S(1)}, bf16[1024,128]{1,0:T(8,128)(2,1)S(1)}, u32[]{:S(2)}, u32[]{:S(2)}) collective-permute-start(bf16[1024,128]{1,0:T(8,128)(2,1)S(1)} %collective-permute-done.7.refs_5_), channel_id=1, source_target_pairs={{0,192},{4,52},{8,200},{12,60},{16,208},{20,4},{24,216},{28,12},{3... | collective-permute-start | bytes 786440 | tf_op jit(solution)/shard_map/ppermute | solution.py:68
  32.9 6.7 %collective-permute-start.4 = (bf16[1024,128]{1,0:T(8,128)(2,1)S(1)}, bf16[1024,128]{1,0:T(8,128)(2,1)S(1)}, u32[]{:S(2)}, u32[]{:S(2)}) collective-permute-start(bf16[1024,128]{1,0:T(8,128)(2,1)S(1)} %collective-permute-done.3.refs_2_), channel_id=1, source_target_pairs={{0,64},{4,20},{8,72},{12,28},{16,80},{20,36},{24,88},{28,44},{32,9... | collective-permute-start | bytes 786440 | tf_op jit(solution)/shard_map/ppermute | solution.py:68
  46.7 7.6 %collective-permute-start.14 = (bf16[256,128]{1,0:T(8,128)(2,1)S(1)}, bf16[256,128]{1,0:T(8,128)(2,1)S(1)}, u32[]{:S(2)}, u32[]{:S(2)}) collective-permute-start(bf16[256,128]{1,0:T(8,128)(2,1)S(1)} %get-tuple-element.36), channel_id=1, source_target_pairs={{0,2},{1,3},{2,0},{3,1},{4,6},{5,7},{6,4},{7,5},{8,10},{9,11},{10,... | collective-permute-start | bytes 196616 | tf_op jit(solution)/shard_map/ppermute | solution.py:94
  57.1 8.0 %collective-permute-start.17 = (bf16[320,128]{1,0:T(8,128)(2,1)S(1)}, bf16[320,128]{1,0:T(8,128)(2,1)S(1)}, u32[]{:S(2)}, u32[]{:S(2)}) collective-permute-start(bf16[320,128]{1,0:T(8,128)(2,1)S(1)} %get-tuple-element.41), channel_id=1, source_target_pairs={{0,2},{1,3},{2,0},{3,1},{4,6},{5,7},{6,4},{7,5},{8,10},{9,11},{10,... | collective-permute-start | bytes 245768 | tf_op jit(solution)/shard_map/ppermute | solution.py:94
  58.1 7.0 %collective-permute-start.18 = (bf16[320,128]{1,0:T(8,128)(2,1)S(1)}, bf16[320,128]{1,0:T(8,128)(2,1)S(1)}, u32[]{:S(2)}, u32[]{:S(2)}) collective-permute-start(bf16[320,128]{1,0:T(8,128)(2,1)S(1)} %get-tuple-element.42), channel_id=1, source_target_pairs={{0,3},{1,0},{2,1},{3,2},{4,7},{5,4},{6,5},{7,6},{8,11},{9,8},{10,9... | collective-permute-start | bytes 245768 | tf_op jit(solution)/shard_map/ppermute | solution.py:94
  70.4 8.8 %collective-permute-start.19 = (bf16[4096,128]{1,0:T(8,128)(2,1)S(1)}, bf16[4096,128]{1,0:T(8,128)(2,1)S(1)}, u32[]{:S(2)}, u32[]{:S(2)}) collective-permute-start(bf16[4096,128]{1,0:T(8,128)(2,1)S(1)} %backward_slots.5.refs_9_), channel_id=1, source_target_pairs={{0,4},{4,0},{8,12},{12,8},{16,20},{20,16},{24,28},{28,24},{32,36},... | collective-permute-start | bytes 3145736 | tf_op jit(solution)/shard_map/ppermute | solution.py:68
  72.9 9.6 %collective-permute-start.21 = (bf16[2048,128]{1,0:T(8,128)(2,1)S(1)}, bf16[2048,128]{1,0:T(8,128)(2,1)S(1)}, u32[]{:S(2)}, u32[]{:S(2)}) collective-permute-start(bf16[2048,128]{1,0:T(8,128)(2,1)S(1)} %get-tuple-element.46.refs_7_), channel_id=1, source_target_pairs={{0,64},{4,20},{8,72},{12,28},{16,80},{20,36},{24,88},{28,44},{32,9... | collective-permute-start | bytes 1572872 | tf_op jit(solution)/shard_map/ppermute | solution.py:68
  73.3 9.2 %collective-permute-start.22 = (bf16[2048,128]{1,0:T(8,128)(2,1)S(1)}, bf16[2048,128]{1,0:T(8,128)(2,1)S(1)}, u32[]{:S(2)}, u32[]{:S(2)}) collective-permute-start(bf16[2048,128]{1,0:T(8,128)(2,1)S(1)} %get-tuple-element.48), channel_id=1, source_target_pairs={{0,192},{4,52},{8,200},{12,60},{16,208},{20,4},{24,216},{28,12},{3... | collective-permute-start | bytes 1572872 | tf_op jit(solution)/shard_map/ppermute | solution.py:68
  75.6 6.5 %collective-permute-start.23 = (bf16[64,128]{1,0:T(8,128)(2,1)S(1)}, bf16[64,128]{1,0:T(8,128)(2,1)S(1)}, u32[]{:S(2)}, u32[]{:S(2)}) collective-permute-start(bf16[64,128]{1,0:T(8,128)(2,1)S(1)} %get-tuple-element.51.own), channel_id=1, source_target_pairs={{0,8},{4,12},{8,0},{12,4},{16,24},{20,28},{24,16},{28,20},{32,40},... | collective-permute-start | bytes 49160 | tf_op jit(solution)/shard_map/ppermute | solution.py:68
  82.6 7.7 %collective-permute-start.24 = (bf16[1088,128]{1,0:T(8,128)(2,1)S(1)}, bf16[1088,128]{1,0:T(8,128)(2,1)S(1)}, u32[]{:S(2)}, u32[]{:S(2)}) collective-permute-start(bf16[1088,128]{1,0:T(8,128)(2,1)S(1)} %get-tuple-element.52), channel_id=1, source_target_pairs={{0,64},{4,20},{8,72},{12,28},{16,80},{20,36},{24,88},{28,44},{32,9... | collective-permute-start | bytes 835592 | tf_op jit(solution)/shard_map/ppermute | solution.py:68
  82.7 7.7 %collective-permute-start.25 = (bf16[1088,128]{1,0:T(8,128)(2,1)S(1)}, bf16[1088,128]{1,0:T(8,128)(2,1)S(1)}, u32[]{:S(2)}, u32[]{:S(2)}) collective-permute-start(bf16[1088,128]{1,0:T(8,128)(2,1)S(1)} %get-tuple-element.53), channel_id=1, source_target_pairs={{0,192},{4,52},{8,200},{12,60},{16,208},{20,4},{24,216},{28,12},{3... | collective-permute-start | bytes 835592 | tf_op jit(solution)/shard_map/ppermute | solution.py:68
  90.6 8.1 %collective-permute-start.27 = (bf16[704,128]{1,0:T(8,128)(2,1)S(1)}, bf16[704,128]{1,0:T(8,128)(2,1)S(1)}, u32[]{:S(2)}, u32[]{:S(2)}) collective-permute-start(bf16[704,128]{1,0:T(8,128)(2,1)S(1)} %get-tuple-element.56), channel_id=1, source_target_pairs={{0,16},{4,68},{8,24},{12,76},{16,32},{20,84},{24,40},{28,92},{32,4... | collective-permute-start | bytes 540680 | tf_op jit(solution)/shard_map/ppermute | solution.py:68
  90.9 7.8 %collective-permute-start.28 = (bf16[704,128]{1,0:T(8,128)(2,1)S(1)}, bf16[704,128]{1,0:T(8,128)(2,1)S(1)}, u32[]{:S(2)}, u32[]{:S(2)}) collective-permute-start(bf16[704,128]{1,0:T(8,128)(2,1)S(1)} %get-tuple-element.57), channel_id=1, source_target_pairs={{0,32},{4,132},{8,40},{12,140},{16,48},{20,148},{24,56},{28,156},{... | collective-permute-start | bytes 540680 | tf_op jit(solution)/shard_map/ppermute | solution.py:68
  92.1 7.2 %collective-permute-start.29 = (bf16[704,128]{1,0:T(8,128)(2,1)S(1)}, bf16[704,128]{1,0:T(8,128)(2,1)S(1)}, u32[]{:S(2)}, u32[]{:S(2)}) collective-permute-start(bf16[704,128]{1,0:T(8,128)(2,1)S(1)} %get-tuple-element.58), channel_id=1, source_target_pairs={{0,48},{4,196},{8,56},{12,204},{16,0},{20,212},{24,8},{28,220},{32... | collective-permute-start | bytes 540680 | tf_op jit(solution)/shard_map/ppermute | solution.py:68
  99.4 14.9 %collective-permute-start.30 = (bf16[256,128]{1,0:T(8,128)(2,1)S(1)}, bf16[256,128]{1,0:T(8,128)(2,1)S(1)}, u32[]{:S(2)}, u32[]{:S(2)}) collective-permute-start(bf16[256,128]{1,0:T(8,128)(2,1)S(1)} %get-tuple-element.60), channel_id=1, source_target_pairs={{0,0},{4,12},{8,8},{12,4},{16,16},{20,28},{24,24},{28,20},{32,32},... | collective-permute-start | bytes 196616 | tf_op jit(solution)/shard_map/ppermute | solution.py:68
  104.9 9.4 %collective-permute-start.31 = (bf16[256,128]{1,0:T(8,128)(2,1)S(1)}, bf16[256,128]{1,0:T(8,128)(2,1)S(1)}, u32[]{:S(2)}, u32[]{:S(2)}) collective-permute-start(bf16[256,128]{1,0:T(8,128)(2,1)S(1)} %get-tuple-element.61), channel_id=1, source_target_pairs={{0,4},{4,8},{8,12},{12,0},{16,20},{20,24},{24,28},{28,16},{32,36},... | collective-permute-start | bytes 196616 | tf_op jit(solution)/shard_map/ppermute | solution.py:68
  (15 other events, 88.3 us)

commit v10 on v9

--- a/solution.py
+++ b/solution.py
@@ -17,6 +17,7 @@
 SPLIT = 3 * PIECE
 COST = B * B * 8
 LONG = 1 << 40
+TURNS = (2, 1, 3)
 F32 = jnp.float32
 BF16 = jnp.bfloat16
 VMEM = pl.BlockSpec(memory_space=pltpu.VMEM)
@@ -304,9 +305,9 @@
     extra, refs = refs[:extras], refs[extras:]
     out_refs, extra_outs, values = refs[: len(sizes)], refs[len(sizes) : -1], refs[-1]
     rep = meta[PLACE]
-    for d in range(4):
+    for d, value_ref in zip((0, *TURNS), value_refs):
         for b in range(2):
-            values[lax.rem(rep + 4 - d, 4) * 2 + b] = value_refs[d][b * B : (b + 1) * B]
+            values[lax.rem(rep + 4 - d, 4) * 2 + b] = value_ref[b * B : (b + 1) * B]
     values[BROWS] = jnp.zeros((B, B), BF16)
 
     begin = 0
@@ -413,7 +414,7 @@
         part = pl.ds(pl.multiple_of(unit * ROWS, ROWS), ROWS)
         total = a[part].astype(F32) + b[part].astype(F32) + c[part].astype(F32) + d[part].astype(F32)
         out[...] = total.astype(BF16)
-    w[...] = (own[...] + joined(c, 2 * ROWS)) + (joined(b, 2 * ROWS) + joined(d, 2 * ROWS))
+    w[...] = (own[...] + joined(b, 2 * ROWS)) + (joined(c, 2 * ROWS) + joined(d, 2 * ROWS))
 
 
 def sum_pairs(*arrays):
@@ -433,7 +434,7 @@
         part = slice(s * B, (s + 1) * B)
         out[part] = (far[part].astype(F32) + crossed[part].astype(F32)).T.astype(BF16)
     rep = lax.axis_index("rep")
-    for back, piece in enumerate((w0, w1, w2, w3)):
+    for back, piece in zip((0, *TURNS), (w0, w1, w2, w3)):
         rows = pl.ds(pl.multiple_of(lax.rem(rep + 4 - back, 4) * 32, 32), 32)
         weight_grad[rows, 0:B] = piece[0:32] * scaling
         weight_grad[rows, B : 2 * B] = piece[32:64] * scaling
@@ -471,7 +472,7 @@
 
     near_unit, far_unit = cross(features, True), other_z(features)
     pair = pair_up(near_unit, far_unit)
-    x1, x2, x3 = small_axis(pair, 1), small_axis(pair, 2), small_axis(pair, 3)
+    x2, x1, x3 = small_axis(pair, 2), small_axis(pair, 1), small_axis(pair, 3)
     touched = touch(meta, stored)
     (low,) = place("place_low", [[(0, 0, 2), (1, 0, 2)]], [pair, x1])
     n1_low, n3_low = large_axis(low, 1), large_axis(low, 3)
@@ -488,9 +489,9 @@
     (acc,) = forward(meta, stored, 24, [near_s], acc, False)
     own_part, *pieces = forward(meta, stored, 48, [far, far_s], acc, True)
 
-    pieces = [turn(piece, d + 1) for d, piece in enumerate(pieces)]
+    pieces = [turn(pieces[d - 1], d) for d in TURNS]
     activations, values, m1, m2, m3, w = middle(own_part, pieces, weight, cotangent)
-    messages = [turn(m1, 1), turn(m2, 2), turn(m3, 3)]
+    messages = [turn((m1, m2, m3)[d - 1], d) for d in TURNS]
 
     bwd = functools.partial(backward, meta, stored, [values] + messages)
     first_b, w4 = bwd(0, (16,), extra=[w] + messages, finish=gather_terms, tails=(SPLIT,), extra_out=[w])
@@ -512,11 +513,11 @@
     l1, l3, w16 = add_late(l1, l3, r1, r3, w8, w8_z)
     l1, l3, w16_two = large_axis(l1, 1), large_axis(l3, 3), large_axis(w16, 2)
     t0, t1, t2, t3, w64 = sum_groups(g0, r1, r3, l1, l3, w16, w16_two)
-    sums = [t0, small_axis(t1, 1), small_axis(t2, 2), small_axis(t3, 3)]
+    sums = [t0, small_axis(t2, 2), small_axis(t1, 1), small_axis(t3, 3)]
     mine, other, w = sum_pairs(*sums, w64)
     far, crossed = other_z(mine), cross(other, False)
     feature_grad, weight_grad = last_sum(
-        nodes ** (-0.5), far, crossed, w, *[turn(w, d) for d in (1, 2, 3)]
+        nodes ** (-0.5), far, crossed, w, *[turn(w, d) for d in TURNS]
     )
     return activations, feature_grad, weight_grad
 

time: 115 us -> 113 us (0.983)
  waiting for transfers between devices: 28.8 us -> 22 us
  starting transfers between devices: 59.9 us -> 64.7 us
    ppermute x9, waiting for transfers between devices: 13.1 us -> 7.18 us  [turn(): return lax.ppermute(array, 'rep', [(q, (q + d) % 4) for q in range(4)])]
    ppermute x26, starting transfers between devices: 48.3 us -> 51.4 us  [row_permute(): return lax.ppermute(array, 'row', pairs)]
    ppermute x9, starting transfers between devices: 11.6 us -> 13.3 us  [turn(): return lax.ppermute(array, 'rep', [(q, (q + d) % 4) for q in range(4)])]
  transfers between devices with their start and end apart: 35 -> 35, of which waited for: 15 -> 13; matrix products, arithmetic and copies ran while one was open for 2% -> 2% of each run, Pallas kernels for 11% -> 11%
where the time goes in v10:
time: 113 us
  starting transfers between devices  64.7 us (57%)
  waiting for transfers between devices  22 us (19%)
  Pallas kernels  19.5 us (17%)
  local copies, waits for them, and re-layouts  5.16 us (5%)
    ppermute x26, starting transfers between devices, row_permute(): return lax.ppermute(array, 'row', pairs)  51.4 us
    ppermute x26, waiting for transfers between devices, row_permute(): return lax.ppermute(array, 'row', pairs)  14.8 us
    ppermute x9, starting transfers between devices, turn(): return lax.ppermute(array, 'rep', [(q, (q + d) % 4) for q in range(4)])  13.3 us
    pallas_call x4, Pallas kernels, backward(): pl.pallas_call(functools.partial(backward_kernel, first_section, sizes, a...  9.23 us
    ppermute x9, waiting for transfers between devices, turn(): return lax.ppermute(array, 'rep', [(q, (q + d) % 4) for q in range(4)])  7.18 us
    pallas_call x4, Pallas kernels, forward(): pl.pallas_call(functools.partial(forward_kernel, first_section, sizes, fi...  7.12 us
    unnamed x9, local copies, waits for them, and re-layouts  4.21 us
  transfers between devices with their start and end apart: 35, of which 13 were waited for; matrix products, arithmetic and copies ran while one was open for 2% of the time, Pallas kernels for 11%

profile of v10, /device:TPU:1, one launch (start us, length us, event | category | flops | bytes accessed | tf_op | source)
XLA Modules:
  0.0 113.1 jit_solution(1537145500356311874)
XLA Ops:
  0.6 3.3 %collective-permute-start = (bf16[256,128]{1,0:T(8,128)(2,1)}, bf16[256,128]{1,0:T(8,128)(2,1)S(1)}, u32[]{:S(2)}, u32[]{:S(2)}) collective-permute-start(bf16[256,128]{1,0:T(8,128)(2,1)} %param.14), channel_id=1, source_target_pairs={{0,12},{4,0},{8,4},{12,8},{16,28},{20,16},{24,20},{28,24},{32,44},... | collective-permute-start | bytes 196616 | tf_op jit(solution)/shard_map/ppermute | solution.py:69
  3.9 7.1 %collective-permute-start.1 = (bf16[256,128]{1,0:T(8,128)(2,1)}, bf16[256,128]{1,0:T(8,128)(2,1)S(1)}, u32[]{:S(2)}, u32[]{:S(2)}) collective-permute-start(bf16[256,128]{1,0:T(8,128)(2,1)} %param.14), channel_id=1, source_target_pairs={{0,0},{4,12},{8,8},{12,4},{16,16},{20,28},{24,24},{28,20},{32,32},... | collective-permute-start | bytes 196616 | tf_op jit(solution)/shard_map/ppermute | solution.py:69
  14.3 2.6 %collective-permute-start.5 = (bf16[512,128]{1,0:T(8,128)(2,1)S(1)}, bf16[512,128]{1,0:T(8,128)(2,1)S(1)}, u32[]{:S(2)}, u32[]{:S(2)}) collective-permute-start(bf16[512,128]{1,0:T(8,128)(2,1)S(1)} %pair_up.1.refs_0_), channel_id=1, source_target_pairs={{0,32},{4,132},{8,40},{12,140},{16,48},{20,148},{24,56},{28,156},{... | collective-permute-start | bytes 393224 | tf_op jit(solution)/shard_map/ppermute | solution.py:69
  19.5 3.4 %copy-done = bf16[1,1,256,128,128]{4,3,2,1,0:T(8,128)(2,1)S(1)} copy-done((bf16[1,1,256,128,128]{4,3,2,1,0:T(8,128)(2,1)S(1)}, bf16[1,1,256,128,128]{4,3,2,1,0:T(8,128)(2,1)}, u32[]{:S(2)}) %copy-start) | copy-done | bytes 8388632
  23.6 2.6 %collective-permute-start.7 = (bf16[1024,128]{1,0:T(8,128)(2,1)S(1)}, bf16[1024,128]{1,0:T(8,128)(2,1)S(1)}, u32[]{:S(2)}, u32[]{:S(2)}) collective-permute-start(bf16[1024,128]{1,0:T(8,128)(2,1)S(1)} %place_high.1.refs_3_.refs_1_), channel_id=1, source_target_pairs={{0,192},{4,52},{8,200},{12,60},{16,208},{20,4},{24,216},{28,12},{3... | collective-permute-start | bytes 786440 | tf_op jit(solution)/shard_map/ppermute | solution.py:69
  26.4 2.5 %collective-permute-start.10 = (bf16[1024,128]{1,0:T(8,128)(2,1)S(1)}, bf16[1024,128]{1,0:T(8,128)(2,1)S(1)}, u32[]{:S(2)}, u32[]{:S(2)}) collective-permute-start(bf16[1024,128]{1,0:T(8,128)(2,1)S(1)} %place_low.1.refs_3_.refs_2_.refs_0_), channel_id=1, source_target_pairs={{0,192},{4,52},{8,200},{12,60},{16,208},{20,4},{24,216},{28,12},{3... | collective-permute-start | bytes 786440 | tf_op jit(solution)/shard_map/ppermute | solution.py:69
  29.5 3.4 %collective-permute-start.8 = (bf16[1024,128]{1,0:T(8,128)(2,1)S(1)}, bf16[1024,128]{1,0:T(8,128)(2,1)S(1)}, u32[]{:S(2)}, u32[]{:S(2)}) collective-permute-start(bf16[1024,128]{1,0:T(8,128)(2,1)S(1)} %collective-permute-done.7.refs_5_), channel_id=1, source_target_pairs={{0,192},{4,52},{8,200},{12,60},{16,208},{20,4},{24,216},{28,12},{3... | collective-permute-start | bytes 786440 | tf_op jit(solution)/shard_map/ppermute | solution.py:69
  41.2 2.5 %forward_slots.6.refs_4_ = f32[8,128,128]{2,1,0:T(8,128)S(1)} custom-call(s32[961]{0:T(1024)S(1)} %concatenate.3.meta.refs_0_, bf16[256,128,128]{2,1,0:T(8,128)(2,1)S(1)} %bitcast.6, bf16[6144,128]{1,0:T(8,128)(2,1)S(1)} %collective-permute-done.12.refs_2_, f32[8,128,128]{2,1,0:T(8,128)S(1)} %forward_slots.5.refs_2_.refs_3_), custom_call_target="tpu_custom_call" | custom-call | flops 12582912 | bytes 12582912 | tf_op jit(solution)/shard_map/forward_slots/pallas_call | solution.py:222
  47.9 2.5 %collective-permute-start.15 = (bf16[256,128]{1,0:T(8,128)(2,1)S(1)}, bf16[256,128]{1,0:T(8,128)(2,1)S(1)}, u32[]{:S(2)}, u32[]{:S(2)}) collective-permute-start(bf16[256,128]{1,0:T(8,128)(2,1)S(1)} %get-tuple-element.37), channel_id=1, source_target_pairs={{0,3},{1,0},{2,1},{3,2},{4,7},{5,4},{6,5},{7,6},{8,11},{9,8},{10,9... | collective-permute-start | bytes 196616 | tf_op jit(solution)/shard_map/ppermute | solution.py:95
  50.4 2.5 %collective-permute-done.13.p1 = bf16[256,128]{1,0:T(8,128)(2,1)S(1)} collective-permute-done((bf16[256,128]{1,0:T(8,128)(2,1)S(1)}, bf16[256,128]{1,0:T(8,128)(2,1)S(1)}, u32[]{:S(2)}, u32[]{:S(2)}) %collective-permute-start.13) | collective-permute-done | bytes 65568 | tf_op jit(solution)/shard_map/ppermute | solution.py:95
  58.5 3.0 %collective-permute-done.17.refs_4_.refs_8_ = bf16[320,128]{1,0:T(8,128)(2,1)S(1)} collective-permute-done((bf16[320,128]{1,0:T(8,128)(2,1)S(1)}, bf16[320,128]{1,0:T(8,128)(2,1)S(1)}, u32[]{:S(2)}, u32[]{:S(2)}) %collective-permute-start.17) | collective-permute-done | bytes 81952 | tf_op jit(solution)/shard_map/ppermute | solution.py:95
  61.5 2.3 %backward_slots.4 = (bf16[4288,128]{1,0:T(8,128)(2,1)S(1)}, f32[64,128]{1,0:T(8,128)S(1)}) custom-call(s32[961]{0:T(1024)S(1)} %concatenate.3.meta.refs_0_, bf16[256,128,128]{2,1,0:T(8,128)(2,1)S(1)} %bitcast.8, bf16[256,128]{1,0:T(8,128)(2,1)S(1)} %get-tuple-element.39.refs_2_, bf16[320,128]{1,0:T(8,128)(2,1)S(1)} %collective-permute-done.16.refs_3_.refs_7_, ...), custom_call_target="tpu_custom_call" | custom-call | flops 8388608 | bytes 8388608 | tf_op jit(solution)/shard_map/backward_slots/pallas_call | solution.py:349
  63.9 3.7 %collective-permute-start.20 = (bf16[4288,128]{1,0:T(8,128)(2,1)S(1)}, bf16[4288,128]{1,0:T(8,128)(2,1)S(1)}, u32[]{:S(2)}, u32[]{:S(2)}) collective-permute-start(bf16[4288,128]{1,0:T(8,128)(2,1)S(1)} %get-tuple-element.44.refs_6_), channel_id=1, source_target_pairs={{0,4},{4,0},{8,12},{12,8},{16,20},{20,16},{24,28},{28,24},{32,36},... | collective-permute-start | bytes 3293192 | tf_op jit(solution)/shard_map/ppermute | solution.py:69
  67.6 2.3 %backward_slots.5.refs_9_ = bf16[4096,128]{1,0:T(8,128)(2,1)S(1)} custom-call(s32[961]{0:T(1024)S(1)} %concatenate.3.meta.refs_0_, bf16[256,128,128]{2,1,0:T(8,128)(2,1)S(1)} %bitcast.9, bf16[256,128]{1,0:T(8,128)(2,1)S(1)} %get-tuple-element.39.refs_2_, bf16[320,128]{1,0:T(8,128)(2,1)S(1)} %collective-permute-done.16.refs_3_.refs_7_, ...), custom_call_target="tpu_custom_call" | custom-call | flops 8388608 | bytes 8388608 | tf_op jit(solution)/shard_map/backward_slots/pallas_call | solution.py:349
  70.1 2.3 %backward_slots.6 = (bf16[2048,128]{1,0:T(8,128)(2,1)S(1)}, bf16[2048,128]{1,0:T(8,128)(2,1)S(1)}, bf16[64,128]{1,0:T(8,128)(2,1)S(1)}) custom-call(s32[961]{0:T(1024)S(1)} %concatenate.3.meta.refs_0_, bf16[256,128,128]{2,1,0:T(8,128)(2,1)S(1)} %bitcast.10, bf16[256,128]{1,0:T(8,128)(2,1)S(1)} %get-tuple-element.39.refs_2_, ...), custom_call_target="tpu_custom_call" | custom-call | flops 17179869184 | bytes 17179869184 | tf_op jit(solution)/shard_map/backward_slots/pallas_call | solution.py:349
  72.8 2.4 %collective-permute-start.22 = (bf16[2048,128]{1,0:T(8,128)(2,1)S(1)}, bf16[2048,128]{1,0:T(8,128)(2,1)S(1)}, u32[]{:S(2)}, u32[]{:S(2)}) collective-permute-start(bf16[2048,128]{1,0:T(8,128)(2,1)S(1)} %get-tuple-element.48), channel_id=1, source_target_pairs={{0,192},{4,52},{8,200},{12,60},{16,208},{20,4},{24,216},{28,12},{3... | collective-permute-start | bytes 1572872 | tf_op jit(solution)/shard_map/ppermute | solution.py:69
  75.2 3.8 %collective-permute-start.23 = (bf16[64,128]{1,0:T(8,128)(2,1)S(1)}, bf16[64,128]{1,0:T(8,128)(2,1)S(1)}, u32[]{:S(2)}, u32[]{:S(2)}) collective-permute-start(bf16[64,128]{1,0:T(8,128)(2,1)S(1)} %get-tuple-element.51.own), channel_id=1, source_target_pairs={{0,8},{4,12},{8,0},{12,4},{16,24},{20,28},{24,16},{28,20},{32,40},... | collective-permute-start | bytes 49160 | tf_op jit(solution)/shard_map/ppermute | solution.py:69
  79.0 2.2 %backward_slots.7 = (bf16[1024,128]{1,0:T(8,128)(2,1)S(1)}, bf16[1024,128]{1,0:T(8,128)(2,1)S(1)}, bf16[2048,128]{1,0:T(8,128)(2,1)S(1)}) custom-call(s32[961]{0:T(1024)S(1)} %concatenate.3.meta.refs_0_, bf16[256,128,128]{2,1,0:T(8,128)(2,1)S(1)} %bitcast.11, bf16[256,128]{1,0:T(8,128)(2,1)S(1)} %get-tuple-element.39.refs_2_, ...), custom_call_target="tpu_custom_call" | custom-call | flops 8388608 | bytes 8388608 | tf_op jit(solution)/shard_map/backward_slots/pallas_call | solution.py:349
  82.2 2.7 %collective-permute-start.25 = (bf16[1088,128]{1,0:T(8,128)(2,1)S(1)}, bf16[1088,128]{1,0:T(8,128)(2,1)S(1)}, u32[]{:S(2)}, u32[]{:S(2)}) collective-permute-start(bf16[1088,128]{1,0:T(8,128)(2,1)S(1)} %get-tuple-element.53), channel_id=1, source_target_pairs={{0,192},{4,52},{8,200},{12,60},{16,208},{20,4},{24,216},{28,12},{3... | collective-permute-start | bytes 835592 | tf_op jit(solution)/shard_map/ppermute | solution.py:69
  85.8 4.1 %collective-permute-done.26.two = bf16[64,128]{1,0:T(8,128)(2,1)S(1)} collective-permute-done((bf16[64,128]{1,0:T(8,128)(2,1)S(1)}, bf16[64,128]{1,0:T(8,128)(2,1)S(1)}, u32[]{:S(2)}, u32[]{:S(2)}) %collective-permute-start.26) | collective-permute-done | bytes 16416 | tf_op jit(solution)/shard_map/ppermute | solution.py:69
  93.0 3.2 %collective-permute-done.27.b = bf16[704,128]{1,0:T(8,128)(2,1)S(1)} collective-permute-done((bf16[704,128]{1,0:T(8,128)(2,1)S(1)}, bf16[704,128]{1,0:T(8,128)(2,1)S(1)}, u32[]{:S(2)}, u32[]{:S(2)}) %collective-permute-start.27) | collective-permute-done | bytes 180256 | tf_op jit(solution)/shard_map/ppermute | solution.py:69
  98.2 5.9 %collective-permute-start.30 = (bf16[256,128]{1,0:T(8,128)(2,1)S(1)}, bf16[256,128]{1,0:T(8,128)(2,1)S(1)}, u32[]{:S(2)}, u32[]{:S(2)}) collective-permute-start(bf16[256,128]{1,0:T(8,128)(2,1)S(1)} %get-tuple-element.60), channel_id=1, source_target_pairs={{0,0},{4,12},{8,8},{12,4},{16,16},{20,28},{24,24},{28,20},{32,32},... | collective-permute-start | bytes 196616 | tf_op jit(solution)/shard_map/ppermute | solution.py:69
  104.1 2.4 %collective-permute-start.31 = (bf16[256,128]{1,0:T(8,128)(2,1)S(1)}, bf16[256,128]{1,0:T(8,128)(2,1)S(1)}, u32[]{:S(2)}, u32[]{:S(2)}) collective-permute-start(bf16[256,128]{1,0:T(8,128)(2,1)S(1)} %get-tuple-element.61), channel_id=1, source_target_pairs={{0,4},{4,8},{8,12},{12,0},{16,20},{20,24},{24,28},{28,16},{32,36},... | collective-permute-start | bytes 196616 | tf_op jit(solution)/shard_map/ppermute | solution.py:69
  108.7 2.1 %collective-permute-start.34 = (f32[64,128]{1,0:T(8,128)S(1)}, f32[64,128]{1,0:T(8,128)S(1)}, u32[]{:S(2)}, u32[]{:S(2)}) collective-permute-start(f32[64,128]{1,0:T(8,128)S(1)} %get-tuple-element.62.w0), channel_id=1, source_target_pairs={{0,3},{1,0},{2,1},{3,2},{4,7},{5,4},{6,5},{7,6},{8,11},{9,8},{10,9... | collective-permute-start | bytes 98312 | tf_op jit(solution)/shard_map/ppermute | solution.py:95
  (77 shorter events, 37.1 us)
Async XLA Ops:
  0.6 11.5 %collective-permute-start = (bf16[256,128]{1,0:T(8,128)(2,1)}, bf16[256,128]{1,0:T(8,128)(2,1)S(1)}, u32[]{:S(2)}, u32[]{:S(2)}) collective-permute-start(bf16[256,128]{1,0:T(8,128)(2,1)} %param.14), channel_id=1, source_target_pairs={{0,12},{4,0},{8,4},{12,8},{16,28},{20,16},{24,20},{28,24},{32,44},... | collective-permute-start | bytes 196616 | tf_op jit(solution)/shard_map/ppermute | solution.py:69
  3.9 9.1 %collective-permute-start.1 = (bf16[256,128]{1,0:T(8,128)(2,1)}, bf16[256,128]{1,0:T(8,128)(2,1)S(1)}, u32[]{:S(2)}, u32[]{:S(2)}) collective-permute-start(bf16[256,128]{1,0:T(8,128)(2,1)} %param.14), channel_id=1, source_target_pairs={{0,0},{4,12},{8,8},{12,4},{16,16},{20,28},{24,24},{28,20},{32,32},... | collective-permute-start | bytes 196616 | tf_op jit(solution)/shard_map/ppermute | solution.py:69
  13.1 10.4 %collective-permute-start.2 = (bf16[512,128]{1,0:T(8,128)(2,1)S(1)}, bf16[512,128]{1,0:T(8,128)(2,1)S(1)}, u32[]{:S(2)}, u32[]{:S(2)}) collective-permute-start(bf16[512,128]{1,0:T(8,128)(2,1)S(1)} %pair_up.1.refs_0_), channel_id=1, source_target_pairs={{0,16},{4,68},{8,24},{12,76},{16,32},{20,84},{24,40},{28,92},{32,4... | collective-permute-start | bytes 393224 | tf_op jit(solution)/shard_map/ppermute | solution.py:69
  14.3 9.2 %collective-permute-start.5 = (bf16[512,128]{1,0:T(8,128)(2,1)S(1)}, bf16[512,128]{1,0:T(8,128)(2,1)S(1)}, u32[]{:S(2)}, u32[]{:S(2)}) collective-permute-start(bf16[512,128]{1,0:T(8,128)(2,1)S(1)} %pair_up.1.refs_0_), channel_id=1, source_target_pairs={{0,32},{4,132},{8,40},{12,140},{16,48},{20,148},{24,56},{28,156},{... | collective-permute-start | bytes 393224 | tf_op jit(solution)/shard_map/ppermute | solution.py:69
  17.0 6.6 %collective-permute-start.6 = (bf16[512,128]{1,0:T(8,128)(2,1)S(1)}, bf16[512,128]{1,0:T(8,128)(2,1)S(1)}, u32[]{:S(2)}, u32[]{:S(2)}) collective-permute-start(bf16[512,128]{1,0:T(8,128)(2,1)S(1)} %pair_up.1.refs_0_), channel_id=1, source_target_pairs={{0,48},{4,196},{8,56},{12,204},{16,0},{20,212},{24,8},{28,220},{32... | collective-permute-start | bytes 393224 | tf_op jit(solution)/shard_map/ppermute | solution.py:69
  26.2 6.7 %collective-permute-start.3 = (bf16[1024,128]{1,0:T(8,128)(2,1)S(1)}, bf16[1024,128]{1,0:T(8,128)(2,1)S(1)}, u32[]{:S(2)}, u32[]{:S(2)}) collective-permute-start(bf16[1024,128]{1,0:T(8,128)(2,1)S(1)} %place_low.1.refs_3_.refs_2_.refs_0_), channel_id=1, source_target_pairs={{0,64},{4,20},{8,72},{12,28},{16,80},{20,36},{24,88},{28,44},{32,9... | collective-permute-start | bytes 786440 | tf_op jit(solution)/shard_map/ppermute | solution.py:69
  26.2 9.5 %collective-permute-start.9 = (bf16[1024,128]{1,0:T(8,128)(2,1)S(1)}, bf16[1024,128]{1,0:T(8,128)(2,1)S(1)}, u32[]{:S(2)}, u32[]{:S(2)}) collective-permute-start(bf16[1024,128]{1,0:T(8,128)(2,1)S(1)} %place_high.1.refs_3_.refs_1_), channel_id=1, source_target_pairs={{0,64},{4,20},{8,72},{12,28},{16,80},{20,36},{24,88},{28,44},{32,9... | collective-permute-start | bytes 786440 | tf_op jit(solution)/shard_map/ppermute | solution.py:69
  26.4 9.3 %collective-permute-start.10 = (bf16[1024,128]{1,0:T(8,128)(2,1)S(1)}, bf16[1024,128]{1,0:T(8,128)(2,1)S(1)}, u32[]{:S(2)}, u32[]{:S(2)}) collective-permute-start(bf16[1024,128]{1,0:T(8,128)(2,1)S(1)} %place_low.1.refs_3_.refs_2_.refs_0_), channel_id=1, source_target_pairs={{0,192},{4,52},{8,200},{12,60},{16,208},{20,4},{24,216},{28,12},{3... | collective-permute-start | bytes 786440 | tf_op jit(solution)/shard_map/ppermute | solution.py:69
  29.5 8.5 %collective-permute-start.8 = (bf16[1024,128]{1,0:T(8,128)(2,1)S(1)}, bf16[1024,128]{1,0:T(8,128)(2,1)S(1)}, u32[]{:S(2)}, u32[]{:S(2)}) collective-permute-start(bf16[1024,128]{1,0:T(8,128)(2,1)S(1)} %collective-permute-done.7.refs_5_), channel_id=1, source_target_pairs={{0,192},{4,52},{8,200},{12,60},{16,208},{20,4},{24,216},{28,12},{3... | collective-permute-start | bytes 786440 | tf_op jit(solution)/shard_map/ppermute | solution.py:69
  32.9 6.7 %collective-permute-start.4 = (bf16[1024,128]{1,0:T(8,128)(2,1)S(1)}, bf16[1024,128]{1,0:T(8,128)(2,1)S(1)}, u32[]{:S(2)}, u32[]{:S(2)}) collective-permute-start(bf16[1024,128]{1,0:T(8,128)(2,1)S(1)} %collective-permute-done.3.refs_2_), channel_id=1, source_target_pairs={{0,64},{4,20},{8,72},{12,28},{16,80},{20,36},{24,88},{28,44},{32,9... | collective-permute-start | bytes 786440 | tf_op jit(solution)/shard_map/ppermute | solution.py:69
  45.7 7.2 %collective-permute-start.13 = (bf16[256,128]{1,0:T(8,128)(2,1)S(1)}, bf16[256,128]{1,0:T(8,128)(2,1)S(1)}, u32[]{:S(2)}, u32[]{:S(2)}) collective-permute-start(bf16[256,128]{1,0:T(8,128)(2,1)S(1)} %get-tuple-element.35), channel_id=1, source_target_pairs={{0,2},{1,3},{2,0},{3,1},{4,6},{5,7},{6,4},{7,5},{8,10},{9,11},{10,... | collective-permute-start | bytes 196616 | tf_op jit(solution)/shard_map/ppermute | solution.py:95
  55.2 6.3 %collective-permute-start.17 = (bf16[320,128]{1,0:T(8,128)(2,1)S(1)}, bf16[320,128]{1,0:T(8,128)(2,1)S(1)}, u32[]{:S(2)}, u32[]{:S(2)}) collective-permute-start(bf16[320,128]{1,0:T(8,128)(2,1)S(1)} %get-tuple-element.41), channel_id=1, source_target_pairs={{0,1},{1,2},{2,3},{3,0},{4,5},{5,6},{6,7},{7,4},{8,9},{9,10},{10,1... | collective-permute-start | bytes 245768 | tf_op jit(solution)/shard_map/ppermute | solution.py:95
  63.9 6.2 %collective-permute-start.20 = (bf16[4288,128]{1,0:T(8,128)(2,1)S(1)}, bf16[4288,128]{1,0:T(8,128)(2,1)S(1)}, u32[]{:S(2)}, u32[]{:S(2)}) collective-permute-start(bf16[4288,128]{1,0:T(8,128)(2,1)S(1)} %get-tuple-element.44.refs_6_), channel_id=1, source_target_pairs={{0,4},{4,0},{8,12},{12,8},{16,20},{20,16},{24,28},{28,24},{32,36},... | collective-permute-start | bytes 3293192 | tf_op jit(solution)/shard_map/ppermute | solution.py:69
  69.9 9.1 %collective-permute-start.19 = (bf16[4096,128]{1,0:T(8,128)(2,1)S(1)}, bf16[4096,128]{1,0:T(8,128)(2,1)S(1)}, u32[]{:S(2)}, u32[]{:S(2)}) collective-permute-start(bf16[4096,128]{1,0:T(8,128)(2,1)S(1)} %backward_slots.5.refs_9_), channel_id=1, source_target_pairs={{0,4},{4,0},{8,12},{12,8},{16,20},{20,16},{24,28},{28,24},{32,36},... | collective-permute-start | bytes 3145736 | tf_op jit(solution)/shard_map/ppermute | solution.py:69
  72.4 9.6 %collective-permute-start.21 = (bf16[2048,128]{1,0:T(8,128)(2,1)S(1)}, bf16[2048,128]{1,0:T(8,128)(2,1)S(1)}, u32[]{:S(2)}, u32[]{:S(2)}) collective-permute-start(bf16[2048,128]{1,0:T(8,128)(2,1)S(1)} %get-tuple-element.46.refs_7_), channel_id=1, source_target_pairs={{0,64},{4,20},{8,72},{12,28},{16,80},{20,36},{24,88},{28,44},{32,9... | collective-permute-start | bytes 1572872 | tf_op jit(solution)/shard_map/ppermute | solution.py:69
  72.8 9.2 %collective-permute-start.22 = (bf16[2048,128]{1,0:T(8,128)(2,1)S(1)}, bf16[2048,128]{1,0:T(8,128)(2,1)S(1)}, u32[]{:S(2)}, u32[]{:S(2)}) collective-permute-start(bf16[2048,128]{1,0:T(8,128)(2,1)S(1)} %get-tuple-element.48), channel_id=1, source_target_pairs={{0,192},{4,52},{8,200},{12,60},{16,208},{20,4},{24,216},{28,12},{3... | collective-permute-start | bytes 1572872 | tf_op jit(solution)/shard_map/ppermute | solution.py:69
  75.2 6.5 %collective-permute-start.23 = (bf16[64,128]{1,0:T(8,128)(2,1)S(1)}, bf16[64,128]{1,0:T(8,128)(2,1)S(1)}, u32[]{:S(2)}, u32[]{:S(2)}) collective-permute-start(bf16[64,128]{1,0:T(8,128)(2,1)S(1)} %get-tuple-element.51.own), channel_id=1, source_target_pairs={{0,8},{4,12},{8,0},{12,4},{16,24},{20,28},{24,16},{28,20},{32,40},... | collective-permute-start | bytes 49160 | tf_op jit(solution)/shard_map/ppermute | solution.py:69
  82.2 7.7 %collective-permute-start.24 = (bf16[1088,128]{1,0:T(8,128)(2,1)S(1)}, bf16[1088,128]{1,0:T(8,128)(2,1)S(1)}, u32[]{:S(2)}, u32[]{:S(2)}) collective-permute-start(bf16[1088,128]{1,0:T(8,128)(2,1)S(1)} %get-tuple-element.52), channel_id=1, source_target_pairs={{0,64},{4,20},{8,72},{12,28},{16,80},{20,36},{24,88},{28,44},{32,9... | collective-permute-start | bytes 835592 | tf_op jit(solution)/shard_map/ppermute | solution.py:69
  82.2 7.7 %collective-permute-start.25 = (bf16[1088,128]{1,0:T(8,128)(2,1)S(1)}, bf16[1088,128]{1,0:T(8,128)(2,1)S(1)}, u32[]{:S(2)}, u32[]{:S(2)}) collective-permute-start(bf16[1088,128]{1,0:T(8,128)(2,1)S(1)} %get-tuple-element.53), channel_id=1, source_target_pairs={{0,192},{4,52},{8,200},{12,60},{16,208},{20,4},{24,216},{28,12},{3... | collective-permute-start | bytes 835592 | tf_op jit(solution)/shard_map/ppermute | solution.py:69
  90.1 6.0 %collective-permute-start.27 = (bf16[704,128]{1,0:T(8,128)(2,1)S(1)}, bf16[704,128]{1,0:T(8,128)(2,1)S(1)}, u32[]{:S(2)}, u32[]{:S(2)}) collective-permute-start(bf16[704,128]{1,0:T(8,128)(2,1)S(1)} %get-tuple-element.56), channel_id=1, source_target_pairs={{0,32},{4,132},{8,40},{12,140},{16,48},{20,148},{24,56},{28,156},{... | collective-permute-start | bytes 540680 | tf_op jit(solution)/shard_map/ppermute | solution.py:69
  90.2 7.9 %collective-permute-start.28 = (bf16[704,128]{1,0:T(8,128)(2,1)S(1)}, bf16[704,128]{1,0:T(8,128)(2,1)S(1)}, u32[]{:S(2)}, u32[]{:S(2)}) collective-permute-start(bf16[704,128]{1,0:T(8,128)(2,1)S(1)} %get-tuple-element.57), channel_id=1, source_target_pairs={{0,16},{4,68},{8,24},{12,76},{16,32},{20,84},{24,40},{28,92},{32,4... | collective-permute-start | bytes 540680 | tf_op jit(solution)/shard_map/ppermute | solution.py:69
  90.9 7.2 %collective-permute-start.29 = (bf16[704,128]{1,0:T(8,128)(2,1)S(1)}, bf16[704,128]{1,0:T(8,128)(2,1)S(1)}, u32[]{:S(2)}, u32[]{:S(2)}) collective-permute-start(bf16[704,128]{1,0:T(8,128)(2,1)S(1)} %get-tuple-element.58), channel_id=1, source_target_pairs={{0,48},{4,196},{8,56},{12,204},{16,0},{20,212},{24,8},{28,220},{32... | collective-permute-start | bytes 540680 | tf_op jit(solution)/shard_map/ppermute | solution.py:69
  98.2 14.2 %collective-permute-start.30 = (bf16[256,128]{1,0:T(8,128)(2,1)S(1)}, bf16[256,128]{1,0:T(8,128)(2,1)S(1)}, u32[]{:S(2)}, u32[]{:S(2)}) collective-permute-start(bf16[256,128]{1,0:T(8,128)(2,1)S(1)} %get-tuple-element.60), channel_id=1, source_target_pairs={{0,0},{4,12},{8,8},{12,4},{16,16},{20,28},{24,24},{28,20},{32,32},... | collective-permute-start | bytes 196616 | tf_op jit(solution)/shard_map/ppermute | solution.py:69
  104.1 8.3 %collective-permute-start.31 = (bf16[256,128]{1,0:T(8,128)(2,1)S(1)}, bf16[256,128]{1,0:T(8,128)(2,1)S(1)}, u32[]{:S(2)}, u32[]{:S(2)}) collective-permute-start(bf16[256,128]{1,0:T(8,128)(2,1)S(1)} %get-tuple-element.61), channel_id=1, source_target_pairs={{0,4},{4,8},{8,12},{12,0},{16,20},{20,24},{24,28},{28,16},{32,36},... | collective-permute-start | bytes 196616 | tf_op jit(solution)/shard_map/ppermute | solution.py:69
  (15 other events, 86.3 us)

commit v11 on v10

--- a/solution.py
+++ b/solution.py
@@ -33,11 +33,12 @@
     return [(flip, e, d, u) for d in ds for u in range(2)]
 
 
+GATHERED = (0, 2, 1, 3)
 FORWARD_GROUPS = [
-    [group(0, 0)],
-    [group(0, 1), group(0, 3)],
-    [group(1, 0), group(1, 1), group(1, 3)],
-    [group(0, 2), group(1, 2)],
+    [group(0, 0, GATHERED)],
+    [group(0, 1, GATHERED), group(0, 3, GATHERED)],
+    [group(1, 0, GATHERED), group(1, 1, GATHERED), group(1, 3, GATHERED)],
+    [group(0, 2, GATHERED), group(1, 2, GATHERED)],
 ]
 LOW, HIGH = (0, 1), (2, 3)
 BACKWARD_GROUPS = [
@@ -474,9 +475,9 @@
     pair = pair_up(near_unit, far_unit)
     x2, x1, x3 = small_axis(pair, 2), small_axis(pair, 1), small_axis(pair, 3)
     touched = touch(meta, stored)
-    (low,) = place("place_low", [[(0, 0, 2), (1, 0, 2)]], [pair, x1])
+    (low,) = place("place_low", [[(0, 0, 2), (1, 0, 2)]], [pair, x2])
     n1_low, n3_low = large_axis(low, 1), large_axis(low, 3)
-    (high,) = place("place_high", [[(0, 0, 2), (1, 0, 2)]], [x2, x3], [touched, low])
+    (high,) = place("place_high", [[(0, 0, 2), (1, 0, 2)]], [x1, x3], [touched, low])
     n1_high, n3_high = large_axis(high, 1), large_axis(high, 3)
     (acc,) = forward(meta, stored, 0, [low, high], None, False)
     f1, f3 = large_axis(n1_low, 1), large_axis(n3_high, 3)

time: 113 us -> 114 us (level)
  no operation moved by 1% of the time
where the time goes in v11:
time: 114 us
  starting transfers between devices  65.3 us (57%)
  waiting for transfers between devices  22.2 us (19%)
  Pallas kernels  19.5 us (17%)
  local copies, waits for them, and re-layouts  5.16 us (5%)
    ppermute x26, starting transfers between devices, row_permute(): return lax.ppermute(array, 'row', pairs)  52 us
    ppermute x26, waiting for transfers between devices, row_permute(): return lax.ppermute(array, 'row', pairs)  14.9 us
    ppermute x9, starting transfers between devices, turn(): return lax.ppermute(array, 'rep', [(q, (q + d) % 4) for q in range(4)])  13.3 us
    pallas_call x4, Pallas kernels, backward(): pl.pallas_call(functools.partial(backward_kernel, first_section, sizes, a...  9.22 us
    ppermute x9, waiting for transfers between devices, turn(): return lax.ppermute(array, 'rep', [(q, (q + d) % 4) for q in range(4)])  7.34 us
    pallas_call x4, Pallas kernels, forward(): pl.pallas_call(functools.partial(forward_kernel, first_section, sizes, fi...  7.13 us
    unnamed x9, local copies, waits for them, and re-layouts  4.21 us
  transfers between devices with their start and end apart: 35, of which 13 were waited for; matrix products, arithmetic and copies ran while one was open for 2% of the time, Pallas kernels for 11%

profile of v11, /device:TPU:1, one launch (start us, length us, event | category | flops | bytes accessed | tf_op | source)
XLA Modules:
  0.0 113.9 jit_solution(17502235063716080329)
XLA Ops:
  0.6 3.3 %collective-permute-start = (bf16[256,128]{1,0:T(8,128)(2,1)}, bf16[256,128]{1,0:T(8,128)(2,1)S(1)}, u32[]{:S(2)}, u32[]{:S(2)}) collective-permute-start(bf16[256,128]{1,0:T(8,128)(2,1)} %param.14), channel_id=1, source_target_pairs={{0,12},{4,0},{8,4},{12,8},{16,28},{20,16},{24,20},{28,24},{32,44},... | collective-permute-start | bytes 196616 | tf_op jit(solution)/shard_map/ppermute | solution.py:70
  3.9 7.1 %collective-permute-start.1 = (bf16[256,128]{1,0:T(8,128)(2,1)}, bf16[256,128]{1,0:T(8,128)(2,1)S(1)}, u32[]{:S(2)}, u32[]{:S(2)}) collective-permute-start(bf16[256,128]{1,0:T(8,128)(2,1)} %param.14), channel_id=1, source_target_pairs={{0,0},{4,12},{8,8},{12,4},{16,16},{20,28},{24,24},{28,20},{32,32},... | collective-permute-start | bytes 196616 | tf_op jit(solution)/shard_map/ppermute | solution.py:70
  13.1 2.9 %collective-permute-start.2 = (bf16[512,128]{1,0:T(8,128)(2,1)S(1)}, bf16[512,128]{1,0:T(8,128)(2,1)S(1)}, u32[]{:S(2)}, u32[]{:S(2)}) collective-permute-start(bf16[512,128]{1,0:T(8,128)(2,1)S(1)} %pair_up.1.refs_0_), channel_id=1, source_target_pairs={{0,32},{4,132},{8,40},{12,140},{16,48},{20,148},{24,56},{28,156},{... | collective-permute-start | bytes 393224 | tf_op jit(solution)/shard_map/ppermute | solution.py:70
  16.4 2.3 %collective-permute-start.6 = (bf16[512,128]{1,0:T(8,128)(2,1)S(1)}, bf16[512,128]{1,0:T(8,128)(2,1)S(1)}, u32[]{:S(2)}, u32[]{:S(2)}) collective-permute-start(bf16[512,128]{1,0:T(8,128)(2,1)S(1)} %pair_up.1.refs_0_), channel_id=1, source_target_pairs={{0,48},{4,196},{8,56},{12,204},{16,0},{20,212},{24,8},{28,220},{32... | collective-permute-start | bytes 393224 | tf_op jit(solution)/shard_map/ppermute | solution.py:70
  20.2 3.4 %copy-done = bf16[1,1,256,128,128]{4,3,2,1,0:T(8,128)(2,1)S(1)} copy-done((bf16[1,1,256,128,128]{4,3,2,1,0:T(8,128)(2,1)S(1)}, bf16[1,1,256,128,128]{4,3,2,1,0:T(8,128)(2,1)}, u32[]{:S(2)}) %copy-start) | copy-done | bytes 8388632
  24.2 2.6 %collective-permute-start.7 = (bf16[1024,128]{1,0:T(8,128)(2,1)S(1)}, bf16[1024,128]{1,0:T(8,128)(2,1)S(1)}, u32[]{:S(2)}, u32[]{:S(2)}) collective-permute-start(bf16[1024,128]{1,0:T(8,128)(2,1)S(1)} %place_high.1.refs_3_.refs_1_), channel_id=1, source_target_pairs={{0,192},{4,52},{8,200},{12,60},{16,208},{20,4},{24,216},{28,12},{3... | collective-permute-start | bytes 786440 | tf_op jit(solution)/shard_map/ppermute | solution.py:70
  27.0 2.5 %collective-permute-start.10 = (bf16[1024,128]{1,0:T(8,128)(2,1)S(1)}, bf16[1024,128]{1,0:T(8,128)(2,1)S(1)}, u32[]{:S(2)}, u32[]{:S(2)}) collective-permute-start(bf16[1024,128]{1,0:T(8,128)(2,1)S(1)} %place_low.1.refs_3_.refs_2_.refs_0_), channel_id=1, source_target_pairs={{0,192},{4,52},{8,200},{12,60},{16,208},{20,4},{24,216},{28,12},{3... | collective-permute-start | bytes 786440 | tf_op jit(solution)/shard_map/ppermute | solution.py:70
  30.1 3.4 %collective-permute-start.8 = (bf16[1024,128]{1,0:T(8,128)(2,1)S(1)}, bf16[1024,128]{1,0:T(8,128)(2,1)S(1)}, u32[]{:S(2)}, u32[]{:S(2)}) collective-permute-start(bf16[1024,128]{1,0:T(8,128)(2,1)S(1)} %collective-permute-done.7.refs_5_), channel_id=1, source_target_pairs={{0,192},{4,52},{8,200},{12,60},{16,208},{20,4},{24,216},{28,12},{3... | collective-permute-start | bytes 786440 | tf_op jit(solution)/shard_map/ppermute | solution.py:70
  41.8 2.5 %forward_slots.6.refs_4_ = f32[8,128,128]{2,1,0:T(8,128)S(1)} custom-call(s32[961]{0:T(1024)S(1)} %concatenate.3.meta.refs_0_, bf16[256,128,128]{2,1,0:T(8,128)(2,1)S(1)} %bitcast.6, bf16[6144,128]{1,0:T(8,128)(2,1)S(1)} %collective-permute-done.12.refs_2_, f32[8,128,128]{2,1,0:T(8,128)S(1)} %forward_slots.5.refs_2_.refs_3_), custom_call_target="tpu_custom_call" | custom-call | flops 12582912 | bytes 12582912 | tf_op jit(solution)/shard_map/forward_slots/pallas_call | solution.py:223
  48.5 2.5 %collective-permute-start.15 = (bf16[256,128]{1,0:T(8,128)(2,1)S(1)}, bf16[256,128]{1,0:T(8,128)(2,1)S(1)}, u32[]{:S(2)}, u32[]{:S(2)}) collective-permute-start(bf16[256,128]{1,0:T(8,128)(2,1)S(1)} %get-tuple-element.37), channel_id=1, source_target_pairs={{0,3},{1,0},{2,1},{3,2},{4,7},{5,4},{6,5},{7,6},{8,11},{9,8},{10,9... | collective-permute-start | bytes 196616 | tf_op jit(solution)/shard_map/ppermute | solution.py:96
  51.0 2.5 %collective-permute-done.13.p1 = bf16[256,128]{1,0:T(8,128)(2,1)S(1)} collective-permute-done((bf16[256,128]{1,0:T(8,128)(2,1)S(1)}, bf16[256,128]{1,0:T(8,128)(2,1)S(1)}, u32[]{:S(2)}, u32[]{:S(2)}) %collective-permute-start.13) | collective-permute-done | bytes 65568 | tf_op jit(solution)/shard_map/ppermute | solution.py:96
  59.1 3.0 %collective-permute-done.17.refs_4_.refs_8_ = bf16[320,128]{1,0:T(8,128)(2,1)S(1)} collective-permute-done((bf16[320,128]{1,0:T(8,128)(2,1)S(1)}, bf16[320,128]{1,0:T(8,128)(2,1)S(1)}, u32[]{:S(2)}, u32[]{:S(2)}) %collective-permute-start.17) | collective-permute-done | bytes 81952 | tf_op jit(solution)/shard_map/ppermute | solution.py:96
  62.1 2.3 %backward_slots.4 = (bf16[4288,128]{1,0:T(8,128)(2,1)S(1)}, f32[64,128]{1,0:T(8,128)S(1)}) custom-call(s32[961]{0:T(1024)S(1)} %concatenate.3.meta.refs_0_, bf16[256,128,128]{2,1,0:T(8,128)(2,1)S(1)} %bitcast.8, bf16[256,128]{1,0:T(8,128)(2,1)S(1)} %get-tuple-element.39.refs_2_, bf16[320,128]{1,0:T(8,128)(2,1)S(1)} %collective-permute-done.16.refs_3_.refs_7_, ...), custom_call_target="tpu_custom_call" | custom-call | flops 8388608 | bytes 8388608 | tf_op jit(solution)/shard_map/backward_slots/pallas_call | solution.py:350
  64.5 3.7 %collective-permute-start.20 = (bf16[4288,128]{1,0:T(8,128)(2,1)S(1)}, bf16[4288,128]{1,0:T(8,128)(2,1)S(1)}, u32[]{:S(2)}, u32[]{:S(2)}) collective-permute-start(bf16[4288,128]{1,0:T(8,128)(2,1)S(1)} %get-tuple-element.44.refs_6_), channel_id=1, source_target_pairs={{0,4},{4,0},{8,12},{12,8},{16,20},{20,16},{24,28},{28,24},{32,36},... | collective-permute-start | bytes 3293192 | tf_op jit(solution)/shard_map/ppermute | solution.py:70
  68.2 2.3 %backward_slots.5.refs_9_ = bf16[4096,128]{1,0:T(8,128)(2,1)S(1)} custom-call(s32[961]{0:T(1024)S(1)} %concatenate.3.meta.refs_0_, bf16[256,128,128]{2,1,0:T(8,128)(2,1)S(1)} %bitcast.9, bf16[256,128]{1,0:T(8,128)(2,1)S(1)} %get-tuple-element.39.refs_2_, bf16[320,128]{1,0:T(8,128)(2,1)S(1)} %collective-permute-done.16.refs_3_.refs_7_, ...), custom_call_target="tpu_custom_call" | custom-call | flops 8388608 | bytes 8388608 | tf_op jit(solution)/shard_map/backward_slots/pallas_call | solution.py:350
  70.7 2.3 %backward_slots.6 = (bf16[2048,128]{1,0:T(8,128)(2,1)S(1)}, bf16[2048,128]{1,0:T(8,128)(2,1)S(1)}, bf16[64,128]{1,0:T(8,128)(2,1)S(1)}) custom-call(s32[961]{0:T(1024)S(1)} %concatenate.3.meta.refs_0_, bf16[256,128,128]{2,1,0:T(8,128)(2,1)S(1)} %bitcast.10, bf16[256,128]{1,0:T(8,128)(2,1)S(1)} %get-tuple-element.39.refs_2_, ...), custom_call_target="tpu_custom_call" | custom-call | flops 17179869184 | bytes 17179869184 | tf_op jit(solution)/shard_map/backward_slots/pallas_call | solution.py:350
  73.1 2.7 %collective-permute-start.22 = (bf16[2048,128]{1,0:T(8,128)(2,1)S(1)}, bf16[2048,128]{1,0:T(8,128)(2,1)S(1)}, u32[]{:S(2)}, u32[]{:S(2)}) collective-permute-start(bf16[2048,128]{1,0:T(8,128)(2,1)S(1)} %get-tuple-element.48), channel_id=1, source_target_pairs={{0,192},{4,52},{8,200},{12,60},{16,208},{20,4},{24,216},{28,12},{3... | collective-permute-start | bytes 1572872 | tf_op jit(solution)/shard_map/ppermute | solution.py:70
  75.8 3.8 %collective-permute-start.23 = (bf16[64,128]{1,0:T(8,128)(2,1)S(1)}, bf16[64,128]{1,0:T(8,128)(2,1)S(1)}, u32[]{:S(2)}, u32[]{:S(2)}) collective-permute-start(bf16[64,128]{1,0:T(8,128)(2,1)S(1)} %get-tuple-element.51.own), channel_id=1, source_target_pairs={{0,8},{4,12},{8,0},{12,4},{16,24},{20,28},{24,16},{28,20},{32,40},... | collective-permute-start | bytes 49160 | tf_op jit(solution)/shard_map/ppermute | solution.py:70
  79.6 2.2 %backward_slots.7 = (bf16[1024,128]{1,0:T(8,128)(2,1)S(1)}, bf16[1024,128]{1,0:T(8,128)(2,1)S(1)}, bf16[2048,128]{1,0:T(8,128)(2,1)S(1)}) custom-call(s32[961]{0:T(1024)S(1)} %concatenate.3.meta.refs_0_, bf16[256,128,128]{2,1,0:T(8,128)(2,1)S(1)} %bitcast.11, bf16[256,128]{1,0:T(8,128)(2,1)S(1)} %get-tuple-element.39.refs_2_, ...), custom_call_target="tpu_custom_call" | custom-call | flops 8388608 | bytes 8388608 | tf_op jit(solution)/shard_map/backward_slots/pallas_call | solution.py:350
  82.9 2.7 %collective-permute-start.25 = (bf16[1088,128]{1,0:T(8,128)(2,1)S(1)}, bf16[1088,128]{1,0:T(8,128)(2,1)S(1)}, u32[]{:S(2)}, u32[]{:S(2)}) collective-permute-start(bf16[1088,128]{1,0:T(8,128)(2,1)S(1)} %get-tuple-element.53), channel_id=1, source_target_pairs={{0,192},{4,52},{8,200},{12,60},{16,208},{20,4},{24,216},{28,12},{3... | collective-permute-start | bytes 835592 | tf_op jit(solution)/shard_map/ppermute | solution.py:70
  86.4 4.1 %collective-permute-done.26.two = bf16[64,128]{1,0:T(8,128)(2,1)S(1)} collective-permute-done((bf16[64,128]{1,0:T(8,128)(2,1)S(1)}, bf16[64,128]{1,0:T(8,128)(2,1)S(1)}, u32[]{:S(2)}, u32[]{:S(2)}) %collective-permute-start.26) | collective-permute-done | bytes 16416 | tf_op jit(solution)/shard_map/ppermute | solution.py:70
  93.6 3.2 %collective-permute-done.27.b = bf16[704,128]{1,0:T(8,128)(2,1)S(1)} collective-permute-done((bf16[704,128]{1,0:T(8,128)(2,1)S(1)}, bf16[704,128]{1,0:T(8,128)(2,1)S(1)}, u32[]{:S(2)}, u32[]{:S(2)}) %collective-permute-start.27) | collective-permute-done | bytes 180256 | tf_op jit(solution)/shard_map/ppermute | solution.py:70
  98.8 5.7 %collective-permute-start.30 = (bf16[256,128]{1,0:T(8,128)(2,1)S(1)}, bf16[256,128]{1,0:T(8,128)(2,1)S(1)}, u32[]{:S(2)}, u32[]{:S(2)}) collective-permute-start(bf16[256,128]{1,0:T(8,128)(2,1)S(1)} %get-tuple-element.60), channel_id=1, source_target_pairs={{0,0},{4,12},{8,8},{12,4},{16,16},{20,28},{24,24},{28,20},{32,32},... | collective-permute-start | bytes 196616 | tf_op jit(solution)/shard_map/ppermute | solution.py:70
  104.5 2.6 %collective-permute-start.31 = (bf16[256,128]{1,0:T(8,128)(2,1)S(1)}, bf16[256,128]{1,0:T(8,128)(2,1)S(1)}, u32[]{:S(2)}, u32[]{:S(2)}) collective-permute-start(bf16[256,128]{1,0:T(8,128)(2,1)S(1)} %get-tuple-element.61), channel_id=1, source_target_pairs={{0,4},{4,8},{8,12},{12,0},{16,20},{20,24},{24,28},{28,16},{32,36},... | collective-permute-start | bytes 196616 | tf_op jit(solution)/shard_map/ppermute | solution.py:70
  (77 shorter events, 37.1 us)
Async XLA Ops:
  0.6 11.5 %collective-permute-start = (bf16[256,128]{1,0:T(8,128)(2,1)}, bf16[256,128]{1,0:T(8,128)(2,1)S(1)}, u32[]{:S(2)}, u32[]{:S(2)}) collective-permute-start(bf16[256,128]{1,0:T(8,128)(2,1)} %param.14), channel_id=1, source_target_pairs={{0,12},{4,0},{8,4},{12,8},{16,28},{20,16},{24,20},{28,24},{32,44},... | collective-permute-start | bytes 196616 | tf_op jit(solution)/shard_map/ppermute | solution.py:70
  3.9 9.1 %collective-permute-start.1 = (bf16[256,128]{1,0:T(8,128)(2,1)}, bf16[256,128]{1,0:T(8,128)(2,1)S(1)}, u32[]{:S(2)}, u32[]{:S(2)}) collective-permute-start(bf16[256,128]{1,0:T(8,128)(2,1)} %param.14), channel_id=1, source_target_pairs={{0,0},{4,12},{8,8},{12,4},{16,16},{20,28},{24,24},{28,20},{32,32},... | collective-permute-start | bytes 196616 | tf_op jit(solution)/shard_map/ppermute | solution.py:70
  13.1 11.1 %collective-permute-start.2 = (bf16[512,128]{1,0:T(8,128)(2,1)S(1)}, bf16[512,128]{1,0:T(8,128)(2,1)S(1)}, u32[]{:S(2)}, u32[]{:S(2)}) collective-permute-start(bf16[512,128]{1,0:T(8,128)(2,1)S(1)} %pair_up.1.refs_0_), channel_id=1, source_target_pairs={{0,32},{4,132},{8,40},{12,140},{16,48},{20,148},{24,56},{28,156},{... | collective-permute-start | bytes 393224 | tf_op jit(solution)/shard_map/ppermute | solution.py:70
  16.0 8.2 %collective-permute-start.5 = (bf16[512,128]{1,0:T(8,128)(2,1)S(1)}, bf16[512,128]{1,0:T(8,128)(2,1)S(1)}, u32[]{:S(2)}, u32[]{:S(2)}) collective-permute-start(bf16[512,128]{1,0:T(8,128)(2,1)S(1)} %pair_up.1.refs_0_), channel_id=1, source_target_pairs={{0,16},{4,68},{8,24},{12,76},{16,32},{20,84},{24,40},{28,92},{32,4... | collective-permute-start | bytes 393224 | tf_op jit(solution)/shard_map/ppermute | solution.py:70
  16.4 7.8 %collective-permute-start.6 = (bf16[512,128]{1,0:T(8,128)(2,1)S(1)}, bf16[512,128]{1,0:T(8,128)(2,1)S(1)}, u32[]{:S(2)}, u32[]{:S(2)}) collective-permute-start(bf16[512,128]{1,0:T(8,128)(2,1)S(1)} %pair_up.1.refs_0_), channel_id=1, source_target_pairs={{0,48},{4,196},{8,56},{12,204},{16,0},{20,212},{24,8},{28,220},{32... | collective-permute-start | bytes 393224 | tf_op jit(solution)/shard_map/ppermute | solution.py:70
  26.8 6.7 %collective-permute-start.3 = (bf16[1024,128]{1,0:T(8,128)(2,1)S(1)}, bf16[1024,128]{1,0:T(8,128)(2,1)S(1)}, u32[]{:S(2)}, u32[]{:S(2)}) collective-permute-start(bf16[1024,128]{1,0:T(8,128)(2,1)S(1)} %place_low.1.refs_3_.refs_2_.refs_0_), channel_id=1, source_target_pairs={{0,64},{4,20},{8,72},{12,28},{16,80},{20,36},{24,88},{28,44},{32,9... | collective-permute-start | bytes 786440 | tf_op jit(solution)/shard_map/ppermute | solution.py:70
  26.8 9.5 %collective-permute-start.9 = (bf16[1024,128]{1,0:T(8,128)(2,1)S(1)}, bf16[1024,128]{1,0:T(8,128)(2,1)S(1)}, u32[]{:S(2)}, u32[]{:S(2)}) collective-permute-start(bf16[1024,128]{1,0:T(8,128)(2,1)S(1)} %place_high.1.refs_3_.refs_1_), channel_id=1, source_target_pairs={{0,64},{4,20},{8,72},{12,28},{16,80},{20,36},{24,88},{28,44},{32,9... | collective-permute-start | bytes 786440 | tf_op jit(solution)/shard_map/ppermute | solution.py:70
  27.0 9.3 %collective-permute-start.10 = (bf16[1024,128]{1,0:T(8,128)(2,1)S(1)}, bf16[1024,128]{1,0:T(8,128)(2,1)S(1)}, u32[]{:S(2)}, u32[]{:S(2)}) collective-permute-start(bf16[1024,128]{1,0:T(8,128)(2,1)S(1)} %place_low.1.refs_3_.refs_2_.refs_0_), channel_id=1, source_target_pairs={{0,192},{4,52},{8,200},{12,60},{16,208},{20,4},{24,216},{28,12},{3... | collective-permute-start | bytes 786440 | tf_op jit(solution)/shard_map/ppermute | solution.py:70
  30.1 8.5 %collective-permute-start.8 = (bf16[1024,128]{1,0:T(8,128)(2,1)S(1)}, bf16[1024,128]{1,0:T(8,128)(2,1)S(1)}, u32[]{:S(2)}, u32[]{:S(2)}) collective-permute-start(bf16[1024,128]{1,0:T(8,128)(2,1)S(1)} %collective-permute-done.7.refs_5_), channel_id=1, source_target_pairs={{0,192},{4,52},{8,200},{12,60},{16,208},{20,4},{24,216},{28,12},{3... | collective-permute-start | bytes 786440 | tf_op jit(solution)/shard_map/ppermute | solution.py:70
  33.5 6.7 %collective-permute-start.4 = (bf16[1024,128]{1,0:T(8,128)(2,1)S(1)}, bf16[1024,128]{1,0:T(8,128)(2,1)S(1)}, u32[]{:S(2)}, u32[]{:S(2)}) collective-permute-start(bf16[1024,128]{1,0:T(8,128)(2,1)S(1)} %collective-permute-done.3.refs_2_), channel_id=1, source_target_pairs={{0,64},{4,20},{8,72},{12,28},{16,80},{20,36},{24,88},{28,44},{32,9... | collective-permute-start | bytes 786440 | tf_op jit(solution)/shard_map/ppermute | solution.py:70
  46.3 7.3 %collective-permute-start.13 = (bf16[256,128]{1,0:T(8,128)(2,1)S(1)}, bf16[256,128]{1,0:T(8,128)(2,1)S(1)}, u32[]{:S(2)}, u32[]{:S(2)}) collective-permute-start(bf16[256,128]{1,0:T(8,128)(2,1)S(1)} %get-tuple-element.35), channel_id=1, source_target_pairs={{0,2},{1,3},{2,0},{3,1},{4,6},{5,7},{6,4},{7,5},{8,10},{9,11},{10,... | collective-permute-start | bytes 196616 | tf_op jit(solution)/shard_map/ppermute | solution.py:96
  55.8 6.3 %collective-permute-start.17 = (bf16[320,128]{1,0:T(8,128)(2,1)S(1)}, bf16[320,128]{1,0:T(8,128)(2,1)S(1)}, u32[]{:S(2)}, u32[]{:S(2)}) collective-permute-start(bf16[320,128]{1,0:T(8,128)(2,1)S(1)} %get-tuple-element.41), channel_id=1, source_target_pairs={{0,1},{1,2},{2,3},{3,0},{4,5},{5,6},{6,7},{7,4},{8,9},{9,10},{10,1... | collective-permute-start | bytes 245768 | tf_op jit(solution)/shard_map/ppermute | solution.py:96
  64.5 6.2 %collective-permute-start.20 = (bf16[4288,128]{1,0:T(8,128)(2,1)S(1)}, bf16[4288,128]{1,0:T(8,128)(2,1)S(1)}, u32[]{:S(2)}, u32[]{:S(2)}) collective-permute-start(bf16[4288,128]{1,0:T(8,128)(2,1)S(1)} %get-tuple-element.44.refs_6_), channel_id=1, source_target_pairs={{0,4},{4,0},{8,12},{12,8},{16,20},{20,16},{24,28},{28,24},{32,36},... | collective-permute-start | bytes 3293192 | tf_op jit(solution)/shard_map/ppermute | solution.py:70
  70.6 9.0 %collective-permute-start.19 = (bf16[4096,128]{1,0:T(8,128)(2,1)S(1)}, bf16[4096,128]{1,0:T(8,128)(2,1)S(1)}, u32[]{:S(2)}, u32[]{:S(2)}) collective-permute-start(bf16[4096,128]{1,0:T(8,128)(2,1)S(1)} %backward_slots.5.refs_9_), channel_id=1, source_target_pairs={{0,4},{4,0},{8,12},{12,8},{16,20},{20,16},{24,28},{28,24},{32,36},... | collective-permute-start | bytes 3145736 | tf_op jit(solution)/shard_map/ppermute | solution.py:70
  73.0 9.6 %collective-permute-start.21 = (bf16[2048,128]{1,0:T(8,128)(2,1)S(1)}, bf16[2048,128]{1,0:T(8,128)(2,1)S(1)}, u32[]{:S(2)}, u32[]{:S(2)}) collective-permute-start(bf16[2048,128]{1,0:T(8,128)(2,1)S(1)} %get-tuple-element.46.refs_7_), channel_id=1, source_target_pairs={{0,64},{4,20},{8,72},{12,28},{16,80},{20,36},{24,88},{28,44},{32,9... | collective-permute-start | bytes 1572872 | tf_op jit(solution)/shard_map/ppermute | solution.py:70
  73.1 9.5 %collective-permute-start.22 = (bf16[2048,128]{1,0:T(8,128)(2,1)S(1)}, bf16[2048,128]{1,0:T(8,128)(2,1)S(1)}, u32[]{:S(2)}, u32[]{:S(2)}) collective-permute-start(bf16[2048,128]{1,0:T(8,128)(2,1)S(1)} %get-tuple-element.48), channel_id=1, source_target_pairs={{0,192},{4,52},{8,200},{12,60},{16,208},{20,4},{24,216},{28,12},{3... | collective-permute-start | bytes 1572872 | tf_op jit(solution)/shard_map/ppermute | solution.py:70
  75.8 6.5 %collective-permute-start.23 = (bf16[64,128]{1,0:T(8,128)(2,1)S(1)}, bf16[64,128]{1,0:T(8,128)(2,1)S(1)}, u32[]{:S(2)}, u32[]{:S(2)}) collective-permute-start(bf16[64,128]{1,0:T(8,128)(2,1)S(1)} %get-tuple-element.51.own), channel_id=1, source_target_pairs={{0,8},{4,12},{8,0},{12,4},{16,24},{20,28},{24,16},{28,20},{32,40},... | collective-permute-start | bytes 49160 | tf_op jit(solution)/shard_map/ppermute | solution.py:70
  82.8 7.7 %collective-permute-start.24 = (bf16[1088,128]{1,0:T(8,128)(2,1)S(1)}, bf16[1088,128]{1,0:T(8,128)(2,1)S(1)}, u32[]{:S(2)}, u32[]{:S(2)}) collective-permute-start(bf16[1088,128]{1,0:T(8,128)(2,1)S(1)} %get-tuple-element.52), channel_id=1, source_target_pairs={{0,64},{4,20},{8,72},{12,28},{16,80},{20,36},{24,88},{28,44},{32,9... | collective-permute-start | bytes 835592 | tf_op jit(solution)/shard_map/ppermute | solution.py:70
  82.9 7.7 %collective-permute-start.25 = (bf16[1088,128]{1,0:T(8,128)(2,1)S(1)}, bf16[1088,128]{1,0:T(8,128)(2,1)S(1)}, u32[]{:S(2)}, u32[]{:S(2)}) collective-permute-start(bf16[1088,128]{1,0:T(8,128)(2,1)S(1)} %get-tuple-element.53), channel_id=1, source_target_pairs={{0,192},{4,52},{8,200},{12,60},{16,208},{20,4},{24,216},{28,12},{3... | collective-permute-start | bytes 835592 | tf_op jit(solution)/shard_map/ppermute | solution.py:70
  90.7 6.0 %collective-permute-start.27 = (bf16[704,128]{1,0:T(8,128)(2,1)S(1)}, bf16[704,128]{1,0:T(8,128)(2,1)S(1)}, u32[]{:S(2)}, u32[]{:S(2)}) collective-permute-start(bf16[704,128]{1,0:T(8,128)(2,1)S(1)} %get-tuple-element.56), channel_id=1, source_target_pairs={{0,32},{4,132},{8,40},{12,140},{16,48},{20,148},{24,56},{28,156},{... | collective-permute-start | bytes 540680 | tf_op jit(solution)/shard_map/ppermute | solution.py:70
  90.8 7.9 %collective-permute-start.28 = (bf16[704,128]{1,0:T(8,128)(2,1)S(1)}, bf16[704,128]{1,0:T(8,128)(2,1)S(1)}, u32[]{:S(2)}, u32[]{:S(2)}) collective-permute-start(bf16[704,128]{1,0:T(8,128)(2,1)S(1)} %get-tuple-element.57), channel_id=1, source_target_pairs={{0,16},{4,68},{8,24},{12,76},{16,32},{20,84},{24,40},{28,92},{32,4... | collective-permute-start | bytes 540680 | tf_op jit(solution)/shard_map/ppermute | solution.py:70
  91.5 7.2 %collective-permute-start.29 = (bf16[704,128]{1,0:T(8,128)(2,1)S(1)}, bf16[704,128]{1,0:T(8,128)(2,1)S(1)}, u32[]{:S(2)}, u32[]{:S(2)}) collective-permute-start(bf16[704,128]{1,0:T(8,128)(2,1)S(1)} %get-tuple-element.58), channel_id=1, source_target_pairs={{0,48},{4,196},{8,56},{12,204},{16,0},{20,212},{24,8},{28,220},{32... | collective-permute-start | bytes 540680 | tf_op jit(solution)/shard_map/ppermute | solution.py:70
  98.8 14.3 %collective-permute-start.30 = (bf16[256,128]{1,0:T(8,128)(2,1)S(1)}, bf16[256,128]{1,0:T(8,128)(2,1)S(1)}, u32[]{:S(2)}, u32[]{:S(2)}) collective-permute-start(bf16[256,128]{1,0:T(8,128)(2,1)S(1)} %get-tuple-element.60), channel_id=1, source_target_pairs={{0,0},{4,12},{8,8},{12,4},{16,16},{20,28},{24,24},{28,20},{32,32},... | collective-permute-start | bytes 196616 | tf_op jit(solution)/shard_map/ppermute | solution.py:70
  104.5 8.6 %collective-permute-start.31 = (bf16[256,128]{1,0:T(8,128)(2,1)S(1)}, bf16[256,128]{1,0:T(8,128)(2,1)S(1)}, u32[]{:S(2)}, u32[]{:S(2)}) collective-permute-start(bf16[256,128]{1,0:T(8,128)(2,1)S(1)} %get-tuple-element.61), channel_id=1, source_target_pairs={{0,4},{4,8},{8,12},{12,0},{16,20},{20,24},{24,28},{28,16},{32,36},... | collective-permute-start | bytes 196616 | tf_op jit(solution)/shard_map/ppermute | solution.py:70
  (15 other events, 86.4 us)
